TPU v7x, 128 devices: a whole 4x4x4 slice. The times are simulated.
128 devices in a mesh: row: 16 (over x_lo, z, core), col: 8 (over y, x_hi).
Axes of the slice: x: 4 (x_hi: 2, x_lo: 2; x = x_hi * 2 + x_lo), y: 4, z: 4, core: 2. Of those that a mesh axis runs over, the one named last changes fastest.
Arguments:
- pair_rep: bfloat16 [512, 512, 128], P('row', 'col'), may hold values from -12 to 12
- cotangent: bfloat16 [512, 512, 128], P('row', 'col'), may hold values from -6 to 6
- ln_gain: float32 [128], replicated, may hold values from 0.1 to 1.9
- w_query: bfloat16 [128, 128], replicated, may hold values from -9 to 9
- w_key: bfloat16 [128, 128], replicated, may hold values from -9 to 9
- w_value: bfloat16 [128, 128], replicated, may hold values from -0.5 to 0.5
- w_gate: bfloat16 [128, 128], replicated, may hold values from -0.5 to 0.5
- gate_offset: float32 [128], replicated, may hold values from -4 to 4
- w_bias: bfloat16 [128, 4], replicated, may hold values from -0.5 to 0.5
- w_out: bfloat16 [128, 128], replicated, may hold values from -0.5 to 0.5
Outputs:
- update: bfloat16 [512, 512, 128], P('row', 'col')
- grad_pair: bfloat16 [512, 512, 128], P('row', 'col')
- grad_gain: float32 [128], replicated
- grad_query: float32 [128, 128], replicated
- grad_key: float32 [128, 128], replicated
- grad_value: float32 [128, 128], replicated
- grad_gate: float32 [128, 128], replicated
- grad_offset: float32 [128], replicated
- grad_bias: float32 [128, 4], replicated
- grad_out: float32 [128, 128], replicated
All inputs are finite; a program needn't handle non-finite values.
Results may differ from a plain program's by a relative error of at most 0.035.
The roundings to bfloat16 on the way count: a program that leaves them out, or rounds other values in their place, can miss the bound.
Values may be sent and summed in bfloat16 or wider, within the bound.
No kernel may reach another device: no remote copies, remote signals or barrier semaphores. Data moves between devices by JAX's collectives and lax.ppermute only.
A program may use at most 64 MiB of HBM per device.

v0:
```python
import jax
import jax.numpy as jnp
from jax import lax
from jax.sharding import PartitionSpec as P

EPS = 1e-05


def normalize(pair_rows, ln_gain):
    values = pair_rows.astype(jnp.float32)
    average = jnp.mean(values, axis=-1, keepdims=True)
    centered = values - average
    variance = jnp.mean(centered * centered, axis=-1, keepdims=True)
    inverse = lax.rsqrt(variance + EPS)
    unit_pair = centered * inverse
    normed = (unit_pair * ln_gain).astype(jnp.bfloat16)
    return (unit_pair, inverse, normed)


def row_probs(query_row, key_row, bias_full):
    scores = jnp.einsum("jhc,khc->hjk", query_row, key_row, preferred_element_type=jnp.float32)
    return jax.nn.softmax(scores + bias_full.astype(jnp.float32), axis=-1)


def body(pair_rep, cotangent, ln_gain, w_query, w_key, w_value, w_gate, gate_offset, w_bias, w_out):
    pair_rows, cot_rows = (
        lax.all_to_all(pair_rep, "col", split_axis=0, concat_axis=1, tiled=True),
        lax.all_to_all(cotangent, "col", split_axis=0, concat_axis=1, tiled=True),
    )
    row_count, col_count, channels = pair_rows.shape
    head_count = w_bias.shape[1]
    all_heads = w_query.shape[1]
    head_size = all_heads // head_count
    positions = row_count * col_count
    query_scale = head_size ** (-0.5)
    unit_pair, inverse, normed = normalize(pair_rows, ln_gain)
    flat_normed = normed.reshape(positions, channels)

    def project(weight):
        return jnp.dot(flat_normed, weight, preferred_element_type=jnp.float32)

    bias_local = (
        project(w_bias)
        .astype(jnp.bfloat16)
        .reshape(row_count, col_count, head_count)
        .transpose(2, 0, 1)
    )
    bias_full = lax.all_gather(bias_local, ("row", "col"), axis=1, tiled=True)
    row_shape = (row_count, col_count, head_count, head_size)
    query = (project(w_query) * query_scale).astype(jnp.bfloat16).reshape(row_shape)
    keys = (project(w_key) * query_scale).astype(jnp.bfloat16).reshape(row_shape)
    values = project(w_value).astype(jnp.bfloat16).reshape(row_shape)
    gate_value = jax.nn.sigmoid(project(w_gate) + gate_offset)

    def forward_row(state_in, row_item):
        query_row, key_row, value_row = row_item
        probs_low = row_probs(query_row, key_row, bias_full).astype(jnp.bfloat16)
        return (
            state_in,
            jnp.einsum("hjk,khc->jhc", probs_low, value_row, preferred_element_type=jnp.float32),
        )

    unused, attended = lax.scan(forward_row, jnp.zeros((), jnp.float32), (query, keys, values))
    attended = attended.reshape(positions, all_heads)
    gated = (gate_value * attended).astype(jnp.bfloat16)
    update_rows = (
        jnp.dot(gated, w_out, preferred_element_type=jnp.float32)
        .astype(jnp.bfloat16)
        .reshape(row_count, col_count, channels)
    )
    flat_cot = cot_rows.reshape(positions, channels)
    grad_gated = jnp.dot(flat_cot, w_out.T, preferred_element_type=jnp.float32)
    out_part = jnp.einsum("pa,pc->ac", gated, flat_cot, preferred_element_type=jnp.float32)
    grad_att = (grad_gated * gate_value).astype(jnp.bfloat16).reshape(row_shape)
    grad_gpre = (grad_gated * attended * gate_value * (1.0 - gate_value)).astype(jnp.bfloat16)

    def backward_row(bias_grad, row_item):
        query_row, key_row, value_row, att_row = row_item
        soft_probs = row_probs(query_row, key_row, bias_full)
        probs_low = soft_probs.astype(jnp.bfloat16)
        value_grad = jnp.einsum(
            "hjk,jhc->khc", probs_low, att_row, preferred_element_type=jnp.float32
        )
        grad_probs = jnp.einsum(
            "jhc,khc->hjk", att_row, value_row, preferred_element_type=jnp.float32
        )
        score_grad = soft_probs * (
            grad_probs - jnp.sum(soft_probs * grad_probs, axis=-1, keepdims=True)
        )
        score_low = score_grad.astype(jnp.bfloat16)
        query_grad = jnp.einsum(
            "hjk,khc->jhc", score_low, key_row, preferred_element_type=jnp.float32
        )
        key_grad = jnp.einsum(
            "hjk,jhc->khc", score_low, query_row, preferred_element_type=jnp.float32
        )
        return (bias_grad + score_grad, (query_grad, key_grad, value_grad))

    bias_start = jnp.zeros((head_count, bias_full.shape[1], bias_full.shape[2]), jnp.float32)
    bias_grad, (query_grad, key_grad, value_grad) = lax.scan(
        backward_row, bias_start, (query, keys, values, grad_att)
    )
    bias_mine = lax.psum_scatter(bias_grad, ("row", "col"), scatter_dimension=1, tiled=True)
    bias_pos = bias_mine.transpose(1, 2, 0).reshape(positions, head_count)
    qpre = (query_grad.reshape(positions, all_heads) * query_scale).astype(jnp.bfloat16)
    kpre = (key_grad.reshape(positions, all_heads) * query_scale).astype(jnp.bfloat16)
    vpre = value_grad.reshape(positions, all_heads).astype(jnp.bfloat16)
    grad_normed = jnp.dot(qpre, w_query.T, preferred_element_type=jnp.float32)
    grad_normed = grad_normed + jnp.dot(kpre, w_key.T, preferred_element_type=jnp.float32)
    grad_normed = grad_normed + jnp.dot(vpre, w_value.T, preferred_element_type=jnp.float32)
    grad_normed = grad_normed + jnp.dot(grad_gpre, w_gate.T, preferred_element_type=jnp.float32)
    grad_normed = grad_normed + jnp.dot(
        bias_pos, w_bias.astype(jnp.float32).T, precision=lax.Precision.HIGHEST
    )
    query_part = jnp.einsum("pc,pa->ca", flat_normed, qpre, preferred_element_type=jnp.float32)
    key_part = jnp.einsum("pc,pa->ca", flat_normed, kpre, preferred_element_type=jnp.float32)
    value_part = jnp.einsum("pc,pa->ca", flat_normed, vpre, preferred_element_type=jnp.float32)
    gate_part = jnp.einsum("pc,pa->ca", flat_normed, grad_gpre, preferred_element_type=jnp.float32)
    offset_part = jnp.sum(grad_gpre.astype(jnp.float32), axis=0)
    bias_part = jnp.einsum("pc,ph->ch", flat_normed, bias_pos, precision=lax.Precision.HIGHEST)
    flat_unit = unit_pair.reshape(positions, channels)
    gain_part = jnp.sum(grad_normed * flat_unit, axis=0)
    scaled = grad_normed * ln_gain
    first = jnp.mean(scaled, axis=-1, keepdims=True)
    second = jnp.mean(scaled * flat_unit, axis=-1, keepdims=True)
    grad_rows = ((scaled - first - flat_unit * second) * inverse.reshape(positions, 1)).astype(
        jnp.bfloat16
    )
    grad_rows = grad_rows.reshape(row_count, col_count, channels)
    totals = lax.psum(
        (gain_part, query_part, key_part, value_part, gate_part, offset_part, bias_part, out_part),
        ("row", "col"),
    )
    update, grad_pair = (
        lax.all_to_all(update_rows, "col", split_axis=1, concat_axis=0, tiled=True),
        lax.all_to_all(grad_rows, "col", split_axis=1, concat_axis=0, tiled=True),
    )
    return (
        update,
        grad_pair,
        totals[0],
        totals[1],
        totals[2],
        totals[3],
        totals[4],
        totals[5],
        totals[6],
        totals[7],
    )


def solution(mesh):
    return jax.shard_map(
        body,
        mesh=mesh,
        in_specs=(
            P("row", "col", None),
            P("row", "col", None),
            P(),
            P(),
            P(),
            P(),
            P(),
            P(),
            P(),
            P(),
        ),
        out_specs=(
            P("row", "col", None),
            P("row", "col", None),
            P(),
            P(),
            P(),
            P(),
            P(),
            P(),
            P(),
            P(),
        ),
        check_vma=False,
    )
```

profile of v0, /device:TPU:0, one launch (start us, length us, event | category | flops | bytes accessed | tf_op | source)
XLA Modules:
  0.0 743.9 jit_solution(3879349328584850068)
XLA Ops:
  7.3 18.6 %all_to_all.60 = bf16[32,64,128]{2,1,0:T(8,128)(2,1)S(1)} all-to-all(bf16[32,64,128]{2,1,0:T(8,128)(2,1)} %param.14), channel_id=1, replica_groups=mesh['row'=16,'col'=8] {'col'}, dimensions={0} | all-to-all | bytes 1048576 | tf_op jit(solution)/shard_map/all_to_all | solution.py:27
  28.8 3.5 all-to-all-start.2
  32.4 10.6 %all-to-all-done.2 = bf16[32,64,128]{2,1,0:T(8,128)(2,1)S(1)} async-done(((bf16[32,64,128]{2,1,0:T(8,128)(2,1)}), bf16[32,64,128]{2,1,0:T(8,128)(2,1)S(1)}, u32[]{:S(2)}, u32[]{:S(2)}) %all-to-all-start.2) | async-done | bytes 524320 | tf_op jit(solution)/shard_map/all_to_all | solution.py:28
  58.4 266.4 %all-gather.2.cloned.1.call-done = bf16[4,512,512]{2,0,1:T(4,128)(2,1)} async-done(((bf16[4,4,512]{2,0,1:T(4,128)(2,1)}), bf16[4,512,512]{2,0,1:T(4,128)(2,1)}) %all-gather.2.cloned.1.call-update) | async-done | bytes 2097168 | tf_op jit(solution)/shard_map/all_gather | solution.py:48
  327.8 53.5 %while.27 = (s32[]{:T(128)}, f32[4,512,4,32]{1,0,3,2:T(4,128)}, bf16[4,512,4,32]{1,3,2,0:T(8,128)(2,1)}, bf16[4,512,4,32]{1,3,2,0:T(8,128)(2,1)}, bf16[4,512,4,3...) while((s32[]{:T(128)}, f32[4,512,4,32]{1,0,3,2:T(4,128)}, ...), condition=%wide.region_5.6_spmd, body=%wide.region_2.5_spmd.sunk | while | flops 210766848 | bytes 6179425 | solution.py:63
  330.2 3.6 fusion.187
  335.0 6.1 dynamic_update_slice.23
  343.6 3.6 fusion.187
  348.4 6.1 dynamic_update_slice.23
  356.9 3.6 fusion.187
  361.8 6.1 dynamic_update_slice.23
  370.3 3.6 fusion.187
  375.1 6.1 dynamic_update_slice.23
  386.5 3.3 convert_reduce_fusion
  398.1 78.9 %while.28 = (s32[]{:T(128)}, f32[4,512,512]{1,2,0:T(8,128)}, f32[4,512,4,32]{1,3,2,0:T(8,128)}, f32[4,512,4,32]{1,3,2,0:T(8,128)}, bf16[4,512,4,32]{1,3,2,0:T(8,...) while((s32[]{:T(128)}, f32[4,512,512]{1,2,0:T(8,128)}, ...), condition=%wide.region_10.11_spmd.clone, body=%wide.region_6.10_spmd.clone.sunk | while | flops 421528576 | bytes 92199120 | solution.py:100
  398.1 4.5 fusion.198
  402.6 3.5 fusion.202
  406.2 3.2 multiply_reduce_fusion.6
  417.9 4.5 fusion.198
  422.4 3.5 fusion.202
  425.9 3.2 multiply_reduce_fusion.6
  437.6 4.5 fusion.198
  442.1 3.5 fusion.202
  445.6 3.2 multiply_reduce_fusion.6
  457.3 4.5 fusion.198
  461.8 3.5 fusion.202
  465.3 3.2 multiply_reduce_fusion.6
  484.5 5.5 copy.120
  492.5 6.0 all-to-all-start.1
  499.9 153.1 %all-reduce.5.cloned.1.call-done = (f32[4,512,512]{2,0,1:T(4,128)}, f32[128,128]{1,0:T(8,128)}, f32[128,128]{1,0:T(8,128)}, f32[128,128]{1,0:T(8,128)}, f32[128,128]{1,0:T(8,128)}, /*index=5*/f32[128,128]{1,0:T(8,128)}) async-done(((f32[4,512,512]{2,0,1:T(4,128)}, f32[128,128]{1,0:T(8,128)}, f32[128,128]{1,0:T(8,128)}, f32[128,128]{1,0:T(8,128)}, f32[128,128]{1,0:T(8,128)}, ...) | async-done | bytes 4522000
  658.7 5.2 all-to-all-start.3
  667.0 65.9 %all-reduce.1 = (f32[128]{0:T(128)}, f32[128]{0:T(128)}, f32[128,4]{0,1:T(4,128)}) all-reduce(f32[128]{0:T(128)S(1)} %get-tuple-element.199, f32[128]{0:T(128)S(1)} %get-tuple-element.243, f32[128,4]{0,1:T(4,128)S(1)} %convolution_bitcast_fusion.2), channel_id=1, replica_groups=mesh['row'=16,'col'=8] {'row','col'}, use_global_device_ids=true, to_apply=%region_15.16 | all-reduce | flops 768 | bytes 6144 | tf_op jit(solution)/shard_map/psum | solution.py:130
  (173 shorter events, 107.0 us)
Async XLA Ops:
  7.2 379.3 %copy-start = (bf16[128,128]{1,0:T(8,128)(2,1)S(1)}, bf16[128,128]{1,0:T(8,128)(2,1)}, u32[]{:S(2)}) copy-start(bf16[128,128]{1,0:T(8,128)(2,1)} %param.20) | copy-start | bytes 98308
  7.2 20.1 %copy-start.24 = (f32[128]{0:T(128)S(1)}, f32[128]{0:T(128)}, u32[]{:S(2)}) copy-start(f32[128]{0:T(128)} %param.16) | copy-start | bytes 1540
  7.2 20.7 %copy-start.26 = (bf16[128,4]{0,1:T(4,128)(2,1)S(1)}, bf16[128,4]{0,1:T(4,128)(2,1)}, u32[]{:S(2)}) copy-start(bf16[128,4]{0,1:T(4,128)(2,1)} %param.22) | copy-start | bytes 3076
  7.2 317.6 %all-gather.2.cloned.1.call-start = ((), (), s32[]{:S(2)}) async-start(), calls=%async_computation.4 | async-start | bytes 2113536 | tf_op jit(solution)/shard_map/all_gather | solution.py:48
  26.0 17.1 %copy-start.15 = (bf16[128,128]{1,0:T(8,128)(2,1)S(1)}, bf16[128,128]{1,0:T(8,128)(2,1)}, u32[]{:S(2)}) copy-start(bf16[128,128]{1,0:T(8,128)(2,1)} %param.18) | copy-start | bytes 98308
  27.3 21.2 %copy-start.14 = (bf16[128,128]{1,0:T(8,128)(2,1)S(1)}, bf16[128,128]{1,0:T(8,128)(2,1)}, u32[]{:S(2)}) copy-start(bf16[128,128]{1,0:T(8,128)(2,1)} %param.17) | copy-start | bytes 98308
  27.9 26.0 %copy-start.4 = (bf16[2048,128]{1,0:T(8,128)(2,1)}, bf16[2048,128]{1,0:T(8,128)(2,1)S(1)}, u32[]{:S(2)}) copy-start(bf16[2048,128]{1,0:T(8,128)(2,1)S(1)} %multiply_convert_fusion.7) | copy-start | bytes 1572868
  28.8 14.2 %all-to-all-start.2 = ((bf16[32,64,128]{2,1,0:T(8,128)(2,1)}), bf16[32,64,128]{2,1,0:T(8,128)(2,1)S(1)}, u32[]{:S(2)}, u32[]{:S(2)}) async-start(bf16[32,64,128]{2,1,0:T(8,128)(2,1)} %param.15), calls=%async_computation.2 | async-start | bytes 1048576 | tf_op jit(solution)/shard_map/all_to_all | solution.py:28
  32.3 620.7 %all-reduce.5.cloned.1.call-start = ((), (), s32[]{:S(2)}) async-start(), calls=%async_computation.5 | async-start | bytes 9043968
  43.1 14.1 %copy-start.7 = (bf16[4,8,64,128]{3,2,1,0:T(8,128)(2,1)}, bf16[4,8,64,128]{3,2,1,0:T(8,128)(2,1)S(1)}, u32[]{:S(2)}) copy-start(bf16[4,8,64,128]{3,2,1,0:T(8,128)(2,1)S(1)} %copy.109) | copy-start | bytes 1572868
  43.1 10.9 %copy-start.17 = (bf16[128,128]{1,0:T(8,128)(2,1)S(1)}, bf16[128,128]{1,0:T(8,128)(2,1)}, u32[]{:S(2)}) copy-start(bf16[128,128]{1,0:T(8,128)(2,1)} %param.19) | copy-start | bytes 98308
  49.6 7.5 %copy-start.13 = (bf16[128,128]{1,0:T(8,128)(2,1)S(1)}, bf16[128,128]{1,0:T(8,128)(2,1)}, u32[]{:S(2)}) copy-start(bf16[128,128]{1,0:T(8,128)(2,1)} %param.23) | copy-start | bytes 98308
  381.3 5.2 copy-start.28
  406.2 4.9 copy-start.2
  413.3 4.6 copy-start.3
  425.9 4.9 copy-start.2
  433.0 4.6 copy-start.3
  445.6 4.9 copy-start.2
  452.7 4.6 copy-start.3
  465.3 4.9 copy-start.2
  472.5 4.6 copy-start.3
  490.0 8.9 %copy-start.16 = (bf16[128,128]{1,0:T(8,128)(2,1)S(1)}, bf16[128,128]{1,0:T(8,128)(2,1)}, u32[]{:S(2)}) copy-start(bf16[128,128]{1,0:T(8,128)(2,1)} %param.18) | copy-start | bytes 98308
  490.0 9.2 %copy-start.18 = (bf16[128,128]{1,0:T(8,128)(2,1)S(1)}, bf16[128,128]{1,0:T(8,128)(2,1)}, u32[]{:S(2)}) copy-start(bf16[128,128]{1,0:T(8,128)(2,1)} %param.19) | copy-start | bytes 98308
  492.5 166.3 %all-to-all-start.1 = ((bf16[4,512,128]{2,0,1:T(4,128)(2,1)}), bf16[4,512,128]{2,0,1:T(4,128)(2,1)}, u32[]{:S(2)}, u32[]{:S(2)}) async-start(bf16[4,512,128]{2,0,1:T(4,128)(2,1)} %copy.107), calls=%async_computation.1 | async-start | bytes 1048576 | tf_op jit(solution)/shard_map/all_to_all | solution.py:135
  498.8 154.9 %copy-start.25 = (f32[128]{0:T(128)S(1)}, f32[128]{0:T(128)}, u32[]{:S(2)}) copy-start(f32[128]{0:T(128)} %param.16) | copy-start | bytes 1540
  498.9 154.9 %copy-start.27 = (bf16[128,4]{0,1:T(4,128)(2,1)S(1)}, bf16[128,4]{0,1:T(4,128)(2,1)}, u32[]{:S(2)}) copy-start(bf16[128,4]{0,1:T(4,128)(2,1)} %param.22) | copy-start | bytes 3076
  655.8 78.0 %copy-start.23 = (f32[128,128]{1,0:T(8,128)S(1)}, f32[128,128]{1,0:T(8,128)}, u32[]{:S(2)}) copy-start(f32[128,128]{1,0:T(8,128)} %get-tuple-element.429) | copy-start | bytes 196612
  655.8 78.7 %copy-start.22 = (f32[128,128]{1,0:T(8,128)S(1)}, f32[128,128]{1,0:T(8,128)}, u32[]{:S(2)}) copy-start(f32[128,128]{1,0:T(8,128)} %get-tuple-element.430) | copy-start | bytes 196612
  655.9 79.3 %copy-start.21 = (f32[128,128]{1,0:T(8,128)S(1)}, f32[128,128]{1,0:T(8,128)}, u32[]{:S(2)}) copy-start(f32[128,128]{1,0:T(8,128)} %get-tuple-element.431) | copy-start | bytes 196612
  655.9 79.9 %copy-start.20 = (f32[128,128]{1,0:T(8,128)S(1)}, f32[128,128]{1,0:T(8,128)}, u32[]{:S(2)}) copy-start(f32[128,128]{1,0:T(8,128)} %get-tuple-element.432) | copy-start | bytes 196612
  655.9 80.5 %copy-start.19 = (f32[128,128]{1,0:T(8,128)S(1)}, f32[128,128]{1,0:T(8,128)}, u32[]{:S(2)}) copy-start(f32[128,128]{1,0:T(8,128)} %get-tuple-element.435) | copy-start | bytes 196612
  658.7 74.2 %all-to-all-start.3 = ((bf16[4,512,128]{2,0,1:T(4,128)(2,1)}), bf16[4,512,128]{2,0,1:T(4,128)(2,1)S(1)}, u32[]{:S(2)}, u32[]{:S(2)}) async-start(bf16[4,512,128]{2,0,1:T(4,128)(2,1)} %copy.121), calls=%async_computation.3 | async-start | bytes 1048576 | tf_op jit(solution)/shard_map/all_to_all | solution.py:136
  (11 other events, 32.3 us)
Sparse Core Ops, SparseCore 0:
  28.9 295.8 all-gather.1
  490.1 162.8 all-reduce.4
where the time goes:
time: 747 us; the launch traced here: 744 us
  waiting for transfers between devices  430 us (58%)
  matrix products  104 us (14%)
  blocking collectives  84.5 us (11%)
  local copies, waits for them, and re-layouts  79.4 us (11%)
  other arithmetic  16.3 us (2%)
  starting transfers between devices  14.8 us (2%)
  between operations  14.5 us (2%)
    all_gather x1, waiting for transfers between devices, body(): bias_full = lax.all_gather(bias_local, ('row', 'col'), axis=1, tiled=True)  266 us
    unnamed x3, waiting for transfers between devices  153 us
    psum x1, blocking collectives, body(): lax.psum((gain_part, query_part, key_part, value_part, gate_part, offset_...  65.9 us
    dynamic_update_slice x8, local copies, waits for them, and re-layouts, body(): lax.scan(forward_row, jnp.zeros((), jnp.float32), (query, keys, values))  29.4 us
    sub x8, matrix products, row_probs(): return jax.nn.softmax(scores + bias_full.astype(jnp.float32), axis=-1)  27.5 us
    all_to_all x1, blocking collectives, body(): lax.all_to_all(pair_rep, 'col', split_axis=0, concat_axis=1, tiled=True)  18.6 us
  transfers between devices with their start and end apart: 5, of which 3 were waited for; matrix products, arithmetic and copies ran while one was open for 4% of the time, Pallas kernels for 0%

commit v1 on v0

v1 whole, which is shorter than its diff:
```python
import functools

import jax
import jax.numpy as jnp
from jax import lax
from jax.experimental import pallas as pl
from jax.experimental.pallas import tpu as pltpu
from jax.sharding import PartitionSpec as P

EPS = 1e-05
F32 = jnp.float32
BF16 = jnp.bfloat16
NT = (((1,), (1,)), ((), ()))
TN = (((0,), (0,)), ((), ()))
PARAMS = pltpu.CompilerParams(vmem_limit_bytes=56 * 1024 * 1024)


def dot(left, right, dims=(((1,), (0,)), ((), ()))):
    return lax.dot_general(left, right, dims, preferred_element_type=F32)


def normalize(values, gain):
    average = jnp.mean(values, axis=-1, keepdims=True)
    centered = values - average
    variance = jnp.mean(centered * centered, axis=-1, keepdims=True)
    inverse = lax.rsqrt(variance + EPS)
    unit = centered * inverse
    return unit, inverse, (unit * gain).astype(BF16)


def low_lanes(shape):
    return lax.broadcasted_iota(jnp.int32, shape, len(shape) - 1) < 64


def join_low(left, right):
    return jnp.where(low_lanes(left.shape), left, pltpu.roll(right, 64, left.ndim - 1))


def join_high(left, right):
    return jnp.where(low_lanes(left.shape), pltpu.roll(left, 64, left.ndim - 1), right)


def head_mask(heads, channels, dtype):
    lane = lax.broadcasted_iota(jnp.int32, (1, heads, 1, channels), 3)
    head = lax.broadcasted_iota(jnp.int32, (1, heads, 1, channels), 1)
    return jnp.where(lane // (channels // heads) == head, 1.0, 0.0).astype(dtype)


def tile_bias_kernel(pair_ref, gain_ref, wb_ref, msg_ref, rows_ref):
    unit, inverse, normed = normalize(pair_ref[...].astype(F32), gain_ref[...])
    bias = dot(wb_ref[...], normed, NT)
    for half in range(8):
        first = bias[0:8, half * 128 : half * 128 + 128]
        second = bias[0:8, (8 + half) * 128 : (8 + half) * 128 + 128]
        even = join_low(first, second)
        odd = join_high(first, second)
        for head in range(4):
            base = head * 16 + 2 * half
            rows_ref[base : base + 1, :] = even[head : head + 1]
            rows_ref[base + 1 : base + 2, :] = odd[head : head + 1]
    msg_ref[...] = jnp.broadcast_to(rows_ref[...].astype(BF16)[None], msg_ref.shape)


def project_kernel(scale, pair_ref, cot_ref, gain_ref, wcat_ref, off_ref, wout_ref,
                   q_ref, k_ref, v_ref, a_ref, gate_ref, gg_ref, n_ref):
    values = pair_ref[...].reshape(512, 128).astype(F32)
    unit, inverse, normed = normalize(values, gain_ref[...])
    projected = dot(normed, wcat_ref[...])
    gate = jax.nn.sigmoid(projected[:, 384:512] + off_ref[...])
    grad_gated = dot(cot_ref[...].reshape(512, 128), wout_ref[...], NT)
    q_ref[0] = (projected[:, 0:128] * scale).astype(BF16)
    k_ref[0] = (projected[:, 128:256] * scale).astype(BF16)
    v_ref[0] = projected[:, 256:384].astype(BF16)
    a_ref[0] = (grad_gated * gate).astype(BF16)
    gate_ref[0] = gate
    gg_ref[0] = grad_gated
    n_ref[0] = normed


def attend_kernel(q_ref, k_ref, v_ref, a_ref, bias_ref,
                  att_ref, dq_ref, dk_ref, dv_ref, out_ref, bias_scr, sum_scr):
    chunk = pl.program_id(0)
    for r in range(4):
        for m in range(4):
            left = bias_ref[r, 2 * m].astype(F32)
            right = bias_ref[r, 2 * m + 1].astype(F32)
            lanes = slice(m * 128, m * 128 + 128)
            bias_scr[r * 128 : r * 128 + 64, lanes] = join_low(left, right)
            bias_scr[r * 128 + 64 : r * 128 + 128, lanes] = join_high(left, right)
    mask = head_mask(4, 128, BF16)
    mask_f = head_mask(4, 128, F32)

    def spread(rows):
        return (rows.reshape(8, 1, 16, 128) * mask).reshape(512, 128)

    def collect(rows):
        return jnp.sum(rows.reshape(8, 4, 16, 128) * mask_f, axis=1).reshape(128, 128)

    def step(row, carry):
        at = pl.ds(pl.multiple_of(chunk * 128, 128), 128)
        q_big = spread(q_ref[row, at, :])
        a_big = spread(a_ref[row, at, :])
        keys = k_ref[row]
        values = v_ref[row]
        scores = dot(q_big, keys, NT) + bias_scr[...]
        top = jnp.max(scores, axis=-1, keepdims=True)
        powers = jnp.exp(scores - top)
        probs = powers * (1.0 / jnp.sum(powers, axis=-1, keepdims=True))
        probs_low = probs.astype(BF16)
        att_ref[row, at, :] = collect(dot(probs_low, values))
        grad_probs = dot(a_big, values, NT)
        inner = jnp.sum(probs * grad_probs, axis=-1, keepdims=True)
        score_grad = probs * (grad_probs - inner)
        score_low = score_grad.astype(BF16)
        dq_ref[row, at, :] = collect(dot(score_low, keys))
        dk = dot(q_big, score_low, TN)
        dv = dot(a_big, probs_low, TN)

        @pl.when(chunk == 0)
        def _():
            dk_ref[row] = dk
            dv_ref[row] = dv

        @pl.when(chunk > 0)
        def _():
            dk_ref[row] += dk
            dv_ref[row] += dv

        @pl.when(row == 0)
        def _():
            sum_scr[...] = score_grad

        @pl.when(row > 0)
        def _():
            sum_scr[...] += score_grad

        return carry

    lax.fori_loop(0, 4, step, 0)
    for r in range(4):
        for m in range(4):
            lanes = slice(m * 128, m * 128 + 128)
            low = sum_scr[r * 128 : r * 128 + 64, lanes]
            high = sum_scr[r * 128 + 64 : r * 128 + 128, lanes]
            out_ref[r, 2 * m] = join_low(low, high).astype(BF16)
            out_ref[r, 2 * m + 1] = join_high(low, high).astype(BF16)


def post_kernel(scale, att_ref, dq_ref, dk_ref, dv_ref, gate_ref, gg_ref, n_ref, cot_ref, wcat_ref,
                wout_ref, up_ref, gn_ref, par_ref, off_ref, w_scr, o_scr, s_scr):
    row = pl.program_id(0)
    attended = att_ref[0]
    gate = gate_ref[0]
    grad_gated = gg_ref[0]
    gated = (gate * attended).astype(BF16)
    cot = cot_ref[...].reshape(512, 128)
    up_ref[...] = dot(gated, wout_ref[...]).astype(BF16).reshape(8, 1, 64, 128)
    out_part = dot(gated, cot, TN)
    gpre = (grad_gated * attended * gate * (1.0 - gate)).astype(BF16)
    qpre = (dq_ref[0] * scale).astype(BF16)
    kpre = (jnp.transpose(dk_ref[0]) * scale).astype(BF16)
    vpre = jnp.transpose(dv_ref[0]).astype(BF16)
    cat = jnp.concatenate([qpre, kpre, vpre, gpre], axis=1)
    gn_ref[...] = dot(cat, wcat_ref[...], NT).astype(BF16).reshape(8, 1, 64, 128)
    w_part = dot(n_ref[0], cat, TN)
    off = jnp.sum(gpre.astype(F32), axis=0, keepdims=True)

    @pl.when(row == 0)
    def _():
        w_scr[...] = w_part
        o_scr[...] = out_part
        s_scr[...] = off

    @pl.when(row > 0)
    def _():
        w_scr[...] += w_part
        o_scr[...] += out_part
        s_scr[...] += off

    @pl.when(row == 3)
    def _():
        for t in range(4):
            par_ref[:, t, :] = w_scr[:, t * 128 : t * 128 + 128]
        par_ref[:, 4, :] = o_scr[...]
        for t in range(5, 8):
            par_ref[:, t, :] = jnp.zeros((128, 128), F32)
        off_ref[...] = jnp.broadcast_to(s_scr[...], off_ref.shape)


def tile_final_kernel(pair_ref, gn_ref, bg_ref, par_ref, off_ref, gain_ref, wb_ref,
                      gp_ref, msg_ref, rows_ref, bg_scr):
    rows_ref[...] = jnp.sum(bg_ref[...].astype(F32), axis=0)
    bg_scr[...] = jnp.zeros(bg_scr.shape, F32)
    for half in range(8):
        for head in range(4):
            base = head * 16 + 2 * half
            left = rows_ref[base : base + 1, :]
            right = rows_ref[base + 1 : base + 2, :]
            bg_scr[head : head + 1, half * 128 : half * 128 + 128] = join_low(left, right)
            bg_scr[head : head + 1, (8 + half) * 128 : (8 + half) * 128 + 128] = join_high(left, right)
    bg = bg_scr[...]
    high = bg.astype(BF16)
    low = (bg - high.astype(F32)).astype(BF16)
    both = jnp.concatenate([high.astype(F32), low.astype(F32)], axis=0).astype(BF16)
    unit, inverse, normed = normalize(pair_ref[...].astype(F32), gain_ref[...])
    total = gn_ref[...].astype(F32) + dot(both, wb_ref[...], TN)
    bias_part = dot(both, normed)
    gain_part = jnp.sum(total * unit, axis=0, keepdims=True)
    scaled = total * gain_ref[...]
    first = jnp.mean(scaled, axis=-1, keepdims=True)
    second = jnp.mean(scaled * unit, axis=-1, keepdims=True)
    gp_ref[...] = ((scaled - first - unit * second) * inverse).astype(BF16)
    params = jnp.sum(par_ref[...], axis=0)
    row = lax.broadcasted_iota(jnp.int32, (8, 128), 0)
    params = jnp.where(row == 5, off_ref[...], jnp.where(row == 6, gain_part, params))
    small = bias_part[0:8] + bias_part[8:16]
    msg_ref[...] = jnp.broadcast_to(jnp.concatenate([params, small], axis=0)[None], msg_ref.shape)


def finish_kernel(msg_ref, q_ref, k_ref, v_ref, g_ref, o_ref, small_ref):
    for t, ref in enumerate((q_ref, k_ref, v_ref, g_ref, o_ref)):
        ref[...] = msg_ref[:, t, :]
    small_ref[...] = jnp.sum(msg_ref[...], axis=0)


def sds(shape, dtype):
    return jax.ShapeDtypeStruct(shape, dtype)


def whole(shape):
    return pl.BlockSpec(shape, lambda *_: (0,) * len(shape))


def body(pair_rep, cotangent, ln_gain, w_query, w_key, w_value, w_gate, gate_offset, w_bias, w_out):
    scale = 32 ** (-0.5)
    gain = ln_gain.reshape(1, 128)
    offset = gate_offset.reshape(1, 128)
    wcat = jnp.concatenate([w_query, w_key, w_value, w_gate], axis=1)
    wb_pad = jnp.pad(w_bias.T, ((0, 4), (0, 0)))
    wb_two = jnp.concatenate([wb_pad, wb_pad], axis=0)
    everyone = ("row", "col")
    pair_tile = pair_rep.reshape(2048, 128)

    def swap(value, axes):
        return lax.all_to_all(value, axes, split_axis=0, concat_axis=0, tiled=True)

    bias_msg = pl.pallas_call(
        tile_bias_kernel,
        out_shape=sds((128, 64, 128), BF16),
        scratch_shapes=[pltpu.VMEM((64, 128), F32)],
        compiler_params=PARAMS,
        name="tile_bias",
    )(pair_tile, gain, wb_two)
    pair_rows = swap(pair_rep, "col").reshape(8, 4, 64, 128)
    cot_rows = swap(cotangent, "col").reshape(8, 4, 64, 128)
    bias_all = swap(bias_msg, everyone).reshape(16, 8, 64, 128)

    from_rows = pl.BlockSpec((8, 1, 64, 128), lambda i: (0, i, 0, 0))
    by_row = pl.BlockSpec((1, 512, 128), lambda i: (i, 0, 0))
    query, keys, values, grad_att, gate, grad_gated, normed = pl.pallas_call(
        functools.partial(project_kernel, scale),
        grid=(4,),
        in_specs=[from_rows, from_rows, whole((1, 128)), whole((128, 512)), whole((1, 128)), whole((128, 128))],
        out_specs=[by_row] * 7,
        out_shape=[sds((4, 512, 128), t) for t in (BF16, BF16, BF16, BF16, F32, F32, BF16)],
        compiler_params=PARAMS,
        name="project",
    )(pair_rows, cot_rows, gain, wcat, offset, w_out)

    full = whole((4, 512, 128))
    full_t = whole((4, 128, 512))
    blocks = pl.BlockSpec((4, 8, 64, 128), lambda c: (c, 0, 0, 0))
    attended, dq, dk, dv, bias_out = pl.pallas_call(
        attend_kernel,
        grid=(4,),
        in_specs=[full, full, full, full, blocks],
        out_specs=[full, full, full_t, full_t, blocks],
        out_shape=[sds((4, 512, 128), F32), sds((4, 512, 128), F32), sds((4, 128, 512), F32),
                   sds((4, 128, 512), F32), sds((16, 8, 64, 128), BF16)],
        scratch_shapes=[pltpu.VMEM((512, 512), F32), pltpu.VMEM((512, 512), F32)],
        compiler_params=PARAMS,
        name="attend",
    )(query, keys, values, grad_att, bias_all)
    bias_in = swap(bias_out.reshape(128, 64, 128), everyone)

    by_row_t = pl.BlockSpec((1, 128, 512), lambda i: (i, 0, 0))
    update, grad_n, params, off = pl.pallas_call(
        functools.partial(post_kernel, scale),
        grid=(4,),
        in_specs=[by_row, by_row, by_row_t, by_row_t, by_row, by_row, by_row, from_rows,
                  whole((128, 512)), whole((128, 128))],
        out_specs=[from_rows, from_rows, whole((128, 8, 128)), whole((8, 128))],
        out_shape=[sds((8, 4, 64, 128), BF16), sds((8, 4, 64, 128), BF16), sds((128, 8, 128), F32),
                   sds((8, 128), F32)],
        scratch_shapes=[pltpu.VMEM((128, 512), F32), pltpu.VMEM((128, 128), F32), pltpu.VMEM((1, 128), F32)],
        compiler_params=PARAMS,
        name="post",
    )(attended, dq, dk, dv, gate, grad_gated, normed, cot_rows, wcat, w_out)
    grad_tile = swap(grad_n.reshape(32, 64, 128), "col").reshape(2048, 128)
    params_in = swap(params, everyone)
    grad_pair, final_msg = pl.pallas_call(
        tile_final_kernel,
        out_shape=[sds((2048, 128), BF16), sds((128, 16, 128), F32)],
        scratch_shapes=[pltpu.VMEM((64, 128), F32), pltpu.VMEM((8, 2048), F32)],
        compiler_params=PARAMS,
        name="tile_final",
    )(pair_tile, grad_tile, bias_in, params_in, off, gain, wb_two)
    final_in = swap(final_msg, everyone)
    update_tile = swap(update.reshape(32, 64, 128), "col")
    g_query, g_key, g_value, g_gate, g_out, small = pl.pallas_call(
        finish_kernel,
        out_shape=[sds((128, 128), F32)] * 5 + [sds((16, 128), F32)],
        compiler_params=PARAMS,
        name="finish",
    )(final_in)
    return (
        update_tile,
        grad_pair.reshape(32, 64, 128),
        small[6],
        g_query,
        g_key,
        g_value,
        g_gate,
        small[5],
        small[8:12].T,
        g_out,
    )


def solution(mesh):
    tile = P("row", "col", None)
    return jax.shard_map(
        body,
        mesh=mesh,
        in_specs=(tile, tile) + (P(),) * 8,
        out_specs=(tile, tile) + (P(),) * 8,
        check_vma=False,
    )
```

time: 747 us -> 220 us (0.29)
  waiting for transfers between devices: 430 us -> 37.2 us
  matrix products: 104 us -> 0 us
  local copies, waits for them, and re-layouts: 79.4 us -> 6.16 us
  Pallas kernels: 0 us -> 48.5 us
  blocking collectives: 84.5 us -> 111 us
  other arithmetic: 16.3 us -> 0.6 us
  between operations: 14.5 us -> 0.78 us
    all_gather x1 -> x0, waiting for transfers between devices: 266 us -> none  [body(): bias_full = lax.all_gather(bias_local, ('row', 'col'), axis=1, tiled=True)]
    unnamed x3 -> x0, waiting for transfers between devices: 153 us -> none
    all_to_all x1 -> x5, blocking collectives: 18.6 us -> 111 us  [swap(): return lax.all_to_all(value, axes, split_axis=0, concat_axis=0, tiled=True)]
    dot_general x38 -> x0, matrix products: 76.5 us -> none  [the longest x4 14.5 us: forward_row(): jnp.einsum('hjk,khc->jhc', probs_low, value_row, preferred_element_type=j...]
    psum x1 -> x0, blocking collectives: 65.9 us -> none  [body(): lax.psum((gain_part, query_part, key_part, value_part, gate_part, offset_...]
    pallas_call x0 -> x6, Pallas kernels: none -> 48.5 us  [the longest x1 27.2 us: body(): pl.pallas_call(attend_kernel, grid=(4,), in_specs=[full, full, full, full...]
    dynamic_update_slice x8 -> x0, local copies, waits for them, and re-layouts: 29.4 us -> none  [body(): lax.scan(forward_row, jnp.zeros((), jnp.float32), (query, keys, values))]
    sub x8 -> x0, matrix products: 27.5 us -> none  [row_probs(): return jax.nn.softmax(scores + bias_full.astype(jnp.float32), axis=-1)]
  transfers between devices with their start and end apart: 5 -> 3, of which waited for: 3 -> 3; matrix products, arithmetic and copies ran while one was open for 4% -> 0% of each run, Pallas kernels for 0% -> 6%
where the time goes in v1:
time: 220 us; the launch traced here: 219 us
  blocking collectives  111 us (50%)
  Pallas kernels  48.5 us (22%)
  waiting for transfers between devices  37.2 us (17%)
  starting transfers between devices  13.9 us (6%)
  local copies, waits for them, and re-layouts  6.16 us (3%)
    all_to_all x5, blocking collectives, swap(): return lax.all_to_all(value, axes, split_axis=0, concat_axis=0, tiled=True)  111 us
    all_to_all x3, waiting for transfers between devices, swap(): return lax.all_to_all(value, axes, split_axis=0, concat_axis=0, tiled=True)  37.2 us
    pallas_call x1, Pallas kernels, body(): pl.pallas_call(attend_kernel, grid=(4,), in_specs=[full, full, full, full...  27.2 us
    all_to_all x3, starting transfers between devices, swap(): return lax.all_to_all(value, axes, split_axis=0, concat_axis=0, tiled=True)  13.9 us
    pallas_call x1, Pallas kernels, body(): pl.pallas_call(functools.partial(post_kernel, scale), grid=(4,), in_specs...  5.96 us
    pallas_call x1, Pallas kernels, body(): pl.pallas_call(functools.partial(project_kernel, scale), grid=(4,), in_sp...  5.04 us
    pallas_call x1, Pallas kernels, body(): pl.pallas_call(tile_final_kernel, out_shape=[sds((2048, 128), BF16), sds(...  4.82 us
  transfers between devices with their start and end apart: 3, of which 3 were waited for; matrix products, arithmetic and copies ran while one was open for 0% of the time, Pallas kernels for 6%

profile of v1, /device:TPU:0, one launch (start us, length us, event | category | flops | bytes accessed | tf_op | source)
XLA Modules:
  0.0 218.6 jit_solution(8971200538973675426)
XLA Ops:
  0.6 0.0 copy-start.8
  0.7 18.7 %all_to_all.40 = bf16[32,64,128]{2,1,0:T(8,128)(2,1)} all-to-all(bf16[32,64,128]{2,1,0:T(8,128)(2,1)} %param.11), channel_id=1, replica_groups=mesh['row'=16,'col'=8] {'col'}, dimensions={0} | all-to-all | bytes 1048576 | tf_op jit(solution)/shard_map/all_to_all | solution.py:245
  19.4 3.5 %all-to-all-start = ((bf16[32,64,128]{2,1,0:T(8,128)(2,1)}), bf16[32,64,128]{2,1,0:T(8,128)(2,1)S(1)}, u32[]{:S(2)}, u32[]{:S(2)}) async-start(bf16[32,64,128]{2,1,0:T(8,128)(2,1)} %param.10), calls=%async_computation | async-start | bytes 1048576 | tf_op jit(solution)/shard_map/all_to_all | solution.py:245
  22.9 0.0 copy-done.8
  22.9 0.6 pad_maximum_fusion.wb_ref
  23.5 3.4 %tile_bias.1 = bf16[128,64,128]{2,1,0:T(8,128)(2,1)} custom-call(bf16[2048,128]{1,0:T(8,128)(2,1)} %bitcast.21, f32[1,128]{1,0:T(1,128)} %bitcast.27, bf16[16,128]{1,0:T(8,128)(2,1)} %pad_maximum_fusion.wb_ref), custom_call_target="tpu_custom_call" | custom-call | tf_op jit(solution)/shard_map/tile_bias/pallas_call | solution.py:247
  26.9 6.6 %all-to-all-done = bf16[32,64,128]{2,1,0:T(8,128)(2,1)S(1)} async-done(((bf16[32,64,128]{2,1,0:T(8,128)(2,1)}), bf16[32,64,128]{2,1,0:T(8,128)(2,1)S(1)}, u32[]{:S(2)}, u32[]{:S(2)}) %all-to-all-start) | async-done | bytes 524320 | tf_op jit(solution)/shard_map/all_to_all | solution.py:245
  33.5 0.8 copy-done.2
  34.3 6.8 %all-to-all-start.2 = ((bf16[128,64,128]{2,1,0:T(8,128)(2,1)}), bf16[128,64,128]{2,1,0:T(8,128)(2,1)S(1)}, u32[]{:S(2)}, u32[]{:S(2)}) async-start(bf16[128,64,128]{2,1,0:T(8,128)(2,1)} %tile_bias.1), calls=%async_computation.2 | async-start | bytes 4194304 | tf_op jit(solution)/shard_map/all_to_all | solution.py:245
  41.1 0.0 copy-done.4
  41.1 0.0 copy-done.5
  41.2 0.0 copy-done.6
  41.2 0.0 copy-done.7
  41.2 0.0 copy-start.3
  41.2 0.6 copy-done.3
  41.9 5.0 %project.1 = (bf16[4,512,128]{2,1,0:T(8,128)(2,1)}, bf16[4,512,128]{2,1,0:T(8,128)(2,1)}, bf16[4,512,128]{2,1,0:T(8,128)(2,1)}, bf16[4,512,128]{2,1,0:T(8,128)(2...) custom-call(bf16[8,4,64,128]{3,2,1,0:T(8,128)(2,1)} %bitcast.24, ...), custom_call_target="tpu_custom_call" | custom-call | tf_op jit(solution)/shard_map/project/pallas_call | solution.py:260
  46.9 23.7 %all-to-all-done.2 = bf16[128,64,128]{2,1,0:T(8,128)(2,1)S(1)} async-done(((bf16[128,64,128]{2,1,0:T(8,128)(2,1)}), bf16[128,64,128]{2,1,0:T(8,128)(2,1)S(1)}, u32[]{:S(2)}, u32[]{:S(2)}) %all-to-all-start.2) | async-done | bytes 2097184 | tf_op jit(solution)/shard_map/all_to_all | solution.py:245
  70.6 1.3 copy-done
  71.9 27.2 %attend.1 = (f32[4,512,128]{2,1,0:T(8,128)}, f32[4,512,128]{2,1,0:T(8,128)}, f32[4,128,512]{2,1,0:T(8,128)}, f32[4,128,512]{2,1,0:T(8,128)}, bf16[16,8,64,128]{3,2,1,0:T(8,128)(2,1)}) custom-call(bf16[4,512,128]{2,1,0:T(8,128)(2,1)} %get-tuple-element.34.q_ref, bf16[4,512,128]{2,1,0:T(8,128)(2,1)} %get-tuple-element.35.k_ref, ...), custom_call_target="tpu_custom_call" | custom-call | tf_op jit(solution)/shard_map/attend/pallas_call | solution.py:273
  99.0 6.0 %post.1 = (bf16[8,4,64,128]{3,2,1,0:T(8,128)(2,1)}, bf16[8,4,64,128]{3,2,1,0:T(8,128)(2,1)}, f32[128,8,128]{2,1,0:T(8,128)}, f32[8,128]{1,0:T(8,128)}) custom-call(f32[4,512,128]{2,1,0:T(8,128)} %get-tuple-element.38.att_ref, f32[4,512,128]{2,1,0:T(8,128)} %get-tuple-element.39.dq_ref, f32[4,128,512]{2,1,0:T(8,128)} %get-tuple-element.40.dk_ref, ...), custom_call_target="tpu_custom_call" | custom-call | tf_op jit(solution)/shard_map/post/pallas_call | solution.py:287
  105.0 0.0 copy-start.1
  105.0 15.6 %all_to_all.41 = bf16[32,64,128]{2,1,0:T(8,128)(2,1)} all-to-all(bf16[32,64,128]{2,1,0:T(8,128)(2,1)} %bitcast.26), channel_id=1, replica_groups=mesh['row'=16,'col'=8] {'col'}, dimensions={0} | all-to-all | bytes 1048576 | tf_op jit(solution)/shard_map/all_to_all | solution.py:245
  120.6 18.9 %all_to_all.42.par_ref = f32[128,8,128]{2,1,0:T(8,128)} all-to-all(f32[128,8,128]{2,1,0:T(8,128)} %get-tuple-element.48), channel_id=1, replica_groups=mesh['row'=16,'col'=8] {'row','col'}, dimensions={0} | all-to-all | bytes 1048576 | tf_op jit(solution)/shard_map/all_to_all | solution.py:245
  139.5 34.1 %all_to_all.43.bg_ref = bf16[128,64,128]{2,1,0:T(8,128)(2,1)} all-to-all(bf16[128,64,128]{2,1,0:T(8,128)(2,1)S(1)} %bitcast.23), channel_id=1, replica_groups=mesh['row'=16,'col'=8] {'row','col'}, dimensions={0} | all-to-all | bytes 4194304 | tf_op jit(solution)/shard_map/all_to_all | solution.py:245
  173.6 3.6 %all-to-all-start.3 = ((bf16[32,64,128]{2,1,0:T(8,128)(2,1)}), bf16[32,64,128]{2,1,0:T(8,128)(2,1)S(1)}, u32[]{:S(2)}, u32[]{:S(2)}) async-start(bf16[32,64,128]{2,1,0:T(8,128)(2,1)} %bitcast.7), calls=%async_computation.3 | async-start | bytes 1048576 | tf_op jit(solution)/shard_map/all_to_all | solution.py:245
  177.2 4.8 %tile_final.1 = (bf16[2048,128]{1,0:T(8,128)(2,1)}, f32[128,16,128]{2,1,0:T(8,128)}) custom-call(bf16[2048,128]{1,0:T(8,128)(2,1)} %bitcast.22, bf16[2048,128]{1,0:T(8,128)(2,1)} %bitcast.25, bf16[128,64,128]{2,1,0:T(8,128)(2,1)} %all_to_all.43.bg_ref, f32[128,8,128]{2,1,0:T(8,128)} %all_to_all.42.par_ref, f32[8,128]{1,0:T(8,128)} %get-tuple-element.49.off_ref, ...), custom_call_target="tpu_custom_call" | custom-call | tf_op jit(solution)/shard_map/tile_final/pallas_call | solution.py:301
  182.0 6.9 %all-to-all-done.3 = bf16[32,64,128]{2,1,0:T(8,128)(2,1)S(1)} async-done(((bf16[32,64,128]{2,1,0:T(8,128)(2,1)}), bf16[32,64,128]{2,1,0:T(8,128)(2,1)S(1)}, u32[]{:S(2)}, u32[]{:S(2)}) %all-to-all-start.3) | async-done | bytes 524320 | tf_op jit(solution)/shard_map/all_to_all | solution.py:245
  189.0 24.1 %all_to_all.44.msg_ref = f32[128,16,128]{2,1,0:T(8,128)} all-to-all(f32[128,16,128]{2,1,0:T(8,128)} %get-tuple-element.51), channel_id=1, replica_groups=mesh['row'=16,'col'=8] {'row','col'}, dimensions={0} | all-to-all | bytes 2097152 | tf_op jit(solution)/shard_map/all_to_all | solution.py:245
  213.1 2.1 finish.1
  215.2 1.3 slice_bitcast_fusion.1
  216.5 1.3 slice_bitcast_fusion
  217.8 0.8 copy.24
  (12 shorter events, 0.1 us)
Async XLA Ops:
  0.6 22.2 %copy-start.8 = (bf16[128,4]{0,1:T(4,128)(2,1)S(1)}, bf16[128,4]{0,1:T(4,128)(2,1)}, u32[]{:S(2)}) copy-start(bf16[128,4]{0,1:T(4,128)(2,1)} %param.18) | copy-start | bytes 3076
  19.4 14.1 %all-to-all-start = ((bf16[32,64,128]{2,1,0:T(8,128)(2,1)}), bf16[32,64,128]{2,1,0:T(8,128)(2,1)S(1)}, u32[]{:S(2)}, u32[]{:S(2)}) async-start(bf16[32,64,128]{2,1,0:T(8,128)(2,1)} %param.10), calls=%async_computation | async-start | bytes 1048576 | tf_op jit(solution)/shard_map/all_to_all | solution.py:245
  26.9 14.2 %copy-start.4 = (bf16[128,128]{1,0:T(8,128)(2,1)S(1)}, bf16[128,128]{1,0:T(8,128)(2,1)}, u32[]{:S(2)}) copy-start(bf16[128,128]{1,0:T(8,128)(2,1)} %param.13) | copy-start | bytes 98308
  26.9 14.3 %copy-start.5 = (bf16[128,128]{1,0:T(8,128)(2,1)S(1)}, bf16[128,128]{1,0:T(8,128)(2,1)}, u32[]{:S(2)}) copy-start(bf16[128,128]{1,0:T(8,128)(2,1)} %param.14) | copy-start | bytes 98308
  26.9 14.3 %copy-start.6 = (bf16[128,128]{1,0:T(8,128)(2,1)S(1)}, bf16[128,128]{1,0:T(8,128)(2,1)}, u32[]{:S(2)}) copy-start(bf16[128,128]{1,0:T(8,128)(2,1)} %param.15) | copy-start | bytes 98308
  26.9 14.3 %copy-start.7 = (bf16[128,128]{1,0:T(8,128)(2,1)S(1)}, bf16[128,128]{1,0:T(8,128)(2,1)}, u32[]{:S(2)}) copy-start(bf16[128,128]{1,0:T(8,128)(2,1)} %param.16) | copy-start | bytes 98308
  33.5 0.8 copy-start.2
  34.3 36.3 %all-to-all-start.2 = ((bf16[128,64,128]{2,1,0:T(8,128)(2,1)}), bf16[128,64,128]{2,1,0:T(8,128)(2,1)S(1)}, u32[]{:S(2)}, u32[]{:S(2)}) async-start(bf16[128,64,128]{2,1,0:T(8,128)(2,1)} %tile_bias.1), calls=%async_computation.2 | async-start | bytes 4194304 | tf_op jit(solution)/shard_map/all_to_all | solution.py:245
  41.2 0.6 copy-start.3
  70.6 1.3 copy-start
  105.0 34.5 %copy-start.1 = (bf16[16,8,64,128]{3,2,1,0:T(8,128)(2,1)S(1)}, bf16[16,8,64,128]{3,2,1,0:T(8,128)(2,1)}, u32[]{:S(2)}) copy-start(bf16[16,8,64,128]{3,2,1,0:T(8,128)(2,1)} %get-tuple-element.47) | copy-start | bytes 6291460
  173.6 15.3 %all-to-all-start.3 = ((bf16[32,64,128]{2,1,0:T(8,128)(2,1)}), bf16[32,64,128]{2,1,0:T(8,128)(2,1)S(1)}, u32[]{:S(2)}, u32[]{:S(2)}) async-start(bf16[32,64,128]{2,1,0:T(8,128)(2,1)} %bitcast.7), calls=%async_computation.3 | async-start | bytes 1048576 | tf_op jit(solution)/shard_map/all_to_all | solution.py:245

commit v2 on v1

--- a/solution.py
+++ b/solution.py
@@ -61,13 +61,18 @@
     msg_ref[...] = jnp.broadcast_to(rows_ref[...].astype(BF16)[None], msg_ref.shape)
 
 
-def project_kernel(scale, pair_ref, cot_ref, gain_ref, wcat_ref, off_ref, wout_ref,
+def pack_kernel(pair_ref, cot_ref, out_ref):
+    out_ref[:, 0] = pair_ref[...]
+    out_ref[:, 1] = cot_ref[...]
+
+
+def project_kernel(scale, rows_ref, gain_ref, wcat_ref, off_ref, wout_ref,
                    q_ref, k_ref, v_ref, a_ref, gate_ref, gg_ref, n_ref):
-    values = pair_ref[...].reshape(512, 128).astype(F32)
+    values = rows_ref[:, 0, 0].reshape(512, 128).astype(F32)
     unit, inverse, normed = normalize(values, gain_ref[...])
     projected = dot(normed, wcat_ref[...])
     gate = jax.nn.sigmoid(projected[:, 384:512] + off_ref[...])
-    grad_gated = dot(cot_ref[...].reshape(512, 128), wout_ref[...], NT)
+    grad_gated = dot(rows_ref[:, 1, 0].reshape(512, 128), wout_ref[...], NT)
     q_ref[0] = (projected[:, 0:128] * scale).astype(BF16)
     k_ref[0] = (projected[:, 128:256] * scale).astype(BF16)
     v_ref[0] = projected[:, 256:384].astype(BF16)
@@ -146,22 +151,22 @@
             out_ref[r, 2 * m + 1] = join_high(low, high).astype(BF16)
 
 
-def post_kernel(scale, att_ref, dq_ref, dk_ref, dv_ref, gate_ref, gg_ref, n_ref, cot_ref, wcat_ref,
-                wout_ref, up_ref, gn_ref, par_ref, off_ref, w_scr, o_scr, s_scr):
+def post_kernel(scale, att_ref, dq_ref, dk_ref, dv_ref, gate_ref, gg_ref, n_ref, rows_ref, wcat_ref,
+                wout_ref, held_ref, ug_ref, par_ref, off_ref, w_scr, o_scr, s_scr, p_scr):
     row = pl.program_id(0)
     attended = att_ref[0]
     gate = gate_ref[0]
     grad_gated = gg_ref[0]
     gated = (gate * attended).astype(BF16)
-    cot = cot_ref[...].reshape(512, 128)
-    up_ref[...] = dot(gated, wout_ref[...]).astype(BF16).reshape(8, 1, 64, 128)
+    cot = rows_ref[:, 0, 0].reshape(512, 128)
+    ug_ref[:, 0, 0] = dot(gated, wout_ref[...]).astype(BF16).reshape(8, 64, 128)
     out_part = dot(gated, cot, TN)
     gpre = (grad_gated * attended * gate * (1.0 - gate)).astype(BF16)
     qpre = (dq_ref[0] * scale).astype(BF16)
     kpre = (jnp.transpose(dk_ref[0]) * scale).astype(BF16)
     vpre = jnp.transpose(dv_ref[0]).astype(BF16)
     cat = jnp.concatenate([qpre, kpre, vpre, gpre], axis=1)
-    gn_ref[...] = dot(cat, wcat_ref[...], NT).astype(BF16).reshape(8, 1, 64, 128)
+    ug_ref[:, 1, 0] = dot(cat, wcat_ref[...], NT).astype(BF16).reshape(8, 64, 128)
     w_part = dot(n_ref[0], cat, TN)
     off = jnp.sum(gpre.astype(F32), axis=0, keepdims=True)
 
@@ -179,17 +184,22 @@
 
     @pl.when(row == 3)
     def _():
-        for t in range(4):
-            par_ref[:, t, :] = w_scr[:, t * 128 : t * 128 + 128]
-        par_ref[:, 4, :] = o_scr[...]
+        for t in range(5):
+            part = w_scr[:, t * 128 : t * 128 + 128] if t < 4 else o_scr[...]
+            high = part.astype(BF16).astype(F32)
+            p_scr[:, t, :] = high
+            p_scr[:, 8 + t, :] = part - high
         for t in range(5, 8):
-            par_ref[:, t, :] = jnp.zeros((128, 128), F32)
+            p_scr[:, t, :] = jnp.zeros((128, 128), F32)
+            p_scr[:, 8 + t, :] = jnp.zeros((128, 128), F32)
+        par_ref[...] = p_scr[...].astype(BF16)
         off_ref[...] = jnp.broadcast_to(s_scr[...], off_ref.shape)
 
 
-def tile_final_kernel(pair_ref, gn_ref, bg_ref, par_ref, off_ref, gain_ref, wb_ref,
-                      gp_ref, msg_ref, rows_ref, bg_scr):
-    rows_ref[...] = jnp.sum(bg_ref[...].astype(F32), axis=0)
+def tile_final_kernel(pair_ref, ug_ref, sums_ref, off_ref, gain_ref, wb_ref,
+                      up_ref, gp_ref, msg_ref, rows_ref, bg_scr):
+    up_ref[...] = ug_ref[:, 0].reshape(2048, 128)
+    rows_ref[...] = jnp.sum(sums_ref[...].astype(F32), axis=0)
     bg_scr[...] = jnp.zeros(bg_scr.shape, F32)
     for half in range(8):
         for head in range(4):
@@ -203,24 +213,27 @@
     low = (bg - high.astype(F32)).astype(BF16)
     both = jnp.concatenate([high.astype(F32), low.astype(F32)], axis=0).astype(BF16)
     unit, inverse, normed = normalize(pair_ref[...].astype(F32), gain_ref[...])
-    total = gn_ref[...].astype(F32) + dot(both, wb_ref[...], TN)
+    total = ug_ref[:, 1].reshape(2048, 128).astype(F32) + dot(both, wb_ref[...], TN)
     bias_part = dot(both, normed)
     gain_part = jnp.sum(total * unit, axis=0, keepdims=True)
     scaled = total * gain_ref[...]
     first = jnp.mean(scaled, axis=-1, keepdims=True)
     second = jnp.mean(scaled * unit, axis=-1, keepdims=True)
     gp_ref[...] = ((scaled - first - unit * second) * inverse).astype(BF16)
-    params = jnp.sum(par_ref[...], axis=0)
+    params = rows_ref[64:72, :] + rows_ref[72:80, :]
     row = lax.broadcasted_iota(jnp.int32, (8, 128), 0)
     params = jnp.where(row == 5, off_ref[...], jnp.where(row == 6, gain_part, params))
     small = bias_part[0:8] + bias_part[8:16]
     msg_ref[...] = jnp.broadcast_to(jnp.concatenate([params, small], axis=0)[None], msg_ref.shape)
 
 
-def finish_kernel(msg_ref, q_ref, k_ref, v_ref, g_ref, o_ref, small_ref):
+def finish_kernel(msg_ref, q_ref, k_ref, v_ref, g_ref, o_ref, off_ref, gain_ref, bias_ref):
     for t, ref in enumerate((q_ref, k_ref, v_ref, g_ref, o_ref)):
         ref[...] = msg_ref[:, t, :]
-    small_ref[...] = jnp.sum(msg_ref[...], axis=0)
+    small = jnp.sum(msg_ref[...], axis=0)
+    off_ref[...] = small[5]
+    gain_ref[...] = small[6]
+    bias_ref[...] = small[8:12]
 
 
 def sds(shape, dtype):
@@ -251,21 +264,27 @@
         compiler_params=PARAMS,
         name="tile_bias",
     )(pair_tile, gain, wb_two)
-    pair_rows = swap(pair_rep, "col").reshape(8, 4, 64, 128)
-    cot_rows = swap(cotangent, "col").reshape(8, 4, 64, 128)
+    packed = pl.pallas_call(
+        pack_kernel,
+        out_shape=sds((8, 2, 4, 64, 128), BF16),
+        compiler_params=PARAMS,
+        name="pack",
+    )(pair_rep.reshape(8, 4, 64, 128), cotangent.reshape(8, 4, 64, 128))
+    both_rows = swap(packed, "col")
     bias_all = swap(bias_msg, everyone).reshape(16, 8, 64, 128)
 
-    from_rows = pl.BlockSpec((8, 1, 64, 128), lambda i: (0, i, 0, 0))
+    from_rows = pl.BlockSpec((8, 2, 1, 64, 128), lambda i: (0, 0, i, 0, 0))
+    from_cot = pl.BlockSpec((8, 1, 1, 64, 128), lambda i: (0, 1, i, 0, 0))
     by_row = pl.BlockSpec((1, 512, 128), lambda i: (i, 0, 0))
     query, keys, values, grad_att, gate, grad_gated, normed = pl.pallas_call(
         functools.partial(project_kernel, scale),
         grid=(4,),
-        in_specs=[from_rows, from_rows, whole((1, 128)), whole((128, 512)), whole((1, 128)), whole((128, 128))],
+        in_specs=[from_rows, whole((1, 128)), whole((128, 512)), whole((1, 128)), whole((128, 128))],
         out_specs=[by_row] * 7,
         out_shape=[sds((4, 512, 128), t) for t in (BF16, BF16, BF16, BF16, F32, F32, BF16)],
         compiler_params=PARAMS,
         name="project",
-    )(pair_rows, cot_rows, gain, wcat, offset, w_out)
+    )(both_rows, gain, wcat, offset, w_out)
 
     full = whole((4, 512, 128))
     full_t = whole((4, 128, 512))
@@ -276,53 +295,52 @@
         in_specs=[full, full, full, full, blocks],
         out_specs=[full, full, full_t, full_t, blocks],
         out_shape=[sds((4, 512, 128), F32), sds((4, 512, 128), F32), sds((4, 128, 512), F32),
-                   sds((4, 128, 512), F32), sds((16, 8, 64, 128), BF16)],
+                   sds((4, 128, 512), F32), sds((16, 8, 80, 128), BF16)],
         scratch_shapes=[pltpu.VMEM((512, 512), F32), pltpu.VMEM((512, 512), F32)],
         compiler_params=PARAMS,
         name="attend",
     )(query, keys, values, grad_att, bias_all)
-    bias_in = swap(bias_out.reshape(128, 64, 128), everyone)
 
     by_row_t = pl.BlockSpec((1, 128, 512), lambda i: (i, 0, 0))
-    update, grad_n, params, off = pl.pallas_call(
+    ug_rows, sums_out, off = pl.pallas_call(
         functools.partial(post_kernel, scale),
         grid=(4,),
-        in_specs=[by_row, by_row, by_row_t, by_row_t, by_row, by_row, by_row, from_rows,
-                  whole((128, 512)), whole((128, 128))],
-        out_specs=[from_rows, from_rows, whole((128, 8, 128)), whole((8, 128))],
-        out_shape=[sds((8, 4, 64, 128), BF16), sds((8, 4, 64, 128), BF16), sds((128, 8, 128), F32),
-                   sds((8, 128), F32)],
-        scratch_shapes=[pltpu.VMEM((128, 512), F32), pltpu.VMEM((128, 128), F32), pltpu.VMEM((1, 128), F32)],
+        in_specs=[by_row, by_row, by_row_t, by_row_t, by_row, by_row, by_row, from_cot,
+                  whole((128, 512)), whole((128, 128)), pl.BlockSpec(memory_space=pl.ANY)],
+        out_specs=[from_rows, pl.BlockSpec((128, 16, 128), lambda i: (0, 4, 0)), whole((8, 128))],
+        out_shape=[sds((8, 2, 4, 64, 128), BF16), sds((128, 80, 128), BF16), sds((8, 128), F32)],
+        scratch_shapes=[pltpu.VMEM((128, 512), F32), pltpu.VMEM((128, 128), F32), pltpu.VMEM((1, 128), F32),
+                        pltpu.VMEM((128, 16, 128), F32)],
+        input_output_aliases={10: 1},
         compiler_params=PARAMS,
         name="post",
-    )(attended, dq, dk, dv, gate, grad_gated, normed, cot_rows, wcat, w_out)
-    grad_tile = swap(grad_n.reshape(32, 64, 128), "col").reshape(2048, 128)
-    params_in = swap(params, everyone)
-    grad_pair, final_msg = pl.pallas_call(
+    )(attended, dq, dk, dv, gate, grad_gated, normed, both_rows, wcat, w_out, bias_out.reshape(128, 80, 128))
+    ug_tile = swap(ug_rows, "col")
+    sums_in = swap(sums_out, everyone)
+    update, grad_pair, final_msg = pl.pallas_call(
         tile_final_kernel,
-        out_shape=[sds((2048, 128), BF16), sds((128, 16, 128), F32)],
-        scratch_shapes=[pltpu.VMEM((64, 128), F32), pltpu.VMEM((8, 2048), F32)],
+        out_shape=[sds((2048, 128), BF16), sds((2048, 128), BF16), sds((128, 16, 128), F32)],
+        scratch_shapes=[pltpu.VMEM((80, 128), F32), pltpu.VMEM((8, 2048), F32)],
         compiler_params=PARAMS,
         name="tile_final",
-    )(pair_tile, grad_tile, bias_in, params_in, off, gain, wb_two)
+    )(pair_tile, ug_tile.reshape(8, 2, 256, 128), sums_in, off, gain, wb_two)
     final_in = swap(final_msg, everyone)
-    update_tile = swap(update.reshape(32, 64, 128), "col")
-    g_query, g_key, g_value, g_gate, g_out, small = pl.pallas_call(
+    g_query, g_key, g_value, g_gate, g_out, g_off, g_gain, g_bias = pl.pallas_call(
         finish_kernel,
-        out_shape=[sds((128, 128), F32)] * 5 + [sds((16, 128), F32)],
+        out_shape=[sds((128, 128), F32)] * 5 + [sds((128,), F32)] * 2 + [sds((4, 128), F32)],
         compiler_params=PARAMS,
         name="finish",
     )(final_in)
     return (
-        update_tile,
+        update.reshape(32, 64, 128),
         grad_pair.reshape(32, 64, 128),
-        small[6],
+        g_gain,
         g_query,
         g_key,
         g_value,
         g_gate,
-        small[5],
-        small[8:12].T,
+        g_off,
+        g_bias.T,
         g_out,
     )
 

time: 220 us -> 193 us (0.88)
  blocking collectives: 111 us -> 86 us
  local copies, waits for them, and re-layouts: 6.16 us -> 2.04 us
  Pallas kernels: 48.5 us -> 51.7 us
    all_to_all x5 -> x3, blocking collectives: 111 us -> 86 us  [swap(): return lax.all_to_all(value, axes, split_axis=0, concat_axis=0, tiled=True)]
    pallas_call x0 -> x1, Pallas kernels: none -> 2.24 us  [body(): pl.pallas_call(pack_kernel, out_shape=sds((8, 2, 4, 64, 128), BF16), comp...]
    all_to_all x3 -> x2, waiting for transfers between devices: 37.2 us -> 36.9 us  [swap(): return lax.all_to_all(value, axes, split_axis=0, concat_axis=0, tiled=True)]
    all_to_all x3 -> x2, starting transfers between devices: 13.9 us -> 13.9 us  [swap(): return lax.all_to_all(value, axes, split_axis=0, concat_axis=0, tiled=True)]
  transfers between devices with their start and end apart: 3 -> 2, of which waited for: 3 -> 2; matrix products, arithmetic and copies ran while one was open for 0% -> 0% of each run, Pallas kernels for 6% -> 4%
where the time goes in v2:
time: 193 us; the launch traced here: 192 us
  blocking collectives  86 us (45%)
  Pallas kernels  51.7 us (27%)
  waiting for transfers between devices  36.9 us (19%)
  starting transfers between devices  13.9 us (7%)
  local copies, waits for them, and re-layouts  2.04 us (1%)
    all_to_all x3, blocking collectives, swap(): return lax.all_to_all(value, axes, split_axis=0, concat_axis=0, tiled=True)  86 us
    all_to_all x2, waiting for transfers between devices, swap(): return lax.all_to_all(value, axes, split_axis=0, concat_axis=0, tiled=True)  36.9 us
    pallas_call x1, Pallas kernels, body(): pl.pallas_call(attend_kernel, grid=(4,), in_specs=[full, full, full, full...  27.1 us
    all_to_all x2, starting transfers between devices, swap(): return lax.all_to_all(value, axes, split_axis=0, concat_axis=0, tiled=True)  13.9 us
    pallas_call x1, Pallas kernels, body(): pl.pallas_call(functools.partial(post_kernel, scale), grid=(4,), in_specs...  6.44 us
    pallas_call x1, Pallas kernels, body(): pl.pallas_call(tile_final_kernel, out_shape=[sds((2048, 128), BF16), sds(...  5.5 us
    pallas_call x1, Pallas kernels, body(): pl.pallas_call(functools.partial(project_kernel, scale), grid=(4,), in_sp...  4.97 us
  transfers between devices with their start and end apart: 2, of which 2 were waited for; matrix products, arithmetic and copies ran while one was open for 0% of the time, Pallas kernels for 4%

profile of v2, /device:TPU:0, one launch (start us, length us, event | category | flops | bytes accessed | tf_op | source)
XLA Modules:
  0.0 191.9 jit_solution(8703553951251017698)
XLA Ops:
  0.6 0.0 copy-start.7
  0.7 2.2 %pack.1 = bf16[8,2,4,64,128]{4,3,2,1,0:T(8,128)(2,1)} custom-call(bf16[8,4,64,128]{3,2,1,0:T(8,128)(2,1)} %bitcast.14, bf16[8,4,64,128]{3,2,1,0:T(8,128)(2,1)} %bitcast.18), custom_call_target="tpu_custom_call" | custom-call | tf_op jit(solution)/shard_map/pack/pallas_call | solution.py:267
  2.9 7.0 %all-to-all-start = ((bf16[8,2,4,64,128]{4,3,2,1,0:T(8,128)(2,1)}), bf16[8,2,4,64,128]{4,3,2,1,0:T(8,128)(2,1)S(1)}, u32[]{:S(2)}, u32[]{:S(2)}) async-start(bf16[8,2,4,64,128]{4,3,2,1,0:T(8,128)(2,1)} %pack.1), calls=%async_computation | async-start | bytes 2097152 | tf_op jit(solution)/shard_map/all_to_all | solution.py:258
  9.9 0.0 copy-done.7
  9.9 0.6 pad_maximum_fusion.wb_ref
  10.5 3.4 %tile_bias.1 = bf16[128,64,128]{2,1,0:T(8,128)(2,1)} custom-call(bf16[2048,128]{1,0:T(8,128)(2,1)} %bitcast.15, f32[1,128]{1,0:T(1,128)} %bitcast.19, bf16[16,128]{1,0:T(8,128)(2,1)} %pad_maximum_fusion.wb_ref), custom_call_target="tpu_custom_call" | custom-call | tf_op jit(solution)/shard_map/tile_bias/pallas_call | solution.py:260
  13.9 0.0 copy-start.3
  13.9 0.0 copy-start.4
  13.9 0.0 copy-start.5
  13.9 0.0 copy-start.6
  13.9 13.2 %all-to-all-done.rows_ref = bf16[8,2,4,64,128]{4,3,2,1,0:T(8,128)(2,1)S(1)} async-done(((bf16[8,2,4,64,128]{4,3,2,1,0:T(8,128)(2,1)}), bf16[8,2,4,64,128]{4,3,2,1,0:T(8,128)(2,1)S(1)}, u32[]{:S(2)}, u32[]{:S(2)}) %all-to-all-start) | async-done | bytes 1048608 | tf_op jit(solution)/shard_map/all_to_all | solution.py:258
  27.1 0.0 copy-start
  27.1 6.9 %all-to-all-start.1 = ((bf16[128,64,128]{2,1,0:T(8,128)(2,1)}), bf16[128,64,128]{2,1,0:T(8,128)(2,1)S(1)}, u32[]{:S(2)}, u32[]{:S(2)}) async-start(bf16[128,64,128]{2,1,0:T(8,128)(2,1)} %tile_bias.1), calls=%async_computation.1 | async-start | bytes 4194304 | tf_op jit(solution)/shard_map/all_to_all | solution.py:258
  34.0 0.0 copy-done.3
  34.0 0.0 copy-done.4
  34.0 0.0 copy-done.5
  34.1 0.0 copy-done.6
  34.1 0.0 copy-start.2
  34.1 0.0 copy-done
  34.1 0.6 copy-done.2
  34.7 5.0 %project.1 = (bf16[4,512,128]{2,1,0:T(8,128)(2,1)}, bf16[4,512,128]{2,1,0:T(8,128)(2,1)}, bf16[4,512,128]{2,1,0:T(8,128)(2,1)}, bf16[4,512,128]{2,1,0:T(8,128)(2...) custom-call(bf16[8,2,4,64,128]{4,3,2,1,0:T(8,128)(2,1)} %copy-done, ...), custom_call_target="tpu_custom_call" | custom-call | tf_op jit(solution)/shard_map/project/pallas_call | solution.py:279
  39.7 23.7 %all-to-all-done.1 = bf16[128,64,128]{2,1,0:T(8,128)(2,1)S(1)} async-done(((bf16[128,64,128]{2,1,0:T(8,128)(2,1)}), bf16[128,64,128]{2,1,0:T(8,128)(2,1)S(1)}, u32[]{:S(2)}, u32[]{:S(2)}) %all-to-all-start.1) | async-done | bytes 2097184 | tf_op jit(solution)/shard_map/all_to_all | solution.py:258
  63.4 0.0 copy-start.1
  63.4 1.3 copy-done.1
  64.8 27.1 %attend.1 = (f32[4,512,128]{2,1,0:T(8,128)}, f32[4,512,128]{2,1,0:T(8,128)}, f32[4,128,512]{2,1,0:T(8,128)}, f32[4,128,512]{2,1,0:T(8,128)}, bf16[16,8,80,128]{3,2,1,0:T(8,128)(2,1)}) custom-call(bf16[4,512,128]{2,1,0:T(8,128)(2,1)} %get-tuple-element.36.q_ref, bf16[4,512,128]{2,1,0:T(8,128)(2,1)} %get-tuple-element.37.k_ref, ...), custom_call_target="tpu_custom_call" | custom-call | tf_op jit(solution)/shard_map/attend/pallas_call | solution.py:292
  91.9 6.4 %post.1 = (bf16[8,2,4,64,128]{4,3,2,1,0:T(8,128)(2,1)}, bf16[128,80,128]{2,1,0:T(8,128)(2,1)}, f32[8,128]{1,0:T(8,128)}) custom-call(f32[4,512,128]{2,1,0:T(8,128)} %get-tuple-element.40.att_ref, f32[4,512,128]{2,1,0:T(8,128)} %get-tuple-element.41.dq_ref, f32[4,128,512]{2,1,0:T(8,128)} %get-tuple-element.42.dk_ref, ...), custom_call_target="tpu_custom_call", output_to_operand_aliasing={{1}: (10, {})} | custom-call | tf_op jit(solution)/shard_map/post/pallas_call | solution.py:305
  98.3 21.1 %all_to_all.25 = bf16[8,2,4,64,128]{4,3,2,1,0:T(8,128)(2,1)} all-to-all(bf16[8,2,4,64,128]{4,3,2,1,0:T(8,128)(2,1)} %get-tuple-element.48), channel_id=1, replica_groups=mesh['row'=16,'col'=8] {'col'}, dimensions={0} | all-to-all | bytes 2097152 | tf_op jit(solution)/shard_map/all_to_all | solution.py:258
  119.4 40.8 %all_to_all.26.sums_ref = bf16[128,80,128]{2,1,0:T(8,128)(2,1)} all-to-all(bf16[128,80,128]{2,1,0:T(8,128)(2,1)} %get-tuple-element.49), channel_id=1, replica_groups=mesh['row'=16,'col'=8] {'row','col'}, dimensions={0} | all-to-all | bytes 5242880 | tf_op jit(solution)/shard_map/all_to_all | solution.py:258
  160.2 5.5 %tile_final.1 = (bf16[2048,128]{1,0:T(8,128)(2,1)}, bf16[2048,128]{1,0:T(8,128)(2,1)}, f32[128,16,128]{2,1,0:T(8,128)}) custom-call(bf16[2048,128]{1,0:T(8,128)(2,1)} %bitcast.16, bf16[8,2,256,128]{3,2,1,0:T(8,128)(2,1)} %bitcast.17, bf16[128,80,128]{2,1,0:T(8,128)(2,1)} %all_to_all.26.sums_ref, f32[8,128]{1,0:T(8,128)} %get-tuple-element.50.off_ref, ...), custom_call_target="tpu_custom_call" | custom-call | tf_op jit(solution)/shard_map/tile_final/pallas_call | solution.py:320
  165.7 24.1 %all_to_all.27.msg_ref = f32[128,16,128]{2,1,0:T(8,128)} all-to-all(f32[128,16,128]{2,1,0:T(8,128)} %get-tuple-element.53), channel_id=1, replica_groups=mesh['row'=16,'col'=8] {'row','col'}, dimensions={0} | all-to-all | bytes 2097152 | tf_op jit(solution)/shard_map/all_to_all | solution.py:258
  189.8 2.1 %finish.1 = (f32[128,128]{1,0:T(8,128)}, f32[128,128]{1,0:T(8,128)}, f32[128,128]{1,0:T(8,128)}, f32[128,128]{1,0:T(8,128)}, f32[128,128]{1,0:T(8,128)}, /*index...) custom-call(f32[128,16,128]{2,1,0:T(8,128)} %all_to_all.27.msg_ref), custom_call_target="tpu_custom_call" | custom-call | tf_op jit(solution)/shard_map/finish/pallas_call | solution.py:328
  (5 shorter events, 0.1 us)
Async XLA Ops:
  0.6 9.3 %copy-start.7 = (bf16[128,4]{0,1:T(4,128)(2,1)S(1)}, bf16[128,4]{0,1:T(4,128)(2,1)}, u32[]{:S(2)}) copy-start(bf16[128,4]{0,1:T(4,128)(2,1)} %param.18) | copy-start | bytes 3076
  2.9 24.2 %all-to-all-start = ((bf16[8,2,4,64,128]{4,3,2,1,0:T(8,128)(2,1)}), bf16[8,2,4,64,128]{4,3,2,1,0:T(8,128)(2,1)S(1)}, u32[]{:S(2)}, u32[]{:S(2)}) async-start(bf16[8,2,4,64,128]{4,3,2,1,0:T(8,128)(2,1)} %pack.1), calls=%async_computation | async-start | bytes 2097152 | tf_op jit(solution)/shard_map/all_to_all | solution.py:258
  13.9 20.1 %copy-start.3 = (bf16[128,128]{1,0:T(8,128)(2,1)S(1)}, bf16[128,128]{1,0:T(8,128)(2,1)}, u32[]{:S(2)}) copy-start(bf16[128,128]{1,0:T(8,128)(2,1)} %param.13) | copy-start | bytes 98308
  13.9 20.1 %copy-start.4 = (bf16[128,128]{1,0:T(8,128)(2,1)S(1)}, bf16[128,128]{1,0:T(8,128)(2,1)}, u32[]{:S(2)}) copy-start(bf16[128,128]{1,0:T(8,128)(2,1)} %param.14) | copy-start | bytes 98308
  13.9 20.1 %copy-start.5 = (bf16[128,128]{1,0:T(8,128)(2,1)S(1)}, bf16[128,128]{1,0:T(8,128)(2,1)}, u32[]{:S(2)}) copy-start(bf16[128,128]{1,0:T(8,128)(2,1)} %param.15) | copy-start | bytes 98308
  13.9 20.2 %copy-start.6 = (bf16[128,128]{1,0:T(8,128)(2,1)S(1)}, bf16[128,128]{1,0:T(8,128)(2,1)}, u32[]{:S(2)}) copy-start(bf16[128,128]{1,0:T(8,128)(2,1)} %param.16) | copy-start | bytes 98308
  27.1 7.0 %copy-start = (bf16[8,2,4,64,128]{4,3,2,1,0:T(8,128)(2,1)}, bf16[8,2,4,64,128]{4,3,2,1,0:T(8,128)(2,1)S(1)}, u32[]{:S(2)}) copy-start(bf16[8,2,4,64,128]{4,3,2,1,0:T(8,128)(2,1)S(1)} %all-to-all-done.rows_ref) | copy-start | bytes 3145732
  27.1 36.3 %all-to-all-start.1 = ((bf16[128,64,128]{2,1,0:T(8,128)(2,1)}), bf16[128,64,128]{2,1,0:T(8,128)(2,1)S(1)}, u32[]{:S(2)}, u32[]{:S(2)}) async-start(bf16[128,64,128]{2,1,0:T(8,128)(2,1)} %tile_bias.1), calls=%async_computation.1 | async-start | bytes 4194304 | tf_op jit(solution)/shard_map/all_to_all | solution.py:258
  34.1 0.6 copy-start.2
  63.4 1.3 copy-start.1

commit v3 on v2

--- a/solution.py
+++ b/solution.py
@@ -12,6 +12,7 @@
 BF16 = jnp.bfloat16
 NT = (((1,), (1,)), ((), ()))
 TN = (((0,), (0,)), ((), ()))
+SHIFTS = tuple((y, x) for y in range(4) for x in range(2))
 PARAMS = pltpu.CompilerParams(vmem_limit_bytes=56 * 1024 * 1024)
 
 
@@ -46,9 +47,18 @@
     return jnp.where(lane // (channels // heads) == head, 1.0, 0.0).astype(dtype)
 
 
-def tile_bias_kernel(pair_ref, gain_ref, wb_ref, msg_ref, rows_ref):
-    unit, inverse, normed = normalize(pair_ref[...].astype(F32), gain_ref[...])
+def col_pairs(shift):
+    return [(c, ((c // 2 + shift[0]) % 4) * 2 + (c % 2 + shift[1]) % 2) for c in range(8)]
+
+
+def prepare_kernel(to_ref, pair_ref, cot_ref, gain_ref, wb_ref, msg_ref, *refs):
+    rows_ref = refs[8]
+    unit, inverse, normed = normalize(pair_ref[...].reshape(2048, 128).astype(F32), gain_ref[...])
     bias = dot(wb_ref[...], normed, NT)
+    for at in range(8):
+        dest = to_ref[at]
+        refs[at][0] = pair_ref[dest]
+        refs[at][1] = cot_ref[dest]
     for half in range(8):
         first = bias[0:8, half * 128 : half * 128 + 128]
         second = bias[0:8, (8 + half) * 128 : (8 + half) * 128 + 128]
@@ -61,18 +71,18 @@
     msg_ref[...] = jnp.broadcast_to(rows_ref[...].astype(BF16)[None], msg_ref.shape)
 
 
-def pack_kernel(pair_ref, cot_ref, out_ref):
-    out_ref[:, 0] = pair_ref[...]
-    out_ref[:, 1] = cot_ref[...]
-
-
-def project_kernel(scale, rows_ref, gain_ref, wcat_ref, off_ref, wout_ref,
-                   q_ref, k_ref, v_ref, a_ref, gate_ref, gg_ref, n_ref):
-    values = rows_ref[:, 0, 0].reshape(512, 128).astype(F32)
-    unit, inverse, normed = normalize(values, gain_ref[...])
+def project_kernel(scale, from_ref, *refs):
+    pieces = refs[:8]
+    gain_ref, wcat_ref, off_ref, wout_ref = refs[8:12]
+    q_ref, k_ref, v_ref, a_ref, gate_ref, gg_ref, n_ref, cot_ref, pair_scr = refs[12:]
+    for at in range(8):
+        rows = pl.ds(pl.multiple_of(from_ref[at] * 64, 64), 64)
+        pair_scr[rows, :] = pieces[at][0, 0]
+        cot_ref[0, rows, :] = pieces[at][1, 0]
+    unit, inverse, normed = normalize(pair_scr[...].astype(F32), gain_ref[...])
     projected = dot(normed, wcat_ref[...])
     gate = jax.nn.sigmoid(projected[:, 384:512] + off_ref[...])
-    grad_gated = dot(rows_ref[:, 1, 0].reshape(512, 128), wout_ref[...], NT)
+    grad_gated = dot(cot_ref[0], wout_ref[...], NT)
     q_ref[0] = (projected[:, 0:128] * scale).astype(BF16)
     k_ref[0] = (projected[:, 128:256] * scale).astype(BF16)
     v_ref[0] = projected[:, 256:384].astype(BF16)
@@ -151,22 +161,28 @@
             out_ref[r, 2 * m + 1] = join_high(low, high).astype(BF16)
 
 
-def post_kernel(scale, att_ref, dq_ref, dk_ref, dv_ref, gate_ref, gg_ref, n_ref, rows_ref, wcat_ref,
-                wout_ref, held_ref, ug_ref, par_ref, off_ref, w_scr, o_scr, s_scr, p_scr):
+def post_kernel(scale, to_ref, att_ref, dq_ref, dk_ref, dv_ref, gate_ref, gg_ref, n_ref, cot_ref, wcat_ref,
+                wout_ref, held_ref, par_ref, off_ref, *refs):
+    pieces = refs[:8]
+    w_scr, o_scr, s_scr, p_scr, up_scr, gn_scr = refs[8:]
     row = pl.program_id(0)
     attended = att_ref[0]
     gate = gate_ref[0]
     grad_gated = gg_ref[0]
     gated = (gate * attended).astype(BF16)
-    cot = rows_ref[:, 0, 0].reshape(512, 128)
-    ug_ref[:, 0, 0] = dot(gated, wout_ref[...]).astype(BF16).reshape(8, 64, 128)
+    cot = cot_ref[0]
+    up_scr[...] = dot(gated, wout_ref[...]).astype(BF16)
     out_part = dot(gated, cot, TN)
     gpre = (grad_gated * attended * gate * (1.0 - gate)).astype(BF16)
     qpre = (dq_ref[0] * scale).astype(BF16)
     kpre = (jnp.transpose(dk_ref[0]) * scale).astype(BF16)
     vpre = jnp.transpose(dv_ref[0]).astype(BF16)
     cat = jnp.concatenate([qpre, kpre, vpre, gpre], axis=1)
-    ug_ref[:, 1, 0] = dot(cat, wcat_ref[...], NT).astype(BF16).reshape(8, 64, 128)
+    gn_scr[...] = dot(cat, wcat_ref[...], NT).astype(BF16)
+    for at in range(8):
+        rows = pl.ds(pl.multiple_of(to_ref[at] * 64, 64), 64)
+        pieces[at][0, 0] = up_scr[rows, :]
+        pieces[at][1, 0] = gn_scr[rows, :]
     w_part = dot(n_ref[0], cat, TN)
     off = jnp.sum(gpre.astype(F32), axis=0, keepdims=True)
 
@@ -196,9 +212,13 @@
         off_ref[...] = jnp.broadcast_to(s_scr[...], off_ref.shape)
 
 
-def tile_final_kernel(pair_ref, ug_ref, sums_ref, off_ref, gain_ref, wb_ref,
-                      up_ref, gp_ref, msg_ref, rows_ref, bg_scr):
-    up_ref[...] = ug_ref[:, 0].reshape(2048, 128)
+def tile_final_kernel(from_ref, pair_ref, sums_ref, off_ref, gain_ref, wb_ref, *refs):
+    pieces = refs[:8]
+    up_ref, gp_ref, msg_ref, rows_ref, bg_scr, gn_scr = refs[8:]
+    for at in range(8):
+        rows = pl.ds(pl.multiple_of(from_ref[at] * 256, 256), 256)
+        up_ref[rows, :] = pieces[at][0]
+        gn_scr[rows, :] = pieces[at][1]
     rows_ref[...] = jnp.sum(sums_ref[...].astype(F32), axis=0)
     bg_scr[...] = jnp.zeros(bg_scr.shape, F32)
     for half in range(8):
@@ -213,7 +233,7 @@
     low = (bg - high.astype(F32)).astype(BF16)
     both = jnp.concatenate([high.astype(F32), low.astype(F32)], axis=0).astype(BF16)
     unit, inverse, normed = normalize(pair_ref[...].astype(F32), gain_ref[...])
-    total = ug_ref[:, 1].reshape(2048, 128).astype(F32) + dot(both, wb_ref[...], TN)
+    total = gn_scr[...].astype(F32) + dot(both, wb_ref[...], TN)
     bias_part = dot(both, normed)
     gain_part = jnp.sum(total * unit, axis=0, keepdims=True)
     scaled = total * gain_ref[...]
@@ -257,34 +277,39 @@
     def swap(value, axes):
         return lax.all_to_all(value, axes, split_axis=0, concat_axis=0, tiled=True)
 
-    bias_msg = pl.pallas_call(
-        tile_bias_kernel,
-        out_shape=sds((128, 64, 128), BF16),
+    col = lax.axis_index("col")
+    to_col = jnp.stack([((col // 2 + y) % 4) * 2 + (col % 2 + x) % 2 for y, x in SHIFTS])
+    from_col = jnp.stack([((col // 2 + 4 - y) % 4) * 2 + (col % 2 + x) % 2 for y, x in SHIFTS])
+    smem = pl.BlockSpec(memory_space=pltpu.SMEM)
+
+    def exchange(pieces):
+        return [pieces[0]] + [
+            lax.ppermute(piece, "col", col_pairs(shift)) for piece, shift in zip(pieces[1:], SHIFTS[1:])
+        ]
+
+    bias_msg, *pieces = pl.pallas_call(
+        prepare_kernel,
+        in_specs=[smem] + [whole((8, 4, 64, 128))] * 2 + [whole((1, 128)), whole((16, 128))],
+        out_shape=[sds((128, 64, 128), BF16)] + [sds((2, 4, 64, 128), BF16)] * 8,
         scratch_shapes=[pltpu.VMEM((64, 128), F32)],
         compiler_params=PARAMS,
-        name="tile_bias",
-    )(pair_tile, gain, wb_two)
-    packed = pl.pallas_call(
-        pack_kernel,
-        out_shape=sds((8, 2, 4, 64, 128), BF16),
-        compiler_params=PARAMS,
-        name="pack",
-    )(pair_rep.reshape(8, 4, 64, 128), cotangent.reshape(8, 4, 64, 128))
-    both_rows = swap(packed, "col")
+        name="prepare",
+    )(to_col, pair_rep.reshape(8, 4, 64, 128), cotangent.reshape(8, 4, 64, 128), gain, wb_two)
     bias_all = swap(bias_msg, everyone).reshape(16, 8, 64, 128)
-
-    from_rows = pl.BlockSpec((8, 2, 1, 64, 128), lambda i: (0, 0, i, 0, 0))
-    from_cot = pl.BlockSpec((8, 1, 1, 64, 128), lambda i: (0, 1, i, 0, 0))
+    pieces = exchange(pieces)
+
+    piece_row = pl.BlockSpec((2, 1, 64, 128), lambda i: (0, i, 0, 0))
     by_row = pl.BlockSpec((1, 512, 128), lambda i: (i, 0, 0))
-    query, keys, values, grad_att, gate, grad_gated, normed = pl.pallas_call(
+    query, keys, values, grad_att, gate, grad_gated, normed, cot_rows = pl.pallas_call(
         functools.partial(project_kernel, scale),
         grid=(4,),
-        in_specs=[from_rows, whole((1, 128)), whole((128, 512)), whole((1, 128)), whole((128, 128))],
-        out_specs=[by_row] * 7,
-        out_shape=[sds((4, 512, 128), t) for t in (BF16, BF16, BF16, BF16, F32, F32, BF16)],
+        in_specs=[smem] + [piece_row] * 8 + [whole((1, 128)), whole((128, 512)), whole((1, 128)), whole((128, 128))],
+        out_specs=[by_row] * 8,
+        out_shape=[sds((4, 512, 128), t) for t in (BF16, BF16, BF16, BF16, F32, F32, BF16, BF16)],
+        scratch_shapes=[pltpu.VMEM((512, 128), BF16)],
         compiler_params=PARAMS,
         name="project",
-    )(both_rows, gain, wcat, offset, w_out)
+    )(from_col, *pieces, gain, wcat, offset, w_out)
 
     full = whole((4, 512, 128))
     full_t = whole((4, 128, 512))
@@ -302,28 +327,30 @@
     )(query, keys, values, grad_att, bias_all)
 
     by_row_t = pl.BlockSpec((1, 128, 512), lambda i: (i, 0, 0))
-    ug_rows, sums_out, off = pl.pallas_call(
+    sums_out, off, *pieces = pl.pallas_call(
         functools.partial(post_kernel, scale),
         grid=(4,),
-        in_specs=[by_row, by_row, by_row_t, by_row_t, by_row, by_row, by_row, from_cot,
+        in_specs=[smem, by_row, by_row, by_row_t, by_row_t, by_row, by_row, by_row, by_row,
                   whole((128, 512)), whole((128, 128)), pl.BlockSpec(memory_space=pl.ANY)],
-        out_specs=[from_rows, pl.BlockSpec((128, 16, 128), lambda i: (0, 4, 0)), whole((8, 128))],
-        out_shape=[sds((8, 2, 4, 64, 128), BF16), sds((128, 80, 128), BF16), sds((8, 128), F32)],
+        out_specs=[pl.BlockSpec((128, 16, 128), lambda i: (0, 4, 0)), whole((8, 128))] + [piece_row] * 8,
+        out_shape=[sds((128, 80, 128), BF16), sds((8, 128), F32)] + [sds((2, 4, 64, 128), BF16)] * 8,
         scratch_shapes=[pltpu.VMEM((128, 512), F32), pltpu.VMEM((128, 128), F32), pltpu.VMEM((1, 128), F32),
-                        pltpu.VMEM((128, 16, 128), F32)],
-        input_output_aliases={10: 1},
+                        pltpu.VMEM((128, 16, 128), F32), pltpu.VMEM((512, 128), BF16), pltpu.VMEM((512, 128), BF16)],
+        input_output_aliases={11: 0},
         compiler_params=PARAMS,
         name="post",
-    )(attended, dq, dk, dv, gate, grad_gated, normed, both_rows, wcat, w_out, bias_out.reshape(128, 80, 128))
-    ug_tile = swap(ug_rows, "col")
+    )(to_col, attended, dq, dk, dv, gate, grad_gated, normed, cot_rows, wcat, w_out, bias_out.reshape(128, 80, 128))
     sums_in = swap(sums_out, everyone)
+    pieces = [piece.reshape(2, 256, 128) for piece in exchange(pieces)]
     update, grad_pair, final_msg = pl.pallas_call(
         tile_final_kernel,
+        in_specs=[smem, whole((2048, 128)), whole((128, 80, 128)), whole((8, 128)), whole((1, 128)), whole((16, 128))]
+        + [whole((2, 256, 128))] * 8,
         out_shape=[sds((2048, 128), BF16), sds((2048, 128), BF16), sds((128, 16, 128), F32)],
-        scratch_shapes=[pltpu.VMEM((80, 128), F32), pltpu.VMEM((8, 2048), F32)],
+        scratch_shapes=[pltpu.VMEM((80, 128), F32), pltpu.VMEM((8, 2048), F32), pltpu.VMEM((2048, 128), BF16)],
         compiler_params=PARAMS,
         name="tile_final",
-    )(pair_tile, ug_tile.reshape(8, 2, 256, 128), sums_in, off, gain, wb_two)
+    )(from_col, pair_tile, sums_in, off, gain, wb_two, *pieces)
     final_in = swap(final_msg, everyone)
     g_query, g_key, g_value, g_gate, g_out, g_off, g_gain, g_bias = pl.pallas_call(
         finish_kernel,

time: 193 us -> 195 us (1.010)
  blocking collectives: 86 us -> 30.6 us
  starting transfers between devices: 13.9 us -> 61.6 us
  waiting for transfers between devices: 36.9 us -> 44.4 us
  local copies, waits for them, and re-layouts: 2.04 us -> 5.47 us
    all_to_all x3 -> x1, blocking collectives: 86 us -> 30.6 us  [swap(): return lax.all_to_all(value, axes, split_axis=0, concat_axis=0, tiled=True)]
    ppermute x0 -> x14, waiting for transfers between devices: none -> 44.4 us  [exchange(): lax.ppermute(piece, 'col', col_pairs(shift))]
    ppermute x0 -> x14, starting transfers between devices: none -> 39.5 us  [exchange(): lax.ppermute(piece, 'col', col_pairs(shift))]
    all_to_all x2, waiting for transfers between devices: 36.9 us -> 0.01 us  [swap(): return lax.all_to_all(value, axes, split_axis=0, concat_axis=0, tiled=True)]
    all_to_all x2, starting transfers between devices: 13.9 us -> 22.1 us  [swap(): return lax.all_to_all(value, axes, split_axis=0, concat_axis=0, tiled=True)]
    pallas_call x3 -> x2, Pallas kernels: 11.1 us -> 9.16 us  [the longest x1 5.47 us: body(): pl.pallas_call(tile_final_kernel, in_specs=[smem, whole((2048, 128)), who...]
  transfers between devices with their start and end apart: 2 -> 16, of which waited for: 2 -> 6; matrix products, arithmetic and copies ran while one was open for 0% -> 0% of each run, Pallas kernels for 4% -> 3%
where the time goes in v3:
time: 195 us; the launch traced here: 194 us
  starting transfers between devices  61.6 us (32%)
  Pallas kernels  50.2 us (26%)
  waiting for transfers between devices  44.4 us (23%)
  blocking collectives  30.6 us (16%)
  local copies, waits for them, and re-layouts  5.47 us (3%)
    ppermute x14, waiting for transfers between devices, exchange(): lax.ppermute(piece, 'col', col_pairs(shift))  44.4 us
    ppermute x14, starting transfers between devices, exchange(): lax.ppermute(piece, 'col', col_pairs(shift))  39.5 us
    all_to_all x1, blocking collectives, swap(): return lax.all_to_all(value, axes, split_axis=0, concat_axis=0, tiled=True)  30.6 us
    pallas_call x1, Pallas kernels, body(): pl.pallas_call(attend_kernel, grid=(4,), in_specs=[full, full, full, full...  27.2 us
    all_to_all x2, starting transfers between devices, swap(): return lax.all_to_all(value, axes, split_axis=0, concat_axis=0, tiled=True)  22.1 us
    pallas_call x1, Pallas kernels, body(): pl.pallas_call(functools.partial(post_kernel, scale), grid=(4,), in_specs...  6.62 us
    pallas_call x1, Pallas kernels, body(): pl.pallas_call(tile_final_kernel, in_specs=[smem, whole((2048, 128)), who...  5.47 us
    pallas_call x1, Pallas kernels, body(): pl.pallas_call(functools.partial(project_kernel, scale), grid=(4,), in_sp...  5.09 us
  transfers between devices with their start and end apart: 16, of which 6 were waited for; matrix products, arithmetic and copies ran while one was open for 0% of the time, Pallas kernels for 3%

profile of v3, /device:TPU:0, one launch (start us, length us, event | category | flops | bytes accessed | tf_op | source)
XLA Modules:
  0.0 194.0 jit_solution(10473458360148518965)
XLA Ops:
  0.8 0.7 pad.4
  2.0 0.6 stack.53.to_ref
  2.7 3.7 %prepare.1 = (bf16[128,64,128]{2,1,0:T(8,128)(2,1)}, bf16[2,4,64,128]{3,2,1,0:T(8,128)(2,1)}, bf16[2,4,64,128]{3,2,1,0:T(8,128)(2,1)}, bf16[2,4,64,128]{3,2,1,0:...) custom-call(s32[8]{0:T(128)} %stack.53.to_ref, ...), custom_call_target="tpu_custom_call" | custom-call | tf_op jit(solution)/shard_map/prepare/pallas_call | solution.py:290
  6.4 11.1 %all-to-all-start = ((bf16[128,64,128]{2,1,0:T(8,128)(2,1)}), bf16[128,64,128]{2,1,0:T(8,128)(2,1)S(1)}, u32[]{:S(2)}, u32[]{:S(2)}) async-start(bf16[128,64,128]{2,1,0:T(8,128)(2,1)} %get-tuple-element.65), calls=%async_computation | async-start | bytes 4194304 | tf_op jit(solution)/shard_map/all_to_all | solution.py:278
  17.6 2.5 %collective-permute-start = (bf16[2,4,64,128]{3,2,1,0:T(8,128)(2,1)}, bf16[2,4,64,128]{3,2,1,0:T(8,128)(2,1)S(1)}, u32[]{:S(2)}, u32[]{:S(2)}) collective-permute-start(bf16[2,4,64,128]{3,2,1,0:T(8,128)(2,1)} %get-tuple-element.54), channel_id=1, source_target_pairs={{0,1},{1,0},{2,3},{3,2},{4,5},{5,4},{6,7},{7,6},{8,9},{9,8},{10,11... | collective-permute-start | bytes 393224 | tf_op jit(solution)/shard_map/ppermute | solution.py:287
  20.1 1.5 collective-permute-start.1
  21.6 1.5 collective-permute-start.2
  23.0 2.3 %collective-permute-start.3 = (bf16[2,4,64,128]{3,2,1,0:T(8,128)(2,1)}, bf16[2,4,64,128]{3,2,1,0:T(8,128)(2,1)S(1)}, u32[]{:S(2)}, u32[]{:S(2)}) collective-permute-start(bf16[2,4,64,128]{3,2,1,0:T(8,128)(2,1)} %get-tuple-element.57), channel_id=1, source_target_pairs={{0,4},{1,5},{2,6},{3,7},{4,0},{5,1},{6,2},{7,3},{8,12},{9,13},{10,... | collective-permute-start | bytes 393224 | tf_op jit(solution)/shard_map/ppermute | solution.py:287
  25.3 3.7 %collective-permute-start.4 = (bf16[2,4,64,128]{3,2,1,0:T(8,128)(2,1)}, bf16[2,4,64,128]{3,2,1,0:T(8,128)(2,1)S(1)}, u32[]{:S(2)}, u32[]{:S(2)}) collective-permute-start(bf16[2,4,64,128]{3,2,1,0:T(8,128)(2,1)} %get-tuple-element.58), channel_id=1, source_target_pairs={{0,5},{1,4},{2,7},{3,6},{4,1},{5,0},{6,3},{7,2},{8,13},{9,12},{10,... | collective-permute-start | bytes 393224 | tf_op jit(solution)/shard_map/ppermute | solution.py:287
  29.0 17.1 %collective-permute-done.refs_1_ = bf16[2,4,64,128]{3,2,1,0:T(8,128)(2,1)S(1)} collective-permute-done((bf16[2,4,64,128]{3,2,1,0:T(8,128)(2,1)}, bf16[2,4,64,128]{3,2,1,0:T(8,128)(2,1)S(1)}, u32[]{:S(2)}, u32[]{:S(2)}) %collective-permute-start) | collective-permute-done | bytes 131104 | tf_op jit(solution)/shard_map/ppermute | solution.py:287
  46.1 2.8 %collective-permute-start.5 = (bf16[2,4,64,128]{3,2,1,0:T(8,128)(2,1)S(1)}, bf16[2,4,64,128]{3,2,1,0:T(8,128)(2,1)S(1)}, u32[]{:S(2)}, u32[]{:S(2)}) collective-permute-start(bf16[2,4,64,128]{3,2,1,0:T(8,128)(2,1)S(1)} %copy-done.22), channel_id=1, source_target_pairs={{0,6},{1,7},{2,0},{3,1},{4,2},{5,3},{6,4},{7,5},{8,14},{9,15},{10,... | collective-permute-start | bytes 393224 | tf_op jit(solution)/shard_map/ppermute | solution.py:287
  48.9 5.5 %collective-permute-start.6 = (bf16[2,4,64,128]{3,2,1,0:T(8,128)(2,1)S(1)}, bf16[2,4,64,128]{3,2,1,0:T(8,128)(2,1)S(1)}, u32[]{:S(2)}, u32[]{:S(2)}) collective-permute-start(bf16[2,4,64,128]{3,2,1,0:T(8,128)(2,1)S(1)} %copy-done.21), channel_id=1, source_target_pairs={{0,7},{1,6},{2,1},{3,0},{4,3},{5,2},{6,5},{7,4},{8,15},{9,14},{10,... | collective-permute-start | bytes 393224 | tf_op jit(solution)/shard_map/ppermute | solution.py:287
  55.1 1.4 collective-permute-done.5.refs_6_
  57.5 5.1 %project.1 = (bf16[4,512,128]{2,1,0:T(8,128)(2,1)}, bf16[4,512,128]{2,1,0:T(8,128)(2,1)}, bf16[4,512,128]{2,1,0:T(8,128)(2,1)}, bf16[4,512,128]{2,1,0:T(8,128)(2...) custom-call(s32[8]{0:T(128)} %stack.50.from_ref, ...), custom_call_target="tpu_custom_call" | custom-call | tf_op jit(solution)/shard_map/project/pallas_call | solution.py:303
  62.6 1.3 copy-done.1
  64.0 27.2 %attend.1 = (f32[4,512,128]{2,1,0:T(8,128)}, f32[4,512,128]{2,1,0:T(8,128)}, f32[4,128,512]{2,1,0:T(8,128)}, f32[4,128,512]{2,1,0:T(8,128)}, bf16[16,8,80,128]{3,2,1,0:T(8,128)(2,1)}) custom-call(bf16[4,512,128]{2,1,0:T(8,128)(2,1)} %get-tuple-element.61.q_ref, bf16[4,512,128]{2,1,0:T(8,128)(2,1)} %get-tuple-element.62.k_ref, ...), custom_call_target="tpu_custom_call" | custom-call | tf_op jit(solution)/shard_map/attend/pallas_call | solution.py:317
  91.2 6.6 %post.1 = (bf16[128,80,128]{2,1,0:T(8,128)(2,1)}, f32[8,128]{1,0:T(8,128)}, bf16[2,4,64,128]{3,2,1,0:T(8,128)(2,1)}, bf16[2,4,64,128]{3,2,1,0:T(8,128)(2,1)}, bf...) custom-call(s32[8]{0:T(128)} %stack.53.to_ref, ...), custom_call_target="tpu_custom_call", output_to_operand_aliasing={{0}: (11, {})} | custom-call | tf_op jit(solution)/shard_map/post/pallas_call | solution.py:330
  97.8 11.0 %all-to-all-start.1 = ((bf16[128,80,128]{2,1,0:T(8,128)(2,1)}), bf16[128,80,128]{2,1,0:T(8,128)(2,1)S(1)}, u32[]{:S(2)}, u32[]{:S(2)}) async-start(bf16[128,80,128]{2,1,0:T(8,128)(2,1)} %get-tuple-element.75), calls=%async_computation.1 | async-start | bytes 5242880 | tf_op jit(solution)/shard_map/all_to_all | solution.py:278
  108.8 2.5 %collective-permute-start.7 = (bf16[2,4,64,128]{3,2,1,0:T(8,128)(2,1)S(1)}, bf16[2,4,64,128]{3,2,1,0:T(8,128)(2,1)S(1)}, u32[]{:S(2)}, u32[]{:S(2)}) collective-permute-start(bf16[2,4,64,128]{3,2,1,0:T(8,128)(2,1)S(1)} %copy-done.24), channel_id=1, source_target_pairs={{0,1},{1,0},{2,3},{3,2},{4,5},{5,4},{6,7},{7,6},{8,9},{9,8},{10,11... | collective-permute-start | bytes 393224 | tf_op jit(solution)/shard_map/ppermute | solution.py:287
  111.4 1.5 collective-permute-start.8
  112.8 1.5 collective-permute-start.9
  114.3 2.3 %collective-permute-start.10 = (bf16[2,4,64,128]{3,2,1,0:T(8,128)(2,1)}, bf16[2,4,64,128]{3,2,1,0:T(8,128)(2,1)S(1)}, u32[]{:S(2)}, u32[]{:S(2)}) collective-permute-start(bf16[2,4,64,128]{3,2,1,0:T(8,128)(2,1)} %get-tuple-element.81), channel_id=1, source_target_pairs={{0,4},{1,5},{2,6},{3,7},{4,0},{5,1},{6,2},{7,3},{8,12},{9,13},{10,... | collective-permute-start | bytes 393224 | tf_op jit(solution)/shard_map/ppermute | solution.py:287
  116.6 3.7 %collective-permute-start.11 = (bf16[2,4,64,128]{3,2,1,0:T(8,128)(2,1)}, bf16[2,4,64,128]{3,2,1,0:T(8,128)(2,1)S(1)}, u32[]{:S(2)}, u32[]{:S(2)}) collective-permute-start(bf16[2,4,64,128]{3,2,1,0:T(8,128)(2,1)} %get-tuple-element.82), channel_id=1, source_target_pairs={{0,5},{1,4},{2,7},{3,6},{4,1},{5,0},{6,3},{7,2},{8,13},{9,12},{10,... | collective-permute-start | bytes 393224 | tf_op jit(solution)/shard_map/ppermute | solution.py:287
  120.2 22.7 %collective-permute-done.7 = bf16[2,4,64,128]{3,2,1,0:T(8,128)(2,1)S(1)} collective-permute-done((bf16[2,4,64,128]{3,2,1,0:T(8,128)(2,1)S(1)}, bf16[2,4,64,128]{3,2,1,0:T(8,128)(2,1)S(1)}, u32[]{:S(2)}, u32[]{:S(2)}) %collective-permute-start.7) | collective-permute-done | bytes 131104 | tf_op jit(solution)/shard_map/ppermute | solution.py:287
  143.0 2.8 %collective-permute-start.12 = (bf16[2,4,64,128]{3,2,1,0:T(8,128)(2,1)}, bf16[2,4,64,128]{3,2,1,0:T(8,128)(2,1)S(1)}, u32[]{:S(2)}, u32[]{:S(2)}) collective-permute-start(bf16[2,4,64,128]{3,2,1,0:T(8,128)(2,1)} %get-tuple-element.83), channel_id=1, source_target_pairs={{0,6},{1,7},{2,0},{3,1},{4,2},{5,3},{6,4},{7,5},{8,14},{9,15},{10,... | collective-permute-start | bytes 393224 | tf_op jit(solution)/shard_map/ppermute | solution.py:287
  145.7 5.7 %collective-permute-start.13 = (bf16[2,4,64,128]{3,2,1,0:T(8,128)(2,1)}, bf16[2,4,64,128]{3,2,1,0:T(8,128)(2,1)S(1)}, u32[]{:S(2)}, u32[]{:S(2)}) collective-permute-start(bf16[2,4,64,128]{3,2,1,0:T(8,128)(2,1)} %get-tuple-element.84), channel_id=1, source_target_pairs={{0,7},{1,6},{2,1},{3,0},{4,3},{5,2},{6,5},{7,4},{8,15},{9,14},{10,... | collective-permute-start | bytes 393224 | tf_op jit(solution)/shard_map/ppermute | solution.py:287
  151.5 2.0 %collective-permute-done.12 = bf16[2,4,64,128]{3,2,1,0:T(8,128)(2,1)S(1)} collective-permute-done((bf16[2,4,64,128]{3,2,1,0:T(8,128)(2,1)}, bf16[2,4,64,128]{3,2,1,0:T(8,128)(2,1)S(1)}, u32[]{:S(2)}, u32[]{:S(2)}) %collective-permute-start.12) | collective-permute-done | bytes 131104 | tf_op jit(solution)/shard_map/ppermute | solution.py:287
  153.5 0.8 collective-permute-done.13
  154.9 0.9 copy-done
  155.8 5.5 %tile_final.1 = (bf16[2048,128]{1,0:T(8,128)(2,1)}, bf16[2048,128]{1,0:T(8,128)(2,1)}, f32[128,16,128]{2,1,0:T(8,128)}) custom-call(s32[8]{0:T(128)} %stack.50.from_ref, bf16[2048,128]{1,0:T(8,128)(2,1)} %bitcast.32, bf16[128,80,128]{2,1,0:T(8,128)(2,1)} %copy-done, f32[8,128]{1,0:T(8,128)} %get-tuple-element.76.off_ref, f32[1,128]{1,0:T(1,128)} %bitcast.44, ...), custom_call_target="tpu_custom_call" | custom-call | tf_op jit(solution)/shard_map/tile_final/pallas_call | solution.py:345
  161.3 30.6 %all_to_all.15.msg_ref = f32[128,16,128]{2,1,0:T(8,128)} all-to-all(f32[128,16,128]{2,1,0:T(8,128)} %get-tuple-element.87), channel_id=1, replica_groups=mesh['row'=16,'col'=8] {'row','col'}, dimensions={0} | all-to-all | bytes 2097152 | tf_op jit(solution)/shard_map/all_to_all | solution.py:278
  191.9 2.1 %finish.1 = (f32[128,128]{1,0:T(8,128)}, f32[128,128]{1,0:T(8,128)}, f32[128,128]{1,0:T(8,128)}, f32[128,128]{1,0:T(8,128)}, f32[128,128]{1,0:T(8,128)}, /*index...) custom-call(f32[128,16,128]{2,1,0:T(8,128)} %all_to_all.15.msg_ref), custom_call_target="tpu_custom_call" | custom-call | tf_op jit(solution)/shard_map/finish/pallas_call | solution.py:355
  (67 shorter events, 3.0 us)
Async XLA Ops:
  2.7 26.3 %copy-start.17 = (bf16[128,128]{1,0:T(8,128)(2,1)S(1)}, bf16[128,128]{1,0:T(8,128)(2,1)}, u32[]{:S(2)}) copy-start(bf16[128,128]{1,0:T(8,128)(2,1)} %param.13) | copy-start | bytes 98308
  2.7 26.3 %copy-start.18 = (bf16[128,128]{1,0:T(8,128)(2,1)S(1)}, bf16[128,128]{1,0:T(8,128)(2,1)}, u32[]{:S(2)}) copy-start(bf16[128,128]{1,0:T(8,128)(2,1)} %param.14) | copy-start | bytes 98308
  2.7 51.7 %copy-start.19 = (bf16[128,128]{1,0:T(8,128)(2,1)S(1)}, bf16[128,128]{1,0:T(8,128)(2,1)}, u32[]{:S(2)}) copy-start(bf16[128,128]{1,0:T(8,128)(2,1)} %param.15) | copy-start | bytes 98308
  2.7 52.3 %copy-start.20 = (bf16[128,128]{1,0:T(8,128)(2,1)S(1)}, bf16[128,128]{1,0:T(8,128)(2,1)}, u32[]{:S(2)}) copy-start(bf16[128,128]{1,0:T(8,128)(2,1)} %param.16) | copy-start | bytes 98308
  6.4 13.7 %copy-start.25 = (bf16[2,4,64,128]{3,2,1,0:T(8,128)(2,1)S(1)}, bf16[2,4,64,128]{3,2,1,0:T(8,128)(2,1)}, u32[]{:S(2)}) copy-start(bf16[2,4,64,128]{3,2,1,0:T(8,128)(2,1)} %get-tuple-element.55) | copy-start | bytes 393220
  6.4 39.7 %copy-start.22 = (bf16[2,4,64,128]{3,2,1,0:T(8,128)(2,1)S(1)}, bf16[2,4,64,128]{3,2,1,0:T(8,128)(2,1)}, u32[]{:S(2)}) copy-start(bf16[2,4,64,128]{3,2,1,0:T(8,128)(2,1)} %get-tuple-element.59) | copy-start | bytes 393220
  6.4 42.5 %copy-start.21 = (bf16[2,4,64,128]{3,2,1,0:T(8,128)(2,1)S(1)}, bf16[2,4,64,128]{3,2,1,0:T(8,128)(2,1)}, u32[]{:S(2)}) copy-start(bf16[2,4,64,128]{3,2,1,0:T(8,128)(2,1)} %get-tuple-element.60) | copy-start | bytes 393220
  6.4 56.2 %all-to-all-start = ((bf16[128,64,128]{2,1,0:T(8,128)(2,1)}), bf16[128,64,128]{2,1,0:T(8,128)(2,1)S(1)}, u32[]{:S(2)}, u32[]{:S(2)}) async-start(bf16[128,64,128]{2,1,0:T(8,128)(2,1)} %get-tuple-element.65), calls=%async_computation | async-start | bytes 4194304 | tf_op jit(solution)/shard_map/all_to_all | solution.py:278
  17.6 28.6 %collective-permute-start = (bf16[2,4,64,128]{3,2,1,0:T(8,128)(2,1)}, bf16[2,4,64,128]{3,2,1,0:T(8,128)(2,1)S(1)}, u32[]{:S(2)}, u32[]{:S(2)}) collective-permute-start(bf16[2,4,64,128]{3,2,1,0:T(8,128)(2,1)} %get-tuple-element.54), channel_id=1, source_target_pairs={{0,1},{1,0},{2,3},{3,2},{4,5},{5,4},{6,7},{7,6},{8,9},{9,8},{10,11... | collective-permute-start | bytes 393224 | tf_op jit(solution)/shard_map/ppermute | solution.py:287
  20.1 28.8 %collective-permute-start.1 = (bf16[2,4,64,128]{3,2,1,0:T(8,128)(2,1)S(1)}, bf16[2,4,64,128]{3,2,1,0:T(8,128)(2,1)S(1)}, u32[]{:S(2)}, u32[]{:S(2)}) collective-permute-start(bf16[2,4,64,128]{3,2,1,0:T(8,128)(2,1)S(1)} %copy-done.25), channel_id=1, source_target_pairs={{0,2},{1,3},{2,4},{3,5},{4,6},{5,7},{6,0},{7,1},{8,10},{9,11},{10,... | collective-permute-start | bytes 393224 | tf_op jit(solution)/shard_map/ppermute | solution.py:287
  21.6 33.4 %collective-permute-start.2 = (bf16[2,4,64,128]{3,2,1,0:T(8,128)(2,1)}, bf16[2,4,64,128]{3,2,1,0:T(8,128)(2,1)S(1)}, u32[]{:S(2)}, u32[]{:S(2)}) collective-permute-start(bf16[2,4,64,128]{3,2,1,0:T(8,128)(2,1)} %get-tuple-element.56), channel_id=1, source_target_pairs={{0,3},{1,2},{2,5},{3,4},{4,7},{5,6},{6,1},{7,0},{8,11},{9,10},{10,... | collective-permute-start | bytes 393224 | tf_op jit(solution)/shard_map/ppermute | solution.py:287
  23.0 32.0 %collective-permute-start.3 = (bf16[2,4,64,128]{3,2,1,0:T(8,128)(2,1)}, bf16[2,4,64,128]{3,2,1,0:T(8,128)(2,1)S(1)}, u32[]{:S(2)}, u32[]{:S(2)}) collective-permute-start(bf16[2,4,64,128]{3,2,1,0:T(8,128)(2,1)} %get-tuple-element.57), channel_id=1, source_target_pairs={{0,4},{1,5},{2,6},{3,7},{4,0},{5,1},{6,2},{7,3},{8,12},{9,13},{10,... | collective-permute-start | bytes 393224 | tf_op jit(solution)/shard_map/ppermute | solution.py:287
  25.3 29.7 %collective-permute-start.4 = (bf16[2,4,64,128]{3,2,1,0:T(8,128)(2,1)}, bf16[2,4,64,128]{3,2,1,0:T(8,128)(2,1)S(1)}, u32[]{:S(2)}, u32[]{:S(2)}) collective-permute-start(bf16[2,4,64,128]{3,2,1,0:T(8,128)(2,1)} %get-tuple-element.58), channel_id=1, source_target_pairs={{0,5},{1,4},{2,7},{3,6},{4,1},{5,0},{6,3},{7,2},{8,13},{9,12},{10,... | collective-permute-start | bytes 393224 | tf_op jit(solution)/shard_map/ppermute | solution.py:287
  46.1 10.8 %copy-start.3 = (bf16[2,4,64,128]{3,2,1,0:T(8,128)(2,1)}, bf16[2,4,64,128]{3,2,1,0:T(8,128)(2,1)S(1)}, u32[]{:S(2)}) copy-start(bf16[2,4,64,128]{3,2,1,0:T(8,128)(2,1)S(1)} %collective-permute-done.refs_1_) | copy-start | bytes 393220
  46.1 10.3 %collective-permute-start.5 = (bf16[2,4,64,128]{3,2,1,0:T(8,128)(2,1)S(1)}, bf16[2,4,64,128]{3,2,1,0:T(8,128)(2,1)S(1)}, u32[]{:S(2)}, u32[]{:S(2)}) collective-permute-start(bf16[2,4,64,128]{3,2,1,0:T(8,128)(2,1)S(1)} %copy-done.22), channel_id=1, source_target_pairs={{0,6},{1,7},{2,0},{3,1},{4,2},{5,3},{6,4},{7,5},{8,14},{9,15},{10,... | collective-permute-start | bytes 393224 | tf_op jit(solution)/shard_map/ppermute | solution.py:287
  48.9 8.0 %copy-start.4 = (bf16[2,4,64,128]{3,2,1,0:T(8,128)(2,1)}, bf16[2,4,64,128]{3,2,1,0:T(8,128)(2,1)S(1)}, u32[]{:S(2)}) copy-start(bf16[2,4,64,128]{3,2,1,0:T(8,128)(2,1)S(1)} %collective-permute-done.1.refs_2_) | copy-start | bytes 393220
  48.9 8.0 %collective-permute-start.6 = (bf16[2,4,64,128]{3,2,1,0:T(8,128)(2,1)S(1)}, bf16[2,4,64,128]{3,2,1,0:T(8,128)(2,1)S(1)}, u32[]{:S(2)}, u32[]{:S(2)}) collective-permute-start(bf16[2,4,64,128]{3,2,1,0:T(8,128)(2,1)S(1)} %copy-done.21), channel_id=1, source_target_pairs={{0,7},{1,6},{2,1},{3,0},{4,3},{5,2},{6,5},{7,4},{8,15},{9,14},{10,... | collective-permute-start | bytes 393224 | tf_op jit(solution)/shard_map/ppermute | solution.py:287
  97.8 11.0 %copy-start.24 = (bf16[2,4,64,128]{3,2,1,0:T(8,128)(2,1)S(1)}, bf16[2,4,64,128]{3,2,1,0:T(8,128)(2,1)}, u32[]{:S(2)}) copy-start(bf16[2,4,64,128]{3,2,1,0:T(8,128)(2,1)} %get-tuple-element.78) | copy-start | bytes 393220
  97.8 13.6 %copy-start.23 = (bf16[2,4,64,128]{3,2,1,0:T(8,128)(2,1)S(1)}, bf16[2,4,64,128]{3,2,1,0:T(8,128)(2,1)}, u32[]{:S(2)}) copy-start(bf16[2,4,64,128]{3,2,1,0:T(8,128)(2,1)} %get-tuple-element.79) | copy-start | bytes 393220
  97.8 56.5 %all-to-all-start.1 = ((bf16[128,80,128]{2,1,0:T(8,128)(2,1)}), bf16[128,80,128]{2,1,0:T(8,128)(2,1)S(1)}, u32[]{:S(2)}, u32[]{:S(2)}) async-start(bf16[128,80,128]{2,1,0:T(8,128)(2,1)} %get-tuple-element.75), calls=%async_computation.1 | async-start | bytes 5242880 | tf_op jit(solution)/shard_map/all_to_all | solution.py:278
  108.8 34.2 %collective-permute-start.7 = (bf16[2,4,64,128]{3,2,1,0:T(8,128)(2,1)S(1)}, bf16[2,4,64,128]{3,2,1,0:T(8,128)(2,1)S(1)}, u32[]{:S(2)}, u32[]{:S(2)}) collective-permute-start(bf16[2,4,64,128]{3,2,1,0:T(8,128)(2,1)S(1)} %copy-done.24), channel_id=1, source_target_pairs={{0,1},{1,0},{2,3},{3,2},{4,5},{5,4},{6,7},{7,6},{8,9},{9,8},{10,11... | collective-permute-start | bytes 393224 | tf_op jit(solution)/shard_map/ppermute | solution.py:287
  111.4 34.4 %collective-permute-start.8 = (bf16[2,4,64,128]{3,2,1,0:T(8,128)(2,1)S(1)}, bf16[2,4,64,128]{3,2,1,0:T(8,128)(2,1)S(1)}, u32[]{:S(2)}, u32[]{:S(2)}) collective-permute-start(bf16[2,4,64,128]{3,2,1,0:T(8,128)(2,1)S(1)} %copy-done.23), channel_id=1, source_target_pairs={{0,2},{1,3},{2,4},{3,5},{4,6},{5,7},{6,0},{7,1},{8,10},{9,11},{10,... | collective-permute-start | bytes 393224 | tf_op jit(solution)/shard_map/ppermute | solution.py:287
  112.8 38.6 %collective-permute-start.9 = (bf16[2,4,64,128]{3,2,1,0:T(8,128)(2,1)}, bf16[2,4,64,128]{3,2,1,0:T(8,128)(2,1)S(1)}, u32[]{:S(2)}, u32[]{:S(2)}) collective-permute-start(bf16[2,4,64,128]{3,2,1,0:T(8,128)(2,1)} %get-tuple-element.80), channel_id=1, source_target_pairs={{0,3},{1,2},{2,5},{3,4},{4,7},{5,6},{6,1},{7,0},{8,11},{9,10},{10,... | collective-permute-start | bytes 393224 | tf_op jit(solution)/shard_map/ppermute | solution.py:287
  114.3 37.1 %collective-permute-start.10 = (bf16[2,4,64,128]{3,2,1,0:T(8,128)(2,1)}, bf16[2,4,64,128]{3,2,1,0:T(8,128)(2,1)S(1)}, u32[]{:S(2)}, u32[]{:S(2)}) collective-permute-start(bf16[2,4,64,128]{3,2,1,0:T(8,128)(2,1)} %get-tuple-element.81), channel_id=1, source_target_pairs={{0,4},{1,5},{2,6},{3,7},{4,0},{5,1},{6,2},{7,3},{8,12},{9,13},{10,... | collective-permute-start | bytes 393224 | tf_op jit(solution)/shard_map/ppermute | solution.py:287
  116.6 34.9 %collective-permute-start.11 = (bf16[2,4,64,128]{3,2,1,0:T(8,128)(2,1)}, bf16[2,4,64,128]{3,2,1,0:T(8,128)(2,1)S(1)}, u32[]{:S(2)}, u32[]{:S(2)}) collective-permute-start(bf16[2,4,64,128]{3,2,1,0:T(8,128)(2,1)} %get-tuple-element.82), channel_id=1, source_target_pairs={{0,5},{1,4},{2,7},{3,6},{4,1},{5,0},{6,3},{7,2},{8,13},{9,12},{10,... | collective-permute-start | bytes 393224 | tf_op jit(solution)/shard_map/ppermute | solution.py:287
  143.0 11.3 %copy-start.10 = (bf16[2,4,64,128]{3,2,1,0:T(8,128)(2,1)}, bf16[2,4,64,128]{3,2,1,0:T(8,128)(2,1)S(1)}, u32[]{:S(2)}) copy-start(bf16[2,4,64,128]{3,2,1,0:T(8,128)(2,1)S(1)} %collective-permute-done.7) | copy-start | bytes 393220
  143.0 10.5 %collective-permute-start.12 = (bf16[2,4,64,128]{3,2,1,0:T(8,128)(2,1)}, bf16[2,4,64,128]{3,2,1,0:T(8,128)(2,1)S(1)}, u32[]{:S(2)}, u32[]{:S(2)}) collective-permute-start(bf16[2,4,64,128]{3,2,1,0:T(8,128)(2,1)} %get-tuple-element.83), channel_id=1, source_target_pairs={{0,6},{1,7},{2,0},{3,1},{4,2},{5,3},{6,4},{7,5},{8,14},{9,15},{10,... | collective-permute-start | bytes 393224 | tf_op jit(solution)/shard_map/ppermute | solution.py:287
  145.7 8.5 %copy-start.11 = (bf16[2,4,64,128]{3,2,1,0:T(8,128)(2,1)}, bf16[2,4,64,128]{3,2,1,0:T(8,128)(2,1)S(1)}, u32[]{:S(2)}) copy-start(bf16[2,4,64,128]{3,2,1,0:T(8,128)(2,1)S(1)} %collective-permute-done.8) | copy-start | bytes 393220
  145.7 8.5 %collective-permute-start.13 = (bf16[2,4,64,128]{3,2,1,0:T(8,128)(2,1)}, bf16[2,4,64,128]{3,2,1,0:T(8,128)(2,1)S(1)}, u32[]{:S(2)}, u32[]{:S(2)}) collective-permute-start(bf16[2,4,64,128]{3,2,1,0:T(8,128)(2,1)} %get-tuple-element.84), channel_id=1, source_target_pairs={{0,7},{1,6},{2,1},{3,0},{4,3},{5,2},{6,5},{7,4},{8,15},{9,14},{10,... | collective-permute-start | bytes 393224 | tf_op jit(solution)/shard_map/ppermute | solution.py:287
  151.4 2.9 %copy-start.12 = (bf16[2,4,64,128]{3,2,1,0:T(8,128)(2,1)}, bf16[2,4,64,128]{3,2,1,0:T(8,128)(2,1)S(1)}, u32[]{:S(2)}) copy-start(bf16[2,4,64,128]{3,2,1,0:T(8,128)(2,1)S(1)} %collective-permute-done.9) | copy-start | bytes 393220
  151.5 2.9 %copy-start.13 = (bf16[2,4,64,128]{3,2,1,0:T(8,128)(2,1)}, bf16[2,4,64,128]{3,2,1,0:T(8,128)(2,1)S(1)}, u32[]{:S(2)}) copy-start(bf16[2,4,64,128]{3,2,1,0:T(8,128)(2,1)S(1)} %collective-permute-done.10) | copy-start | bytes 393220
  151.5 2.9 %copy-start.14 = (bf16[2,4,64,128]{3,2,1,0:T(8,128)(2,1)}, bf16[2,4,64,128]{3,2,1,0:T(8,128)(2,1)S(1)}, u32[]{:S(2)}) copy-start(bf16[2,4,64,128]{3,2,1,0:T(8,128)(2,1)S(1)} %collective-permute-done.11) | copy-start | bytes 393220
  (10 other events, 13.1 us)

commit v4 on v2

--- a/solution.py
+++ b/solution.py
@@ -12,6 +12,7 @@
 BF16 = jnp.bfloat16
 NT = (((1,), (1,)), ((), ()))
 TN = (((0,), (0,)), ((), ()))
+HOPS = (0, 1, 3, 2)
 PARAMS = pltpu.CompilerParams(vmem_limit_bytes=56 * 1024 * 1024)
 
 
@@ -44,6 +45,61 @@
     lane = lax.broadcasted_iota(jnp.int32, (1, heads, 1, channels), 3)
     head = lax.broadcasted_iota(jnp.int32, (1, heads, 1, channels), 1)
     return jnp.where(lane // (channels // heads) == head, 1.0, 0.0).astype(dtype)
+
+
+def flat_index(x, y, z, core):
+    return (((x % 2) * 4 + z) * 2 + core) * 8 + y * 2 + x // 2
+
+
+def shift_pairs(x=0, y=0, z=0, core=0):
+    pairs = []
+    for a in range(4):
+        for b in range(4):
+            for c in range(4):
+                for d in range(2):
+                    target = flat_index((a + x) % 4, (b + y) % 4, (c + z) % 4, (d + core) % 2)
+                    pairs.append((flat_index(a, b, c, d), target))
+    return sorted(pairs)
+
+
+def seen(place_ref, sign):
+    x, y, z = ([(place_ref[at] + 4 + sign * hop) & 3 for hop in HOPS] for at in range(3))
+    core = [place_ref[3], 1 - place_ref[3]]
+    return (
+        [(a & 1) * 64 + (a >> 1) for a in x],
+        [b * 2 for b in y],
+        [c * 16 for c in z],
+        [d * 8 for d in core],
+    )
+
+
+def slot_of(delta):
+    delta = (delta + 4) & 3
+    return jnp.where(delta < 2, delta, 5 - delta)
+
+
+def send(value, **shift):
+    return lax.ppermute(value, ("row", "col"), shift_pairs(**shift))
+
+
+def gather_bias(message):
+    held = message
+    held = jnp.stack([held] + [send(held, z=hop) for hop in HOPS[1:]])
+    held = jnp.stack([held] + [send(held, y=hop) for hop in HOPS[1:]])
+    held = held.reshape(16, 64, 128)
+    pieces = [held] + [send(held, x=hop) for hop in HOPS[1:]]
+    return pieces + [send(piece, core=1) for piece in pieces]
+
+
+def add_up(parts):
+    return sum(part.astype(F32) for part in parts).astype(BF16)
+
+
+def scatter_sums(mine, other):
+    held = add_up([mine, send(other, core=1)]).reshape(4, 16, 80, 128)
+    held = add_up([held[0]] + [send(held[at], z=HOPS[at]) for at in (1, 2, 3)]).reshape(4, 4, 80, 128)
+    held = add_up([held[0]] + [send(held[at], y=HOPS[at]) for at in (1, 2, 3)])
+    return [held[0]] + [send(held[at], x=HOPS[at]) for at in (1, 2, 3)]
 
 
 def tile_bias_kernel(pair_ref, gain_ref, wb_ref, msg_ref, rows_ref):
@@ -58,7 +114,7 @@
             base = head * 16 + 2 * half
             rows_ref[base : base + 1, :] = even[head : head + 1]
             rows_ref[base + 1 : base + 2, :] = odd[head : head + 1]
-    msg_ref[...] = jnp.broadcast_to(rows_ref[...].astype(BF16)[None], msg_ref.shape)
+    msg_ref[...] = rows_ref[...].astype(BF16)
 
 
 def pack_kernel(pair_ref, cot_ref, out_ref):
@@ -82,13 +138,23 @@
     n_ref[0] = normed
 
 
-def attend_kernel(q_ref, k_ref, v_ref, a_ref, bias_ref,
-                  att_ref, dq_ref, dk_ref, dv_ref, out_ref, bias_scr, sum_scr):
+def attend_kernel(place_ref, q_ref, k_ref, v_ref, a_ref, *refs):
+    pieces = refs[:8]
+    att_ref, dq_ref, dk_ref, dv_ref, mine_ref, other_ref, block_scr, bias_scr, sum_scr = refs[8:]
     chunk = pl.program_id(0)
+
+    @pl.when(chunk == 0)
+    def _():
+        x, y, z, core = seen(place_ref, -1)
+        for at in range(8):
+            for inner in range(16):
+                owner = x[at % 4] + y[inner // 4] + z[inner % 4] + core[at // 4]
+                block_scr[owner] = pieces[at][inner]
+
     for r in range(4):
         for m in range(4):
-            left = bias_ref[r, 2 * m].astype(F32)
-            right = bias_ref[r, 2 * m + 1].astype(F32)
+            left = block_scr[(chunk * 4 + r) * 8 + 2 * m].astype(F32)
+            right = block_scr[(chunk * 4 + r) * 8 + 2 * m + 1].astype(F32)
             lanes = slice(m * 128, m * 128 + 128)
             bias_scr[r * 128 : r * 128 + 64, lanes] = join_low(left, right)
             bias_scr[r * 128 + 64 : r * 128 + 128, lanes] = join_high(left, right)
@@ -142,17 +208,33 @@
         return carry
 
     lax.fori_loop(0, 4, step, 0)
-    for r in range(4):
-        for m in range(4):
-            lanes = slice(m * 128, m * 128 + 128)
-            low = sum_scr[r * 128 : r * 128 + 64, lanes]
-            high = sum_scr[r * 128 + 64 : r * 128 + 128, lanes]
-            out_ref[r, 2 * m] = join_low(low, high).astype(BF16)
-            out_ref[r, 2 * m + 1] = join_high(low, high).astype(BF16)
-
-
-def post_kernel(scale, att_ref, dq_ref, dk_ref, dv_ref, gate_ref, gg_ref, n_ref, rows_ref, wcat_ref,
-                wout_ref, held_ref, ug_ref, par_ref, off_ref, w_scr, o_scr, s_scr, p_scr):
+
+    xs = [slot_of(chunk // 2 + 2 * high - place_ref[0]) for high in range(2)]
+    ys = [slot_of(at - place_ref[1]) * 4 for at in range(4)]
+    zs = [slot_of((chunk % 2) * 2 + at - place_ref[2]) * 16 for at in range(2)]
+
+    def emit(even_ref, odd_ref):
+        for r in range(4):
+            out_ref = odd_ref if r % 2 else even_ref
+            for m in range(4):
+                lanes = slice(m * 128, m * 128 + 128)
+                low = sum_scr[r * 128 : r * 128 + 64, lanes]
+                high = sum_scr[r * 128 + 64 : r * 128 + 128, lanes]
+                spot = zs[r // 2] + ys[m]
+                out_ref[spot + xs[0], 0:64] = join_low(low, high).astype(BF16)
+                out_ref[spot + xs[1], 0:64] = join_high(low, high).astype(BF16)
+
+    @pl.when(place_ref[3] == 0)
+    def _():
+        emit(mine_ref, other_ref)
+
+    @pl.when(place_ref[3] == 1)
+    def _():
+        emit(other_ref, mine_ref)
+
+
+def post_kernel(scale, place_ref, att_ref, dq_ref, dk_ref, dv_ref, gate_ref, gg_ref, n_ref, rows_ref, wcat_ref,
+                wout_ref, held_mine, held_other, ug_ref, mine_ref, other_ref, off_ref, w_scr, o_scr, s_scr, p_scr):
     row = pl.program_id(0)
     attended = att_ref[0]
     gate = gate_ref[0]
@@ -192,14 +274,20 @@
         for t in range(5, 8):
             p_scr[:, t, :] = jnp.zeros((128, 128), F32)
             p_scr[:, 8 + t, :] = jnp.zeros((128, 128), F32)
-        par_ref[...] = p_scr[...].astype(BF16)
+        x, y, z, core = seen(place_ref, 1)
+        for at in range(64):
+            owner = z[at // 16] + y[at // 4 % 4] + x[at % 4]
+            mine_ref[at] = p_scr[owner + core[0]].astype(BF16)
+            other_ref[at] = p_scr[owner + core[1]].astype(BF16)
         off_ref[...] = jnp.broadcast_to(s_scr[...], off_ref.shape)
 
 
-def tile_final_kernel(pair_ref, ug_ref, sums_ref, off_ref, gain_ref, wb_ref,
+def tile_final_kernel(pair_ref, ug_ref, one_ref, two_ref, three_ref, four_ref, off_ref, gain_ref, wb_ref,
                       up_ref, gp_ref, msg_ref, rows_ref, bg_scr):
     up_ref[...] = ug_ref[:, 0].reshape(2048, 128)
-    rows_ref[...] = jnp.sum(sums_ref[...].astype(F32), axis=0)
+    rows_ref[...] = (one_ref[...].astype(F32) + two_ref[...].astype(F32)) + (
+        three_ref[...].astype(F32) + four_ref[...].astype(F32)
+    )
     bg_scr[...] = jnp.zeros(bg_scr.shape, F32)
     for half in range(8):
         for head in range(4):
@@ -259,11 +347,15 @@
 
     bias_msg = pl.pallas_call(
         tile_bias_kernel,
-        out_shape=sds((128, 64, 128), BF16),
+        out_shape=sds((64, 128), BF16),
         scratch_shapes=[pltpu.VMEM((64, 128), F32)],
         compiler_params=PARAMS,
         name="tile_bias",
     )(pair_tile, gain, wb_two)
+    row, col = lax.axis_index("row"), lax.axis_index("col")
+    place = ((col % 2) * 2 + row // 8, col // 2, (row // 2) % 4, row % 2)
+    place = jnp.stack(place).astype(jnp.int32)
+    smem = pl.BlockSpec(memory_space=pltpu.SMEM)
     packed = pl.pallas_call(
         pack_kernel,
         out_shape=sds((8, 2, 4, 64, 128), BF16),
@@ -271,7 +363,7 @@
         name="pack",
     )(pair_rep.reshape(8, 4, 64, 128), cotangent.reshape(8, 4, 64, 128))
     both_rows = swap(packed, "col")
-    bias_all = swap(bias_msg, everyone).reshape(16, 8, 64, 128)
+    bias_pieces = gather_bias(bias_msg)
 
     from_rows = pl.BlockSpec((8, 2, 1, 64, 128), lambda i: (0, 0, i, 0, 0))
     from_cot = pl.BlockSpec((8, 1, 1, 64, 128), lambda i: (0, 1, i, 0, 0))
@@ -288,42 +380,43 @@
 
     full = whole((4, 512, 128))
     full_t = whole((4, 128, 512))
-    blocks = pl.BlockSpec((4, 8, 64, 128), lambda c: (c, 0, 0, 0))
-    attended, dq, dk, dv, bias_out = pl.pallas_call(
+    attended, dq, dk, dv, mine, other = pl.pallas_call(
         attend_kernel,
         grid=(4,),
-        in_specs=[full, full, full, full, blocks],
-        out_specs=[full, full, full_t, full_t, blocks],
+        in_specs=[smem, full, full, full, full] + [whole((16, 64, 128))] * 8,
+        out_specs=[full, full, full_t, full_t, whole((64, 80, 128)), whole((64, 80, 128))],
         out_shape=[sds((4, 512, 128), F32), sds((4, 512, 128), F32), sds((4, 128, 512), F32),
-                   sds((4, 128, 512), F32), sds((16, 8, 80, 128), BF16)],
-        scratch_shapes=[pltpu.VMEM((512, 512), F32), pltpu.VMEM((512, 512), F32)],
+                   sds((4, 128, 512), F32), sds((64, 80, 128), BF16), sds((64, 80, 128), BF16)],
+        scratch_shapes=[pltpu.VMEM((128, 64, 128), BF16), pltpu.VMEM((512, 512), F32), pltpu.VMEM((512, 512), F32)],
         compiler_params=PARAMS,
         name="attend",
-    )(query, keys, values, grad_att, bias_all)
+    )(place, query, keys, values, grad_att, *bias_pieces)
 
     by_row_t = pl.BlockSpec((1, 128, 512), lambda i: (i, 0, 0))
-    ug_rows, sums_out, off = pl.pallas_call(
+    tail = pl.BlockSpec((64, 16, 128), lambda i: (0, 4, 0))
+    ug_rows, mine, other, off = pl.pallas_call(
         functools.partial(post_kernel, scale),
         grid=(4,),
-        in_specs=[by_row, by_row, by_row_t, by_row_t, by_row, by_row, by_row, from_cot,
-                  whole((128, 512)), whole((128, 128)), pl.BlockSpec(memory_space=pl.ANY)],
-        out_specs=[from_rows, pl.BlockSpec((128, 16, 128), lambda i: (0, 4, 0)), whole((8, 128))],
-        out_shape=[sds((8, 2, 4, 64, 128), BF16), sds((128, 80, 128), BF16), sds((8, 128), F32)],
+        in_specs=[smem, by_row, by_row, by_row_t, by_row_t, by_row, by_row, by_row, from_cot,
+                  whole((128, 512)), whole((128, 128))] + [pl.BlockSpec(memory_space=pl.ANY)] * 2,
+        out_specs=[from_rows, tail, tail, whole((8, 128))],
+        out_shape=[sds((8, 2, 4, 64, 128), BF16), sds((64, 80, 128), BF16), sds((64, 80, 128), BF16),
+                   sds((8, 128), F32)],
         scratch_shapes=[pltpu.VMEM((128, 512), F32), pltpu.VMEM((128, 128), F32), pltpu.VMEM((1, 128), F32),
                         pltpu.VMEM((128, 16, 128), F32)],
-        input_output_aliases={10: 1},
+        input_output_aliases={11: 1, 12: 2},
         compiler_params=PARAMS,
         name="post",
-    )(attended, dq, dk, dv, gate, grad_gated, normed, both_rows, wcat, w_out, bias_out.reshape(128, 80, 128))
+    )(place, attended, dq, dk, dv, gate, grad_gated, normed, both_rows, wcat, w_out, mine, other)
     ug_tile = swap(ug_rows, "col")
-    sums_in = swap(sums_out, everyone)
+    sums = scatter_sums(mine, other)
     update, grad_pair, final_msg = pl.pallas_call(
         tile_final_kernel,
         out_shape=[sds((2048, 128), BF16), sds((2048, 128), BF16), sds((128, 16, 128), F32)],
         scratch_shapes=[pltpu.VMEM((80, 128), F32), pltpu.VMEM((8, 2048), F32)],
         compiler_params=PARAMS,
         name="tile_final",
-    )(pair_tile, ug_tile.reshape(8, 2, 256, 128), sums_in, off, gain, wb_two)
+    )(pair_tile, ug_tile.reshape(8, 2, 256, 128), *sums, off, gain, wb_two)
     final_in = swap(final_msg, everyone)
     g_query, g_key, g_value, g_gate, g_out, g_off, g_gain, g_bias = pl.pallas_call(
         finish_kernel,

time: 193 us -> 165 us (0.85)
  blocking collectives: 86 us -> 24.1 us
  starting transfers between devices: 13.9 us -> 42.2 us
  other arithmetic: 0.6 us -> 3.83 us
  local copies, waits for them, and re-layouts: 2.04 us -> 4.14 us
    all_to_all x3 -> x1, blocking collectives: 86 us -> 24.1 us  [swap(): return lax.all_to_all(value, axes, split_axis=0, concat_axis=0, tiled=True)]
    ppermute x0 -> x23, waiting for transfers between devices: none -> 37.2 us  [send(): return lax.ppermute(value, ('row', 'col'), shift_pairs(**shift))]
    all_to_all x2, waiting for transfers between devices: 36.9 us -> 0.01 us  [swap(): return lax.all_to_all(value, axes, split_axis=0, concat_axis=0, tiled=True)]
    ppermute x0 -> x23, starting transfers between devices: none -> 30.2 us  [send(): return lax.ppermute(value, ('row', 'col'), shift_pairs(**shift))]
    all_to_all x2, starting transfers between devices: 13.9 us -> 11.9 us  [swap(): return lax.all_to_all(value, axes, split_axis=0, concat_axis=0, tiled=True)]
  transfers between devices with their start and end apart: 2 -> 25, of which waited for: 2 -> 14; matrix products, arithmetic and copies ran while one was open for 0% -> 2% of each run, Pallas kernels for 4% -> 5%
where the time goes in v4:
time: 165 us; the launch traced here: 164 us
  Pallas kernels  51.5 us (31%)
  starting transfers between devices  42.2 us (26%)
  waiting for transfers between devices  37.3 us (23%)
  blocking collectives  24.1 us (15%)
  local copies, waits for them, and re-layouts  4.14 us (3%)
  other arithmetic  3.83 us (2%)
    ppermute x23, waiting for transfers between devices, send(): return lax.ppermute(value, ('row', 'col'), shift_pairs(**shift))  37.2 us
    ppermute x23, starting transfers between devices, send(): return lax.ppermute(value, ('row', 'col'), shift_pairs(**shift))  30.2 us
    pallas_call x1, Pallas kernels, body(): pl.pallas_call(attend_kernel, grid=(4,), in_specs=[smem, full, full, full...  28.8 us
    all_to_all x1, blocking collectives, swap(): return lax.all_to_all(value, axes, split_axis=0, concat_axis=0, tiled=True)  24.1 us
    all_to_all x2, starting transfers between devices, swap(): return lax.all_to_all(value, axes, split_axis=0, concat_axis=0, tiled=True)  11.9 us
    pallas_call x1, Pallas kernels, body(): pl.pallas_call(functools.partial(post_kernel, scale), grid=(4,), in_specs...  6.55 us
    pallas_call x1, Pallas kernels, body(): pl.pallas_call(functools.partial(project_kernel, scale), grid=(4,), in_sp...  4.94 us
    pallas_call x1, Pallas kernels, body(): pl.pallas_call(tile_final_kernel, out_shape=[sds((2048, 128), BF16), sds(...  4.41 us
  transfers between devices with their start and end apart: 25, of which 14 were waited for; matrix products, arithmetic and copies ran while one was open for 2% of the time, Pallas kernels for 5%

profile of v4, /device:TPU:0, one launch (start us, length us, event | category | flops | bytes accessed | tf_op | source)
XLA Modules:
  0.0 164.0 jit_solution(7949460531611014371)
XLA Ops:
  0.6 2.3 %pack.1 = bf16[8,2,4,64,128]{4,3,2,1,0:T(8,128)(2,1)} custom-call(bf16[8,4,64,128]{3,2,1,0:T(8,128)(2,1)} %bitcast.32, bf16[8,4,64,128]{3,2,1,0:T(8,128)(2,1)} %bitcast.41), custom_call_target="tpu_custom_call" | custom-call | tf_op jit(solution)/shard_map/pack/pallas_call | solution.py:359
  2.9 7.1 %all-to-all-start = ((bf16[8,2,4,64,128]{4,3,2,1,0:T(8,128)(2,1)}), bf16[8,2,4,64,128]{4,3,2,1,0:T(8,128)(2,1)S(1)}, u32[]{:S(2)}, u32[]{:S(2)}) async-start(bf16[8,2,4,64,128]{4,3,2,1,0:T(8,128)(2,1)} %pack.1), calls=%async_computation | async-start | bytes 2097152 | tf_op jit(solution)/shard_map/all_to_all | solution.py:346
  10.7 2.5 %tile_bias.1 = bf16[64,128]{1,0:T(8,128)(2,1)} custom-call(bf16[2048,128]{1,0:T(8,128)(2,1)} %bitcast.33, f32[1,128]{1,0:T(1,128)} %bitcast.49, bf16[16,128]{1,0:T(8,128)(2,1)} %pad_maximum_fusion.2.wb_ref), custom_call_target="tpu_custom_call" | custom-call | tf_op jit(solution)/shard_map/tile_bias/pallas_call | solution.py:348
  13.2 3.9 %collective-permute-start.2 = (bf16[64,128]{1,0:T(8,128)(2,1)}, bf16[64,128]{1,0:T(8,128)(2,1)S(1)}, u32[]{:S(2)}, u32[]{:S(2)}) collective-permute-start(bf16[64,128]{1,0:T(8,128)(2,1)} %tile_bias.1), channel_id=1, source_target_pairs={{0,32},{1,33},{2,34},{3,35},{4,36},{5,37},{6,38},{7,39},{8,40},{9,... | collective-permute-start | bytes 49160 | tf_op jit(solution)/shard_map/ppermute | solution.py:82
  17.8 1.3 collective-permute-start
  19.1 1.9 %collective-permute-done.1 = bf16[64,128]{1,0:T(8,128)(2,1)S(1)} collective-permute-done((bf16[64,128]{1,0:T(8,128)(2,1)}, bf16[64,128]{1,0:T(8,128)(2,1)S(1)}, u32[]{:S(2)}, u32[]{:S(2)}) %collective-permute-start.1) | collective-permute-done | bytes 16416 | tf_op jit(solution)/shard_map/ppermute | solution.py:82
  21.0 1.9 %collective-permute-done = bf16[64,128]{1,0:T(8,128)(2,1)S(1)} collective-permute-done((bf16[64,128]{1,0:T(8,128)(2,1)}, bf16[64,128]{1,0:T(8,128)(2,1)S(1)}, u32[]{:S(2)}, u32[]{:S(2)}) %collective-permute-start) | collective-permute-done | bytes 16416 | tf_op jit(solution)/shard_map/ppermute | solution.py:82
  23.7 3.3 %collective-permute-start.4 = (bf16[4,64,128]{2,1,0:T(8,128)(2,1)S(1)}, bf16[4,64,128]{2,1,0:T(8,128)(2,1)S(1)}, u32[]{:S(2)}, u32[]{:S(2)}) collective-permute-start(bf16[4,64,128]{2,1,0:T(8,128)(2,1)S(1)} %get-tuple-element.77), channel_id=1, source_target_pairs={{0,6},{1,7},{2,0},{3,1},{4,2},{5,3},{6,4},{7,5},{8,14},{9,15},{10,... | collective-permute-start | bytes 196616 | tf_op jit(solution)/shard_map/ppermute | solution.py:82
  27.0 2.3 %collective-permute-start.5 = (bf16[4,64,128]{2,1,0:T(8,128)(2,1)S(1)}, bf16[4,64,128]{2,1,0:T(8,128)(2,1)S(1)}, u32[]{:S(2)}, u32[]{:S(2)}) collective-permute-start(bf16[4,64,128]{2,1,0:T(8,128)(2,1)S(1)} %get-tuple-element.77), channel_id=1, source_target_pairs={{0,4},{1,5},{2,6},{3,7},{4,0},{5,1},{6,2},{7,3},{8,12},{9,13},{10,... | collective-permute-start | bytes 196616 | tf_op jit(solution)/shard_map/ppermute | solution.py:82
  29.3 3.8 %collective-permute-done.3 = bf16[4,64,128]{2,1,0:T(8,128)(2,1)S(1)} collective-permute-done((bf16[4,64,128]{2,1,0:T(8,128)(2,1)S(1)}, bf16[4,64,128]{2,1,0:T(8,128)(2,1)S(1)}, u32[]{:S(2)}, u32[]{:S(2)}) %collective-permute-start.3) | collective-permute-done | bytes 65568 | tf_op jit(solution)/shard_map/ppermute | solution.py:82
  33.2 3.0 %collective-permute-start.8 = (bf16[16,64,128]{2,1,0:T(8,128)(2,1)S(1)}, bf16[16,64,128]{2,1,0:T(8,128)(2,1)S(1)}, u32[]{:S(2)}, u32[]{:S(2)}) collective-permute-start(bf16[16,64,128]{2,1,0:T(8,128)(2,1)S(1)} %bitcast.36), channel_id=1, source_target_pairs={{0,1},{1,0},{2,3},{3,2},{4,5},{5,4},{6,7},{7,6},{8,9},{9,8},{10,11... | collective-permute-start | bytes 786440 | tf_op jit(solution)/shard_map/ppermute | solution.py:82
  36.5 1.7 %collective-permute-start.6 = (bf16[16,64,128]{2,1,0:T(8,128)(2,1)S(1)}, bf16[16,64,128]{2,1,0:T(8,128)(2,1)S(1)}, u32[]{:S(2)}, u32[]{:S(2)}) collective-permute-start(bf16[16,64,128]{2,1,0:T(8,128)(2,1)S(1)} %bitcast.38), channel_id=1, source_target_pairs={{0,64},{1,65},{2,66},{3,67},{4,68},{5,69},{6,70},{7,71},{8,72},{9,... | collective-permute-start | bytes 786440 | tf_op jit(solution)/shard_map/ppermute | solution.py:82
  38.4 3.9 %collective-permute-done.8.refs_3_ = bf16[16,64,128]{2,1,0:T(8,128)(2,1)S(1)} collective-permute-done((bf16[16,64,128]{2,1,0:T(8,128)(2,1)S(1)}, bf16[16,64,128]{2,1,0:T(8,128)(2,1)S(1)}, u32[]{:S(2)}, u32[]{:S(2)}) %collective-permute-start.8) | collective-permute-done | bytes 262176 | tf_op jit(solution)/shard_map/ppermute | solution.py:82
  42.3 2.8 %collective-permute-done.7.refs_2_ = bf16[16,64,128]{2,1,0:T(8,128)(2,1)S(1)} collective-permute-done((bf16[16,64,128]{2,1,0:T(8,128)(2,1)S(1)}, bf16[16,64,128]{2,1,0:T(8,128)(2,1)S(1)}, u32[]{:S(2)}, u32[]{:S(2)}) %collective-permute-start.7) | collective-permute-done | bytes 262176 | tf_op jit(solution)/shard_map/ppermute | solution.py:82
  47.3 4.9 %project.1 = (bf16[4,512,128]{2,1,0:T(8,128)(2,1)}, bf16[4,512,128]{2,1,0:T(8,128)(2,1)}, bf16[4,512,128]{2,1,0:T(8,128)(2,1)}, bf16[4,512,128]{2,1,0:T(8,128)(2...) custom-call(bf16[8,2,4,64,128]{4,3,2,1,0:T(8,128)(2,1)} %copy-done, ...), custom_call_target="tpu_custom_call" | custom-call | tf_op jit(solution)/shard_map/project/pallas_call | solution.py:371
  53.2 28.8 %attend.1 = (f32[4,512,128]{2,1,0:T(8,128)}, f32[4,512,128]{2,1,0:T(8,128)}, f32[4,128,512]{2,1,0:T(8,128)}, f32[4,128,512]{2,1,0:T(8,128)}, bf16[64,80,128]{2,1,0:T(8,128)(2,1)}, /*index=5*/bf16[64,80,128]{2,1,0:T(8,128)(2,1)}) custom-call(s32[4]{0:T(128)} %pad_add_fusion.place_ref, bf16[4,512,128]{2,1,0:T(8,128)(2,1)} %get-tuple-element.38.q_ref, ...), custom_call_target="tpu_custom_call" | custom-call | tf_op jit(solution)/shard_map/attend/pallas_call | solution.py:383
  82.0 6.5 %post.1 = (bf16[8,2,4,64,128]{4,3,2,1,0:T(8,128)(2,1)}, bf16[64,80,128]{2,1,0:T(8,128)(2,1)}, bf16[64,80,128]{2,1,0:T(8,128)(2,1)}, f32[8,128]{1,0:T(8,128)}) custom-call(s32[4]{0:T(128)} %pad_add_fusion.place_ref, f32[4,512,128]{2,1,0:T(8,128)} %get-tuple-element.42.att_ref, ...), custom_call_target="tpu_custom_call", output_to_operand_aliasing={{1}: (11, {}), {2}: (12, {})} | custom-call | tf_op jit(solution)/shard_map/post/pallas_call | solution.py:397
  88.7 3.1 %collective-permute-done.13 = bf16[64,80,128]{2,1,0:T(8,128)(2,1)S(1)} collective-permute-done((bf16[64,80,128]{2,1,0:T(8,128)(2,1)}, bf16[64,80,128]{2,1,0:T(8,128)(2,1)S(1)}, u32[]{:S(2)}, u32[]{:S(2)}) %collective-permute-start.13) | collective-permute-done | bytes 1310752 | tf_op jit(solution)/shard_map/ppermute | solution.py:82
  91.9 1.7 %add_convert_fusion = bf16[64,80,128]{2,1,0:T(8,128)(2,1)S(1)} fusion(bf16[64,80,128]{2,1,0:T(8,128)(2,1)S(1)} %collective-permute-done.13, bf16[64,80,128]{2,1,0:T(8,128)(2,1)} %get-tuple-element.52), kind=kLoop, calls=%fused_computation | loop fusion | flops 2621440 | bytes 3932160 | tf_op jit(solution)/shard_map/convert_element_type | solution.py:95
  94.9 3.5 %collective-permute-start.16 = (bf16[16,80,128]{2,1,0:T(8,128)(2,1)}, bf16[16,80,128]{2,1,0:T(8,128)(2,1)S(1)}, u32[]{:S(2)}, u32[]{:S(2)}) collective-permute-start(bf16[16,80,128]{2,1,0:T(8,128)(2,1)} %get-tuple-element.67), channel_id=1, source_target_pairs={{0,32},{1,33},{2,34},{3,35},{4,36},{5,37},{6,38},{7,39},{8,40},{9,... | collective-permute-start | bytes 983048 | tf_op jit(solution)/shard_map/ppermute | solution.py:82
  99.3 4.8 %all-to-all-start.1 = ((bf16[8,2,4,64,128]{4,3,2,1,0:T(8,128)(2,1)}), bf16[8,2,4,64,128]{4,3,2,1,0:T(8,128)(2,1)S(1)}, u32[]{:S(2)}, u32[]{:S(2)}) async-start(bf16[8,2,4,64,128]{4,3,2,1,0:T(8,128)(2,1)} %get-tuple-element.51), calls=%async_computation.1 | async-start | bytes 2097152 | tf_op jit(solution)/shard_map/all_to_all | solution.py:346
  104.1 1.6 collective-permute-done.14
  105.7 7.9 %collective-permute-done.16 = bf16[16,80,128]{2,1,0:T(8,128)(2,1)S(1)} collective-permute-done((bf16[16,80,128]{2,1,0:T(8,128)(2,1)}, bf16[16,80,128]{2,1,0:T(8,128)(2,1)S(1)}, u32[]{:S(2)}, u32[]{:S(2)}) %collective-permute-start.16) | collective-permute-done | bytes 327712 | tf_op jit(solution)/shard_map/ppermute | solution.py:82
  114.0 3.8 %collective-permute-start.19 = (bf16[4,80,128]{2,1,0:T(8,128)(2,1)S(1)}, bf16[4,80,128]{2,1,0:T(8,128)(2,1)S(1)}, u32[]{:S(2)}, u32[]{:S(2)}) collective-permute-start(bf16[4,80,128]{2,1,0:T(8,128)(2,1)S(1)} %get-tuple-element.70), channel_id=1, source_target_pairs={{0,4},{1,5},{2,6},{3,7},{4,0},{5,1},{6,2},{7,3},{8,12},{9,13},{10,... | collective-permute-start | bytes 245768 | tf_op jit(solution)/shard_map/ppermute | solution.py:82
  117.9 4.5 %collective-permute-done.17 = bf16[4,80,128]{2,1,0:T(8,128)(2,1)S(1)} collective-permute-done((bf16[4,80,128]{2,1,0:T(8,128)(2,1)S(1)}, bf16[4,80,128]{2,1,0:T(8,128)(2,1)S(1)}, u32[]{:S(2)}, u32[]{:S(2)}) %collective-permute-start.17) | collective-permute-done | bytes 81952 | tf_op jit(solution)/shard_map/ppermute | solution.py:82
  124.1 2.0 %collective-permute-start.22 = (bf16[80,128]{1,0:T(8,128)(2,1)S(1)}, bf16[80,128]{1,0:T(8,128)(2,1)S(1)}, u32[]{:S(2)}, u32[]{:S(2)}) collective-permute-start(bf16[80,128]{1,0:T(8,128)(2,1)S(1)} %get-tuple-element.72), channel_id=1, source_target_pairs={{0,1},{1,0},{2,3},{3,2},{4,5},{5,4},{6,7},{7,6},{8,9},{9,8},{10,11... | collective-permute-start | bytes 61448 | tf_op jit(solution)/shard_map/ppermute | solution.py:82
  126.0 1.7 %collective-permute-start.21 = (bf16[80,128]{1,0:T(8,128)(2,1)S(1)}, bf16[80,128]{1,0:T(8,128)(2,1)S(1)}, u32[]{:S(2)}, u32[]{:S(2)}) collective-permute-start(bf16[80,128]{1,0:T(8,128)(2,1)S(1)} %get-tuple-element.73), channel_id=1, source_target_pairs={{0,65},{1,64},{2,67},{3,66},{4,69},{5,68},{6,71},{7,70},{8,73},{9,... | collective-permute-start | bytes 61448 | tf_op jit(solution)/shard_map/ppermute | solution.py:82
  128.1 1.3 collective-permute-done.22.four_ref
  129.8 2.9 %collective-permute-done.20.two_ref = bf16[80,128]{1,0:T(8,128)(2,1)S(1)} collective-permute-done((bf16[80,128]{1,0:T(8,128)(2,1)S(1)}, bf16[80,128]{1,0:T(8,128)(2,1)S(1)}, u32[]{:S(2)}, u32[]{:S(2)}) %collective-permute-start.20) | collective-permute-done | bytes 20512 | tf_op jit(solution)/shard_map/ppermute | solution.py:82
  133.3 4.4 %tile_final.1 = (bf16[2048,128]{1,0:T(8,128)(2,1)}, bf16[2048,128]{1,0:T(8,128)(2,1)}, f32[128,16,128]{2,1,0:T(8,128)}) custom-call(bf16[2048,128]{1,0:T(8,128)(2,1)} %bitcast.34, bf16[8,2,256,128]{3,2,1,0:T(8,128)(2,1)} %bitcast.35, bf16[80,128]{1,0:T(8,128)(2,1)} %get-tuple-element.75.one_ref, bf16[80,128]{1,0:T(8,128)(2,1)} %copy-done.17, ...), custom_call_target="tpu_custom_call" | custom-call | tf_op jit(solution)/shard_map/tile_final/pallas_call | solution.py:413
  137.7 24.1 %all_to_all.15.msg_ref = f32[128,16,128]{2,1,0:T(8,128)} all-to-all(f32[128,16,128]{2,1,0:T(8,128)} %get-tuple-element.57), channel_id=1, replica_groups=mesh['row'=16,'col'=8] {'row','col'}, dimensions={0} | all-to-all | bytes 2097152 | tf_op jit(solution)/shard_map/all_to_all | solution.py:346
  161.9 2.1 %finish.1 = (f32[128,128]{1,0:T(8,128)}, f32[128,128]{1,0:T(8,128)}, f32[128,128]{1,0:T(8,128)}, f32[128,128]{1,0:T(8,128)}, f32[128,128]{1,0:T(8,128)}, /*index...) custom-call(f32[128,16,128]{2,1,0:T(8,128)} %all_to_all.15.msg_ref), custom_call_target="tpu_custom_call" | custom-call | tf_op jit(solution)/shard_map/finish/pallas_call | solution.py:421
  (79 shorter events, 11.6 us)
Async XLA Ops:
  2.9 35.4 %copy-start.11 = (bf16[128,128]{1,0:T(8,128)(2,1)S(1)}, bf16[128,128]{1,0:T(8,128)(2,1)}, u32[]{:S(2)}) copy-start(bf16[128,128]{1,0:T(8,128)(2,1)} %param.13) | copy-start | bytes 98308
  2.9 35.4 %copy-start.12 = (bf16[128,128]{1,0:T(8,128)(2,1)S(1)}, bf16[128,128]{1,0:T(8,128)(2,1)}, u32[]{:S(2)}) copy-start(bf16[128,128]{1,0:T(8,128)(2,1)} %param.14) | copy-start | bytes 98308
  2.9 43.4 %all-to-all-start = ((bf16[8,2,4,64,128]{4,3,2,1,0:T(8,128)(2,1)}), bf16[8,2,4,64,128]{4,3,2,1,0:T(8,128)(2,1)S(1)}, u32[]{:S(2)}, u32[]{:S(2)}) async-start(bf16[8,2,4,64,128]{4,3,2,1,0:T(8,128)(2,1)} %pack.1), calls=%async_computation | async-start | bytes 2097152 | tf_op jit(solution)/shard_map/all_to_all | solution.py:346
  10.1 36.2 %copy-start.13 = (bf16[128,128]{1,0:T(8,128)(2,1)S(1)}, bf16[128,128]{1,0:T(8,128)(2,1)}, u32[]{:S(2)}) copy-start(bf16[128,128]{1,0:T(8,128)(2,1)} %param.15) | copy-start | bytes 98308
  10.1 36.2 %copy-start.14 = (bf16[128,128]{1,0:T(8,128)(2,1)S(1)}, bf16[128,128]{1,0:T(8,128)(2,1)}, u32[]{:S(2)}) copy-start(bf16[128,128]{1,0:T(8,128)(2,1)} %param.16) | copy-start | bytes 98308
  13.2 5.9 %collective-permute-start.2 = (bf16[64,128]{1,0:T(8,128)(2,1)}, bf16[64,128]{1,0:T(8,128)(2,1)S(1)}, u32[]{:S(2)}, u32[]{:S(2)}) collective-permute-start(bf16[64,128]{1,0:T(8,128)(2,1)} %tile_bias.1), channel_id=1, source_target_pairs={{0,32},{1,33},{2,34},{3,35},{4,36},{5,37},{6,38},{7,39},{8,40},{9,... | collective-permute-start | bytes 49160 | tf_op jit(solution)/shard_map/ppermute | solution.py:82
  17.1 3.9 %collective-permute-start.1 = (bf16[64,128]{1,0:T(8,128)(2,1)}, bf16[64,128]{1,0:T(8,128)(2,1)S(1)}, u32[]{:S(2)}, u32[]{:S(2)}) collective-permute-start(bf16[64,128]{1,0:T(8,128)(2,1)} %tile_bias.1), channel_id=1, source_target_pairs={{0,48},{1,49},{2,50},{3,51},{4,52},{5,53},{6,54},{7,55},{8,56},{9,... | collective-permute-start | bytes 49160 | tf_op jit(solution)/shard_map/ppermute | solution.py:82
  17.8 5.2 %collective-permute-start = (bf16[64,128]{1,0:T(8,128)(2,1)}, bf16[64,128]{1,0:T(8,128)(2,1)S(1)}, u32[]{:S(2)}, u32[]{:S(2)}) collective-permute-start(bf16[64,128]{1,0:T(8,128)(2,1)} %tile_bias.1), channel_id=1, source_target_pairs={{0,16},{1,17},{2,18},{3,19},{4,20},{5,21},{6,22},{7,23},{8,24},{9,... | collective-permute-start | bytes 49160 | tf_op jit(solution)/shard_map/ppermute | solution.py:82
  23.7 5.7 %collective-permute-start.4 = (bf16[4,64,128]{2,1,0:T(8,128)(2,1)S(1)}, bf16[4,64,128]{2,1,0:T(8,128)(2,1)S(1)}, u32[]{:S(2)}, u32[]{:S(2)}) collective-permute-start(bf16[4,64,128]{2,1,0:T(8,128)(2,1)S(1)} %get-tuple-element.77), channel_id=1, source_target_pairs={{0,6},{1,7},{2,0},{3,1},{4,2},{5,3},{6,4},{7,5},{8,14},{9,15},{10,... | collective-permute-start | bytes 196616 | tf_op jit(solution)/shard_map/ppermute | solution.py:82
  27.0 6.2 %collective-permute-start.3 = (bf16[4,64,128]{2,1,0:T(8,128)(2,1)S(1)}, bf16[4,64,128]{2,1,0:T(8,128)(2,1)S(1)}, u32[]{:S(2)}, u32[]{:S(2)}) collective-permute-start(bf16[4,64,128]{2,1,0:T(8,128)(2,1)S(1)} %get-tuple-element.77), channel_id=1, source_target_pairs={{0,2},{1,3},{2,4},{3,5},{4,6},{5,7},{6,0},{7,1},{8,10},{9,11},{10,... | collective-permute-start | bytes 196616 | tf_op jit(solution)/shard_map/ppermute | solution.py:82
  27.0 6.2 %collective-permute-start.5 = (bf16[4,64,128]{2,1,0:T(8,128)(2,1)S(1)}, bf16[4,64,128]{2,1,0:T(8,128)(2,1)S(1)}, u32[]{:S(2)}, u32[]{:S(2)}) collective-permute-start(bf16[4,64,128]{2,1,0:T(8,128)(2,1)S(1)} %get-tuple-element.77), channel_id=1, source_target_pairs={{0,4},{1,5},{2,6},{3,7},{4,0},{5,1},{6,2},{7,3},{8,12},{9,13},{10,... | collective-permute-start | bytes 196616 | tf_op jit(solution)/shard_map/ppermute | solution.py:82
  33.2 19.2 %copy-start.2 = (bf16[4,4,64,128]{3,2,1,0:T(8,128)(2,1)}, bf16[4,4,64,128]{3,2,1,0:T(8,128)(2,1)S(1)}, u32[]{:S(2)}) copy-start(bf16[4,4,64,128]{3,2,1,0:T(8,128)(2,1)S(1)} %pad_maximum_fusion) | copy-start | bytes 786436
  33.2 9.1 %collective-permute-start.8 = (bf16[16,64,128]{2,1,0:T(8,128)(2,1)S(1)}, bf16[16,64,128]{2,1,0:T(8,128)(2,1)S(1)}, u32[]{:S(2)}, u32[]{:S(2)}) collective-permute-start(bf16[16,64,128]{2,1,0:T(8,128)(2,1)S(1)} %bitcast.36), channel_id=1, source_target_pairs={{0,1},{1,0},{2,3},{3,2},{4,5},{5,4},{6,7},{7,6},{8,9},{9,8},{10,11... | collective-permute-start | bytes 786440 | tf_op jit(solution)/shard_map/ppermute | solution.py:82
  36.2 8.9 %collective-permute-start.7 = (bf16[16,64,128]{2,1,0:T(8,128)(2,1)S(1)}, bf16[16,64,128]{2,1,0:T(8,128)(2,1)S(1)}, u32[]{:S(2)}, u32[]{:S(2)}) collective-permute-start(bf16[16,64,128]{2,1,0:T(8,128)(2,1)S(1)} %bitcast.37), channel_id=1, source_target_pairs={{0,65},{1,64},{2,67},{3,66},{4,69},{5,68},{6,71},{7,70},{8,73},{9,... | collective-permute-start | bytes 786440 | tf_op jit(solution)/shard_map/ppermute | solution.py:82
  36.5 8.6 %collective-permute-start.6 = (bf16[16,64,128]{2,1,0:T(8,128)(2,1)S(1)}, bf16[16,64,128]{2,1,0:T(8,128)(2,1)S(1)}, u32[]{:S(2)}, u32[]{:S(2)}) collective-permute-start(bf16[16,64,128]{2,1,0:T(8,128)(2,1)S(1)} %bitcast.38), channel_id=1, source_target_pairs={{0,64},{1,65},{2,66},{3,67},{4,68},{5,69},{6,70},{7,71},{8,72},{9,... | collective-permute-start | bytes 786440 | tf_op jit(solution)/shard_map/ppermute | solution.py:82
  38.3 14.0 %collective-permute-start.9 = (bf16[16,64,128]{2,1,0:T(8,128)(2,1)S(1)}, bf16[16,64,128]{2,1,0:T(8,128)(2,1)S(1)}, u32[]{:S(2)}, u32[]{:S(2)}) collective-permute-start(bf16[16,64,128]{2,1,0:T(8,128)(2,1)S(1)} %bitcast.39), channel_id=1, source_target_pairs={{0,8},{1,9},{2,10},{3,11},{4,12},{5,13},{6,14},{7,15},{8,0},{9,1},... | collective-permute-start | bytes 786440 | tf_op jit(solution)/shard_map/ppermute | solution.py:82
  42.3 10.0 %copy-start.4 = (bf16[16,64,128]{2,1,0:T(8,128)(2,1)}, bf16[16,64,128]{2,1,0:T(8,128)(2,1)S(1)}, u32[]{:S(2)}) copy-start(bf16[16,64,128]{2,1,0:T(8,128)(2,1)S(1)} %collective-permute-done.8.refs_3_) | copy-start | bytes 786436
  42.3 10.0 %collective-permute-start.12 = (bf16[16,64,128]{2,1,0:T(8,128)(2,1)S(1)}, bf16[16,64,128]{2,1,0:T(8,128)(2,1)S(1)}, u32[]{:S(2)}, u32[]{:S(2)}) collective-permute-start(bf16[16,64,128]{2,1,0:T(8,128)(2,1)S(1)} %collective-permute-done.8.refs_3_), channel_id=1, source_target_pairs={{0,8},{1,9},{2,10},{3,11},{4,12},{5,13},{6,14},{7,15},{8,0},{9,1},... | collective-permute-start | bytes 786440 | tf_op jit(solution)/shard_map/ppermute | solution.py:82
  45.1 7.2 %copy-start.5 = (bf16[16,64,128]{2,1,0:T(8,128)(2,1)}, bf16[16,64,128]{2,1,0:T(8,128)(2,1)S(1)}, u32[]{:S(2)}) copy-start(bf16[16,64,128]{2,1,0:T(8,128)(2,1)S(1)} %collective-permute-done.7.refs_2_) | copy-start | bytes 786436
  45.1 7.2 %collective-permute-start.11 = (bf16[16,64,128]{2,1,0:T(8,128)(2,1)S(1)}, bf16[16,64,128]{2,1,0:T(8,128)(2,1)S(1)}, u32[]{:S(2)}, u32[]{:S(2)}) collective-permute-start(bf16[16,64,128]{2,1,0:T(8,128)(2,1)S(1)} %collective-permute-done.7.refs_2_), channel_id=1, source_target_pairs={{0,8},{1,9},{2,10},{3,11},{4,12},{5,13},{6,14},{7,15},{8,0},{9,1},... | collective-permute-start | bytes 786440 | tf_op jit(solution)/shard_map/ppermute | solution.py:82
  45.2 7.2 %collective-permute-start.10 = (bf16[16,64,128]{2,1,0:T(8,128)(2,1)S(1)}, bf16[16,64,128]{2,1,0:T(8,128)(2,1)S(1)}, u32[]{:S(2)}, u32[]{:S(2)}) collective-permute-start(bf16[16,64,128]{2,1,0:T(8,128)(2,1)S(1)} %collective-permute-done.6.refs_1_), channel_id=1, source_target_pairs={{0,8},{1,9},{2,10},{3,11},{4,12},{5,13},{6,14},{7,15},{8,0},{9,1},... | collective-permute-start | bytes 786440 | tf_op jit(solution)/shard_map/ppermute | solution.py:82
  88.6 3.3 %collective-permute-start.13 = (bf16[64,80,128]{2,1,0:T(8,128)(2,1)}, bf16[64,80,128]{2,1,0:T(8,128)(2,1)S(1)}, u32[]{:S(2)}, u32[]{:S(2)}) collective-permute-start(bf16[64,80,128]{2,1,0:T(8,128)(2,1)} %get-tuple-element.53), channel_id=1, source_target_pairs={{0,8},{1,9},{2,10},{3,11},{4,12},{5,13},{6,14},{7,15},{8,0},{9,1},... | collective-permute-start | bytes 3932168 | tf_op jit(solution)/shard_map/ppermute | solution.py:82
  94.5 11.2 %collective-permute-start.14 = (bf16[16,80,128]{2,1,0:T(8,128)(2,1)}, bf16[16,80,128]{2,1,0:T(8,128)(2,1)S(1)}, u32[]{:S(2)}, u32[]{:S(2)}) collective-permute-start(bf16[16,80,128]{2,1,0:T(8,128)(2,1)} %get-tuple-element.66), channel_id=1, source_target_pairs={{0,16},{1,17},{2,18},{3,19},{4,20},{5,21},{6,22},{7,23},{8,24},{9,... | collective-permute-start | bytes 983048 | tf_op jit(solution)/shard_map/ppermute | solution.py:82
  94.9 18.7 %collective-permute-start.16 = (bf16[16,80,128]{2,1,0:T(8,128)(2,1)}, bf16[16,80,128]{2,1,0:T(8,128)(2,1)S(1)}, u32[]{:S(2)}, u32[]{:S(2)}) collective-permute-start(bf16[16,80,128]{2,1,0:T(8,128)(2,1)} %get-tuple-element.67), channel_id=1, source_target_pairs={{0,32},{1,33},{2,34},{3,35},{4,36},{5,37},{6,38},{7,39},{8,40},{9,... | collective-permute-start | bytes 983048 | tf_op jit(solution)/shard_map/ppermute | solution.py:82
  98.4 15.2 %collective-permute-start.15 = (bf16[16,80,128]{2,1,0:T(8,128)(2,1)}, bf16[16,80,128]{2,1,0:T(8,128)(2,1)S(1)}, u32[]{:S(2)}, u32[]{:S(2)}) collective-permute-start(bf16[16,80,128]{2,1,0:T(8,128)(2,1)} %get-tuple-element.68), channel_id=1, source_target_pairs={{0,48},{1,49},{2,50},{3,51},{4,52},{5,53},{6,54},{7,55},{8,56},{9,... | collective-permute-start | bytes 983048 | tf_op jit(solution)/shard_map/ppermute | solution.py:82
  99.3 28.8 %all-to-all-start.1 = ((bf16[8,2,4,64,128]{4,3,2,1,0:T(8,128)(2,1)}), bf16[8,2,4,64,128]{4,3,2,1,0:T(8,128)(2,1)S(1)}, u32[]{:S(2)}, u32[]{:S(2)}) async-start(bf16[8,2,4,64,128]{4,3,2,1,0:T(8,128)(2,1)} %get-tuple-element.51), calls=%async_computation.1 | async-start | bytes 2097152 | tf_op jit(solution)/shard_map/all_to_all | solution.py:346
  113.8 8.6 %collective-permute-start.17 = (bf16[4,80,128]{2,1,0:T(8,128)(2,1)S(1)}, bf16[4,80,128]{2,1,0:T(8,128)(2,1)S(1)}, u32[]{:S(2)}, u32[]{:S(2)}) collective-permute-start(bf16[4,80,128]{2,1,0:T(8,128)(2,1)S(1)} %get-tuple-element.69), channel_id=1, source_target_pairs={{0,2},{1,3},{2,4},{3,5},{4,6},{5,7},{6,0},{7,1},{8,10},{9,11},{10,... | collective-permute-start | bytes 245768 | tf_op jit(solution)/shard_map/ppermute | solution.py:82
  114.0 9.4 %collective-permute-start.19 = (bf16[4,80,128]{2,1,0:T(8,128)(2,1)S(1)}, bf16[4,80,128]{2,1,0:T(8,128)(2,1)S(1)}, u32[]{:S(2)}, u32[]{:S(2)}) collective-permute-start(bf16[4,80,128]{2,1,0:T(8,128)(2,1)S(1)} %get-tuple-element.70), channel_id=1, source_target_pairs={{0,4},{1,5},{2,6},{3,7},{4,0},{5,1},{6,2},{7,3},{8,12},{9,13},{10,... | collective-permute-start | bytes 245768 | tf_op jit(solution)/shard_map/ppermute | solution.py:82
  117.9 5.5 %collective-permute-start.18 = (bf16[4,80,128]{2,1,0:T(8,128)(2,1)S(1)}, bf16[4,80,128]{2,1,0:T(8,128)(2,1)S(1)}, u32[]{:S(2)}, u32[]{:S(2)}) collective-permute-start(bf16[4,80,128]{2,1,0:T(8,128)(2,1)S(1)} %get-tuple-element.71), channel_id=1, source_target_pairs={{0,6},{1,7},{2,0},{3,1},{4,2},{5,3},{6,4},{7,5},{8,14},{9,15},{10,... | collective-permute-start | bytes 245768 | tf_op jit(solution)/shard_map/ppermute | solution.py:82
  124.1 5.3 %collective-permute-start.22 = (bf16[80,128]{1,0:T(8,128)(2,1)S(1)}, bf16[80,128]{1,0:T(8,128)(2,1)S(1)}, u32[]{:S(2)}, u32[]{:S(2)}) collective-permute-start(bf16[80,128]{1,0:T(8,128)(2,1)S(1)} %get-tuple-element.72), channel_id=1, source_target_pairs={{0,1},{1,0},{2,3},{3,2},{4,5},{5,4},{6,7},{7,6},{8,9},{9,8},{10,11... | collective-permute-start | bytes 61448 | tf_op jit(solution)/shard_map/ppermute | solution.py:82
  126.0 3.8 %collective-permute-start.21 = (bf16[80,128]{1,0:T(8,128)(2,1)S(1)}, bf16[80,128]{1,0:T(8,128)(2,1)S(1)}, u32[]{:S(2)}, u32[]{:S(2)}) collective-permute-start(bf16[80,128]{1,0:T(8,128)(2,1)S(1)} %get-tuple-element.73), channel_id=1, source_target_pairs={{0,65},{1,64},{2,67},{3,66},{4,69},{5,68},{6,71},{7,70},{8,73},{9,... | collective-permute-start | bytes 61448 | tf_op jit(solution)/shard_map/ppermute | solution.py:82
  127.7 5.0 %collective-permute-start.20 = (bf16[80,128]{1,0:T(8,128)(2,1)S(1)}, bf16[80,128]{1,0:T(8,128)(2,1)S(1)}, u32[]{:S(2)}, u32[]{:S(2)}) collective-permute-start(bf16[80,128]{1,0:T(8,128)(2,1)S(1)} %get-tuple-element.74), channel_id=1, source_target_pairs={{0,64},{1,65},{2,66},{3,67},{4,68},{5,69},{6,70},{7,71},{8,72},{9,... | collective-permute-start | bytes 61448 | tf_op jit(solution)/shard_map/ppermute | solution.py:82
  (12 other events, 30.8 us)

commit v5 on v4

--- a/solution.py
+++ b/solution.py
@@ -102,8 +102,10 @@
     return [held[0]] + [send(held[at], x=HOPS[at]) for at in (1, 2, 3)]
 
 
-def tile_bias_kernel(pair_ref, gain_ref, wb_ref, msg_ref, rows_ref):
+def tile_bias_kernel(pair_ref, gain_ref, wb_ref, msg_ref, n_ref, u_ref, rows_ref):
     unit, inverse, normed = normalize(pair_ref[...].astype(F32), gain_ref[...])
+    n_ref[...] = normed
+    u_ref[...] = unit.astype(BF16)
     bias = dot(wb_ref[...], normed, NT)
     for half in range(8):
         first = bias[0:8, half * 128 : half * 128 + 128]
@@ -117,13 +119,13 @@
     msg_ref[...] = rows_ref[...].astype(BF16)
 
 
-def pack_kernel(pair_ref, cot_ref, out_ref):
+def pack_kernel(pair_ref, cot_ref, after_ref, out_ref):
     out_ref[:, 0] = pair_ref[...]
     out_ref[:, 1] = cot_ref[...]
 
 
 def project_kernel(scale, rows_ref, gain_ref, wcat_ref, off_ref, wout_ref,
-                   q_ref, k_ref, v_ref, a_ref, gate_ref, gg_ref, n_ref):
+                   q_ref, k_ref, v_ref, a_ref, gate_ref, gg_ref, n_ref, u_ref):
     values = rows_ref[:, 0, 0].reshape(512, 128).astype(F32)
     unit, inverse, normed = normalize(values, gain_ref[...])
     projected = dot(normed, wcat_ref[...])
@@ -136,6 +138,7 @@
     gate_ref[0] = gate
     gg_ref[0] = grad_gated
     n_ref[0] = normed
+    u_ref[0] = unit.astype(BF16)
 
 
 def attend_kernel(place_ref, q_ref, k_ref, v_ref, a_ref, *refs):
@@ -150,11 +153,13 @@
             for inner in range(16):
                 owner = x[at % 4] + y[inner // 4] + z[inner % 4] + core[at // 4]
                 block_scr[owner] = pieces[at][inner]
-
-    for r in range(4):
+        dk_ref[...] = jnp.zeros(dk_ref.shape, F32)
+        dv_ref[...] = jnp.zeros(dv_ref.shape, F32)
+
+    for r in range(8):
         for m in range(4):
-            left = block_scr[(chunk * 4 + r) * 8 + 2 * m].astype(F32)
-            right = block_scr[(chunk * 4 + r) * 8 + 2 * m + 1].astype(F32)
+            left = block_scr[(chunk * 8 + r) * 8 + 2 * m].astype(F32)
+            right = block_scr[(chunk * 8 + r) * 8 + 2 * m + 1].astype(F32)
             lanes = slice(m * 128, m * 128 + 128)
             bias_scr[r * 128 : r * 128 + 64, lanes] = join_low(left, right)
             bias_scr[r * 128 + 64 : r * 128 + 128, lanes] = join_high(left, right)
@@ -162,13 +167,13 @@
     mask_f = head_mask(4, 128, F32)
 
     def spread(rows):
-        return (rows.reshape(8, 1, 16, 128) * mask).reshape(512, 128)
+        return (rows.reshape(16, 1, 16, 128) * mask).reshape(1024, 128)
 
     def collect(rows):
-        return jnp.sum(rows.reshape(8, 4, 16, 128) * mask_f, axis=1).reshape(128, 128)
-
-    def step(row, carry):
-        at = pl.ds(pl.multiple_of(chunk * 128, 128), 128)
+        return jnp.sum(rows.reshape(16, 4, 16, 128) * mask_f, axis=1).reshape(256, 128)
+
+    at = pl.ds(pl.multiple_of(chunk * 256, 256), 256)
+    for row in range(4):
         q_big = spread(q_ref[row, at, :])
         a_big = spread(a_ref[row, at, :])
         keys = k_ref[row]
@@ -176,45 +181,29 @@
         scores = dot(q_big, keys, NT) + bias_scr[...]
         top = jnp.max(scores, axis=-1, keepdims=True)
         powers = jnp.exp(scores - top)
-        probs = powers * (1.0 / jnp.sum(powers, axis=-1, keepdims=True))
-        probs_low = probs.astype(BF16)
-        att_ref[row, at, :] = collect(dot(probs_low, values))
+        inverse = 1.0 / jnp.sum(powers, axis=-1, keepdims=True)
+        powers_low = powers.astype(BF16)
+        attended = dot(powers_low, values) * inverse
+        att_ref[row, at, :] = collect(attended)
+        a_float = a_big.astype(F32)
+        inner = jnp.sum(a_float * attended, axis=-1, keepdims=True)
         grad_probs = dot(a_big, values, NT)
-        inner = jnp.sum(probs * grad_probs, axis=-1, keepdims=True)
-        score_grad = probs * (grad_probs - inner)
+        score_grad = powers * ((grad_probs - inner) * inverse)
         score_low = score_grad.astype(BF16)
         dq_ref[row, at, :] = collect(dot(score_low, keys))
-        dk = dot(q_big, score_low, TN)
-        dv = dot(a_big, probs_low, TN)
-
-        @pl.when(chunk == 0)
-        def _():
-            dk_ref[row] = dk
-            dv_ref[row] = dv
-
-        @pl.when(chunk > 0)
-        def _():
-            dk_ref[row] += dk
-            dv_ref[row] += dv
-
-        @pl.when(row == 0)
-        def _():
+        dk_ref[row] += dot(q_big, score_low, TN)
+        dv_ref[row] += dot((a_float * inverse).astype(BF16), powers_low, TN)
+        if row == 0:
             sum_scr[...] = score_grad
-
-        @pl.when(row > 0)
-        def _():
+        else:
             sum_scr[...] += score_grad
 
-        return carry
-
-    lax.fori_loop(0, 4, step, 0)
-
-    xs = [slot_of(chunk // 2 + 2 * high - place_ref[0]) for high in range(2)]
-    ys = [slot_of(at - place_ref[1]) * 4 for at in range(4)]
-    zs = [slot_of((chunk % 2) * 2 + at - place_ref[2]) * 16 for at in range(2)]
+    xs = [slot_of(chunk + 2 * high - place_ref[0]) for high in range(2)]
+    ys = [slot_of(b - place_ref[1]) * 4 for b in range(4)]
+    zs = [slot_of(c - place_ref[2]) * 16 for c in range(4)]
 
     def emit(even_ref, odd_ref):
-        for r in range(4):
+        for r in range(8):
             out_ref = odd_ref if r % 2 else even_ref
             for m in range(4):
                 lanes = slice(m * 128, m * 128 + 128)
@@ -233,7 +222,7 @@
         emit(other_ref, mine_ref)
 
 
-def post_kernel(scale, place_ref, att_ref, dq_ref, dk_ref, dv_ref, gate_ref, gg_ref, n_ref, rows_ref, wcat_ref,
+def post_kernel(scale, place_ref, att_ref, dq_ref, dk_ref, dv_ref, gate_ref, gg_ref, n_ref, u_ref, rows_ref, wcat_ref,
                 wout_ref, held_mine, held_other, ug_ref, mine_ref, other_ref, off_ref, w_scr, o_scr, s_scr, p_scr):
     row = pl.program_id(0)
     attended = att_ref[0]
@@ -248,9 +237,12 @@
     kpre = (jnp.transpose(dk_ref[0]) * scale).astype(BF16)
     vpre = jnp.transpose(dv_ref[0]).astype(BF16)
     cat = jnp.concatenate([qpre, kpre, vpre, gpre], axis=1)
-    ug_ref[:, 1, 0] = dot(cat, wcat_ref[...], NT).astype(BF16).reshape(8, 64, 128)
+    grad_normed = dot(cat, wcat_ref[...], NT)
+    ug_ref[:, 1, 0] = grad_normed.astype(BF16).reshape(8, 64, 128)
     w_part = dot(n_ref[0], cat, TN)
     off = jnp.sum(gpre.astype(F32), axis=0, keepdims=True)
+    gain = jnp.sum(grad_normed * u_ref[0].astype(F32), axis=0, keepdims=True)
+    off = jnp.concatenate([off, gain], axis=0)
 
     @pl.when(row == 0)
     def _():
@@ -279,12 +271,11 @@
             owner = z[at // 16] + y[at // 4 % 4] + x[at % 4]
             mine_ref[at] = p_scr[owner + core[0]].astype(BF16)
             other_ref[at] = p_scr[owner + core[1]].astype(BF16)
-        off_ref[...] = jnp.broadcast_to(s_scr[...], off_ref.shape)
-
-
-def tile_final_kernel(pair_ref, ug_ref, one_ref, two_ref, three_ref, four_ref, off_ref, gain_ref, wb_ref,
-                      up_ref, gp_ref, msg_ref, rows_ref, bg_scr):
-    up_ref[...] = ug_ref[:, 0].reshape(2048, 128)
+        off_ref[...] = s_scr[...]
+
+
+def tile_sums_kernel(n_ref, u_ref, one_ref, two_ref, three_ref, four_ref, off_ref, wb_ref,
+                     both_ref, msg_ref, rows_ref, bg_scr):
     rows_ref[...] = (one_ref[...].astype(F32) + two_ref[...].astype(F32)) + (
         three_ref[...].astype(F32) + four_ref[...].astype(F32)
     )
@@ -297,31 +288,45 @@
             bg_scr[head : head + 1, half * 128 : half * 128 + 128] = join_low(left, right)
             bg_scr[head : head + 1, (8 + half) * 128 : (8 + half) * 128 + 128] = join_high(left, right)
     bg = bg_scr[...]
-    high = bg.astype(BF16)
-    low = (bg - high.astype(F32)).astype(BF16)
-    both = jnp.concatenate([high.astype(F32), low.astype(F32)], axis=0).astype(BF16)
+    high = bg.astype(BF16).astype(F32)
+    both = jnp.concatenate([high, bg - high], axis=0).astype(BF16)
+    both_ref[...] = both
+    bias_part = dot(both, n_ref[...])
+    unit_part = dot(both, u_ref[...])
+    gain_part = jnp.sum(unit_part * wb_ref[...].astype(F32), axis=0, keepdims=True) + off_ref[1:2]
+    params = rows_ref[64:72, :] + rows_ref[72:80, :]
+    row = lax.broadcasted_iota(jnp.int32, (8, 128), 0)
+    params = jnp.where(row == 5, off_ref[0:1], jnp.where(row == 6, gain_part, params))
+    small = bias_part[0:8] + bias_part[8:16]
+    message = jnp.concatenate([params, small], axis=0).astype(BF16)
+    msg_ref[...] = jnp.broadcast_to(message[None], msg_ref.shape)
+
+
+def tile_final_kernel(pair_ref, ug_ref, both_ref, gain_ref, wb_ref, up_ref, gp_ref):
+    up_ref[...] = ug_ref[:, 0].reshape(2048, 128)
     unit, inverse, normed = normalize(pair_ref[...].astype(F32), gain_ref[...])
-    total = ug_ref[:, 1].reshape(2048, 128).astype(F32) + dot(both, wb_ref[...], TN)
-    bias_part = dot(both, normed)
-    gain_part = jnp.sum(total * unit, axis=0, keepdims=True)
+    total = ug_ref[:, 1].reshape(2048, 128).astype(F32) + dot(both_ref[...], wb_ref[...], TN)
     scaled = total * gain_ref[...]
     first = jnp.mean(scaled, axis=-1, keepdims=True)
     second = jnp.mean(scaled * unit, axis=-1, keepdims=True)
     gp_ref[...] = ((scaled - first - unit * second) * inverse).astype(BF16)
-    params = rows_ref[64:72, :] + rows_ref[72:80, :]
-    row = lax.broadcasted_iota(jnp.int32, (8, 128), 0)
-    params = jnp.where(row == 5, off_ref[...], jnp.where(row == 6, gain_part, params))
-    small = bias_part[0:8] + bias_part[8:16]
-    msg_ref[...] = jnp.broadcast_to(jnp.concatenate([params, small], axis=0)[None], msg_ref.shape)
-
-
-def finish_kernel(msg_ref, q_ref, k_ref, v_ref, g_ref, o_ref, off_ref, gain_ref, bias_ref):
+
+
+def finish_kernel(msg_ref, q_ref, k_ref, v_ref, g_ref, o_ref, off_ref, gain_ref, bias_ref, msg_scr):
+    messages = msg_ref[...].astype(F32)
+    msg_scr[...] = messages
     for t, ref in enumerate((q_ref, k_ref, v_ref, g_ref, o_ref)):
-        ref[...] = msg_ref[:, t, :]
-    small = jnp.sum(msg_ref[...], axis=0)
+        ref[...] = msg_scr[:, t, :]
+    small = jnp.sum(messages, axis=0)
     off_ref[...] = small[5]
     gain_ref[...] = small[6]
     bias_ref[...] = small[8:12]
+
+
+def estimate(microseconds):
+    return pl.CostEstimate(
+        flops=microseconds * 1_000_000_000, bytes_accessed=microseconds * 3_600_000, transcendentals=0
+    )
 
 
 def sds(shape, dtype):
@@ -345,9 +350,9 @@
     def swap(value, axes):
         return lax.all_to_all(value, axes, split_axis=0, concat_axis=0, tiled=True)
 
-    bias_msg = pl.pallas_call(
+    bias_msg, normed_tile, unit_tile = pl.pallas_call(
         tile_bias_kernel,
-        out_shape=sds((64, 128), BF16),
+        out_shape=[sds((64, 128), BF16), sds((2048, 128), BF16), sds((2048, 128), BF16)],
         scratch_shapes=[pltpu.VMEM((64, 128), F32)],
         compiler_params=PARAMS,
         name="tile_bias",
@@ -358,23 +363,26 @@
     smem = pl.BlockSpec(memory_space=pltpu.SMEM)
     packed = pl.pallas_call(
         pack_kernel,
+        in_specs=[whole((8, 4, 64, 128))] * 2 + [pl.BlockSpec(memory_space=pl.ANY)],
+        cost_estimate=estimate(2),
         out_shape=sds((8, 2, 4, 64, 128), BF16),
         compiler_params=PARAMS,
         name="pack",
-    )(pair_rep.reshape(8, 4, 64, 128), cotangent.reshape(8, 4, 64, 128))
+    )(pair_rep.reshape(8, 4, 64, 128), cotangent.reshape(8, 4, 64, 128), bias_msg)
     both_rows = swap(packed, "col")
     bias_pieces = gather_bias(bias_msg)
 
     from_rows = pl.BlockSpec((8, 2, 1, 64, 128), lambda i: (0, 0, i, 0, 0))
     from_cot = pl.BlockSpec((8, 1, 1, 64, 128), lambda i: (0, 1, i, 0, 0))
     by_row = pl.BlockSpec((1, 512, 128), lambda i: (i, 0, 0))
-    query, keys, values, grad_att, gate, grad_gated, normed = pl.pallas_call(
+    query, keys, values, grad_att, gate, grad_gated, normed, unit = pl.pallas_call(
         functools.partial(project_kernel, scale),
         grid=(4,),
         in_specs=[from_rows, whole((1, 128)), whole((128, 512)), whole((1, 128)), whole((128, 128))],
-        out_specs=[by_row] * 7,
-        out_shape=[sds((4, 512, 128), t) for t in (BF16, BF16, BF16, BF16, F32, F32, BF16)],
-        compiler_params=PARAMS,
+        out_specs=[by_row] * 8,
+        out_shape=[sds((4, 512, 128), t) for t in (BF16, BF16, BF16, BF16, F32, F32, BF16, BF16)],
+        compiler_params=PARAMS,
+        cost_estimate=estimate(5),
         name="project",
     )(both_rows, gain, wcat, offset, w_out)
 
@@ -382,12 +390,12 @@
     full_t = whole((4, 128, 512))
     attended, dq, dk, dv, mine, other = pl.pallas_call(
         attend_kernel,
-        grid=(4,),
+        grid=(2,),
         in_specs=[smem, full, full, full, full] + [whole((16, 64, 128))] * 8,
         out_specs=[full, full, full_t, full_t, whole((64, 80, 128)), whole((64, 80, 128))],
         out_shape=[sds((4, 512, 128), F32), sds((4, 512, 128), F32), sds((4, 128, 512), F32),
                    sds((4, 128, 512), F32), sds((64, 80, 128), BF16), sds((64, 80, 128), BF16)],
-        scratch_shapes=[pltpu.VMEM((128, 64, 128), BF16), pltpu.VMEM((512, 512), F32), pltpu.VMEM((512, 512), F32)],
+        scratch_shapes=[pltpu.VMEM((128, 64, 128), BF16), pltpu.VMEM((1024, 512), F32), pltpu.VMEM((1024, 512), F32)],
         compiler_params=PARAMS,
         name="attend",
     )(place, query, keys, values, grad_att, *bias_pieces)
@@ -397,30 +405,38 @@
     ug_rows, mine, other, off = pl.pallas_call(
         functools.partial(post_kernel, scale),
         grid=(4,),
-        in_specs=[smem, by_row, by_row, by_row_t, by_row_t, by_row, by_row, by_row, from_cot,
+        in_specs=[smem, by_row, by_row, by_row_t, by_row_t, by_row, by_row, by_row, by_row, from_cot,
                   whole((128, 512)), whole((128, 128))] + [pl.BlockSpec(memory_space=pl.ANY)] * 2,
-        out_specs=[from_rows, tail, tail, whole((8, 128))],
+        out_specs=[from_rows, tail, tail, whole((2, 128))],
         out_shape=[sds((8, 2, 4, 64, 128), BF16), sds((64, 80, 128), BF16), sds((64, 80, 128), BF16),
-                   sds((8, 128), F32)],
-        scratch_shapes=[pltpu.VMEM((128, 512), F32), pltpu.VMEM((128, 128), F32), pltpu.VMEM((1, 128), F32),
+                   sds((2, 128), F32)],
+        scratch_shapes=[pltpu.VMEM((128, 512), F32), pltpu.VMEM((128, 128), F32), pltpu.VMEM((2, 128), F32),
                         pltpu.VMEM((128, 16, 128), F32)],
-        input_output_aliases={11: 1, 12: 2},
+        input_output_aliases={12: 1, 13: 2},
         compiler_params=PARAMS,
         name="post",
-    )(place, attended, dq, dk, dv, gate, grad_gated, normed, both_rows, wcat, w_out, mine, other)
+    )(place, attended, dq, dk, dv, gate, grad_gated, normed, unit, both_rows, wcat, w_out, mine, other)
     ug_tile = swap(ug_rows, "col")
     sums = scatter_sums(mine, other)
-    update, grad_pair, final_msg = pl.pallas_call(
+    both, final_msg = pl.pallas_call(
+        tile_sums_kernel,
+        out_shape=[sds((16, 2048), BF16), sds((128, 16, 128), BF16)],
+        scratch_shapes=[pltpu.VMEM((80, 128), F32), pltpu.VMEM((8, 2048), F32)],
+        compiler_params=PARAMS,
+        name="tile_sums",
+    )(normed_tile, unit_tile, *sums, off, wb_two)
+    final_in = swap(final_msg, everyone)
+    update, grad_pair = pl.pallas_call(
         tile_final_kernel,
-        out_shape=[sds((2048, 128), BF16), sds((2048, 128), BF16), sds((128, 16, 128), F32)],
-        scratch_shapes=[pltpu.VMEM((80, 128), F32), pltpu.VMEM((8, 2048), F32)],
-        compiler_params=PARAMS,
+        out_shape=[sds((2048, 128), BF16), sds((2048, 128), BF16)],
+        compiler_params=PARAMS,
+        cost_estimate=estimate(5),
         name="tile_final",
-    )(pair_tile, ug_tile.reshape(8, 2, 256, 128), *sums, off, gain, wb_two)
-    final_in = swap(final_msg, everyone)
+    )(pair_tile, ug_tile.reshape(8, 2, 256, 128), both, gain, wb_two)
     g_query, g_key, g_value, g_gate, g_out, g_off, g_gain, g_bias = pl.pallas_call(
         finish_kernel,
         out_shape=[sds((128, 128), F32)] * 5 + [sds((128,), F32)] * 2 + [sds((4, 128), F32)],
+        scratch_shapes=[pltpu.VMEM((128, 16, 128), F32)],
         compiler_params=PARAMS,
         name="finish",
     )(final_in)

time: 165 us -> 154 us (0.933)
  blocking collectives: 24.1 us -> 0 us
  waiting for transfers between devices: 37.3 us -> 47.6 us
  starting transfers between devices: 42.2 us -> 48.3 us
  Pallas kernels: 51.5 us -> 47.2 us
    all_to_all x1 -> x0, blocking collectives: 24.1 us -> none  [swap(): return lax.all_to_all(value, axes, split_axis=0, concat_axis=0, tiled=True)]
    all_to_all x2 -> x3, waiting for transfers between devices: 0.01 us -> 9.67 us  [swap(): return lax.all_to_all(value, axes, split_axis=0, concat_axis=0, tiled=True)]
    all_to_all x2 -> x3, starting transfers between devices: 11.9 us -> 17 us  [swap(): return lax.all_to_all(value, axes, split_axis=0, concat_axis=0, tiled=True)]
    pallas_call x3 -> x4, Pallas kernels: 33.5 us -> 29.8 us  [the longest x1 22.4 us: body(): pl.pallas_call(attend_kernel, grid=(2,), in_specs=[smem, full, full, full...]
    unnamed x41 -> x43, local copies, waits for them, and re-layouts: 2.54 us -> 3.42 us
  transfers between devices with their start and end apart: 25 -> 26, of which waited for: 14 -> 16; matrix products, arithmetic and copies ran while one was open for 2% -> 1% of each run, Pallas kernels for 5% -> 7%
where the time goes in v5:
time: 154 us; the launch traced here: 153 us
  starting transfers between devices  48.3 us (31%)
  waiting for transfers between devices  47.6 us (31%)
  Pallas kernels  47.2 us (31%)
  local copies, waits for them, and re-layouts  5.73 us (4%)
  other arithmetic  3.11 us (2%)
    ppermute x23, waiting for transfers between devices, send(): return lax.ppermute(value, ('row', 'col'), shift_pairs(**shift))  37.9 us
    ppermute x23, starting transfers between devices, send(): return lax.ppermute(value, ('row', 'col'), shift_pairs(**shift))  31.3 us
    pallas_call x1, Pallas kernels, body(): pl.pallas_call(attend_kernel, grid=(2,), in_specs=[smem, full, full, full...  22.4 us
    all_to_all x3, starting transfers between devices, swap(): return lax.all_to_all(value, axes, split_axis=0, concat_axis=0, tiled=True)  17 us
    all_to_all x3, waiting for transfers between devices, swap(): return lax.all_to_all(value, axes, split_axis=0, concat_axis=0, tiled=True)  9.67 us
    pallas_call x1, Pallas kernels, body(): pl.pallas_call(functools.partial(post_kernel, scale), grid=(4,), in_specs...  6.64 us
    pallas_call x1, Pallas kernels, body(): pl.pallas_call(functools.partial(project_kernel, scale), grid=(4,), in_sp...  5.07 us
    pallas_call x1, Pallas kernels, body(): pl.pallas_call(tile_final_kernel, out_shape=[sds((2048, 128), BF16), sds(...  3.71 us
  transfers between devices with their start and end apart: 26, of which 16 were waited for; matrix products, arithmetic and copies ran while one was open for 1% of the time, Pallas kernels for 7%

profile of v5, /device:TPU:0, one launch (start us, length us, event | category | flops | bytes accessed | tf_op | source)
XLA Modules:
  0.0 152.9 jit_solution(13541465660382178585)
XLA Ops:
  1.9 2.7 %tile_bias.1 = (bf16[64,128]{1,0:T(8,128)(2,1)}, bf16[2048,128]{1,0:T(8,128)(2,1)}, bf16[2048,128]{1,0:T(8,128)(2,1)}) custom-call(bf16[2048,128]{1,0:T(8,128)(2,1)} %bitcast.38, f32[1,128]{1,0:T(1,128)} %bitcast.49, bf16[16,128]{1,0:T(8,128)(2,1)} %pad_maximum_fusion.2.wb_ref), custom_call_target="tpu_custom_call" | custom-call | tf_op jit(solution)/shard_map/tile_bias/pallas_call | solution.py:353
  4.6 2.3 %pack.1 = bf16[8,2,4,64,128]{4,3,2,1,0:T(8,128)(2,1)} custom-call(bf16[8,4,64,128]{3,2,1,0:T(8,128)(2,1)} %bitcast.39, bf16[8,4,64,128]{3,2,1,0:T(8,128)(2,1)} %bitcast.52, bf16[64,128]{1,0:T(8,128)(2,1)} %get-tuple-element.43.after_ref), custom_call_target="tpu_custom_call" | custom-call | flops 2000000000 | bytes 7200000 | tf_op jit(solution)/shard_map/pack/pallas_call | solution.py:364
  6.9 7.2 %all-to-all-start = ((bf16[8,2,4,64,128]{4,3,2,1,0:T(8,128)(2,1)}), bf16[8,2,4,64,128]{4,3,2,1,0:T(8,128)(2,1)S(1)}, u32[]{:S(2)}, u32[]{:S(2)}) async-start(bf16[8,2,4,64,128]{4,3,2,1,0:T(8,128)(2,1)} %pack.1), calls=%async_computation | async-start | bytes 2097152 | tf_op jit(solution)/shard_map/all_to_all | solution.py:351
  14.1 4.0 %collective-permute-start.2 = (bf16[64,128]{1,0:T(8,128)(2,1)S(1)}, bf16[64,128]{1,0:T(8,128)(2,1)S(1)}, u32[]{:S(2)}, u32[]{:S(2)}) collective-permute-start(bf16[64,128]{1,0:T(8,128)(2,1)S(1)} %copy-done.19), channel_id=1, source_target_pairs={{0,32},{1,33},{2,34},{3,35},{4,36},{5,37},{6,38},{7,39},{8,40},{9,... | collective-permute-start | bytes 49160 | tf_op jit(solution)/shard_map/ppermute | solution.py:82
  20.1 1.6 %collective-permute-done.1 = bf16[64,128]{1,0:T(8,128)(2,1)S(1)} collective-permute-done((bf16[64,128]{1,0:T(8,128)(2,1)S(1)}, bf16[64,128]{1,0:T(8,128)(2,1)S(1)}, u32[]{:S(2)}, u32[]{:S(2)}) %collective-permute-start.1) | collective-permute-done | bytes 16416 | tf_op jit(solution)/shard_map/ppermute | solution.py:82
  21.8 1.9 %collective-permute-done = bf16[64,128]{1,0:T(8,128)(2,1)S(1)} collective-permute-done((bf16[64,128]{1,0:T(8,128)(2,1)S(1)}, bf16[64,128]{1,0:T(8,128)(2,1)S(1)}, u32[]{:S(2)}, u32[]{:S(2)}) %collective-permute-start) | collective-permute-done | bytes 16416 | tf_op jit(solution)/shard_map/ppermute | solution.py:82
  23.7 3.2 %collective-permute-start.4 = (bf16[4,64,128]{2,1,0:T(8,128)(2,1)S(1)}, bf16[4,64,128]{2,1,0:T(8,128)(2,1)S(1)}, u32[]{:S(2)}, u32[]{:S(2)}) collective-permute-start(bf16[4,64,128]{2,1,0:T(8,128)(2,1)S(1)} %get-tuple-element.87), channel_id=1, source_target_pairs={{0,6},{1,7},{2,0},{3,1},{4,2},{5,3},{6,4},{7,5},{8,14},{9,15},{10,... | collective-permute-start | bytes 196616 | tf_op jit(solution)/shard_map/ppermute | solution.py:82
  26.9 2.3 %collective-permute-start.5 = (bf16[4,64,128]{2,1,0:T(8,128)(2,1)S(1)}, bf16[4,64,128]{2,1,0:T(8,128)(2,1)S(1)}, u32[]{:S(2)}, u32[]{:S(2)}) collective-permute-start(bf16[4,64,128]{2,1,0:T(8,128)(2,1)S(1)} %get-tuple-element.87), channel_id=1, source_target_pairs={{0,4},{1,5},{2,6},{3,7},{4,0},{5,1},{6,2},{7,3},{8,12},{9,13},{10,... | collective-permute-start | bytes 196616 | tf_op jit(solution)/shard_map/ppermute | solution.py:82
  29.4 3.9 %collective-permute-done.3 = bf16[4,64,128]{2,1,0:T(8,128)(2,1)S(1)} collective-permute-done((bf16[4,64,128]{2,1,0:T(8,128)(2,1)S(1)}, bf16[4,64,128]{2,1,0:T(8,128)(2,1)S(1)}, u32[]{:S(2)}, u32[]{:S(2)}) %collective-permute-start.3) | collective-permute-done | bytes 65568 | tf_op jit(solution)/shard_map/ppermute | solution.py:82
  33.3 2.9 %collective-permute-start.8 = (bf16[16,64,128]{2,1,0:T(8,128)(2,1)S(1)}, bf16[16,64,128]{2,1,0:T(8,128)(2,1)S(1)}, u32[]{:S(2)}, u32[]{:S(2)}) collective-permute-start(bf16[16,64,128]{2,1,0:T(8,128)(2,1)S(1)} %bitcast.32), channel_id=1, source_target_pairs={{0,1},{1,0},{2,3},{3,2},{4,5},{5,4},{6,7},{7,6},{8,9},{9,8},{10,11... | collective-permute-start | bytes 786440 | tf_op jit(solution)/shard_map/ppermute | solution.py:82
  36.7 1.6 %collective-permute-start.6 = (bf16[16,64,128]{2,1,0:T(8,128)(2,1)S(1)}, bf16[16,64,128]{2,1,0:T(8,128)(2,1)S(1)}, u32[]{:S(2)}, u32[]{:S(2)}) collective-permute-start(bf16[16,64,128]{2,1,0:T(8,128)(2,1)S(1)} %bitcast.34), channel_id=1, source_target_pairs={{0,64},{1,65},{2,66},{3,67},{4,68},{5,69},{6,70},{7,71},{8,72},{9,... | collective-permute-start | bytes 786440 | tf_op jit(solution)/shard_map/ppermute | solution.py:82
  39.0 5.2 %collective-permute-done.8.refs_3_ = bf16[16,64,128]{2,1,0:T(8,128)(2,1)S(1)} collective-permute-done((bf16[16,64,128]{2,1,0:T(8,128)(2,1)S(1)}, bf16[16,64,128]{2,1,0:T(8,128)(2,1)S(1)}, u32[]{:S(2)}, u32[]{:S(2)}) %collective-permute-start.8) | collective-permute-done | bytes 262176 | tf_op jit(solution)/shard_map/ppermute | solution.py:82
  44.1 2.0 %collective-permute-done.7.refs_2_ = bf16[16,64,128]{2,1,0:T(8,128)(2,1)S(1)} collective-permute-done((bf16[16,64,128]{2,1,0:T(8,128)(2,1)S(1)}, bf16[16,64,128]{2,1,0:T(8,128)(2,1)S(1)}, u32[]{:S(2)}, u32[]{:S(2)}) %collective-permute-start.7) | collective-permute-done | bytes 262176 | tf_op jit(solution)/shard_map/ppermute | solution.py:82
  48.5 5.1 %project.1 = (bf16[4,512,128]{2,1,0:T(8,128)(2,1)}, bf16[4,512,128]{2,1,0:T(8,128)(2,1)}, bf16[4,512,128]{2,1,0:T(8,128)(2,1)}, bf16[4,512,128]{2,1,0:T(8,128)(2...) custom-call(bf16[8,2,4,64,128]{4,3,2,1,0:T(8,128)(2,1)} %copy-done, ...), custom_call_target="tpu_custom_call" | custom-call | flops 5000000000 | bytes 18000000 | tf_op jit(solution)/shard_map/project/pallas_call | solution.py:378
  54.7 22.4 %attend.1 = (f32[4,512,128]{2,1,0:T(8,128)}, f32[4,512,128]{2,1,0:T(8,128)}, f32[4,128,512]{2,1,0:T(8,128)}, f32[4,128,512]{2,1,0:T(8,128)}, bf16[64,80,128]{2,1,0:T(8,128)(2,1)}, /*index=5*/bf16[64,80,128]{2,1,0:T(8,128)(2,1)}) custom-call(s32[4]{0:T(128)} %pad_add_fusion.place_ref, bf16[4,512,128]{2,1,0:T(8,128)(2,1)} %get-tuple-element.44.q_ref, ...), custom_call_target="tpu_custom_call" | custom-call | tf_op jit(solution)/shard_map/attend/pallas_call | solution.py:391
  77.1 6.6 %post.1 = (bf16[8,2,4,64,128]{4,3,2,1,0:T(8,128)(2,1)}, bf16[64,80,128]{2,1,0:T(8,128)(2,1)}, bf16[64,80,128]{2,1,0:T(8,128)(2,1)}, f32[2,128]{1,0:T(2,128)}) custom-call(s32[4]{0:T(128)} %pad_add_fusion.place_ref, f32[4,512,128]{2,1,0:T(8,128)} %get-tuple-element.48.att_ref, ...), custom_call_target="tpu_custom_call", output_to_operand_aliasing={{1}: (12, {}), {2}: (13, {})} | custom-call | tf_op jit(solution)/shard_map/post/pallas_call | solution.py:405
  84.3 2.9 %collective-permute-done.13 = bf16[64,80,128]{2,1,0:T(8,128)(2,1)S(1)} collective-permute-done((bf16[64,80,128]{2,1,0:T(8,128)(2,1)}, bf16[64,80,128]{2,1,0:T(8,128)(2,1)S(1)}, u32[]{:S(2)}, u32[]{:S(2)}) %collective-permute-start.13) | collective-permute-done | bytes 1310752 | tf_op jit(solution)/shard_map/ppermute | solution.py:82
  87.1 1.7 %add_convert_fusion = bf16[64,80,128]{2,1,0:T(8,128)(2,1)S(1)} fusion(bf16[64,80,128]{2,1,0:T(8,128)(2,1)S(1)} %collective-permute-done.13, bf16[64,80,128]{2,1,0:T(8,128)(2,1)} %get-tuple-element.61), kind=kLoop, calls=%fused_computation | loop fusion | flops 2621440 | bytes 3932160 | tf_op jit(solution)/shard_map/convert_element_type | solution.py:95
  90.7 3.6 %collective-permute-start.16 = (bf16[16,80,128]{2,1,0:T(8,128)(2,1)}, bf16[16,80,128]{2,1,0:T(8,128)(2,1)S(1)}, u32[]{:S(2)}, u32[]{:S(2)}) collective-permute-start(bf16[16,80,128]{2,1,0:T(8,128)(2,1)} %get-tuple-element.77), channel_id=1, source_target_pairs={{0,32},{1,33},{2,34},{3,35},{4,36},{5,37},{6,38},{7,39},{8,40},{9,... | collective-permute-start | bytes 983048 | tf_op jit(solution)/shard_map/ppermute | solution.py:82
  95.3 5.2 %all-to-all-start.1 = ((bf16[8,2,4,64,128]{4,3,2,1,0:T(8,128)(2,1)}), bf16[8,2,4,64,128]{4,3,2,1,0:T(8,128)(2,1)S(1)}, u32[]{:S(2)}, u32[]{:S(2)}) async-start(bf16[8,2,4,64,128]{4,3,2,1,0:T(8,128)(2,1)} %get-tuple-element.58), calls=%async_computation.1 | async-start | bytes 2097152 | tf_op jit(solution)/shard_map/all_to_all | solution.py:351
  101.2 8.2 %collective-permute-done.16 = bf16[16,80,128]{2,1,0:T(8,128)(2,1)S(1)} collective-permute-done((bf16[16,80,128]{2,1,0:T(8,128)(2,1)}, bf16[16,80,128]{2,1,0:T(8,128)(2,1)S(1)}, u32[]{:S(2)}, u32[]{:S(2)}) %collective-permute-start.16) | collective-permute-done | bytes 327712 | tf_op jit(solution)/shard_map/ppermute | solution.py:82
  109.6 2.0 %collective-permute-start.17 = (bf16[4,80,128]{2,1,0:T(8,128)(2,1)S(1)}, bf16[4,80,128]{2,1,0:T(8,128)(2,1)S(1)}, u32[]{:S(2)}, u32[]{:S(2)}) collective-permute-start(bf16[4,80,128]{2,1,0:T(8,128)(2,1)S(1)} %get-tuple-element.79), channel_id=1, source_target_pairs={{0,2},{1,3},{2,4},{3,5},{4,6},{5,7},{6,0},{7,1},{8,10},{9,11},{10,... | collective-permute-start | bytes 245768 | tf_op jit(solution)/shard_map/ppermute | solution.py:82
  111.6 2.1 %collective-permute-start.19 = (bf16[4,80,128]{2,1,0:T(8,128)(2,1)S(1)}, bf16[4,80,128]{2,1,0:T(8,128)(2,1)S(1)}, u32[]{:S(2)}, u32[]{:S(2)}) collective-permute-start(bf16[4,80,128]{2,1,0:T(8,128)(2,1)S(1)} %get-tuple-element.80), channel_id=1, source_target_pairs={{0,4},{1,5},{2,6},{3,7},{4,0},{5,1},{6,2},{7,3},{8,12},{9,13},{10,... | collective-permute-start | bytes 245768 | tf_op jit(solution)/shard_map/ppermute | solution.py:82
  114.3 4.1 %collective-permute-done.17 = bf16[4,80,128]{2,1,0:T(8,128)(2,1)S(1)} collective-permute-done((bf16[4,80,128]{2,1,0:T(8,128)(2,1)S(1)}, bf16[4,80,128]{2,1,0:T(8,128)(2,1)S(1)}, u32[]{:S(2)}, u32[]{:S(2)}) %collective-permute-start.17) | collective-permute-done | bytes 81952 | tf_op jit(solution)/shard_map/ppermute | solution.py:82
  120.4 2.0 %collective-permute-start.22 = (bf16[80,128]{1,0:T(8,128)(2,1)S(1)}, bf16[80,128]{1,0:T(8,128)(2,1)S(1)}, u32[]{:S(2)}, u32[]{:S(2)}) collective-permute-start(bf16[80,128]{1,0:T(8,128)(2,1)S(1)} %get-tuple-element.82), channel_id=1, source_target_pairs={{0,1},{1,0},{2,3},{3,2},{4,5},{5,4},{6,7},{7,6},{8,9},{9,8},{10,11... | collective-permute-start | bytes 61448 | tf_op jit(solution)/shard_map/ppermute | solution.py:82
  122.4 1.7 %collective-permute-start.21 = (bf16[80,128]{1,0:T(8,128)(2,1)S(1)}, bf16[80,128]{1,0:T(8,128)(2,1)S(1)}, u32[]{:S(2)}, u32[]{:S(2)}) collective-permute-start(bf16[80,128]{1,0:T(8,128)(2,1)S(1)} %get-tuple-element.83), channel_id=1, source_target_pairs={{0,65},{1,64},{2,67},{3,66},{4,69},{5,68},{6,71},{7,70},{8,73},{9,... | collective-permute-start | bytes 61448 | tf_op jit(solution)/shard_map/ppermute | solution.py:82
  126.2 2.9 %collective-permute-done.20.two_ref = bf16[80,128]{1,0:T(8,128)(2,1)S(1)} collective-permute-done((bf16[80,128]{1,0:T(8,128)(2,1)S(1)}, bf16[80,128]{1,0:T(8,128)(2,1)S(1)}, u32[]{:S(2)}, u32[]{:S(2)}) %collective-permute-start.20) | collective-permute-done | bytes 20512 | tf_op jit(solution)/shard_map/ppermute | solution.py:82
  129.6 2.4 %tile_sums.1 = (bf16[16,2048]{1,0:T(8,128)(2,1)}, bf16[128,16,128]{2,1,0:T(8,128)(2,1)}) custom-call(bf16[2048,128]{1,0:T(8,128)(2,1)} %get-tuple-element.59.n_ref, bf16[2048,128]{1,0:T(8,128)(2,1)} %get-tuple-element.60.u_ref, bf16[80,128]{1,0:T(8,128)(2,1)} %get-tuple-element.85.one_ref, bf16[80,128]{1,0:T(8,128)(2,1)} %copy-done.18, ...), custom_call_target="tpu_custom_call" | custom-call | tf_op jit(solution)/shard_map/tile_sums/pallas_call | solution.py:421
  132.1 4.6 %all-to-all-start.2 = ((bf16[128,16,128]{2,1,0:T(8,128)(2,1)}), bf16[128,16,128]{2,1,0:T(8,128)(2,1)S(1)}, u32[]{:S(2)}, u32[]{:S(2)}) async-start(bf16[128,16,128]{2,1,0:T(8,128)(2,1)} %get-tuple-element.67), calls=%async_computation.2 | async-start | bytes 1048576 | tf_op jit(solution)/shard_map/all_to_all | solution.py:351
  136.7 3.7 %tile_final.1 = (bf16[2048,128]{1,0:T(8,128)(2,1)}, bf16[2048,128]{1,0:T(8,128)(2,1)}) custom-call(bf16[2048,128]{1,0:T(8,128)(2,1)} %bitcast.40, bf16[8,2,256,128]{3,2,1,0:T(8,128)(2,1)} %bitcast.37, bf16[16,2048]{1,0:T(8,128)(2,1)} %get-tuple-element.64.both_ref, f32[1,128]{1,0:T(1,128)} %bitcast.51, bf16[16,128]{1,0:T(8,128)(2,1)} %pad_maximum_fusion.2.wb_ref), custom_call_target="tpu_custom_call" | custom-call | flops 5000000000 | bytes 18000000 | tf_op jit(solution)/shard_map/tile_final/pallas_call | solution.py:429
  140.4 9.7 %all-to-all-done.2.msg_ref = bf16[128,16,128]{2,1,0:T(8,128)(2,1)S(1)} async-done(((bf16[128,16,128]{2,1,0:T(8,128)(2,1)}), bf16[128,16,128]{2,1,0:T(8,128)(2,1)S(1)}, u32[]{:S(2)}, u32[]{:S(2)}) %all-to-all-start.2) | async-done | bytes 524320 | tf_op jit(solution)/shard_map/all_to_all | solution.py:351
  150.9 2.0 %finish.1 = (f32[128,128]{1,0:T(8,128)}, f32[128,128]{1,0:T(8,128)}, f32[128,128]{1,0:T(8,128)}, f32[128,128]{1,0:T(8,128)}, f32[128,128]{1,0:T(8,128)}, /*index...) custom-call(bf16[128,16,128]{2,1,0:T(8,128)(2,1)} %copy-done.1), custom_call_target="tpu_custom_call" | custom-call | tf_op jit(solution)/shard_map/finish/pallas_call | solution.py:436
  (83 shorter events, 18.6 us)
Async XLA Ops:
  6.9 13.2 %copy-start.12 = (bf16[128,128]{1,0:T(8,128)(2,1)S(1)}, bf16[128,128]{1,0:T(8,128)(2,1)}, u32[]{:S(2)}) copy-start(bf16[128,128]{1,0:T(8,128)(2,1)} %param.13) | copy-start | bytes 98308
  6.9 22.4 %copy-start.13 = (bf16[128,128]{1,0:T(8,128)(2,1)S(1)}, bf16[128,128]{1,0:T(8,128)(2,1)}, u32[]{:S(2)}) copy-start(bf16[128,128]{1,0:T(8,128)(2,1)} %param.14) | copy-start | bytes 98308
  6.9 31.9 %copy-start.14 = (bf16[128,128]{1,0:T(8,128)(2,1)S(1)}, bf16[128,128]{1,0:T(8,128)(2,1)}, u32[]{:S(2)}) copy-start(bf16[128,128]{1,0:T(8,128)(2,1)} %param.15) | copy-start | bytes 98308
  6.9 31.9 %copy-start.15 = (bf16[128,128]{1,0:T(8,128)(2,1)S(1)}, bf16[128,128]{1,0:T(8,128)(2,1)}, u32[]{:S(2)}) copy-start(bf16[128,128]{1,0:T(8,128)(2,1)} %param.16) | copy-start | bytes 98308
  6.9 40.6 %all-to-all-start = ((bf16[8,2,4,64,128]{4,3,2,1,0:T(8,128)(2,1)}), bf16[8,2,4,64,128]{4,3,2,1,0:T(8,128)(2,1)S(1)}, u32[]{:S(2)}, u32[]{:S(2)}) async-start(bf16[8,2,4,64,128]{4,3,2,1,0:T(8,128)(2,1)} %pack.1), calls=%async_computation | async-start | bytes 2097152 | tf_op jit(solution)/shard_map/all_to_all | solution.py:351
  14.1 6.1 %collective-permute-start.2 = (bf16[64,128]{1,0:T(8,128)(2,1)S(1)}, bf16[64,128]{1,0:T(8,128)(2,1)S(1)}, u32[]{:S(2)}, u32[]{:S(2)}) collective-permute-start(bf16[64,128]{1,0:T(8,128)(2,1)S(1)} %copy-done.19), channel_id=1, source_target_pairs={{0,32},{1,33},{2,34},{3,35},{4,36},{5,37},{6,38},{7,39},{8,40},{9,... | collective-permute-start | bytes 49160 | tf_op jit(solution)/shard_map/ppermute | solution.py:82
  18.0 3.7 %collective-permute-start.1 = (bf16[64,128]{1,0:T(8,128)(2,1)S(1)}, bf16[64,128]{1,0:T(8,128)(2,1)S(1)}, u32[]{:S(2)}, u32[]{:S(2)}) collective-permute-start(bf16[64,128]{1,0:T(8,128)(2,1)S(1)} %copy-done.19), channel_id=1, source_target_pairs={{0,48},{1,49},{2,50},{3,51},{4,52},{5,53},{6,54},{7,55},{8,56},{9,... | collective-permute-start | bytes 49160 | tf_op jit(solution)/shard_map/ppermute | solution.py:82
  18.7 4.9 %collective-permute-start = (bf16[64,128]{1,0:T(8,128)(2,1)S(1)}, bf16[64,128]{1,0:T(8,128)(2,1)S(1)}, u32[]{:S(2)}, u32[]{:S(2)}) collective-permute-start(bf16[64,128]{1,0:T(8,128)(2,1)S(1)} %copy-done.19), channel_id=1, source_target_pairs={{0,16},{1,17},{2,18},{3,19},{4,20},{5,21},{6,22},{7,23},{8,24},{9,... | collective-permute-start | bytes 49160 | tf_op jit(solution)/shard_map/ppermute | solution.py:82
  23.7 5.7 %collective-permute-start.4 = (bf16[4,64,128]{2,1,0:T(8,128)(2,1)S(1)}, bf16[4,64,128]{2,1,0:T(8,128)(2,1)S(1)}, u32[]{:S(2)}, u32[]{:S(2)}) collective-permute-start(bf16[4,64,128]{2,1,0:T(8,128)(2,1)S(1)} %get-tuple-element.87), channel_id=1, source_target_pairs={{0,6},{1,7},{2,0},{3,1},{4,2},{5,3},{6,4},{7,5},{8,14},{9,15},{10,... | collective-permute-start | bytes 196616 | tf_op jit(solution)/shard_map/ppermute | solution.py:82
  26.9 6.3 %collective-permute-start.3 = (bf16[4,64,128]{2,1,0:T(8,128)(2,1)S(1)}, bf16[4,64,128]{2,1,0:T(8,128)(2,1)S(1)}, u32[]{:S(2)}, u32[]{:S(2)}) collective-permute-start(bf16[4,64,128]{2,1,0:T(8,128)(2,1)S(1)} %get-tuple-element.87), channel_id=1, source_target_pairs={{0,2},{1,3},{2,4},{3,5},{4,6},{5,7},{6,0},{7,1},{8,10},{9,11},{10,... | collective-permute-start | bytes 196616 | tf_op jit(solution)/shard_map/ppermute | solution.py:82
  26.9 6.3 %collective-permute-start.5 = (bf16[4,64,128]{2,1,0:T(8,128)(2,1)S(1)}, bf16[4,64,128]{2,1,0:T(8,128)(2,1)S(1)}, u32[]{:S(2)}, u32[]{:S(2)}) collective-permute-start(bf16[4,64,128]{2,1,0:T(8,128)(2,1)S(1)} %get-tuple-element.87), channel_id=1, source_target_pairs={{0,4},{1,5},{2,6},{3,7},{4,0},{5,1},{6,2},{7,3},{8,12},{9,13},{10,... | collective-permute-start | bytes 196616 | tf_op jit(solution)/shard_map/ppermute | solution.py:82
  33.3 20.3 %copy-start.2 = (bf16[4,4,64,128]{3,2,1,0:T(8,128)(2,1)}, bf16[4,4,64,128]{3,2,1,0:T(8,128)(2,1)S(1)}, u32[]{:S(2)}) copy-start(bf16[4,4,64,128]{3,2,1,0:T(8,128)(2,1)S(1)} %pad_maximum_fusion) | copy-start | bytes 786436
  33.3 10.8 %collective-permute-start.8 = (bf16[16,64,128]{2,1,0:T(8,128)(2,1)S(1)}, bf16[16,64,128]{2,1,0:T(8,128)(2,1)S(1)}, u32[]{:S(2)}, u32[]{:S(2)}) collective-permute-start(bf16[16,64,128]{2,1,0:T(8,128)(2,1)S(1)} %bitcast.32), channel_id=1, source_target_pairs={{0,1},{1,0},{2,3},{3,2},{4,5},{5,4},{6,7},{7,6},{8,9},{9,8},{10,11... | collective-permute-start | bytes 786440 | tf_op jit(solution)/shard_map/ppermute | solution.py:82
  36.2 10.0 %collective-permute-start.7 = (bf16[16,64,128]{2,1,0:T(8,128)(2,1)S(1)}, bf16[16,64,128]{2,1,0:T(8,128)(2,1)S(1)}, u32[]{:S(2)}, u32[]{:S(2)}) collective-permute-start(bf16[16,64,128]{2,1,0:T(8,128)(2,1)S(1)} %bitcast.33), channel_id=1, source_target_pairs={{0,65},{1,64},{2,67},{3,66},{4,69},{5,68},{6,71},{7,70},{8,73},{9,... | collective-permute-start | bytes 786440 | tf_op jit(solution)/shard_map/ppermute | solution.py:82
  36.7 10.9 %collective-permute-start.6 = (bf16[16,64,128]{2,1,0:T(8,128)(2,1)S(1)}, bf16[16,64,128]{2,1,0:T(8,128)(2,1)S(1)}, u32[]{:S(2)}, u32[]{:S(2)}) collective-permute-start(bf16[16,64,128]{2,1,0:T(8,128)(2,1)S(1)} %bitcast.34), channel_id=1, source_target_pairs={{0,64},{1,65},{2,66},{3,67},{4,68},{5,69},{6,70},{7,71},{8,72},{9,... | collective-permute-start | bytes 786440 | tf_op jit(solution)/shard_map/ppermute | solution.py:82
  38.9 14.8 %collective-permute-start.9 = (bf16[16,64,128]{2,1,0:T(8,128)(2,1)S(1)}, bf16[16,64,128]{2,1,0:T(8,128)(2,1)S(1)}, u32[]{:S(2)}, u32[]{:S(2)}) collective-permute-start(bf16[16,64,128]{2,1,0:T(8,128)(2,1)S(1)} %bitcast.35), channel_id=1, source_target_pairs={{0,8},{1,9},{2,10},{3,11},{4,12},{5,13},{6,14},{7,15},{8,0},{9,1},... | collective-permute-start | bytes 786440 | tf_op jit(solution)/shard_map/ppermute | solution.py:82
  44.1 9.5 %copy-start.4 = (bf16[16,64,128]{2,1,0:T(8,128)(2,1)}, bf16[16,64,128]{2,1,0:T(8,128)(2,1)S(1)}, u32[]{:S(2)}) copy-start(bf16[16,64,128]{2,1,0:T(8,128)(2,1)S(1)} %collective-permute-done.8.refs_3_) | copy-start | bytes 786436
  44.1 9.5 %collective-permute-start.12 = (bf16[16,64,128]{2,1,0:T(8,128)(2,1)S(1)}, bf16[16,64,128]{2,1,0:T(8,128)(2,1)S(1)}, u32[]{:S(2)}, u32[]{:S(2)}) collective-permute-start(bf16[16,64,128]{2,1,0:T(8,128)(2,1)S(1)} %collective-permute-done.8.refs_3_), channel_id=1, source_target_pairs={{0,8},{1,9},{2,10},{3,11},{4,12},{5,13},{6,14},{7,15},{8,0},{9,1},... | collective-permute-start | bytes 786440 | tf_op jit(solution)/shard_map/ppermute | solution.py:82
  46.2 7.5 %collective-permute-start.11 = (bf16[16,64,128]{2,1,0:T(8,128)(2,1)S(1)}, bf16[16,64,128]{2,1,0:T(8,128)(2,1)S(1)}, u32[]{:S(2)}, u32[]{:S(2)}) collective-permute-start(bf16[16,64,128]{2,1,0:T(8,128)(2,1)S(1)} %collective-permute-done.7.refs_2_), channel_id=1, source_target_pairs={{0,8},{1,9},{2,10},{3,11},{4,12},{5,13},{6,14},{7,15},{8,0},{9,1},... | collective-permute-start | bytes 786440 | tf_op jit(solution)/shard_map/ppermute | solution.py:82
  47.5 6.2 %collective-permute-start.10 = (bf16[16,64,128]{2,1,0:T(8,128)(2,1)S(1)}, bf16[16,64,128]{2,1,0:T(8,128)(2,1)S(1)}, u32[]{:S(2)}, u32[]{:S(2)}) collective-permute-start(bf16[16,64,128]{2,1,0:T(8,128)(2,1)S(1)} %collective-permute-done.6.refs_1_), channel_id=1, source_target_pairs={{0,8},{1,9},{2,10},{3,11},{4,12},{5,13},{6,14},{7,15},{8,0},{9,1},... | collective-permute-start | bytes 786440 | tf_op jit(solution)/shard_map/ppermute | solution.py:82
  83.7 3.5 %collective-permute-start.13 = (bf16[64,80,128]{2,1,0:T(8,128)(2,1)}, bf16[64,80,128]{2,1,0:T(8,128)(2,1)S(1)}, u32[]{:S(2)}, u32[]{:S(2)}) collective-permute-start(bf16[64,80,128]{2,1,0:T(8,128)(2,1)} %get-tuple-element.62), channel_id=1, source_target_pairs={{0,8},{1,9},{2,10},{3,11},{4,12},{5,13},{6,14},{7,15},{8,0},{9,1},... | collective-permute-start | bytes 3932168 | tf_op jit(solution)/shard_map/ppermute | solution.py:82
  89.8 11.4 %collective-permute-start.14 = (bf16[16,80,128]{2,1,0:T(8,128)(2,1)}, bf16[16,80,128]{2,1,0:T(8,128)(2,1)S(1)}, u32[]{:S(2)}, u32[]{:S(2)}) collective-permute-start(bf16[16,80,128]{2,1,0:T(8,128)(2,1)} %get-tuple-element.76), channel_id=1, source_target_pairs={{0,16},{1,17},{2,18},{3,19},{4,20},{5,21},{6,22},{7,23},{8,24},{9,... | collective-permute-start | bytes 983048 | tf_op jit(solution)/shard_map/ppermute | solution.py:82
  90.7 18.7 %collective-permute-start.16 = (bf16[16,80,128]{2,1,0:T(8,128)(2,1)}, bf16[16,80,128]{2,1,0:T(8,128)(2,1)S(1)}, u32[]{:S(2)}, u32[]{:S(2)}) collective-permute-start(bf16[16,80,128]{2,1,0:T(8,128)(2,1)} %get-tuple-element.77), channel_id=1, source_target_pairs={{0,32},{1,33},{2,34},{3,35},{4,36},{5,37},{6,38},{7,39},{8,40},{9,... | collective-permute-start | bytes 983048 | tf_op jit(solution)/shard_map/ppermute | solution.py:82
  94.3 15.1 %collective-permute-start.15 = (bf16[16,80,128]{2,1,0:T(8,128)(2,1)}, bf16[16,80,128]{2,1,0:T(8,128)(2,1)S(1)}, u32[]{:S(2)}, u32[]{:S(2)}) collective-permute-start(bf16[16,80,128]{2,1,0:T(8,128)(2,1)} %get-tuple-element.78), channel_id=1, source_target_pairs={{0,48},{1,49},{2,50},{3,51},{4,52},{5,53},{6,54},{7,55},{8,56},{9,... | collective-permute-start | bytes 983048 | tf_op jit(solution)/shard_map/ppermute | solution.py:82
  95.3 36.8 %all-to-all-start.1 = ((bf16[8,2,4,64,128]{4,3,2,1,0:T(8,128)(2,1)}), bf16[8,2,4,64,128]{4,3,2,1,0:T(8,128)(2,1)S(1)}, u32[]{:S(2)}, u32[]{:S(2)}) async-start(bf16[8,2,4,64,128]{4,3,2,1,0:T(8,128)(2,1)} %get-tuple-element.58), calls=%async_computation.1 | async-start | bytes 2097152 | tf_op jit(solution)/shard_map/all_to_all | solution.py:351
  109.6 8.9 %collective-permute-start.17 = (bf16[4,80,128]{2,1,0:T(8,128)(2,1)S(1)}, bf16[4,80,128]{2,1,0:T(8,128)(2,1)S(1)}, u32[]{:S(2)}, u32[]{:S(2)}) collective-permute-start(bf16[4,80,128]{2,1,0:T(8,128)(2,1)S(1)} %get-tuple-element.79), channel_id=1, source_target_pairs={{0,2},{1,3},{2,4},{3,5},{4,6},{5,7},{6,0},{7,1},{8,10},{9,11},{10,... | collective-permute-start | bytes 245768 | tf_op jit(solution)/shard_map/ppermute | solution.py:82
  111.6 8.2 %collective-permute-start.19 = (bf16[4,80,128]{2,1,0:T(8,128)(2,1)S(1)}, bf16[4,80,128]{2,1,0:T(8,128)(2,1)S(1)}, u32[]{:S(2)}, u32[]{:S(2)}) collective-permute-start(bf16[4,80,128]{2,1,0:T(8,128)(2,1)S(1)} %get-tuple-element.80), channel_id=1, source_target_pairs={{0,4},{1,5},{2,6},{3,7},{4,0},{5,1},{6,2},{7,3},{8,12},{9,13},{10,... | collective-permute-start | bytes 245768 | tf_op jit(solution)/shard_map/ppermute | solution.py:82
  113.7 6.1 %collective-permute-start.18 = (bf16[4,80,128]{2,1,0:T(8,128)(2,1)S(1)}, bf16[4,80,128]{2,1,0:T(8,128)(2,1)S(1)}, u32[]{:S(2)}, u32[]{:S(2)}) collective-permute-start(bf16[4,80,128]{2,1,0:T(8,128)(2,1)S(1)} %get-tuple-element.81), channel_id=1, source_target_pairs={{0,6},{1,7},{2,0},{3,1},{4,2},{5,3},{6,4},{7,5},{8,14},{9,15},{10,... | collective-permute-start | bytes 245768 | tf_op jit(solution)/shard_map/ppermute | solution.py:82
  120.4 5.4 %collective-permute-start.22 = (bf16[80,128]{1,0:T(8,128)(2,1)S(1)}, bf16[80,128]{1,0:T(8,128)(2,1)S(1)}, u32[]{:S(2)}, u32[]{:S(2)}) collective-permute-start(bf16[80,128]{1,0:T(8,128)(2,1)S(1)} %get-tuple-element.82), channel_id=1, source_target_pairs={{0,1},{1,0},{2,3},{3,2},{4,5},{5,4},{6,7},{7,6},{8,9},{9,8},{10,11... | collective-permute-start | bytes 61448 | tf_op jit(solution)/shard_map/ppermute | solution.py:82
  122.4 3.8 %collective-permute-start.21 = (bf16[80,128]{1,0:T(8,128)(2,1)S(1)}, bf16[80,128]{1,0:T(8,128)(2,1)S(1)}, u32[]{:S(2)}, u32[]{:S(2)}) collective-permute-start(bf16[80,128]{1,0:T(8,128)(2,1)S(1)} %get-tuple-element.83), channel_id=1, source_target_pairs={{0,65},{1,64},{2,67},{3,66},{4,69},{5,68},{6,71},{7,70},{8,73},{9,... | collective-permute-start | bytes 61448 | tf_op jit(solution)/shard_map/ppermute | solution.py:82
  124.0 5.0 %collective-permute-start.20 = (bf16[80,128]{1,0:T(8,128)(2,1)S(1)}, bf16[80,128]{1,0:T(8,128)(2,1)S(1)}, u32[]{:S(2)}, u32[]{:S(2)}) collective-permute-start(bf16[80,128]{1,0:T(8,128)(2,1)S(1)} %get-tuple-element.84), channel_id=1, source_target_pairs={{0,64},{1,65},{2,66},{3,67},{4,68},{5,69},{6,70},{7,71},{8,72},{9,... | collective-permute-start | bytes 61448 | tf_op jit(solution)/shard_map/ppermute | solution.py:82
  132.1 18.0 %all-to-all-start.2 = ((bf16[128,16,128]{2,1,0:T(8,128)(2,1)}), bf16[128,16,128]{2,1,0:T(8,128)(2,1)S(1)}, u32[]{:S(2)}, u32[]{:S(2)}) async-start(bf16[128,16,128]{2,1,0:T(8,128)(2,1)} %get-tuple-element.67), calls=%async_computation.2 | async-start | bytes 1048576 | tf_op jit(solution)/shard_map/all_to_all | solution.py:351
  (14 other events, 46.0 us)

commit v6 on v5

--- a/solution.py
+++ b/solution.py
@@ -82,13 +82,27 @@
     return lax.ppermute(value, ("row", "col"), shift_pairs(**shift))
 
 
-def gather_bias(message):
-    held = message
-    held = jnp.stack([held] + [send(held, z=hop) for hop in HOPS[1:]])
+def gate_kernel(*refs):
+    pass
+
+
+def after(values, other):
+    anywhere = pl.BlockSpec(memory_space=pl.ANY)
+    return pl.pallas_call(
+        gate_kernel,
+        in_specs=[anywhere] * (len(values) + 1),
+        out_specs=[anywhere] * len(values),
+        out_shape=[jax.ShapeDtypeStruct(value.shape, value.dtype) for value in values],
+        input_output_aliases={at: at for at in range(len(values))},
+        name="after",
+    )(*values, other)
+
+
+def gather_in_plane(first):
+    held = jnp.stack(first)
     held = jnp.stack([held] + [send(held, y=hop) for hop in HOPS[1:]])
     held = held.reshape(16, 64, 128)
-    pieces = [held] + [send(held, x=hop) for hop in HOPS[1:]]
-    return pieces + [send(piece, core=1) for piece in pieces]
+    return [held] + [send(held, x=hop) for hop in HOPS[1:]]
 
 
 def add_up(parts):
@@ -96,17 +110,24 @@
 
 
 def scatter_sums(mine, other):
-    held = add_up([mine, send(other, core=1)]).reshape(4, 16, 80, 128)
-    held = add_up([held[0]] + [send(held[at], z=HOPS[at]) for at in (1, 2, 3)]).reshape(4, 4, 80, 128)
-    held = add_up([held[0]] + [send(held[at], y=HOPS[at]) for at in (1, 2, 3)])
+    got = send(other, core=1)
+    held = [add_up([mine[at * 16 : at * 16 + 16], got[at * 16 : at * 16 + 16]]) for at in range(4)]
+    got = [held[0]] + [send(held[at], z=HOPS[at]) for at in (1, 2, 3)]
+    held = [add_up([part[at * 4 : at * 4 + 4] for part in got]) for at in range(4)]
+    got = [held[0]] + [send(held[at], y=HOPS[at]) for at in (1, 2, 3)]
+    held = [add_up([part[at] for part in got]) for at in range(4)]
     return [held[0]] + [send(held[at], x=HOPS[at]) for at in (1, 2, 3)]
 
 
-def tile_bias_kernel(pair_ref, gain_ref, wb_ref, msg_ref, n_ref, u_ref, rows_ref):
+def tile_bias_kernel(pair_ref, gain_ref, w_ref, msg_ref, n_ref, u_ref, wb_ref, rows_ref, w_scr):
+    w_scr[...] = jnp.zeros(w_scr.shape, F32)
+    w_scr[0:4, :] = w_ref[...].astype(F32)
+    w_scr[8:12, :] = w_ref[...].astype(F32)
+    wb_ref[...] = w_scr[...].astype(BF16)
     unit, inverse, normed = normalize(pair_ref[...].astype(F32), gain_ref[...])
     n_ref[...] = normed
     u_ref[...] = unit.astype(BF16)
-    bias = dot(wb_ref[...], normed, NT)
+    bias = dot(w_scr[...].astype(BF16), normed, NT)
     for half in range(8):
         first = bias[0:8, half * 128 : half * 128 + 128]
         second = bias[0:8, (8 + half) * 128 : (8 + half) * 128 + 128]
@@ -119,7 +140,7 @@
     msg_ref[...] = rows_ref[...].astype(BF16)
 
 
-def pack_kernel(pair_ref, cot_ref, after_ref, out_ref):
+def pack_kernel(pair_ref, cot_ref, out_ref):
     out_ref[:, 0] = pair_ref[...]
     out_ref[:, 1] = cot_ref[...]
 
@@ -141,9 +162,9 @@
     u_ref[0] = unit.astype(BF16)
 
 
-def attend_kernel(place_ref, q_ref, k_ref, v_ref, a_ref, *refs):
+def attend_kernel(scale, place_ref, q_ref, k_ref, v_ref, a_ref, *refs):
     pieces = refs[:8]
-    att_ref, dq_ref, dk_ref, dv_ref, mine_ref, other_ref, block_scr, bias_scr, sum_scr = refs[8:]
+    att_ref, dq_ref, dk_out, dv_out, mine_ref, other_ref, block_scr, bias_scr, sum_scr, dk_ref, dv_ref = refs[8:]
     chunk = pl.program_id(0)
 
     @pl.when(chunk == 0)
@@ -184,19 +205,24 @@
         inverse = 1.0 / jnp.sum(powers, axis=-1, keepdims=True)
         powers_low = powers.astype(BF16)
         attended = dot(powers_low, values) * inverse
-        att_ref[row, at, :] = collect(attended)
+        att_ref[row] = collect(attended).astype(BF16)
         a_float = a_big.astype(F32)
         inner = jnp.sum(a_float * attended, axis=-1, keepdims=True)
         grad_probs = dot(a_big, values, NT)
         score_grad = powers * ((grad_probs - inner) * inverse)
         score_low = score_grad.astype(BF16)
-        dq_ref[row, at, :] = collect(dot(score_low, keys))
+        dq_ref[row] = (collect(dot(score_low, keys)) * scale).astype(BF16)
         dk_ref[row] += dot(q_big, score_low, TN)
         dv_ref[row] += dot((a_float * inverse).astype(BF16), powers_low, TN)
         if row == 0:
             sum_scr[...] = score_grad
         else:
             sum_scr[...] += score_grad
+
+    @pl.when(chunk == 1)
+    def _():
+        dk_out[...] = (dk_ref[...] * scale).astype(BF16)
+        dv_out[...] = dv_ref[...].astype(BF16)
 
     xs = [slot_of(chunk + 2 * high - place_ref[0]) for high in range(2)]
     ys = [slot_of(b - place_ref[1]) * 4 for b in range(4)]
@@ -222,26 +248,31 @@
         emit(other_ref, mine_ref)
 
 
-def post_kernel(scale, place_ref, att_ref, dq_ref, dk_ref, dv_ref, gate_ref, gg_ref, n_ref, u_ref, rows_ref, wcat_ref,
+def post_kernel(place_ref, att_ref, dq_ref, dk_ref, dv_ref, gate_ref, gg_ref, n_ref, u_ref, rows_ref, wcat_ref,
                 wout_ref, held_mine, held_other, ug_ref, mine_ref, other_ref, off_ref, w_scr, o_scr, s_scr, p_scr):
     row = pl.program_id(0)
-    attended = att_ref[0]
-    gate = gate_ref[0]
-    grad_gated = gg_ref[0]
+    attended = att_ref[...].reshape(1024, 128).astype(F32)
+    gate = gate_ref[...].reshape(1024, 128)
+    grad_gated = gg_ref[...].reshape(1024, 128)
     gated = (gate * attended).astype(BF16)
-    cot = rows_ref[:, 0, 0].reshape(512, 128)
-    ug_ref[:, 0, 0] = dot(gated, wout_ref[...]).astype(BF16).reshape(8, 64, 128)
+    cot = jnp.concatenate([rows_ref[:, 0, at].reshape(512, 128) for at in range(2)], axis=0)
+    update = dot(gated, wout_ref[...]).astype(BF16).reshape(2, 8, 64, 128)
     out_part = dot(gated, cot, TN)
     gpre = (grad_gated * attended * gate * (1.0 - gate)).astype(BF16)
-    qpre = (dq_ref[0] * scale).astype(BF16)
-    kpre = (jnp.transpose(dk_ref[0]) * scale).astype(BF16)
-    vpre = jnp.transpose(dv_ref[0]).astype(BF16)
+    qpre = dq_ref[...].reshape(1024, 128)
+    kpre, vpre = (
+        jnp.concatenate([jnp.transpose(ref[at].astype(F32)) for at in range(2)], axis=0).astype(BF16)
+        for ref in (dk_ref, dv_ref)
+    )
     cat = jnp.concatenate([qpre, kpre, vpre, gpre], axis=1)
     grad_normed = dot(cat, wcat_ref[...], NT)
-    ug_ref[:, 1, 0] = grad_normed.astype(BF16).reshape(8, 64, 128)
-    w_part = dot(n_ref[0], cat, TN)
+    grad_low = grad_normed.astype(BF16).reshape(2, 8, 64, 128)
+    for at in range(2):
+        ug_ref[:, 0, at] = update[at]
+        ug_ref[:, 1, at] = grad_low[at]
+    w_part = dot(n_ref[...].reshape(1024, 128), cat, TN)
     off = jnp.sum(gpre.astype(F32), axis=0, keepdims=True)
-    gain = jnp.sum(grad_normed * u_ref[0].astype(F32), axis=0, keepdims=True)
+    gain = jnp.sum(grad_normed * u_ref[...].reshape(1024, 128).astype(F32), axis=0, keepdims=True)
     off = jnp.concatenate([off, gain], axis=0)
 
     @pl.when(row == 0)
@@ -256,7 +287,7 @@
         o_scr[...] += out_part
         s_scr[...] += off
 
-    @pl.when(row == 3)
+    @pl.when(row == 1)
     def _():
         for t in range(5):
             part = w_scr[:, t * 128 : t * 128 + 128] if t < 4 else o_scr[...]
@@ -342,38 +373,35 @@
     gain = ln_gain.reshape(1, 128)
     offset = gate_offset.reshape(1, 128)
     wcat = jnp.concatenate([w_query, w_key, w_value, w_gate], axis=1)
-    wb_pad = jnp.pad(w_bias.T, ((0, 4), (0, 0)))
-    wb_two = jnp.concatenate([wb_pad, wb_pad], axis=0)
     everyone = ("row", "col")
     pair_tile = pair_rep.reshape(2048, 128)
 
     def swap(value, axes):
         return lax.all_to_all(value, axes, split_axis=0, concat_axis=0, tiled=True)
 
-    bias_msg, normed_tile, unit_tile = pl.pallas_call(
+    bias_msg, normed_tile, unit_tile, wb_two = pl.pallas_call(
         tile_bias_kernel,
-        out_shape=[sds((64, 128), BF16), sds((2048, 128), BF16), sds((2048, 128), BF16)],
-        scratch_shapes=[pltpu.VMEM((64, 128), F32)],
+        out_shape=[sds((64, 128), BF16), sds((2048, 128), BF16), sds((2048, 128), BF16), sds((16, 128), BF16)],
+        scratch_shapes=[pltpu.VMEM((64, 128), F32), pltpu.VMEM((16, 128), F32)],
         compiler_params=PARAMS,
         name="tile_bias",
-    )(pair_tile, gain, wb_two)
+    )(pair_tile, gain, w_bias.T)
     row, col = lax.axis_index("row"), lax.axis_index("col")
     place = ((col % 2) * 2 + row // 8, col // 2, (row // 2) % 4, row % 2)
     place = jnp.stack(place).astype(jnp.int32)
     smem = pl.BlockSpec(memory_space=pltpu.SMEM)
     packed = pl.pallas_call(
         pack_kernel,
-        in_specs=[whole((8, 4, 64, 128))] * 2 + [pl.BlockSpec(memory_space=pl.ANY)],
         cost_estimate=estimate(2),
         out_shape=sds((8, 2, 4, 64, 128), BF16),
         compiler_params=PARAMS,
         name="pack",
-    )(pair_rep.reshape(8, 4, 64, 128), cotangent.reshape(8, 4, 64, 128), bias_msg)
+    )(pair_rep.reshape(8, 4, 64, 128), cotangent.reshape(8, 4, 64, 128))
+    first = [bias_msg] + [send(bias_msg, z=hop) for hop in HOPS[1:]]
     both_rows = swap(packed, "col")
-    bias_pieces = gather_bias(bias_msg)
+    bias_pieces = gather_in_plane(first)
 
     from_rows = pl.BlockSpec((8, 2, 1, 64, 128), lambda i: (0, 0, i, 0, 0))
-    from_cot = pl.BlockSpec((8, 1, 1, 64, 128), lambda i: (0, 1, i, 0, 0))
     by_row = pl.BlockSpec((1, 512, 128), lambda i: (i, 0, 0))
     query, keys, values, grad_att, gate, grad_gated, normed, unit = pl.pallas_call(
         functools.partial(project_kernel, scale),
@@ -386,28 +414,36 @@
         name="project",
     )(both_rows, gain, wcat, offset, w_out)
 
+    bias_pieces = bias_pieces[:1] + list(after(bias_pieces[1:], query))
+    bias_pieces = bias_pieces + [send(piece, core=1) for piece in bias_pieces]
+
     full = whole((4, 512, 128))
+    half = pl.BlockSpec((4, 256, 128), lambda c: (0, c, 0))
     full_t = whole((4, 128, 512))
     attended, dq, dk, dv, mine, other = pl.pallas_call(
-        attend_kernel,
+        functools.partial(attend_kernel, scale),
         grid=(2,),
         in_specs=[smem, full, full, full, full] + [whole((16, 64, 128))] * 8,
-        out_specs=[full, full, full_t, full_t, whole((64, 80, 128)), whole((64, 80, 128))],
-        out_shape=[sds((4, 512, 128), F32), sds((4, 512, 128), F32), sds((4, 128, 512), F32),
-                   sds((4, 128, 512), F32), sds((64, 80, 128), BF16), sds((64, 80, 128), BF16)],
-        scratch_shapes=[pltpu.VMEM((128, 64, 128), BF16), pltpu.VMEM((1024, 512), F32), pltpu.VMEM((1024, 512), F32)],
+        out_specs=[half, half, full_t, full_t, whole((64, 80, 128)), whole((64, 80, 128))],
+        out_shape=[sds((4, 512, 128), BF16), sds((4, 512, 128), BF16), sds((4, 128, 512), BF16),
+                   sds((4, 128, 512), BF16), sds((64, 80, 128), BF16), sds((64, 80, 128), BF16)],
+        scratch_shapes=[pltpu.VMEM((128, 64, 128), BF16), pltpu.VMEM((1024, 512), F32), pltpu.VMEM((1024, 512), F32),
+                        pltpu.VMEM((4, 128, 512), F32), pltpu.VMEM((4, 128, 512), F32)],
         compiler_params=PARAMS,
         name="attend",
     )(place, query, keys, values, grad_att, *bias_pieces)
 
-    by_row_t = pl.BlockSpec((1, 128, 512), lambda i: (i, 0, 0))
+    two_t = pl.BlockSpec((2, 128, 512), lambda i: (i, 0, 0))
+    two = pl.BlockSpec((2, 512, 128), lambda i: (i, 0, 0))
+    two_rows = pl.BlockSpec((8, 2, 2, 64, 128), lambda i: (0, 0, i, 0, 0))
+    two_cot = pl.BlockSpec((8, 1, 2, 64, 128), lambda i: (0, 1, i, 0, 0))
     tail = pl.BlockSpec((64, 16, 128), lambda i: (0, 4, 0))
     ug_rows, mine, other, off = pl.pallas_call(
-        functools.partial(post_kernel, scale),
-        grid=(4,),
-        in_specs=[smem, by_row, by_row, by_row_t, by_row_t, by_row, by_row, by_row, by_row, from_cot,
+        post_kernel,
+        grid=(2,),
+        in_specs=[smem, two, two, two_t, two_t, two, two, two, two, two_cot,
                   whole((128, 512)), whole((128, 128))] + [pl.BlockSpec(memory_space=pl.ANY)] * 2,
-        out_specs=[from_rows, tail, tail, whole((2, 128))],
+        out_specs=[two_rows, tail, tail, whole((2, 128))],
         out_shape=[sds((8, 2, 4, 64, 128), BF16), sds((64, 80, 128), BF16), sds((64, 80, 128), BF16),
                    sds((2, 128), F32)],
         scratch_shapes=[pltpu.VMEM((128, 512), F32), pltpu.VMEM((128, 128), F32), pltpu.VMEM((2, 128), F32),

time: 154 us -> 149 us (0.968)
  Pallas kernels: 47.2 us -> 45.4 us
  local copies, waits for them, and re-layouts: 5.73 us -> 3.97 us
    pallas_call x3 -> x4, Pallas kernels: 31.3 us -> 29.4 us  [the longest x1 21.8 us: body(): pl.pallas_call(functools.partial(attend_kernel, scale), grid=(2,), in_spe...]
    unnamed x43 -> x41, local copies, waits for them, and re-layouts: 3.42 us -> 3.96 us
  transfers between devices with their start and end apart: 26 -> 26, of which waited for: 16 -> 17; matrix products, arithmetic and copies ran while one was open for 1% -> 2% of each run, Pallas kernels for 7% -> 9%
where the time goes in v6:
time: 149 us
  starting transfers between devices  49.2 us (33%)
  waiting for transfers between devices  46.5 us (31%)
  Pallas kernels  45.4 us (30%)
  local copies, waits for them, and re-layouts  3.97 us (3%)
  other arithmetic  2.54 us (2%)
    ppermute x23, waiting for transfers between devices, send(): return lax.ppermute(value, ('row', 'col'), shift_pairs(**shift))  36.9 us
    ppermute x23, starting transfers between devices, send(): return lax.ppermute(value, ('row', 'col'), shift_pairs(**shift))  31 us
    pallas_call x1, Pallas kernels, body(): pl.pallas_call(functools.partial(attend_kernel, scale), grid=(2,), in_spe...  21.8 us
    all_to_all x3, starting transfers between devices, swap(): return lax.all_to_all(value, axes, split_axis=0, concat_axis=0, tiled=True)  18.2 us
    all_to_all x3, waiting for transfers between devices, swap(): return lax.all_to_all(value, axes, split_axis=0, concat_axis=0, tiled=True)  9.68 us
    pallas_call x1, Pallas kernels, body(): pl.pallas_call(post_kernel, grid=(2,), in_specs=[smem, two, two, two_t, t...  5.36 us
    pallas_call x1, Pallas kernels, body(): pl.pallas_call(functools.partial(project_kernel, scale), grid=(4,), in_sp...  5.04 us
    unnamed x41, local copies, waits for them, and re-layouts  3.96 us
  transfers between devices with their start and end apart: 26, of which 17 were waited for; matrix products, arithmetic and copies ran while one was open for 2% of the time, Pallas kernels for 9%

profile of v6, /device:TPU:0, one launch (start us, length us, event | category | flops | bytes accessed | tf_op | source)
XLA Modules:
  0.0 148.5 jit_solution(12198903843190989619)
XLA Ops:
  0.6 2.3 %pack.1 = bf16[8,2,4,64,128]{4,3,2,1,0:T(8,128)(2,1)} custom-call(bf16[8,4,64,128]{3,2,1,0:T(8,128)(2,1)} %bitcast.37, bf16[8,4,64,128]{3,2,1,0:T(8,128)(2,1)} %bitcast.51), custom_call_target="tpu_custom_call" | custom-call | flops 2000000000 | bytes 7200000 | tf_op jit(solution)/shard_map/pack/pallas_call | solution.py:393
  2.9 7.2 %all-to-all-start = ((bf16[8,2,4,64,128]{4,3,2,1,0:T(8,128)(2,1)}), bf16[8,2,4,64,128]{4,3,2,1,0:T(8,128)(2,1)S(1)}, u32[]{:S(2)}, u32[]{:S(2)}) async-start(bf16[8,2,4,64,128]{4,3,2,1,0:T(8,128)(2,1)} %pack.1), calls=%async_computation | async-start | bytes 2097152 | tf_op jit(solution)/shard_map/all_to_all | solution.py:380
  10.1 2.8 %tile_bias.1 = (bf16[64,128]{1,0:T(8,128)(2,1)}, bf16[2048,128]{1,0:T(8,128)(2,1)}, bf16[2048,128]{1,0:T(8,128)(2,1)}, bf16[16,128]{1,0:T(8,128)(2,1)}) custom-call(bf16[2048,128]{1,0:T(8,128)(2,1)} %bitcast.38, f32[1,128]{1,0:T(1,128)} %bitcast.48, bf16[4,128]{1,0:T(4,128)(2,1)} %bitcast.47), custom_call_target="tpu_custom_call" | custom-call | tf_op jit(solution)/shard_map/tile_bias/pallas_call | solution.py:382
  12.9 3.9 %collective-permute-start.2 = (bf16[64,128]{1,0:T(8,128)(2,1)}, bf16[64,128]{1,0:T(8,128)(2,1)S(1)}, u32[]{:S(2)}, u32[]{:S(2)}) collective-permute-start(bf16[64,128]{1,0:T(8,128)(2,1)} %get-tuple-element.51), channel_id=1, source_target_pairs={{0,32},{1,33},{2,34},{3,35},{4,36},{5,37},{6,38},{7,39},{8,40},{9,... | collective-permute-start | bytes 49160 | tf_op jit(solution)/shard_map/ppermute | solution.py:82
  18.9 1.8 %collective-permute-done.1 = bf16[64,128]{1,0:T(8,128)(2,1)S(1)} collective-permute-done((bf16[64,128]{1,0:T(8,128)(2,1)}, bf16[64,128]{1,0:T(8,128)(2,1)S(1)}, u32[]{:S(2)}, u32[]{:S(2)}) %collective-permute-start.1) | collective-permute-done | bytes 16416 | tf_op jit(solution)/shard_map/ppermute | solution.py:82
  20.7 1.9 %collective-permute-done = bf16[64,128]{1,0:T(8,128)(2,1)S(1)} collective-permute-done((bf16[64,128]{1,0:T(8,128)(2,1)}, bf16[64,128]{1,0:T(8,128)(2,1)S(1)}, u32[]{:S(2)}, u32[]{:S(2)}) %collective-permute-start) | collective-permute-done | bytes 16416 | tf_op jit(solution)/shard_map/ppermute | solution.py:82
  23.4 3.3 %collective-permute-start.4 = (bf16[4,64,128]{2,1,0:T(8,128)(2,1)S(1)}, bf16[4,64,128]{2,1,0:T(8,128)(2,1)S(1)}, u32[]{:S(2)}, u32[]{:S(2)}) collective-permute-start(bf16[4,64,128]{2,1,0:T(8,128)(2,1)S(1)} %get-tuple-element.97), channel_id=1, source_target_pairs={{0,6},{1,7},{2,0},{3,1},{4,2},{5,3},{6,4},{7,5},{8,14},{9,15},{10,... | collective-permute-start | bytes 196616 | tf_op jit(solution)/shard_map/ppermute | solution.py:82
  26.7 2.3 %collective-permute-start.5 = (bf16[4,64,128]{2,1,0:T(8,128)(2,1)S(1)}, bf16[4,64,128]{2,1,0:T(8,128)(2,1)S(1)}, u32[]{:S(2)}, u32[]{:S(2)}) collective-permute-start(bf16[4,64,128]{2,1,0:T(8,128)(2,1)S(1)} %get-tuple-element.97), channel_id=1, source_target_pairs={{0,4},{1,5},{2,6},{3,7},{4,0},{5,1},{6,2},{7,3},{8,12},{9,13},{10,... | collective-permute-start | bytes 196616 | tf_op jit(solution)/shard_map/ppermute | solution.py:82
  29.0 3.8 %collective-permute-done.3 = bf16[4,64,128]{2,1,0:T(8,128)(2,1)S(1)} collective-permute-done((bf16[4,64,128]{2,1,0:T(8,128)(2,1)S(1)}, bf16[4,64,128]{2,1,0:T(8,128)(2,1)S(1)}, u32[]{:S(2)}, u32[]{:S(2)}) %collective-permute-start.3) | collective-permute-done | bytes 65568 | tf_op jit(solution)/shard_map/ppermute | solution.py:82
  33.0 3.0 %collective-permute-start.8 = (bf16[16,64,128]{2,1,0:T(8,128)(2,1)S(1)}, bf16[16,64,128]{2,1,0:T(8,128)(2,1)S(1)}, u32[]{:S(2)}, u32[]{:S(2)}) collective-permute-start(bf16[16,64,128]{2,1,0:T(8,128)(2,1)S(1)} %bitcast.33), channel_id=1, source_target_pairs={{0,1},{1,0},{2,3},{3,2},{4,5},{5,4},{6,7},{7,6},{8,9},{9,8},{10,11... | collective-permute-start | bytes 786440 | tf_op jit(solution)/shard_map/ppermute | solution.py:82
  36.3 1.7 %collective-permute-start.6 = (bf16[16,64,128]{2,1,0:T(8,128)(2,1)S(1)}, bf16[16,64,128]{2,1,0:T(8,128)(2,1)S(1)}, u32[]{:S(2)}, u32[]{:S(2)}) collective-permute-start(bf16[16,64,128]{2,1,0:T(8,128)(2,1)S(1)} %bitcast.35), channel_id=1, source_target_pairs={{0,64},{1,65},{2,66},{3,67},{4,68},{5,69},{6,70},{7,71},{8,72},{9,... | collective-permute-start | bytes 786440 | tf_op jit(solution)/shard_map/ppermute | solution.py:82
  39.0 5.0 %project.1 = (bf16[4,512,128]{2,1,0:T(8,128)(2,1)}, bf16[4,512,128]{2,1,0:T(8,128)(2,1)}, bf16[4,512,128]{2,1,0:T(8,128)(2,1)}, bf16[4,512,128]{2,1,0:T(8,128)(2...) custom-call(bf16[8,2,4,64,128]{4,3,2,1,0:T(8,128)(2,1)} %copy-done.1, ...), custom_call_target="tpu_custom_call" | custom-call | flops 5000000000 | bytes 18000000 | tf_op jit(solution)/shard_map/project/pallas_call | solution.py:406
  44.1 4.8 %collective-permute-done.7.refs_1_ = bf16[16,64,128]{2,1,0:T(8,128)(2,1)S(1)} collective-permute-done((bf16[16,64,128]{2,1,0:T(8,128)(2,1)S(1)}, bf16[16,64,128]{2,1,0:T(8,128)(2,1)S(1)}, u32[]{:S(2)}, u32[]{:S(2)}) %collective-permute-start.7) | collective-permute-done | bytes 262176 | tf_op jit(solution)/shard_map/ppermute | solution.py:82
  52.9 21.8 %attend.1 = (bf16[4,512,128]{2,1,0:T(8,128)(2,1)}, bf16[4,512,128]{2,1,0:T(8,128)(2,1)}, bf16[4,128,512]{2,1,0:T(8,128)(2,1)}, bf16[4,128,512]{2,1,0:T(8,128)(2,...) custom-call(s32[4]{0:T(128)} %pad_add_fusion.place_ref, ...), custom_call_target="tpu_custom_call" | custom-call | tf_op jit(solution)/shard_map/attend/pallas_call | solution.py:423
  74.7 5.4 %post.1 = (bf16[8,2,4,64,128]{4,3,2,1,0:T(8,128)(2,1)}, bf16[64,80,128]{2,1,0:T(8,128)(2,1)}, bf16[64,80,128]{2,1,0:T(8,128)(2,1)}, f32[2,128]{1,0:T(2,128)}) custom-call(s32[4]{0:T(128)} %pad_add_fusion.place_ref, bf16[4,512,128]{2,1,0:T(8,128)(2,1)} %get-tuple-element.55.att_ref, ...), custom_call_target="tpu_custom_call", output_to_operand_aliasing={{1}: (12, {}), {2}: (13, {})} | custom-call | tf_op jit(solution)/shard_map/post/pallas_call | solution.py:441
  80.3 6.5 %all-to-all-start.1 = ((bf16[8,2,4,64,128]{4,3,2,1,0:T(8,128)(2,1)}), bf16[8,2,4,64,128]{4,3,2,1,0:T(8,128)(2,1)}, u32[]{:S(2)}, u32[]{:S(2)}) async-start(bf16[8,2,4,64,128]{4,3,2,1,0:T(8,128)(2,1)} %get-tuple-element.65), calls=%async_computation.1 | async-start | bytes 2097152 | tf_op jit(solution)/shard_map/all_to_all | solution.py:380
  88.4 1.6 %collective-permute-start.15 = (bf16[16,80,128]{2,1,0:T(8,128)(2,1)S(1)}, bf16[16,80,128]{2,1,0:T(8,128)(2,1)S(1)}, u32[]{:S(2)}, u32[]{:S(2)}) collective-permute-start(bf16[16,80,128]{2,1,0:T(8,128)(2,1)S(1)} %get-tuple-element.86), channel_id=1, source_target_pairs={{0,48},{1,49},{2,50},{3,51},{4,52},{5,53},{6,54},{7,55},{8,56},{9,... | collective-permute-start | bytes 983048 | tf_op jit(solution)/shard_map/ppermute | solution.py:82
  90.4 8.9 %collective-permute-done.16 = bf16[16,80,128]{2,1,0:T(8,128)(2,1)S(1)} collective-permute-done((bf16[16,80,128]{2,1,0:T(8,128)(2,1)S(1)}, bf16[16,80,128]{2,1,0:T(8,128)(2,1)S(1)}, u32[]{:S(2)}, u32[]{:S(2)}) %collective-permute-start.16) | collective-permute-done | bytes 327712 | tf_op jit(solution)/shard_map/ppermute | solution.py:82
  99.3 3.3 %collective-permute-done.15 = bf16[16,80,128]{2,1,0:T(8,128)(2,1)S(1)} collective-permute-done((bf16[16,80,128]{2,1,0:T(8,128)(2,1)S(1)}, bf16[16,80,128]{2,1,0:T(8,128)(2,1)S(1)}, u32[]{:S(2)}, u32[]{:S(2)}) %collective-permute-start.15) | collective-permute-done | bytes 327712 | tf_op jit(solution)/shard_map/ppermute | solution.py:82
  102.7 2.6 %collective-permute-done.14 = bf16[16,80,128]{2,1,0:T(8,128)(2,1)S(1)} collective-permute-done((bf16[16,80,128]{2,1,0:T(8,128)(2,1)S(1)}, bf16[16,80,128]{2,1,0:T(8,128)(2,1)S(1)}, u32[]{:S(2)}, u32[]{:S(2)}) %collective-permute-start.14) | collective-permute-done | bytes 327712 | tf_op jit(solution)/shard_map/ppermute | solution.py:82
  105.5 3.3 %collective-permute-start.19 = (bf16[4,80,128]{2,1,0:T(8,128)(2,1)S(1)}, bf16[4,80,128]{2,1,0:T(8,128)(2,1)S(1)}, u32[]{:S(2)}, u32[]{:S(2)}) collective-permute-start(bf16[4,80,128]{2,1,0:T(8,128)(2,1)S(1)} %get-tuple-element.89), channel_id=1, source_target_pairs={{0,4},{1,5},{2,6},{3,7},{4,0},{5,1},{6,2},{7,3},{8,12},{9,13},{10,... | collective-permute-start | bytes 245768 | tf_op jit(solution)/shard_map/ppermute | solution.py:82
  111.5 2.0 %collective-permute-done.18 = bf16[4,80,128]{2,1,0:T(8,128)(2,1)S(1)} collective-permute-done((bf16[4,80,128]{2,1,0:T(8,128)(2,1)S(1)}, bf16[4,80,128]{2,1,0:T(8,128)(2,1)S(1)}, u32[]{:S(2)}, u32[]{:S(2)}) %collective-permute-start.18) | collective-permute-done | bytes 81952 | tf_op jit(solution)/shard_map/ppermute | solution.py:82
  113.6 2.1 %collective-permute-done.17 = bf16[4,80,128]{2,1,0:T(8,128)(2,1)S(1)} collective-permute-done((bf16[4,80,128]{2,1,0:T(8,128)(2,1)S(1)}, bf16[4,80,128]{2,1,0:T(8,128)(2,1)S(1)}, u32[]{:S(2)}, u32[]{:S(2)}) %collective-permute-start.17) | collective-permute-done | bytes 81952 | tf_op jit(solution)/shard_map/ppermute | solution.py:82
  116.3 3.0 %collective-permute-start.22 = (bf16[80,128]{1,0:T(8,128)(2,1)S(1)}, bf16[80,128]{1,0:T(8,128)(2,1)S(1)}, u32[]{:S(2)}, u32[]{:S(2)}) collective-permute-start(bf16[80,128]{1,0:T(8,128)(2,1)S(1)} %get-tuple-element.92), channel_id=1, source_target_pairs={{0,1},{1,0},{2,3},{3,2},{4,5},{5,4},{6,7},{7,6},{8,9},{9,8},{10,11... | collective-permute-start | bytes 61448 | tf_op jit(solution)/shard_map/ppermute | solution.py:82
  119.6 1.6 %collective-permute-start.20 = (bf16[80,128]{1,0:T(8,128)(2,1)S(1)}, bf16[80,128]{1,0:T(8,128)(2,1)S(1)}, u32[]{:S(2)}, u32[]{:S(2)}) collective-permute-start(bf16[80,128]{1,0:T(8,128)(2,1)S(1)} %get-tuple-element.94), channel_id=1, source_target_pairs={{0,64},{1,65},{2,66},{3,67},{4,68},{5,69},{6,70},{7,71},{8,72},{9,... | collective-permute-start | bytes 61448 | tf_op jit(solution)/shard_map/ppermute | solution.py:82
  121.6 1.4 collective-permute-done.21.three_ref
  123.0 1.6 %collective-permute-done.20.two_ref = bf16[80,128]{1,0:T(8,128)(2,1)S(1)} collective-permute-done((bf16[80,128]{1,0:T(8,128)(2,1)S(1)}, bf16[80,128]{1,0:T(8,128)(2,1)S(1)}, u32[]{:S(2)}, u32[]{:S(2)}) %collective-permute-start.20) | collective-permute-done | bytes 20512 | tf_op jit(solution)/shard_map/ppermute | solution.py:82
  125.2 2.5 %tile_sums.1 = (bf16[16,2048]{1,0:T(8,128)(2,1)}, bf16[128,16,128]{2,1,0:T(8,128)(2,1)}) custom-call(bf16[2048,128]{1,0:T(8,128)(2,1)} %get-tuple-element.66.n_ref, bf16[2048,128]{1,0:T(8,128)(2,1)} %get-tuple-element.67.u_ref, bf16[80,128]{1,0:T(8,128)(2,1)} %get-tuple-element.95.one_ref, bf16[80,128]{1,0:T(8,128)(2,1)} %copy-done.18, ...), custom_call_target="tpu_custom_call" | custom-call | tf_op jit(solution)/shard_map/tile_sums/pallas_call | solution.py:457
  127.7 4.6 %all-to-all-start.2 = ((bf16[128,16,128]{2,1,0:T(8,128)(2,1)}), bf16[128,16,128]{2,1,0:T(8,128)(2,1)S(1)}, u32[]{:S(2)}, u32[]{:S(2)}) async-start(bf16[128,16,128]{2,1,0:T(8,128)(2,1)} %get-tuple-element.75), calls=%async_computation.2 | async-start | bytes 1048576 | tf_op jit(solution)/shard_map/all_to_all | solution.py:380
  132.3 3.7 %tile_final.1 = (bf16[2048,128]{1,0:T(8,128)(2,1)}, bf16[2048,128]{1,0:T(8,128)(2,1)}) custom-call(bf16[2048,128]{1,0:T(8,128)(2,1)} %bitcast.39, bf16[8,2,256,128]{3,2,1,0:T(8,128)(2,1)} %bitcast.19.ug_ref, bf16[16,2048]{1,0:T(8,128)(2,1)} %get-tuple-element.72.both_ref, f32[1,128]{1,0:T(1,128)} %bitcast.50, bf16[16,128]{1,0:T(8,128)(2,1)} %get-tuple-element.71.wb_ref), custom_call_target="tpu_custom_call" | custom-call | flops 5000000000 | bytes 18000000 | tf_op jit(solution)/shard_map/tile_final/pallas_call | solution.py:465
  136.0 9.7 %all-to-all-done.2.msg_ref = bf16[128,16,128]{2,1,0:T(8,128)(2,1)S(1)} async-done(((bf16[128,16,128]{2,1,0:T(8,128)(2,1)}), bf16[128,16,128]{2,1,0:T(8,128)(2,1)S(1)}, u32[]{:S(2)}, u32[]{:S(2)}) %all-to-all-start.2) | async-done | bytes 524320 | tf_op jit(solution)/shard_map/all_to_all | solution.py:380
  146.5 2.0 %finish.1 = (f32[128,128]{1,0:T(8,128)}, f32[128,128]{1,0:T(8,128)}, f32[128,128]{1,0:T(8,128)}, f32[128,128]{1,0:T(8,128)}, f32[128,128]{1,0:T(8,128)}, /*index...) custom-call(bf16[128,16,128]{2,1,0:T(8,128)(2,1)} %copy-done.2), custom_call_target="tpu_custom_call" | custom-call | tf_op jit(solution)/shard_map/finish/pallas_call | solution.py:472
  (77 shorter events, 16.2 us)
Async XLA Ops:
  2.9 15.9 %copy-start.12 = (bf16[128,128]{1,0:T(8,128)(2,1)S(1)}, bf16[128,128]{1,0:T(8,128)(2,1)}, u32[]{:S(2)}) copy-start(bf16[128,128]{1,0:T(8,128)(2,1)} %param.13) | copy-start | bytes 98308
  2.9 15.9 %copy-start.13 = (bf16[128,128]{1,0:T(8,128)(2,1)S(1)}, bf16[128,128]{1,0:T(8,128)(2,1)}, u32[]{:S(2)}) copy-start(bf16[128,128]{1,0:T(8,128)(2,1)} %param.14) | copy-start | bytes 98308
  2.9 15.9 %copy-start.14 = (bf16[128,128]{1,0:T(8,128)(2,1)S(1)}, bf16[128,128]{1,0:T(8,128)(2,1)}, u32[]{:S(2)}) copy-start(bf16[128,128]{1,0:T(8,128)(2,1)} %param.15) | copy-start | bytes 98308
  2.9 26.1 %copy-start.15 = (bf16[128,128]{1,0:T(8,128)(2,1)S(1)}, bf16[128,128]{1,0:T(8,128)(2,1)}, u32[]{:S(2)}) copy-start(bf16[128,128]{1,0:T(8,128)(2,1)} %param.16) | copy-start | bytes 98308
  2.9 35.1 %all-to-all-start = ((bf16[8,2,4,64,128]{4,3,2,1,0:T(8,128)(2,1)}), bf16[8,2,4,64,128]{4,3,2,1,0:T(8,128)(2,1)S(1)}, u32[]{:S(2)}, u32[]{:S(2)}) async-start(bf16[8,2,4,64,128]{4,3,2,1,0:T(8,128)(2,1)} %pack.1), calls=%async_computation | async-start | bytes 2097152 | tf_op jit(solution)/shard_map/all_to_all | solution.py:380
  12.9 6.0 %collective-permute-start.2 = (bf16[64,128]{1,0:T(8,128)(2,1)}, bf16[64,128]{1,0:T(8,128)(2,1)S(1)}, u32[]{:S(2)}, u32[]{:S(2)}) collective-permute-start(bf16[64,128]{1,0:T(8,128)(2,1)} %get-tuple-element.51), channel_id=1, source_target_pairs={{0,32},{1,33},{2,34},{3,35},{4,36},{5,37},{6,38},{7,39},{8,40},{9,... | collective-permute-start | bytes 49160 | tf_op jit(solution)/shard_map/ppermute | solution.py:82
  16.8 3.9 %collective-permute-start.1 = (bf16[64,128]{1,0:T(8,128)(2,1)}, bf16[64,128]{1,0:T(8,128)(2,1)S(1)}, u32[]{:S(2)}, u32[]{:S(2)}) collective-permute-start(bf16[64,128]{1,0:T(8,128)(2,1)} %get-tuple-element.51), channel_id=1, source_target_pairs={{0,48},{1,49},{2,50},{3,51},{4,52},{5,53},{6,54},{7,55},{8,56},{9,... | collective-permute-start | bytes 49160 | tf_op jit(solution)/shard_map/ppermute | solution.py:82
  17.5 5.2 %collective-permute-start = (bf16[64,128]{1,0:T(8,128)(2,1)}, bf16[64,128]{1,0:T(8,128)(2,1)S(1)}, u32[]{:S(2)}, u32[]{:S(2)}) collective-permute-start(bf16[64,128]{1,0:T(8,128)(2,1)} %get-tuple-element.51), channel_id=1, source_target_pairs={{0,16},{1,17},{2,18},{3,19},{4,20},{5,21},{6,22},{7,23},{8,24},{9,... | collective-permute-start | bytes 49160 | tf_op jit(solution)/shard_map/ppermute | solution.py:82
  23.4 5.7 %collective-permute-start.4 = (bf16[4,64,128]{2,1,0:T(8,128)(2,1)S(1)}, bf16[4,64,128]{2,1,0:T(8,128)(2,1)S(1)}, u32[]{:S(2)}, u32[]{:S(2)}) collective-permute-start(bf16[4,64,128]{2,1,0:T(8,128)(2,1)S(1)} %get-tuple-element.97), channel_id=1, source_target_pairs={{0,6},{1,7},{2,0},{3,1},{4,2},{5,3},{6,4},{7,5},{8,14},{9,15},{10,... | collective-permute-start | bytes 196616 | tf_op jit(solution)/shard_map/ppermute | solution.py:82
  26.7 6.2 %collective-permute-start.3 = (bf16[4,64,128]{2,1,0:T(8,128)(2,1)S(1)}, bf16[4,64,128]{2,1,0:T(8,128)(2,1)S(1)}, u32[]{:S(2)}, u32[]{:S(2)}) collective-permute-start(bf16[4,64,128]{2,1,0:T(8,128)(2,1)S(1)} %get-tuple-element.97), channel_id=1, source_target_pairs={{0,2},{1,3},{2,4},{3,5},{4,6},{5,7},{6,0},{7,1},{8,10},{9,11},{10,... | collective-permute-start | bytes 196616 | tf_op jit(solution)/shard_map/ppermute | solution.py:82
  26.7 6.2 %collective-permute-start.5 = (bf16[4,64,128]{2,1,0:T(8,128)(2,1)S(1)}, bf16[4,64,128]{2,1,0:T(8,128)(2,1)S(1)}, u32[]{:S(2)}, u32[]{:S(2)}) collective-permute-start(bf16[4,64,128]{2,1,0:T(8,128)(2,1)S(1)} %get-tuple-element.97), channel_id=1, source_target_pairs={{0,4},{1,5},{2,6},{3,7},{4,0},{5,1},{6,2},{7,3},{8,12},{9,13},{10,... | collective-permute-start | bytes 196616 | tf_op jit(solution)/shard_map/ppermute | solution.py:82
  29.0 9.1 %copy-start.11 = (bf16[128,512]{1,0:T(8,128)(2,1)}, bf16[128,512]{1,0:T(8,128)(2,1)S(1)}, u32[]{:S(2)}) copy-start(bf16[128,512]{1,0:T(8,128)(2,1)S(1)} %constant_dynamic-update-slice_fusion.wcat_ref) | copy-start | bytes 393220
  32.9 11.2 %copy-start.6 = (bf16[4,4,64,128]{3,2,1,0:T(8,128)(2,1)}, bf16[4,4,64,128]{3,2,1,0:T(8,128)(2,1)S(1)}, u32[]{:S(2)}) copy-start(bf16[4,4,64,128]{3,2,1,0:T(8,128)(2,1)S(1)} %pad_maximum_fusion) | copy-start | bytes 786436
  32.9 17.9 %collective-permute-start.9 = (bf16[16,64,128]{2,1,0:T(8,128)(2,1)S(1)}, bf16[16,64,128]{2,1,0:T(8,128)(2,1)S(1)}, u32[]{:S(2)}, u32[]{:S(2)}) collective-permute-start(bf16[16,64,128]{2,1,0:T(8,128)(2,1)S(1)} %bitcast.32), channel_id=1, source_target_pairs={{0,8},{1,9},{2,10},{3,11},{4,12},{5,13},{6,14},{7,15},{8,0},{9,1},... | collective-permute-start | bytes 786440 | tf_op jit(solution)/shard_map/ppermute | solution.py:82
  33.0 11.1 %collective-permute-start.8 = (bf16[16,64,128]{2,1,0:T(8,128)(2,1)S(1)}, bf16[16,64,128]{2,1,0:T(8,128)(2,1)S(1)}, u32[]{:S(2)}, u32[]{:S(2)}) collective-permute-start(bf16[16,64,128]{2,1,0:T(8,128)(2,1)S(1)} %bitcast.33), channel_id=1, source_target_pairs={{0,1},{1,0},{2,3},{3,2},{4,5},{5,4},{6,7},{7,6},{8,9},{9,8},{10,11... | collective-permute-start | bytes 786440 | tf_op jit(solution)/shard_map/ppermute | solution.py:82
  36.0 12.9 %collective-permute-start.7 = (bf16[16,64,128]{2,1,0:T(8,128)(2,1)S(1)}, bf16[16,64,128]{2,1,0:T(8,128)(2,1)S(1)}, u32[]{:S(2)}, u32[]{:S(2)}) collective-permute-start(bf16[16,64,128]{2,1,0:T(8,128)(2,1)S(1)} %bitcast.34), channel_id=1, source_target_pairs={{0,65},{1,64},{2,67},{3,66},{4,69},{5,68},{6,71},{7,70},{8,73},{9,... | collective-permute-start | bytes 786440 | tf_op jit(solution)/shard_map/ppermute | solution.py:82
  36.3 12.6 %collective-permute-start.6 = (bf16[16,64,128]{2,1,0:T(8,128)(2,1)S(1)}, bf16[16,64,128]{2,1,0:T(8,128)(2,1)S(1)}, u32[]{:S(2)}, u32[]{:S(2)}) collective-permute-start(bf16[16,64,128]{2,1,0:T(8,128)(2,1)S(1)} %bitcast.35), channel_id=1, source_target_pairs={{0,64},{1,65},{2,66},{3,67},{4,68},{5,69},{6,70},{7,71},{8,72},{9,... | collective-permute-start | bytes 786440 | tf_op jit(solution)/shard_map/ppermute | solution.py:82
  49.7 1.7 %collective-permute-start.10 = (bf16[16,64,128]{2,1,0:T(8,128)(2,1)}, bf16[16,64,128]{2,1,0:T(8,128)(2,1)S(1)}, u32[]{:S(2)}, u32[]{:S(2)}) collective-permute-start(bf16[16,64,128]{2,1,0:T(8,128)(2,1)} %get-tuple-element.52.refs_1_), channel_id=1, source_target_pairs={{0,8},{1,9},{2,10},{3,11},{4,12},{5,13},{6,14},{7,15},{8,0},{9,1},... | collective-permute-start | bytes 786440 | tf_op jit(solution)/shard_map/ppermute | solution.py:82
  49.7 2.1 %collective-permute-start.11 = (bf16[16,64,128]{2,1,0:T(8,128)(2,1)}, bf16[16,64,128]{2,1,0:T(8,128)(2,1)S(1)}, u32[]{:S(2)}, u32[]{:S(2)}) collective-permute-start(bf16[16,64,128]{2,1,0:T(8,128)(2,1)} %get-tuple-element.53.refs_2_), channel_id=1, source_target_pairs={{0,8},{1,9},{2,10},{3,11},{4,12},{5,13},{6,14},{7,15},{8,0},{9,1},... | collective-permute-start | bytes 786440 | tf_op jit(solution)/shard_map/ppermute | solution.py:82
  50.2 2.0 %collective-permute-start.12 = (bf16[16,64,128]{2,1,0:T(8,128)(2,1)}, bf16[16,64,128]{2,1,0:T(8,128)(2,1)S(1)}, u32[]{:S(2)}, u32[]{:S(2)}) collective-permute-start(bf16[16,64,128]{2,1,0:T(8,128)(2,1)} %get-tuple-element.54.refs_3_), channel_id=1, source_target_pairs={{0,8},{1,9},{2,10},{3,11},{4,12},{5,13},{6,14},{7,15},{8,0},{9,1},... | collective-permute-start | bytes 786440 | tf_op jit(solution)/shard_map/ppermute | solution.py:82
  80.1 6.7 %collective-permute-start.13 = (bf16[64,80,128]{2,1,0:T(8,128)(2,1)}, bf16[64,80,128]{2,1,0:T(8,128)(2,1)S(1)}, u32[]{:S(2)}, u32[]{:S(2)}) collective-permute-start(bf16[64,80,128]{2,1,0:T(8,128)(2,1)} %get-tuple-element.69), channel_id=1, source_target_pairs={{0,8},{1,9},{2,10},{3,11},{4,12},{5,13},{6,14},{7,15},{8,0},{9,1},... | collective-permute-start | bytes 3932168 | tf_op jit(solution)/shard_map/ppermute | solution.py:82
  80.3 47.4 %all-to-all-start.1 = ((bf16[8,2,4,64,128]{4,3,2,1,0:T(8,128)(2,1)}), bf16[8,2,4,64,128]{4,3,2,1,0:T(8,128)(2,1)}, u32[]{:S(2)}, u32[]{:S(2)}) async-start(bf16[8,2,4,64,128]{4,3,2,1,0:T(8,128)(2,1)} %get-tuple-element.65), calls=%async_computation.1 | async-start | bytes 2097152 | tf_op jit(solution)/shard_map/all_to_all | solution.py:380
  87.1 12.2 %collective-permute-start.16 = (bf16[16,80,128]{2,1,0:T(8,128)(2,1)S(1)}, bf16[16,80,128]{2,1,0:T(8,128)(2,1)S(1)}, u32[]{:S(2)}, u32[]{:S(2)}) collective-permute-start(bf16[16,80,128]{2,1,0:T(8,128)(2,1)S(1)} %get-tuple-element.85), channel_id=1, source_target_pairs={{0,32},{1,33},{2,34},{3,35},{4,36},{5,37},{6,38},{7,39},{8,40},{9,... | collective-permute-start | bytes 983048 | tf_op jit(solution)/shard_map/ppermute | solution.py:82
  88.4 14.3 %collective-permute-start.15 = (bf16[16,80,128]{2,1,0:T(8,128)(2,1)S(1)}, bf16[16,80,128]{2,1,0:T(8,128)(2,1)S(1)}, u32[]{:S(2)}, u32[]{:S(2)}) collective-permute-start(bf16[16,80,128]{2,1,0:T(8,128)(2,1)S(1)} %get-tuple-element.86), channel_id=1, source_target_pairs={{0,48},{1,49},{2,50},{3,51},{4,52},{5,53},{6,54},{7,55},{8,56},{9,... | collective-permute-start | bytes 983048 | tf_op jit(solution)/shard_map/ppermute | solution.py:82
  90.0 15.3 %collective-permute-start.14 = (bf16[16,80,128]{2,1,0:T(8,128)(2,1)S(1)}, bf16[16,80,128]{2,1,0:T(8,128)(2,1)S(1)}, u32[]{:S(2)}, u32[]{:S(2)}) collective-permute-start(bf16[16,80,128]{2,1,0:T(8,128)(2,1)S(1)} %get-tuple-element.87), channel_id=1, source_target_pairs={{0,16},{1,17},{2,18},{3,19},{4,20},{5,21},{6,22},{7,23},{8,24},{9,... | collective-permute-start | bytes 983048 | tf_op jit(solution)/shard_map/ppermute | solution.py:82
  105.5 6.0 %collective-permute-start.19 = (bf16[4,80,128]{2,1,0:T(8,128)(2,1)S(1)}, bf16[4,80,128]{2,1,0:T(8,128)(2,1)S(1)}, u32[]{:S(2)}, u32[]{:S(2)}) collective-permute-start(bf16[4,80,128]{2,1,0:T(8,128)(2,1)S(1)} %get-tuple-element.89), channel_id=1, source_target_pairs={{0,4},{1,5},{2,6},{3,7},{4,0},{5,1},{6,2},{7,3},{8,12},{9,13},{10,... | collective-permute-start | bytes 245768 | tf_op jit(solution)/shard_map/ppermute | solution.py:82
  108.8 4.7 %collective-permute-start.18 = (bf16[4,80,128]{2,1,0:T(8,128)(2,1)S(1)}, bf16[4,80,128]{2,1,0:T(8,128)(2,1)S(1)}, u32[]{:S(2)}, u32[]{:S(2)}) collective-permute-start(bf16[4,80,128]{2,1,0:T(8,128)(2,1)S(1)} %get-tuple-element.90), channel_id=1, source_target_pairs={{0,6},{1,7},{2,0},{3,1},{4,2},{5,3},{6,4},{7,5},{8,14},{9,15},{10,... | collective-permute-start | bytes 245768 | tf_op jit(solution)/shard_map/ppermute | solution.py:82
  110.0 5.7 %collective-permute-start.17 = (bf16[4,80,128]{2,1,0:T(8,128)(2,1)S(1)}, bf16[4,80,128]{2,1,0:T(8,128)(2,1)S(1)}, u32[]{:S(2)}, u32[]{:S(2)}) collective-permute-start(bf16[4,80,128]{2,1,0:T(8,128)(2,1)S(1)} %get-tuple-element.91), channel_id=1, source_target_pairs={{0,2},{1,3},{2,4},{3,5},{4,6},{5,7},{6,0},{7,1},{8,10},{9,11},{10,... | collective-permute-start | bytes 245768 | tf_op jit(solution)/shard_map/ppermute | solution.py:82
  116.3 5.3 %collective-permute-start.22 = (bf16[80,128]{1,0:T(8,128)(2,1)S(1)}, bf16[80,128]{1,0:T(8,128)(2,1)S(1)}, u32[]{:S(2)}, u32[]{:S(2)}) collective-permute-start(bf16[80,128]{1,0:T(8,128)(2,1)S(1)} %get-tuple-element.92), channel_id=1, source_target_pairs={{0,1},{1,0},{2,3},{3,2},{4,5},{5,4},{6,7},{7,6},{8,9},{9,8},{10,11... | collective-permute-start | bytes 61448 | tf_op jit(solution)/shard_map/ppermute | solution.py:82
  119.3 3.8 %collective-permute-start.21 = (bf16[80,128]{1,0:T(8,128)(2,1)S(1)}, bf16[80,128]{1,0:T(8,128)(2,1)S(1)}, u32[]{:S(2)}, u32[]{:S(2)}) collective-permute-start(bf16[80,128]{1,0:T(8,128)(2,1)S(1)} %get-tuple-element.93), channel_id=1, source_target_pairs={{0,65},{1,64},{2,67},{3,66},{4,69},{5,68},{6,71},{7,70},{8,73},{9,... | collective-permute-start | bytes 61448 | tf_op jit(solution)/shard_map/ppermute | solution.py:82
  119.6 5.0 %collective-permute-start.20 = (bf16[80,128]{1,0:T(8,128)(2,1)S(1)}, bf16[80,128]{1,0:T(8,128)(2,1)S(1)}, u32[]{:S(2)}, u32[]{:S(2)}) collective-permute-start(bf16[80,128]{1,0:T(8,128)(2,1)S(1)} %get-tuple-element.94), channel_id=1, source_target_pairs={{0,64},{1,65},{2,66},{3,67},{4,68},{5,69},{6,70},{7,71},{8,72},{9,... | collective-permute-start | bytes 61448 | tf_op jit(solution)/shard_map/ppermute | solution.py:82
  127.7 18.0 %all-to-all-start.2 = ((bf16[128,16,128]{2,1,0:T(8,128)(2,1)}), bf16[128,16,128]{2,1,0:T(8,128)(2,1)S(1)}, u32[]{:S(2)}, u32[]{:S(2)}) async-start(bf16[128,16,128]{2,1,0:T(8,128)(2,1)} %get-tuple-element.75), calls=%async_computation.2 | async-start | bytes 1048576 | tf_op jit(solution)/shard_map/all_to_all | solution.py:380
  (13 other events, 23.6 us)

commit v7 on v6

--- a/solution.py
+++ b/solution.py
@@ -13,7 +13,10 @@
 NT = (((1,), (1,)), ((), ()))
 TN = (((0,), (0,)), ((), ()))
 HOPS = (0, 1, 3, 2)
-PARAMS = pltpu.CompilerParams(vmem_limit_bytes=56 * 1024 * 1024)
+
+
+def grant(mebibytes):
+    return pltpu.CompilerParams(vmem_limit_bytes=mebibytes * 1024 * 1024)
 
 
 def dot(left, right, dims=(((1,), (0,)), ((), ()))):
@@ -94,6 +97,7 @@
         out_specs=[anywhere] * len(values),
         out_shape=[jax.ShapeDtypeStruct(value.shape, value.dtype) for value in values],
         input_output_aliases={at: at for at in range(len(values))},
+        compiler_params=grant(1),
         name="after",
     )(*values, other)
 
@@ -145,7 +149,7 @@
     out_ref[:, 1] = cot_ref[...]
 
 
-def project_kernel(scale, rows_ref, gain_ref, wcat_ref, off_ref, wout_ref,
+def project_kernel(scale, place_ref, rows_ref, gain_ref, wcat_ref, off_ref, wout_ref,
                    q_ref, k_ref, v_ref, a_ref, gate_ref, gg_ref, n_ref, u_ref):
     values = rows_ref[:, 0, 0].reshape(512, 128).astype(F32)
     unit, inverse, normed = normalize(values, gain_ref[...])
@@ -383,7 +387,7 @@
         tile_bias_kernel,
         out_shape=[sds((64, 128), BF16), sds((2048, 128), BF16), sds((2048, 128), BF16), sds((16, 128), BF16)],
         scratch_shapes=[pltpu.VMEM((64, 128), F32), pltpu.VMEM((16, 128), F32)],
-        compiler_params=PARAMS,
+        compiler_params=grant(16),
         name="tile_bias",
     )(pair_tile, gain, w_bias.T)
     row, col = lax.axis_index("row"), lax.axis_index("col")
@@ -394,7 +398,7 @@
         pack_kernel,
         cost_estimate=estimate(2),
         out_shape=sds((8, 2, 4, 64, 128), BF16),
-        compiler_params=PARAMS,
+        compiler_params=grant(60),
         name="pack",
     )(pair_rep.reshape(8, 4, 64, 128), cotangent.reshape(8, 4, 64, 128))
     first = [bias_msg] + [send(bias_msg, z=hop) for hop in HOPS[1:]]
@@ -406,13 +410,13 @@
     query, keys, values, grad_att, gate, grad_gated, normed, unit = pl.pallas_call(
         functools.partial(project_kernel, scale),
         grid=(4,),
-        in_specs=[from_rows, whole((1, 128)), whole((128, 512)), whole((1, 128)), whole((128, 128))],
+        in_specs=[smem, from_rows, whole((1, 128)), whole((128, 512)), whole((1, 128)), whole((128, 128))],
         out_specs=[by_row] * 8,
         out_shape=[sds((4, 512, 128), t) for t in (BF16, BF16, BF16, BF16, F32, F32, BF16, BF16)],
-        compiler_params=PARAMS,
+        compiler_params=grant(16),
         cost_estimate=estimate(5),
         name="project",
-    )(both_rows, gain, wcat, offset, w_out)
+    )(place, both_rows, gain, wcat, offset, w_out)
 
     bias_pieces = bias_pieces[:1] + list(after(bias_pieces[1:], query))
     bias_pieces = bias_pieces + [send(piece, core=1) for piece in bias_pieces]
@@ -429,7 +433,7 @@
                    sds((4, 128, 512), BF16), sds((64, 80, 128), BF16), sds((64, 80, 128), BF16)],
         scratch_shapes=[pltpu.VMEM((128, 64, 128), BF16), pltpu.VMEM((1024, 512), F32), pltpu.VMEM((1024, 512), F32),
                         pltpu.VMEM((4, 128, 512), F32), pltpu.VMEM((4, 128, 512), F32)],
-        compiler_params=PARAMS,
+        compiler_params=grant(26),
         name="attend",
     )(place, query, keys, values, grad_att, *bias_pieces)
 
@@ -449,7 +453,7 @@
         scratch_shapes=[pltpu.VMEM((128, 512), F32), pltpu.VMEM((128, 128), F32), pltpu.VMEM((2, 128), F32),
                         pltpu.VMEM((128, 16, 128), F32)],
         input_output_aliases={12: 1, 13: 2},
-        compiler_params=PARAMS,
+        compiler_params=grant(24),
         name="post",
     )(place, attended, dq, dk, dv, gate, grad_gated, normed, unit, both_rows, wcat, w_out, mine, other)
     ug_tile = swap(ug_rows, "col")
@@ -458,14 +462,14 @@
         tile_sums_kernel,
         out_shape=[sds((16, 2048), BF16), sds((128, 16, 128), BF16)],
         scratch_shapes=[pltpu.VMEM((80, 128), F32), pltpu.VMEM((8, 2048), F32)],
-        compiler_params=PARAMS,
+        compiler_params=grant(10),
         name="tile_sums",
     )(normed_tile, unit_tile, *sums, off, wb_two)
     final_in = swap(final_msg, everyone)
     update, grad_pair = pl.pallas_call(
         tile_final_kernel,
         out_shape=[sds((2048, 128), BF16), sds((2048, 128), BF16)],
-        compiler_params=PARAMS,
+        compiler_params=grant(20),
         cost_estimate=estimate(5),
         name="tile_final",
     )(pair_tile, ug_tile.reshape(8, 2, 256, 128), both, gain, wb_two)
@@ -473,7 +477,7 @@
         finish_kernel,
         out_shape=[sds((128, 128), F32)] * 5 + [sds((128,), F32)] * 2 + [sds((4, 128), F32)],
         scratch_shapes=[pltpu.VMEM((128, 16, 128), F32)],
-        compiler_params=PARAMS,
+        compiler_params=grant(8),
         name="finish",
     )(final_in)
     return (

time: 149 us -> 139 us (0.933)
  Pallas kernels: 45.4 us -> 33.7 us
  waiting for transfers between devices: 46.5 us -> 49.6 us
    pallas_call x1, Pallas kernels: 21.8 us -> 19.4 us  [body(): pl.pallas_call(functools.partial(attend_kernel, scale), grid=(2,), in_spe...]
    pallas_call x1, Pallas kernels: 5.04 us -> 2.86 us  [body(): pl.pallas_call(functools.partial(project_kernel, scale), grid=(4,), in_sp...]
    pallas_call x1, Pallas kernels: 2.78 us -> 0.83 us  [body(): pl.pallas_call(tile_bias_kernel, out_shape=[sds((64, 128), BF16), sds((20...]
    ppermute x23, waiting for transfers between devices: 36.9 us -> 38.5 us  [send(): return lax.ppermute(value, ('row', 'col'), shift_pairs(**shift))]
    pallas_call x1, Pallas kernels: 5.36 us -> 3.83 us  [body(): pl.pallas_call(post_kernel, grid=(2,), in_specs=[smem, two, two, two_t, t...]
    unnamed x41 -> x37, local copies, waits for them, and re-layouts: 3.96 us -> 3.29 us
  transfers between devices with their start and end apart: 26 -> 26, of which waited for: 17 -> 18; matrix products, arithmetic and copies ran while one was open for 2% -> 1% of each run, Pallas kernels for 9% -> 5%
where the time goes in v7:
time: 139 us
  waiting for transfers between devices  49.6 us (36%)
  starting transfers between devices  49.3 us (35%)
  Pallas kernels  33.7 us (24%)
  local copies, waits for them, and re-layouts  3.3 us (2%)
  other arithmetic  1.97 us (1%)
    ppermute x23, waiting for transfers between devices, send(): return lax.ppermute(value, ('row', 'col'), shift_pairs(**shift))  38.5 us
    ppermute x23, starting transfers between devices, send(): return lax.ppermute(value, ('row', 'col'), shift_pairs(**shift))  31.1 us
    pallas_call x1, Pallas kernels, body(): pl.pallas_call(functools.partial(attend_kernel, scale), grid=(2,), in_spe...  19.4 us
    all_to_all x3, starting transfers between devices, swap(): return lax.all_to_all(value, axes, split_axis=0, concat_axis=0, tiled=True)  18.2 us
    all_to_all x3, waiting for transfers between devices, swap(): return lax.all_to_all(value, axes, split_axis=0, concat_axis=0, tiled=True)  11 us
    pallas_call x1, Pallas kernels, body(): pl.pallas_call(post_kernel, grid=(2,), in_specs=[smem, two, two, two_t, t...  3.83 us
    unnamed x37, local copies, waits for them, and re-layouts  3.29 us
    pallas_call x1, Pallas kernels, body(): pl.pallas_call(functools.partial(project_kernel, scale), grid=(4,), in_sp...  2.86 us
  transfers between devices with their start and end apart: 26, of which 18 were waited for; matrix products, arithmetic and copies ran while one was open for 1% of the time, Pallas kernels for 5%

profile of v7, /device:TPU:0, one launch (start us, length us, event | category | flops | bytes accessed | tf_op | source)
XLA Modules:
  0.0 138.8 jit_solution(8169693355354043186)
XLA Ops:
  0.6 2.3 %pack.1 = bf16[8,2,4,64,128]{4,3,2,1,0:T(8,128)(2,1)} custom-call(bf16[8,4,64,128]{3,2,1,0:T(8,128)(2,1)} %bitcast.38, bf16[8,4,64,128]{3,2,1,0:T(8,128)(2,1)} %bitcast.53), custom_call_target="tpu_custom_call" | custom-call | flops 2000000000 | bytes 7200000 | tf_op jit(solution)/shard_map/pack/pallas_call | solution.py:397
  3.0 7.2 %all-to-all-start = ((bf16[8,2,4,64,128]{4,3,2,1,0:T(8,128)(2,1)}), bf16[8,2,4,64,128]{4,3,2,1,0:T(8,128)(2,1)S(1)}, u32[]{:S(2)}, u32[]{:S(2)}) async-start(bf16[8,2,4,64,128]{4,3,2,1,0:T(8,128)(2,1)} %pack.1), calls=%async_computation | async-start | bytes 2097152 | tf_op jit(solution)/shard_map/all_to_all | solution.py:384
  11.8 3.9 %collective-permute-start.2 = (bf16[64,128]{1,0:T(8,128)(2,1)S(1)}, bf16[64,128]{1,0:T(8,128)(2,1)S(1)}, u32[]{:S(2)}, u32[]{:S(2)}) collective-permute-start(bf16[64,128]{1,0:T(8,128)(2,1)S(1)} %get-tuple-element.51), channel_id=1, source_target_pairs={{0,32},{1,33},{2,34},{3,35},{4,36},{5,37},{6,38},{7,39},{8,40},{9,... | collective-permute-start | bytes 49160 | tf_op jit(solution)/shard_map/ppermute | solution.py:85
  16.4 1.3 collective-permute-start
  17.9 1.5 %collective-permute-done.1 = bf16[64,128]{1,0:T(8,128)(2,1)S(1)} collective-permute-done((bf16[64,128]{1,0:T(8,128)(2,1)S(1)}, bf16[64,128]{1,0:T(8,128)(2,1)S(1)}, u32[]{:S(2)}, u32[]{:S(2)}) %collective-permute-start.1) | collective-permute-done | bytes 16416 | tf_op jit(solution)/shard_map/ppermute | solution.py:85
  19.4 1.9 %collective-permute-done = bf16[64,128]{1,0:T(8,128)(2,1)S(1)} collective-permute-done((bf16[64,128]{1,0:T(8,128)(2,1)S(1)}, bf16[64,128]{1,0:T(8,128)(2,1)S(1)}, u32[]{:S(2)}, u32[]{:S(2)}) %collective-permute-start) | collective-permute-done | bytes 16416 | tf_op jit(solution)/shard_map/ppermute | solution.py:85
  21.4 3.3 %collective-permute-start.4 = (bf16[4,64,128]{2,1,0:T(8,128)(2,1)S(1)}, bf16[4,64,128]{2,1,0:T(8,128)(2,1)S(1)}, u32[]{:S(2)}, u32[]{:S(2)}) collective-permute-start(bf16[4,64,128]{2,1,0:T(8,128)(2,1)S(1)} %get-tuple-element.97), channel_id=1, source_target_pairs={{0,6},{1,7},{2,0},{3,1},{4,2},{5,3},{6,4},{7,5},{8,14},{9,15},{10,... | collective-permute-start | bytes 196616 | tf_op jit(solution)/shard_map/ppermute | solution.py:85
  24.7 2.3 %collective-permute-start.5 = (bf16[4,64,128]{2,1,0:T(8,128)(2,1)S(1)}, bf16[4,64,128]{2,1,0:T(8,128)(2,1)S(1)}, u32[]{:S(2)}, u32[]{:S(2)}) collective-permute-start(bf16[4,64,128]{2,1,0:T(8,128)(2,1)S(1)} %get-tuple-element.97), channel_id=1, source_target_pairs={{0,4},{1,5},{2,6},{3,7},{4,0},{5,1},{6,2},{7,3},{8,12},{9,13},{10,... | collective-permute-start | bytes 196616 | tf_op jit(solution)/shard_map/ppermute | solution.py:85
  27.1 3.8 %collective-permute-done.3 = bf16[4,64,128]{2,1,0:T(8,128)(2,1)S(1)} collective-permute-done((bf16[4,64,128]{2,1,0:T(8,128)(2,1)S(1)}, bf16[4,64,128]{2,1,0:T(8,128)(2,1)S(1)}, u32[]{:S(2)}, u32[]{:S(2)}) %collective-permute-start.3) | collective-permute-done | bytes 65568 | tf_op jit(solution)/shard_map/ppermute | solution.py:85
  31.0 3.0 %collective-permute-start.8 = (bf16[16,64,128]{2,1,0:T(8,128)(2,1)S(1)}, bf16[16,64,128]{2,1,0:T(8,128)(2,1)S(1)}, u32[]{:S(2)}, u32[]{:S(2)}) collective-permute-start(bf16[16,64,128]{2,1,0:T(8,128)(2,1)S(1)} %bitcast.33), channel_id=1, source_target_pairs={{0,1},{1,0},{2,3},{3,2},{4,5},{5,4},{6,7},{7,6},{8,9},{9,8},{10,11... | collective-permute-start | bytes 786440 | tf_op jit(solution)/shard_map/ppermute | solution.py:85
  34.3 1.7 %collective-permute-start.6 = (bf16[16,64,128]{2,1,0:T(8,128)(2,1)S(1)}, bf16[16,64,128]{2,1,0:T(8,128)(2,1)S(1)}, u32[]{:S(2)}, u32[]{:S(2)}) collective-permute-start(bf16[16,64,128]{2,1,0:T(8,128)(2,1)S(1)} %bitcast.35), channel_id=1, source_target_pairs={{0,64},{1,65},{2,66},{3,67},{4,68},{5,69},{6,70},{7,71},{8,72},{9,... | collective-permute-start | bytes 786440 | tf_op jit(solution)/shard_map/ppermute | solution.py:85
  36.8 2.9 %project.1 = (bf16[4,512,128]{2,1,0:T(8,128)(2,1)S(1)}, bf16[4,512,128]{2,1,0:T(8,128)(2,1)S(1)}, bf16[4,512,128]{2,1,0:T(8,128)(2,1)S(1)}, bf16[4,512,128]{2,1,...) custom-call(s32[4]{0:T(128)S(1)} %pad_add_fusion.place_ref, ...), custom_call_target="tpu_custom_call" | custom-call | flops 5000000000 | bytes 18000000 | tf_op jit(solution)/shard_map/project/pallas_call | solution.py:410
  39.7 2.0 %collective-permute-done.8.refs_2_ = bf16[16,64,128]{2,1,0:T(8,128)(2,1)S(1)} collective-permute-done((bf16[16,64,128]{2,1,0:T(8,128)(2,1)S(1)}, bf16[16,64,128]{2,1,0:T(8,128)(2,1)S(1)}, u32[]{:S(2)}, u32[]{:S(2)}) %collective-permute-start.8) | collective-permute-done | bytes 262176 | tf_op jit(solution)/shard_map/ppermute | solution.py:85
  41.7 5.2 %collective-permute-done.7.refs_1_ = bf16[16,64,128]{2,1,0:T(8,128)(2,1)S(1)} collective-permute-done((bf16[16,64,128]{2,1,0:T(8,128)(2,1)S(1)}, bf16[16,64,128]{2,1,0:T(8,128)(2,1)S(1)}, u32[]{:S(2)}, u32[]{:S(2)}) %collective-permute-start.7) | collective-permute-done | bytes 262176 | tf_op jit(solution)/shard_map/ppermute | solution.py:85
  50.1 19.4 %attend.1 = (bf16[4,512,128]{2,1,0:T(8,128)(2,1)S(1)}, bf16[4,512,128]{2,1,0:T(8,128)(2,1)S(1)}, bf16[4,128,512]{2,1,0:T(8,128)(2,1)S(1)}, bf16[4,128,512]{2,1,0...) custom-call(s32[4]{0:T(128)S(1)} %pad_add_fusion.place_ref, ...), custom_call_target="tpu_custom_call" | custom-call | tf_op jit(solution)/shard_map/attend/pallas_call | solution.py:427
  69.6 3.8 %post.1 = (bf16[8,2,4,64,128]{4,3,2,1,0:T(8,128)(2,1)}, bf16[64,80,128]{2,1,0:T(8,128)(2,1)S(1)}, bf16[64,80,128]{2,1,0:T(8,128)(2,1)}, f32[2,128]{1,0:T(2,128)S(1)}) custom-call(s32[4]{0:T(128)S(1)} %pad_add_fusion.place_ref, bf16[4,512,128]{2,1,0:T(8,128)(2,1)S(1)} %get-tuple-element.55.att_ref, ...), custom_call_target="tpu_custom_call", output_to_operand_aliasing={{1}: (12, {}), {2}: (13, {})} | custom-call | tf_op jit(solution)/shard_map/post/pallas_call | solution.py:445
  73.5 6.4 %all-to-all-start.1 = ((bf16[8,2,4,64,128]{4,3,2,1,0:T(8,128)(2,1)}), bf16[8,2,4,64,128]{4,3,2,1,0:T(8,128)(2,1)S(1)}, u32[]{:S(2)}, u32[]{:S(2)}) async-start(bf16[8,2,4,64,128]{4,3,2,1,0:T(8,128)(2,1)} %get-tuple-element.65), calls=%async_computation.1 | async-start | bytes 2097152 | tf_op jit(solution)/shard_map/all_to_all | solution.py:384
  80.0 1.6 %add_convert_fusion.3 = (bf16[16,80,128]{2,1,0:T(8,128)(2,1)S(1)}, bf16[16,80,128]{2,1,0:T(8,128)(2,1)S(1)}, bf16[16,80,128]{2,1,0:T(8,128)(2,1)S(1)}, bf16[16,80,128]{2,1,0:T(8,128)(2,1)S(1)}) fusion(bf16[64,80,128]{2,1,0:T(8,128)(2,1)} %collective-permute-done.13, bf16[64,80,128]{2,1,0:T(8,128)(2,1)S(1)} %get-tuple-element.68), kind=kLoop, calls=%fused_computation.3 | loop fusion | flops 2621440 | bytes 3932160 | tf_op jit(solution)/shard_map/convert_element_type | solution.py:113
  82.9 1.6 %collective-permute-start.15 = (bf16[16,80,128]{2,1,0:T(8,128)(2,1)S(1)}, bf16[16,80,128]{2,1,0:T(8,128)(2,1)S(1)}, u32[]{:S(2)}, u32[]{:S(2)}) collective-permute-start(bf16[16,80,128]{2,1,0:T(8,128)(2,1)S(1)} %get-tuple-element.86), channel_id=1, source_target_pairs={{0,48},{1,49},{2,50},{3,51},{4,52},{5,53},{6,54},{7,55},{8,56},{9,... | collective-permute-start | bytes 983048 | tf_op jit(solution)/shard_map/ppermute | solution.py:85
  84.9 8.9 %collective-permute-done.16 = bf16[16,80,128]{2,1,0:T(8,128)(2,1)S(1)} collective-permute-done((bf16[16,80,128]{2,1,0:T(8,128)(2,1)S(1)}, bf16[16,80,128]{2,1,0:T(8,128)(2,1)S(1)}, u32[]{:S(2)}, u32[]{:S(2)}) %collective-permute-start.16) | collective-permute-done | bytes 327712 | tf_op jit(solution)/shard_map/ppermute | solution.py:85
  93.8 3.5 %collective-permute-done.15 = bf16[16,80,128]{2,1,0:T(8,128)(2,1)S(1)} collective-permute-done((bf16[16,80,128]{2,1,0:T(8,128)(2,1)S(1)}, bf16[16,80,128]{2,1,0:T(8,128)(2,1)S(1)}, u32[]{:S(2)}, u32[]{:S(2)}) %collective-permute-start.15) | collective-permute-done | bytes 327712 | tf_op jit(solution)/shard_map/ppermute | solution.py:85
  97.3 2.6 %collective-permute-done.14 = bf16[16,80,128]{2,1,0:T(8,128)(2,1)S(1)} collective-permute-done((bf16[16,80,128]{2,1,0:T(8,128)(2,1)S(1)}, bf16[16,80,128]{2,1,0:T(8,128)(2,1)S(1)}, u32[]{:S(2)}, u32[]{:S(2)}) %collective-permute-start.14) | collective-permute-done | bytes 327712 | tf_op jit(solution)/shard_map/ppermute | solution.py:85
  100.1 3.3 %collective-permute-start.19 = (bf16[4,80,128]{2,1,0:T(8,128)(2,1)S(1)}, bf16[4,80,128]{2,1,0:T(8,128)(2,1)S(1)}, u32[]{:S(2)}, u32[]{:S(2)}) collective-permute-start(bf16[4,80,128]{2,1,0:T(8,128)(2,1)S(1)} %get-tuple-element.89), channel_id=1, source_target_pairs={{0,4},{1,5},{2,6},{3,7},{4,0},{5,1},{6,2},{7,3},{8,12},{9,13},{10,... | collective-permute-start | bytes 245768 | tf_op jit(solution)/shard_map/ppermute | solution.py:85
  106.1 2.0 %collective-permute-done.18 = bf16[4,80,128]{2,1,0:T(8,128)(2,1)S(1)} collective-permute-done((bf16[4,80,128]{2,1,0:T(8,128)(2,1)S(1)}, bf16[4,80,128]{2,1,0:T(8,128)(2,1)S(1)}, u32[]{:S(2)}, u32[]{:S(2)}) %collective-permute-start.18) | collective-permute-done | bytes 81952 | tf_op jit(solution)/shard_map/ppermute | solution.py:85
  108.2 2.1 %collective-permute-done.17 = bf16[4,80,128]{2,1,0:T(8,128)(2,1)S(1)} collective-permute-done((bf16[4,80,128]{2,1,0:T(8,128)(2,1)S(1)}, bf16[4,80,128]{2,1,0:T(8,128)(2,1)S(1)}, u32[]{:S(2)}, u32[]{:S(2)}) %collective-permute-start.17) | collective-permute-done | bytes 81952 | tf_op jit(solution)/shard_map/ppermute | solution.py:85
  110.3 3.0 %collective-permute-start.22 = (bf16[80,128]{1,0:T(8,128)(2,1)S(1)}, bf16[80,128]{1,0:T(8,128)(2,1)S(1)}, u32[]{:S(2)}, u32[]{:S(2)}) collective-permute-start(bf16[80,128]{1,0:T(8,128)(2,1)S(1)} %get-tuple-element.92), channel_id=1, source_target_pairs={{0,1},{1,0},{2,3},{3,2},{4,5},{5,4},{6,7},{7,6},{8,9},{9,8},{10,11... | collective-permute-start | bytes 61448 | tf_op jit(solution)/shard_map/ppermute | solution.py:85
  113.7 1.7 %collective-permute-start.20 = (bf16[80,128]{1,0:T(8,128)(2,1)S(1)}, bf16[80,128]{1,0:T(8,128)(2,1)S(1)}, u32[]{:S(2)}, u32[]{:S(2)}) collective-permute-start(bf16[80,128]{1,0:T(8,128)(2,1)S(1)} %get-tuple-element.94), channel_id=1, source_target_pairs={{0,64},{1,65},{2,66},{3,67},{4,68},{5,69},{6,70},{7,71},{8,72},{9,... | collective-permute-start | bytes 61448 | tf_op jit(solution)/shard_map/ppermute | solution.py:85
  115.7 1.5 %collective-permute-done.21.three_ref = bf16[80,128]{1,0:T(8,128)(2,1)S(1)} collective-permute-done((bf16[80,128]{1,0:T(8,128)(2,1)S(1)}, bf16[80,128]{1,0:T(8,128)(2,1)S(1)}, u32[]{:S(2)}, u32[]{:S(2)}) %collective-permute-start.21) | collective-permute-done | bytes 20512 | tf_op jit(solution)/shard_map/ppermute | solution.py:85
  117.1 1.5 %collective-permute-done.20.two_ref = bf16[80,128]{1,0:T(8,128)(2,1)S(1)} collective-permute-done((bf16[80,128]{1,0:T(8,128)(2,1)S(1)}, bf16[80,128]{1,0:T(8,128)(2,1)S(1)}, u32[]{:S(2)}, u32[]{:S(2)}) %collective-permute-start.20) | collective-permute-done | bytes 20512 | tf_op jit(solution)/shard_map/ppermute | solution.py:85
  119.9 4.6 %all-to-all-start.2 = ((bf16[128,16,128]{2,1,0:T(8,128)(2,1)}), bf16[128,16,128]{2,1,0:T(8,128)(2,1)S(1)}, u32[]{:S(2)}, u32[]{:S(2)}) async-start(bf16[128,16,128]{2,1,0:T(8,128)(2,1)} %get-tuple-element.75), calls=%async_computation.2 | async-start | bytes 1048576 | tf_op jit(solution)/shard_map/all_to_all | solution.py:384
  124.5 2.3 %tile_final.1 = (bf16[2048,128]{1,0:T(8,128)(2,1)}, bf16[2048,128]{1,0:T(8,128)(2,1)}) custom-call(bf16[2048,128]{1,0:T(8,128)(2,1)S(1)} %bitcast.40, bf16[8,2,256,128]{3,2,1,0:T(8,128)(2,1)S(1)} %bitcast.37, bf16[16,2048]{1,0:T(8,128)(2,1)S(1)} %get-tuple-element.72.both_ref, f32[1,128]{1,0:T(1,128)S(1)} %bitcast.45, ...), custom_call_target="tpu_custom_call" | custom-call | flops 5000000000 | bytes 18000000 | tf_op jit(solution)/shard_map/tile_final/pallas_call | solution.py:469
  126.8 11.0 %all-to-all-done.2.msg_ref = bf16[128,16,128]{2,1,0:T(8,128)(2,1)S(1)} async-done(((bf16[128,16,128]{2,1,0:T(8,128)(2,1)}), bf16[128,16,128]{2,1,0:T(8,128)(2,1)S(1)}, u32[]{:S(2)}, u32[]{:S(2)}) %all-to-all-start.2) | async-done | bytes 524320 | tf_op jit(solution)/shard_map/all_to_all | solution.py:384
  (73 shorter events, 14.4 us)
Async XLA Ops:
  3.0 33.1 %all-to-all-start = ((bf16[8,2,4,64,128]{4,3,2,1,0:T(8,128)(2,1)}), bf16[8,2,4,64,128]{4,3,2,1,0:T(8,128)(2,1)S(1)}, u32[]{:S(2)}, u32[]{:S(2)}) async-start(bf16[8,2,4,64,128]{4,3,2,1,0:T(8,128)(2,1)} %pack.1), calls=%async_computation | async-start | bytes 2097152 | tf_op jit(solution)/shard_map/all_to_all | solution.py:384
  10.1 25.9 %copy-start.12 = (f32[128]{0:T(128)S(1)}, f32[128]{0:T(128)}, u32[]{:S(2)}) copy-start(f32[128]{0:T(128)} %param.17) | copy-start | bytes 1540
  11.8 27.9 %copy-start.4 = (bf16[2048,128]{1,0:T(8,128)(2,1)}, bf16[2048,128]{1,0:T(8,128)(2,1)S(1)}, u32[]{:S(2)}) copy-start(bf16[2048,128]{1,0:T(8,128)(2,1)S(1)} %get-tuple-element.67.u_ref) | copy-start | bytes 1572868
  11.8 6.1 %collective-permute-start.2 = (bf16[64,128]{1,0:T(8,128)(2,1)S(1)}, bf16[64,128]{1,0:T(8,128)(2,1)S(1)}, u32[]{:S(2)}, u32[]{:S(2)}) collective-permute-start(bf16[64,128]{1,0:T(8,128)(2,1)S(1)} %get-tuple-element.51), channel_id=1, source_target_pairs={{0,32},{1,33},{2,34},{3,35},{4,36},{5,37},{6,38},{7,39},{8,40},{9,... | collective-permute-start | bytes 49160 | tf_op jit(solution)/shard_map/ppermute | solution.py:85
  15.7 3.7 %collective-permute-start.1 = (bf16[64,128]{1,0:T(8,128)(2,1)S(1)}, bf16[64,128]{1,0:T(8,128)(2,1)S(1)}, u32[]{:S(2)}, u32[]{:S(2)}) collective-permute-start(bf16[64,128]{1,0:T(8,128)(2,1)S(1)} %get-tuple-element.51), channel_id=1, source_target_pairs={{0,48},{1,49},{2,50},{3,51},{4,52},{5,53},{6,54},{7,55},{8,56},{9,... | collective-permute-start | bytes 49160 | tf_op jit(solution)/shard_map/ppermute | solution.py:85
  16.4 4.9 %collective-permute-start = (bf16[64,128]{1,0:T(8,128)(2,1)S(1)}, bf16[64,128]{1,0:T(8,128)(2,1)S(1)}, u32[]{:S(2)}, u32[]{:S(2)}) collective-permute-start(bf16[64,128]{1,0:T(8,128)(2,1)S(1)} %get-tuple-element.51), channel_id=1, source_target_pairs={{0,16},{1,17},{2,18},{3,19},{4,20},{5,21},{6,22},{7,23},{8,24},{9,... | collective-permute-start | bytes 49160 | tf_op jit(solution)/shard_map/ppermute | solution.py:85
  21.4 5.7 %collective-permute-start.4 = (bf16[4,64,128]{2,1,0:T(8,128)(2,1)S(1)}, bf16[4,64,128]{2,1,0:T(8,128)(2,1)S(1)}, u32[]{:S(2)}, u32[]{:S(2)}) collective-permute-start(bf16[4,64,128]{2,1,0:T(8,128)(2,1)S(1)} %get-tuple-element.97), channel_id=1, source_target_pairs={{0,6},{1,7},{2,0},{3,1},{4,2},{5,3},{6,4},{7,5},{8,14},{9,15},{10,... | collective-permute-start | bytes 196616 | tf_op jit(solution)/shard_map/ppermute | solution.py:85
  24.7 6.2 %collective-permute-start.3 = (bf16[4,64,128]{2,1,0:T(8,128)(2,1)S(1)}, bf16[4,64,128]{2,1,0:T(8,128)(2,1)S(1)}, u32[]{:S(2)}, u32[]{:S(2)}) collective-permute-start(bf16[4,64,128]{2,1,0:T(8,128)(2,1)S(1)} %get-tuple-element.97), channel_id=1, source_target_pairs={{0,2},{1,3},{2,4},{3,5},{4,6},{5,7},{6,0},{7,1},{8,10},{9,11},{10,... | collective-permute-start | bytes 196616 | tf_op jit(solution)/shard_map/ppermute | solution.py:85
  24.7 6.2 %collective-permute-start.5 = (bf16[4,64,128]{2,1,0:T(8,128)(2,1)S(1)}, bf16[4,64,128]{2,1,0:T(8,128)(2,1)S(1)}, u32[]{:S(2)}, u32[]{:S(2)}) collective-permute-start(bf16[4,64,128]{2,1,0:T(8,128)(2,1)S(1)} %get-tuple-element.97), channel_id=1, source_target_pairs={{0,4},{1,5},{2,6},{3,7},{4,0},{5,1},{6,2},{7,3},{8,12},{9,13},{10,... | collective-permute-start | bytes 196616 | tf_op jit(solution)/shard_map/ppermute | solution.py:85
  30.9 16.6 %collective-permute-start.9 = (bf16[16,64,128]{2,1,0:T(8,128)(2,1)S(1)}, bf16[16,64,128]{2,1,0:T(8,128)(2,1)S(1)}, u32[]{:S(2)}, u32[]{:S(2)}) collective-permute-start(bf16[16,64,128]{2,1,0:T(8,128)(2,1)S(1)} %bitcast.32), channel_id=1, source_target_pairs={{0,8},{1,9},{2,10},{3,11},{4,12},{5,13},{6,14},{7,15},{8,0},{9,1},... | collective-permute-start | bytes 786440 | tf_op jit(solution)/shard_map/ppermute | solution.py:85
  31.0 10.7 %collective-permute-start.8 = (bf16[16,64,128]{2,1,0:T(8,128)(2,1)S(1)}, bf16[16,64,128]{2,1,0:T(8,128)(2,1)S(1)}, u32[]{:S(2)}, u32[]{:S(2)}) collective-permute-start(bf16[16,64,128]{2,1,0:T(8,128)(2,1)S(1)} %bitcast.33), channel_id=1, source_target_pairs={{0,1},{1,0},{2,3},{3,2},{4,5},{5,4},{6,7},{7,6},{8,9},{9,8},{10,11... | collective-permute-start | bytes 786440 | tf_op jit(solution)/shard_map/ppermute | solution.py:85
  34.0 12.9 %collective-permute-start.7 = (bf16[16,64,128]{2,1,0:T(8,128)(2,1)S(1)}, bf16[16,64,128]{2,1,0:T(8,128)(2,1)S(1)}, u32[]{:S(2)}, u32[]{:S(2)}) collective-permute-start(bf16[16,64,128]{2,1,0:T(8,128)(2,1)S(1)} %bitcast.34), channel_id=1, source_target_pairs={{0,65},{1,64},{2,67},{3,66},{4,69},{5,68},{6,71},{7,70},{8,73},{9,... | collective-permute-start | bytes 786440 | tf_op jit(solution)/shard_map/ppermute | solution.py:85
  34.3 12.6 %collective-permute-start.6 = (bf16[16,64,128]{2,1,0:T(8,128)(2,1)S(1)}, bf16[16,64,128]{2,1,0:T(8,128)(2,1)S(1)}, u32[]{:S(2)}, u32[]{:S(2)}) collective-permute-start(bf16[16,64,128]{2,1,0:T(8,128)(2,1)S(1)} %bitcast.35), channel_id=1, source_target_pairs={{0,64},{1,65},{2,66},{3,67},{4,68},{5,69},{6,70},{7,71},{8,72},{9,... | collective-permute-start | bytes 786440 | tf_op jit(solution)/shard_map/ppermute | solution.py:85
  46.9 1.5 %collective-permute-start.10 = (bf16[16,64,128]{2,1,0:T(8,128)(2,1)S(1)}, bf16[16,64,128]{2,1,0:T(8,128)(2,1)S(1)}, u32[]{:S(2)}, u32[]{:S(2)}) collective-permute-start(bf16[16,64,128]{2,1,0:T(8,128)(2,1)S(1)} %get-tuple-element.52.refs_1_), channel_id=1, source_target_pairs={{0,8},{1,9},{2,10},{3,11},{4,12},{5,13},{6,14},{7,15},{8,0},{9,1},... | collective-permute-start | bytes 786440 | tf_op jit(solution)/shard_map/ppermute | solution.py:85
  46.9 1.9 %collective-permute-start.11 = (bf16[16,64,128]{2,1,0:T(8,128)(2,1)S(1)}, bf16[16,64,128]{2,1,0:T(8,128)(2,1)S(1)}, u32[]{:S(2)}, u32[]{:S(2)}) collective-permute-start(bf16[16,64,128]{2,1,0:T(8,128)(2,1)S(1)} %get-tuple-element.53.refs_2_), channel_id=1, source_target_pairs={{0,8},{1,9},{2,10},{3,11},{4,12},{5,13},{6,14},{7,15},{8,0},{9,1},... | collective-permute-start | bytes 786440 | tf_op jit(solution)/shard_map/ppermute | solution.py:85
  47.4 1.8 %collective-permute-start.12 = (bf16[16,64,128]{2,1,0:T(8,128)(2,1)S(1)}, bf16[16,64,128]{2,1,0:T(8,128)(2,1)S(1)}, u32[]{:S(2)}, u32[]{:S(2)}) collective-permute-start(bf16[16,64,128]{2,1,0:T(8,128)(2,1)S(1)} %get-tuple-element.54.refs_3_), channel_id=1, source_target_pairs={{0,8},{1,9},{2,10},{3,11},{4,12},{5,13},{6,14},{7,15},{8,0},{9,1},... | collective-permute-start | bytes 786440 | tf_op jit(solution)/shard_map/ppermute | solution.py:85
  50.1 19.4 %copy-start.9 = (bf16[128,128]{1,0:T(8,128)(2,1)S(1)}, bf16[128,128]{1,0:T(8,128)(2,1)}, u32[]{:S(2)}) copy-start(bf16[128,128]{1,0:T(8,128)(2,1)} %wout_ref.3) | copy-start | bytes 98308
  73.4 6.6 %collective-permute-start.13 = (bf16[64,80,128]{2,1,0:T(8,128)(2,1)}, bf16[64,80,128]{2,1,0:T(8,128)(2,1)}, u32[]{:S(2)}, u32[]{:S(2)}) collective-permute-start(bf16[64,80,128]{2,1,0:T(8,128)(2,1)} %get-tuple-element.69), channel_id=1, source_target_pairs={{0,8},{1,9},{2,10},{3,11},{4,12},{5,13},{6,14},{7,15},{8,0},{9,1},... | collective-permute-start | bytes 3932168 | tf_op jit(solution)/shard_map/ppermute | solution.py:85
  73.5 46.3 %all-to-all-start.1 = ((bf16[8,2,4,64,128]{4,3,2,1,0:T(8,128)(2,1)}), bf16[8,2,4,64,128]{4,3,2,1,0:T(8,128)(2,1)S(1)}, u32[]{:S(2)}, u32[]{:S(2)}) async-start(bf16[8,2,4,64,128]{4,3,2,1,0:T(8,128)(2,1)} %get-tuple-element.65), calls=%async_computation.1 | async-start | bytes 2097152 | tf_op jit(solution)/shard_map/all_to_all | solution.py:384
  81.6 37.1 %copy-start.3 = (bf16[2048,128]{1,0:T(8,128)(2,1)S(1)}, bf16[2048,128]{1,0:T(8,128)(2,1)}, u32[]{:S(2)}) copy-start(bf16[2048,128]{1,0:T(8,128)(2,1)} %copy-done.2) | copy-start | bytes 1572868
  81.6 37.0 %copy-start.5 = (bf16[2048,128]{1,0:T(8,128)(2,1)S(1)}, bf16[2048,128]{1,0:T(8,128)(2,1)}, u32[]{:S(2)}) copy-start(bf16[2048,128]{1,0:T(8,128)(2,1)} %copy-done.4) | copy-start | bytes 1572868
  81.6 12.2 %collective-permute-start.16 = (bf16[16,80,128]{2,1,0:T(8,128)(2,1)S(1)}, bf16[16,80,128]{2,1,0:T(8,128)(2,1)S(1)}, u32[]{:S(2)}, u32[]{:S(2)}) collective-permute-start(bf16[16,80,128]{2,1,0:T(8,128)(2,1)S(1)} %get-tuple-element.85), channel_id=1, source_target_pairs={{0,32},{1,33},{2,34},{3,35},{4,36},{5,37},{6,38},{7,39},{8,40},{9,... | collective-permute-start | bytes 983048 | tf_op jit(solution)/shard_map/ppermute | solution.py:85
  82.9 14.4 %collective-permute-start.15 = (bf16[16,80,128]{2,1,0:T(8,128)(2,1)S(1)}, bf16[16,80,128]{2,1,0:T(8,128)(2,1)S(1)}, u32[]{:S(2)}, u32[]{:S(2)}) collective-permute-start(bf16[16,80,128]{2,1,0:T(8,128)(2,1)S(1)} %get-tuple-element.86), channel_id=1, source_target_pairs={{0,48},{1,49},{2,50},{3,51},{4,52},{5,53},{6,54},{7,55},{8,56},{9,... | collective-permute-start | bytes 983048 | tf_op jit(solution)/shard_map/ppermute | solution.py:85
  84.5 15.4 %collective-permute-start.14 = (bf16[16,80,128]{2,1,0:T(8,128)(2,1)S(1)}, bf16[16,80,128]{2,1,0:T(8,128)(2,1)S(1)}, u32[]{:S(2)}, u32[]{:S(2)}) collective-permute-start(bf16[16,80,128]{2,1,0:T(8,128)(2,1)S(1)} %get-tuple-element.87), channel_id=1, source_target_pairs={{0,16},{1,17},{2,18},{3,19},{4,20},{5,21},{6,22},{7,23},{8,24},{9,... | collective-permute-start | bytes 983048 | tf_op jit(solution)/shard_map/ppermute | solution.py:85
  100.1 24.4 %copy-start.1 = (bf16[32,64,128]{2,1,0:T(8,128)(2,1)S(1)}, bf16[32,64,128]{2,1,0:T(8,128)(2,1)}, u32[]{:S(2)}) copy-start(bf16[32,64,128]{2,1,0:T(8,128)(2,1)} %param.10) | copy-start | bytes 1572868
  100.1 6.0 %collective-permute-start.19 = (bf16[4,80,128]{2,1,0:T(8,128)(2,1)S(1)}, bf16[4,80,128]{2,1,0:T(8,128)(2,1)S(1)}, u32[]{:S(2)}, u32[]{:S(2)}) collective-permute-start(bf16[4,80,128]{2,1,0:T(8,128)(2,1)S(1)} %get-tuple-element.89), channel_id=1, source_target_pairs={{0,4},{1,5},{2,6},{3,7},{4,0},{5,1},{6,2},{7,3},{8,12},{9,13},{10,... | collective-permute-start | bytes 245768 | tf_op jit(solution)/shard_map/ppermute | solution.py:85
  103.4 4.7 %collective-permute-start.18 = (bf16[4,80,128]{2,1,0:T(8,128)(2,1)S(1)}, bf16[4,80,128]{2,1,0:T(8,128)(2,1)S(1)}, u32[]{:S(2)}, u32[]{:S(2)}) collective-permute-start(bf16[4,80,128]{2,1,0:T(8,128)(2,1)S(1)} %get-tuple-element.90), channel_id=1, source_target_pairs={{0,6},{1,7},{2,0},{3,1},{4,2},{5,3},{6,4},{7,5},{8,14},{9,15},{10,... | collective-permute-start | bytes 245768 | tf_op jit(solution)/shard_map/ppermute | solution.py:85
  104.6 5.7 %collective-permute-start.17 = (bf16[4,80,128]{2,1,0:T(8,128)(2,1)S(1)}, bf16[4,80,128]{2,1,0:T(8,128)(2,1)S(1)}, u32[]{:S(2)}, u32[]{:S(2)}) collective-permute-start(bf16[4,80,128]{2,1,0:T(8,128)(2,1)S(1)} %get-tuple-element.91), channel_id=1, source_target_pairs={{0,2},{1,3},{2,4},{3,5},{4,6},{5,7},{6,0},{7,1},{8,10},{9,11},{10,... | collective-permute-start | bytes 245768 | tf_op jit(solution)/shard_map/ppermute | solution.py:85
  110.3 5.4 %collective-permute-start.22 = (bf16[80,128]{1,0:T(8,128)(2,1)S(1)}, bf16[80,128]{1,0:T(8,128)(2,1)S(1)}, u32[]{:S(2)}, u32[]{:S(2)}) collective-permute-start(bf16[80,128]{1,0:T(8,128)(2,1)S(1)} %get-tuple-element.92), channel_id=1, source_target_pairs={{0,1},{1,0},{2,3},{3,2},{4,5},{5,4},{6,7},{7,6},{8,9},{9,8},{10,11... | collective-permute-start | bytes 61448 | tf_op jit(solution)/shard_map/ppermute | solution.py:85
  113.4 3.8 %collective-permute-start.21 = (bf16[80,128]{1,0:T(8,128)(2,1)S(1)}, bf16[80,128]{1,0:T(8,128)(2,1)S(1)}, u32[]{:S(2)}, u32[]{:S(2)}) collective-permute-start(bf16[80,128]{1,0:T(8,128)(2,1)S(1)} %get-tuple-element.93), channel_id=1, source_target_pairs={{0,65},{1,64},{2,67},{3,66},{4,69},{5,68},{6,71},{7,70},{8,73},{9,... | collective-permute-start | bytes 61448 | tf_op jit(solution)/shard_map/ppermute | solution.py:85
  113.7 5.0 %collective-permute-start.20 = (bf16[80,128]{1,0:T(8,128)(2,1)S(1)}, bf16[80,128]{1,0:T(8,128)(2,1)S(1)}, u32[]{:S(2)}, u32[]{:S(2)}) collective-permute-start(bf16[80,128]{1,0:T(8,128)(2,1)S(1)} %get-tuple-element.94), channel_id=1, source_target_pairs={{0,64},{1,65},{2,66},{3,67},{4,68},{5,69},{6,70},{7,71},{8,72},{9,... | collective-permute-start | bytes 61448 | tf_op jit(solution)/shard_map/ppermute | solution.py:85
  119.9 18.0 %all-to-all-start.2 = ((bf16[128,16,128]{2,1,0:T(8,128)(2,1)}), bf16[128,16,128]{2,1,0:T(8,128)(2,1)S(1)}, u32[]{:S(2)}, u32[]{:S(2)}) async-start(bf16[128,16,128]{2,1,0:T(8,128)(2,1)} %get-tuple-element.75), calls=%async_computation.2 | async-start | bytes 1048576 | tf_op jit(solution)/shard_map/all_to_all | solution.py:384
  (11 other events, 84.0 us)

commit v8 on v7

--- a/solution.py
+++ b/solution.py
@@ -418,7 +418,7 @@
         name="project",
     )(place, both_rows, gain, wcat, offset, w_out)
 
-    bias_pieces = bias_pieces[:1] + list(after(bias_pieces[1:], query))
+    bias_pieces = list(after(bias_pieces, query))
     bias_pieces = bias_pieces + [send(piece, core=1) for piece in bias_pieces]
 
     full = whole((4, 512, 128))

time: 139 us -> 135 us (0.971)
  waiting for transfers between devices: 49.6 us -> 47.2 us
  local copies, waits for them, and re-layouts: 3.3 us -> 0.91 us
    ppermute x23, waiting for transfers between devices: 38.5 us -> 36.1 us  [send(): return lax.ppermute(value, ('row', 'col'), shift_pairs(**shift))]
    unnamed x37 -> x33, local copies, waits for them, and re-layouts: 3.29 us -> 0.89 us
    ppermute x23, starting transfers between devices: 31.1 us -> 32.6 us  [send(): return lax.ppermute(value, ('row', 'col'), shift_pairs(**shift))]
  transfers between devices with their start and end apart: 26 -> 26, of which waited for: 18 -> 19; matrix products, arithmetic and copies ran while one was open for 1% -> 1% of each run, Pallas kernels for 5% -> 5%
where the time goes in v8:
time: 135 us
  starting transfers between devices  50.1 us (37%)
  waiting for transfers between devices  47.2 us (35%)
  Pallas kernels  33.8 us (25%)
  other arithmetic  1.97 us (1%)
    ppermute x23, waiting for transfers between devices, send(): return lax.ppermute(value, ('row', 'col'), shift_pairs(**shift))  36.1 us
    ppermute x23, starting transfers between devices, send(): return lax.ppermute(value, ('row', 'col'), shift_pairs(**shift))  32.6 us
    pallas_call x1, Pallas kernels, body(): pl.pallas_call(functools.partial(attend_kernel, scale), grid=(2,), in_spe...  19.4 us
    all_to_all x3, starting transfers between devices, swap(): return lax.all_to_all(value, axes, split_axis=0, concat_axis=0, tiled=True)  17.6 us
    all_to_all x3, waiting for transfers between devices, swap(): return lax.all_to_all(value, axes, split_axis=0, concat_axis=0, tiled=True)  11 us
    pallas_call x1, Pallas kernels, body(): pl.pallas_call(post_kernel, grid=(2,), in_specs=[smem, two, two, two_t, t...  3.85 us
    pallas_call x1, Pallas kernels, body(): pl.pallas_call(functools.partial(project_kernel, scale), grid=(4,), in_sp...  2.88 us
  transfers between devices with their start and end apart: 26, of which 19 were waited for; matrix products, arithmetic and copies ran while one was open for 1% of the time, Pallas kernels for 5%

profile of v8, /device:TPU:0, one launch (start us, length us, event | category | flops | bytes accessed | tf_op | source)
XLA Modules:
  0.0 134.9 jit_solution(15403586800345081632)
XLA Ops:
  0.6 2.3 %pack.1 = bf16[8,2,4,64,128]{4,3,2,1,0:T(8,128)(2,1)} custom-call(bf16[8,4,64,128]{3,2,1,0:T(8,128)(2,1)} %bitcast.37, bf16[8,4,64,128]{3,2,1,0:T(8,128)(2,1)} %bitcast.52), custom_call_target="tpu_custom_call" | custom-call | flops 2000000000 | bytes 7200000 | tf_op jit(solution)/shard_map/pack/pallas_call | solution.py:397
  3.0 7.2 %all-to-all-start = ((bf16[8,2,4,64,128]{4,3,2,1,0:T(8,128)(2,1)}), bf16[8,2,4,64,128]{4,3,2,1,0:T(8,128)(2,1)S(1)}, u32[]{:S(2)}, u32[]{:S(2)}) async-start(bf16[8,2,4,64,128]{4,3,2,1,0:T(8,128)(2,1)} %pack.1), calls=%async_computation | async-start | bytes 2097152 | tf_op jit(solution)/shard_map/all_to_all | solution.py:384
  11.8 3.9 %collective-permute-start.2 = (bf16[64,128]{1,0:T(8,128)(2,1)S(1)}, bf16[64,128]{1,0:T(8,128)(2,1)S(1)}, u32[]{:S(2)}, u32[]{:S(2)}) collective-permute-start(bf16[64,128]{1,0:T(8,128)(2,1)S(1)} %get-tuple-element.52), channel_id=1, source_target_pairs={{0,32},{1,33},{2,34},{3,35},{4,36},{5,37},{6,38},{7,39},{8,40},{9,... | collective-permute-start | bytes 49160 | tf_op jit(solution)/shard_map/ppermute | solution.py:85
  16.4 1.3 collective-permute-start
  17.9 1.5 %collective-permute-done.1 = bf16[64,128]{1,0:T(8,128)(2,1)S(1)} collective-permute-done((bf16[64,128]{1,0:T(8,128)(2,1)S(1)}, bf16[64,128]{1,0:T(8,128)(2,1)S(1)}, u32[]{:S(2)}, u32[]{:S(2)}) %collective-permute-start.1) | collective-permute-done | bytes 16416 | tf_op jit(solution)/shard_map/ppermute | solution.py:85
  19.4 1.9 %collective-permute-done = bf16[64,128]{1,0:T(8,128)(2,1)S(1)} collective-permute-done((bf16[64,128]{1,0:T(8,128)(2,1)S(1)}, bf16[64,128]{1,0:T(8,128)(2,1)S(1)}, u32[]{:S(2)}, u32[]{:S(2)}) %collective-permute-start) | collective-permute-done | bytes 16416 | tf_op jit(solution)/shard_map/ppermute | solution.py:85
  21.4 3.3 %collective-permute-start.4 = (bf16[4,64,128]{2,1,0:T(8,128)(2,1)S(1)}, bf16[4,64,128]{2,1,0:T(8,128)(2,1)S(1)}, u32[]{:S(2)}, u32[]{:S(2)}) collective-permute-start(bf16[4,64,128]{2,1,0:T(8,128)(2,1)S(1)} %get-tuple-element.99), channel_id=1, source_target_pairs={{0,6},{1,7},{2,0},{3,1},{4,2},{5,3},{6,4},{7,5},{8,14},{9,15},{10,... | collective-permute-start | bytes 196616 | tf_op jit(solution)/shard_map/ppermute | solution.py:85
  24.7 2.3 %collective-permute-start.5 = (bf16[4,64,128]{2,1,0:T(8,128)(2,1)S(1)}, bf16[4,64,128]{2,1,0:T(8,128)(2,1)S(1)}, u32[]{:S(2)}, u32[]{:S(2)}) collective-permute-start(bf16[4,64,128]{2,1,0:T(8,128)(2,1)S(1)} %get-tuple-element.99), channel_id=1, source_target_pairs={{0,4},{1,5},{2,6},{3,7},{4,0},{5,1},{6,2},{7,3},{8,12},{9,13},{10,... | collective-permute-start | bytes 196616 | tf_op jit(solution)/shard_map/ppermute | solution.py:85
  27.1 3.8 %collective-permute-done.3 = bf16[4,64,128]{2,1,0:T(8,128)(2,1)S(1)} collective-permute-done((bf16[4,64,128]{2,1,0:T(8,128)(2,1)S(1)}, bf16[4,64,128]{2,1,0:T(8,128)(2,1)S(1)}, u32[]{:S(2)}, u32[]{:S(2)}) %collective-permute-start.3) | collective-permute-done | bytes 65568 | tf_op jit(solution)/shard_map/ppermute | solution.py:85
  30.9 3.0 %collective-permute-start.8 = (bf16[16,64,128]{2,1,0:T(8,128)(2,1)S(1)}, bf16[16,64,128]{2,1,0:T(8,128)(2,1)S(1)}, u32[]{:S(2)}, u32[]{:S(2)}) collective-permute-start(bf16[16,64,128]{2,1,0:T(8,128)(2,1)S(1)} %bitcast.32), channel_id=1, source_target_pairs={{0,1},{1,0},{2,3},{3,2},{4,5},{5,4},{6,7},{7,6},{8,9},{9,8},{10,11... | collective-permute-start | bytes 786440 | tf_op jit(solution)/shard_map/ppermute | solution.py:85
  34.2 1.7 %collective-permute-start.6 = (bf16[16,64,128]{2,1,0:T(8,128)(2,1)S(1)}, bf16[16,64,128]{2,1,0:T(8,128)(2,1)S(1)}, u32[]{:S(2)}, u32[]{:S(2)}) collective-permute-start(bf16[16,64,128]{2,1,0:T(8,128)(2,1)S(1)} %bitcast.34), channel_id=1, source_target_pairs={{0,64},{1,65},{2,66},{3,67},{4,68},{5,69},{6,70},{7,71},{8,72},{9,... | collective-permute-start | bytes 786440 | tf_op jit(solution)/shard_map/ppermute | solution.py:85
  36.0 2.9 %project.1 = (bf16[4,512,128]{2,1,0:T(8,128)(2,1)S(1)}, bf16[4,512,128]{2,1,0:T(8,128)(2,1)S(1)}, bf16[4,512,128]{2,1,0:T(8,128)(2,1)S(1)}, bf16[4,512,128]{2,1,...) custom-call(s32[4]{0:T(128)S(1)} %pad_add_fusion.place_ref, ...), custom_call_target="tpu_custom_call" | custom-call | flops 5000000000 | bytes 18000000 | tf_op jit(solution)/shard_map/project/pallas_call | solution.py:410
  38.9 2.4 %collective-permute-done.8.refs_3_ = bf16[16,64,128]{2,1,0:T(8,128)(2,1)S(1)} collective-permute-done((bf16[16,64,128]{2,1,0:T(8,128)(2,1)S(1)}, bf16[16,64,128]{2,1,0:T(8,128)(2,1)S(1)}, u32[]{:S(2)}, u32[]{:S(2)}) %collective-permute-start.8) | collective-permute-done | bytes 262176 | tf_op jit(solution)/shard_map/ppermute | solution.py:85
  41.3 1.5 %collective-permute-done.7.refs_2_ = bf16[16,64,128]{2,1,0:T(8,128)(2,1)S(1)} collective-permute-done((bf16[16,64,128]{2,1,0:T(8,128)(2,1)S(1)}, bf16[16,64,128]{2,1,0:T(8,128)(2,1)S(1)}, u32[]{:S(2)}, u32[]{:S(2)}) %collective-permute-start.7) | collective-permute-done | bytes 262176 | tf_op jit(solution)/shard_map/ppermute | solution.py:85
  42.8 1.2 collective-permute-done.6.refs_1_
  46.7 19.4 %attend.1 = (bf16[4,512,128]{2,1,0:T(8,128)(2,1)S(1)}, bf16[4,512,128]{2,1,0:T(8,128)(2,1)S(1)}, bf16[4,128,512]{2,1,0:T(8,128)(2,1)S(1)}, bf16[4,128,512]{2,1,0...) custom-call(s32[4]{0:T(128)S(1)} %pad_add_fusion.place_ref, ...), custom_call_target="tpu_custom_call" | custom-call | tf_op jit(solution)/shard_map/attend/pallas_call | solution.py:427
  66.1 3.8 %post.1 = (bf16[8,2,4,64,128]{4,3,2,1,0:T(8,128)(2,1)}, bf16[64,80,128]{2,1,0:T(8,128)(2,1)S(1)}, bf16[64,80,128]{2,1,0:T(8,128)(2,1)}, f32[2,128]{1,0:T(2,128)S(1)}) custom-call(s32[4]{0:T(128)S(1)} %pad_add_fusion.place_ref, bf16[4,512,128]{2,1,0:T(8,128)(2,1)S(1)} %get-tuple-element.57.att_ref, ...), custom_call_target="tpu_custom_call", output_to_operand_aliasing={{1}: (12, {}), {2}: (13, {})} | custom-call | tf_op jit(solution)/shard_map/post/pallas_call | solution.py:445
  70.1 5.0 %all-to-all-start.1 = ((bf16[8,2,4,64,128]{4,3,2,1,0:T(8,128)(2,1)}), bf16[8,2,4,64,128]{4,3,2,1,0:T(8,128)(2,1)S(1)}, u32[]{:S(2)}, u32[]{:S(2)}) async-start(bf16[8,2,4,64,128]{4,3,2,1,0:T(8,128)(2,1)} %get-tuple-element.67), calls=%async_computation.1 | async-start | bytes 2097152 | tf_op jit(solution)/shard_map/all_to_all | solution.py:384
  75.1 1.6 %add_convert_fusion.3 = (bf16[16,80,128]{2,1,0:T(8,128)(2,1)S(1)}, bf16[16,80,128]{2,1,0:T(8,128)(2,1)S(1)}, bf16[16,80,128]{2,1,0:T(8,128)(2,1)S(1)}, bf16[16,80,128]{2,1,0:T(8,128)(2,1)S(1)}) fusion(bf16[64,80,128]{2,1,0:T(8,128)(2,1)} %collective-permute-done.13, bf16[64,80,128]{2,1,0:T(8,128)(2,1)S(1)} %get-tuple-element.70), kind=kLoop, calls=%fused_computation.3 | loop fusion | flops 2621440 | bytes 3932160 | tf_op jit(solution)/shard_map/convert_element_type | solution.py:113
  76.8 2.4 %collective-permute-start.16 = (bf16[16,80,128]{2,1,0:T(8,128)(2,1)S(1)}, bf16[16,80,128]{2,1,0:T(8,128)(2,1)S(1)}, u32[]{:S(2)}, u32[]{:S(2)}) collective-permute-start(bf16[16,80,128]{2,1,0:T(8,128)(2,1)S(1)} %get-tuple-element.87), channel_id=1, source_target_pairs={{0,32},{1,33},{2,34},{3,35},{4,36},{5,37},{6,38},{7,39},{8,40},{9,... | collective-permute-start | bytes 983048 | tf_op jit(solution)/shard_map/ppermute | solution.py:85
  81.2 7.8 %collective-permute-done.16 = bf16[16,80,128]{2,1,0:T(8,128)(2,1)S(1)} collective-permute-done((bf16[16,80,128]{2,1,0:T(8,128)(2,1)S(1)}, bf16[16,80,128]{2,1,0:T(8,128)(2,1)S(1)}, u32[]{:S(2)}, u32[]{:S(2)}) %collective-permute-start.16) | collective-permute-done | bytes 327712 | tf_op jit(solution)/shard_map/ppermute | solution.py:85
  88.9 6.3 %collective-permute-done.15 = bf16[16,80,128]{2,1,0:T(8,128)(2,1)S(1)} collective-permute-done((bf16[16,80,128]{2,1,0:T(8,128)(2,1)S(1)}, bf16[16,80,128]{2,1,0:T(8,128)(2,1)S(1)}, u32[]{:S(2)}, u32[]{:S(2)}) %collective-permute-start.15) | collective-permute-done | bytes 327712 | tf_op jit(solution)/shard_map/ppermute | solution.py:85
  95.4 3.3 %collective-permute-start.19 = (bf16[4,80,128]{2,1,0:T(8,128)(2,1)S(1)}, bf16[4,80,128]{2,1,0:T(8,128)(2,1)S(1)}, u32[]{:S(2)}, u32[]{:S(2)}) collective-permute-start(bf16[4,80,128]{2,1,0:T(8,128)(2,1)S(1)} %get-tuple-element.91), channel_id=1, source_target_pairs={{0,4},{1,5},{2,6},{3,7},{4,0},{5,1},{6,2},{7,3},{8,12},{9,13},{10,... | collective-permute-start | bytes 245768 | tf_op jit(solution)/shard_map/ppermute | solution.py:85
  101.4 2.0 %collective-permute-done.18 = bf16[4,80,128]{2,1,0:T(8,128)(2,1)S(1)} collective-permute-done((bf16[4,80,128]{2,1,0:T(8,128)(2,1)S(1)}, bf16[4,80,128]{2,1,0:T(8,128)(2,1)S(1)}, u32[]{:S(2)}, u32[]{:S(2)}) %collective-permute-start.18) | collective-permute-done | bytes 81952 | tf_op jit(solution)/shard_map/ppermute | solution.py:85
  103.5 2.1 %collective-permute-done.17 = bf16[4,80,128]{2,1,0:T(8,128)(2,1)S(1)} collective-permute-done((bf16[4,80,128]{2,1,0:T(8,128)(2,1)S(1)}, bf16[4,80,128]{2,1,0:T(8,128)(2,1)S(1)}, u32[]{:S(2)}, u32[]{:S(2)}) %collective-permute-start.17) | collective-permute-done | bytes 81952 | tf_op jit(solution)/shard_map/ppermute | solution.py:85
  105.6 3.0 %collective-permute-start.22 = (bf16[80,128]{1,0:T(8,128)(2,1)S(1)}, bf16[80,128]{1,0:T(8,128)(2,1)S(1)}, u32[]{:S(2)}, u32[]{:S(2)}) collective-permute-start(bf16[80,128]{1,0:T(8,128)(2,1)S(1)} %get-tuple-element.94), channel_id=1, source_target_pairs={{0,1},{1,0},{2,3},{3,2},{4,5},{5,4},{6,7},{7,6},{8,9},{9,8},{10,11... | collective-permute-start | bytes 61448 | tf_op jit(solution)/shard_map/ppermute | solution.py:85
  108.9 1.7 %collective-permute-start.20 = (bf16[80,128]{1,0:T(8,128)(2,1)S(1)}, bf16[80,128]{1,0:T(8,128)(2,1)S(1)}, u32[]{:S(2)}, u32[]{:S(2)}) collective-permute-start(bf16[80,128]{1,0:T(8,128)(2,1)S(1)} %get-tuple-element.96), channel_id=1, source_target_pairs={{0,64},{1,65},{2,66},{3,67},{4,68},{5,69},{6,70},{7,71},{8,72},{9,... | collective-permute-start | bytes 61448 | tf_op jit(solution)/shard_map/ppermute | solution.py:85
  111.0 1.5 %collective-permute-done.21.three_ref = bf16[80,128]{1,0:T(8,128)(2,1)S(1)} collective-permute-done((bf16[80,128]{1,0:T(8,128)(2,1)S(1)}, bf16[80,128]{1,0:T(8,128)(2,1)S(1)}, u32[]{:S(2)}, u32[]{:S(2)}) %collective-permute-start.21) | collective-permute-done | bytes 20512 | tf_op jit(solution)/shard_map/ppermute | solution.py:85
  112.4 1.5 %collective-permute-done.20.two_ref = bf16[80,128]{1,0:T(8,128)(2,1)S(1)} collective-permute-done((bf16[80,128]{1,0:T(8,128)(2,1)S(1)}, bf16[80,128]{1,0:T(8,128)(2,1)S(1)}, u32[]{:S(2)}, u32[]{:S(2)}) %collective-permute-start.20) | collective-permute-done | bytes 20512 | tf_op jit(solution)/shard_map/ppermute | solution.py:85
  115.1 5.4 %all-to-all-start.2 = ((bf16[128,16,128]{2,1,0:T(8,128)(2,1)}), bf16[128,16,128]{2,1,0:T(8,128)(2,1)S(1)}, u32[]{:S(2)}, u32[]{:S(2)}) async-start(bf16[128,16,128]{2,1,0:T(8,128)(2,1)} %get-tuple-element.77), calls=%async_computation.2 | async-start | bytes 1048576 | tf_op jit(solution)/shard_map/all_to_all | solution.py:384
  120.5 2.3 %tile_final.1 = (bf16[2048,128]{1,0:T(8,128)(2,1)}, bf16[2048,128]{1,0:T(8,128)(2,1)}) custom-call(bf16[2048,128]{1,0:T(8,128)(2,1)S(1)} %bitcast.39, bf16[8,2,256,128]{3,2,1,0:T(8,128)(2,1)S(1)} %bitcast.36, bf16[16,2048]{1,0:T(8,128)(2,1)S(1)} %get-tuple-element.74.both_ref, f32[1,128]{1,0:T(1,128)S(1)} %bitcast.44, ...), custom_call_target="tpu_custom_call" | custom-call | flops 5000000000 | bytes 18000000 | tf_op jit(solution)/shard_map/tile_final/pallas_call | solution.py:469
  122.9 11.0 %all-to-all-done.2.msg_ref = bf16[128,16,128]{2,1,0:T(8,128)(2,1)S(1)} async-done(((bf16[128,16,128]{2,1,0:T(8,128)(2,1)}), bf16[128,16,128]{2,1,0:T(8,128)(2,1)S(1)}, u32[]{:S(2)}, u32[]{:S(2)}) %all-to-all-start.2) | async-done | bytes 524320 | tf_op jit(solution)/shard_map/all_to_all | solution.py:384
  (69 shorter events, 13.4 us)
Async XLA Ops:
  3.0 33.0 %all-to-all-start = ((bf16[8,2,4,64,128]{4,3,2,1,0:T(8,128)(2,1)}), bf16[8,2,4,64,128]{4,3,2,1,0:T(8,128)(2,1)S(1)}, u32[]{:S(2)}, u32[]{:S(2)}) async-start(bf16[8,2,4,64,128]{4,3,2,1,0:T(8,128)(2,1)} %pack.1), calls=%async_computation | async-start | bytes 2097152 | tf_op jit(solution)/shard_map/all_to_all | solution.py:384
  10.1 25.8 %copy-start.6 = (bf16[128,128]{1,0:T(8,128)(2,1)S(1)}, bf16[128,128]{1,0:T(8,128)(2,1)}, u32[]{:S(2)}) copy-start(bf16[128,128]{1,0:T(8,128)(2,1)} %wout_ref.3) | copy-start | bytes 98308
  10.1 25.8 %copy-start.10 = (f32[128]{0:T(128)S(1)}, f32[128]{0:T(128)}, u32[]{:S(2)}) copy-start(f32[128]{0:T(128)} %param.17) | copy-start | bytes 1540
  11.8 27.0 %copy-start.4 = (bf16[2048,128]{1,0:T(8,128)(2,1)}, bf16[2048,128]{1,0:T(8,128)(2,1)S(1)}, u32[]{:S(2)}) copy-start(bf16[2048,128]{1,0:T(8,128)(2,1)S(1)} %get-tuple-element.69.u_ref) | copy-start | bytes 1572868
  11.8 6.1 %collective-permute-start.2 = (bf16[64,128]{1,0:T(8,128)(2,1)S(1)}, bf16[64,128]{1,0:T(8,128)(2,1)S(1)}, u32[]{:S(2)}, u32[]{:S(2)}) collective-permute-start(bf16[64,128]{1,0:T(8,128)(2,1)S(1)} %get-tuple-element.52), channel_id=1, source_target_pairs={{0,32},{1,33},{2,34},{3,35},{4,36},{5,37},{6,38},{7,39},{8,40},{9,... | collective-permute-start | bytes 49160 | tf_op jit(solution)/shard_map/ppermute | solution.py:85
  15.7 3.7 %collective-permute-start.1 = (bf16[64,128]{1,0:T(8,128)(2,1)S(1)}, bf16[64,128]{1,0:T(8,128)(2,1)S(1)}, u32[]{:S(2)}, u32[]{:S(2)}) collective-permute-start(bf16[64,128]{1,0:T(8,128)(2,1)S(1)} %get-tuple-element.52), channel_id=1, source_target_pairs={{0,48},{1,49},{2,50},{3,51},{4,52},{5,53},{6,54},{7,55},{8,56},{9,... | collective-permute-start | bytes 49160 | tf_op jit(solution)/shard_map/ppermute | solution.py:85
  16.4 4.9 %collective-permute-start = (bf16[64,128]{1,0:T(8,128)(2,1)S(1)}, bf16[64,128]{1,0:T(8,128)(2,1)S(1)}, u32[]{:S(2)}, u32[]{:S(2)}) collective-permute-start(bf16[64,128]{1,0:T(8,128)(2,1)S(1)} %get-tuple-element.52), channel_id=1, source_target_pairs={{0,16},{1,17},{2,18},{3,19},{4,20},{5,21},{6,22},{7,23},{8,24},{9,... | collective-permute-start | bytes 49160 | tf_op jit(solution)/shard_map/ppermute | solution.py:85
  21.4 5.7 %collective-permute-start.4 = (bf16[4,64,128]{2,1,0:T(8,128)(2,1)S(1)}, bf16[4,64,128]{2,1,0:T(8,128)(2,1)S(1)}, u32[]{:S(2)}, u32[]{:S(2)}) collective-permute-start(bf16[4,64,128]{2,1,0:T(8,128)(2,1)S(1)} %get-tuple-element.99), channel_id=1, source_target_pairs={{0,6},{1,7},{2,0},{3,1},{4,2},{5,3},{6,4},{7,5},{8,14},{9,15},{10,... | collective-permute-start | bytes 196616 | tf_op jit(solution)/shard_map/ppermute | solution.py:85
  24.7 6.2 %collective-permute-start.3 = (bf16[4,64,128]{2,1,0:T(8,128)(2,1)S(1)}, bf16[4,64,128]{2,1,0:T(8,128)(2,1)S(1)}, u32[]{:S(2)}, u32[]{:S(2)}) collective-permute-start(bf16[4,64,128]{2,1,0:T(8,128)(2,1)S(1)} %get-tuple-element.99), channel_id=1, source_target_pairs={{0,2},{1,3},{2,4},{3,5},{4,6},{5,7},{6,0},{7,1},{8,10},{9,11},{10,... | collective-permute-start | bytes 196616 | tf_op jit(solution)/shard_map/ppermute | solution.py:85
  24.7 6.2 %collective-permute-start.5 = (bf16[4,64,128]{2,1,0:T(8,128)(2,1)S(1)}, bf16[4,64,128]{2,1,0:T(8,128)(2,1)S(1)}, u32[]{:S(2)}, u32[]{:S(2)}) collective-permute-start(bf16[4,64,128]{2,1,0:T(8,128)(2,1)S(1)} %get-tuple-element.99), channel_id=1, source_target_pairs={{0,4},{1,5},{2,6},{3,7},{4,0},{5,1},{6,2},{7,3},{8,12},{9,13},{10,... | collective-permute-start | bytes 196616 | tf_op jit(solution)/shard_map/ppermute | solution.py:85
  30.9 10.4 %collective-permute-start.8 = (bf16[16,64,128]{2,1,0:T(8,128)(2,1)S(1)}, bf16[16,64,128]{2,1,0:T(8,128)(2,1)S(1)}, u32[]{:S(2)}, u32[]{:S(2)}) collective-permute-start(bf16[16,64,128]{2,1,0:T(8,128)(2,1)S(1)} %bitcast.32), channel_id=1, source_target_pairs={{0,1},{1,0},{2,3},{3,2},{4,5},{5,4},{6,7},{7,6},{8,9},{9,8},{10,11... | collective-permute-start | bytes 786440 | tf_op jit(solution)/shard_map/ppermute | solution.py:85
  33.9 8.9 %collective-permute-start.7 = (bf16[16,64,128]{2,1,0:T(8,128)(2,1)S(1)}, bf16[16,64,128]{2,1,0:T(8,128)(2,1)S(1)}, u32[]{:S(2)}, u32[]{:S(2)}) collective-permute-start(bf16[16,64,128]{2,1,0:T(8,128)(2,1)S(1)} %bitcast.33), channel_id=1, source_target_pairs={{0,65},{1,64},{2,67},{3,66},{4,69},{5,68},{6,71},{7,70},{8,73},{9,... | collective-permute-start | bytes 786440 | tf_op jit(solution)/shard_map/ppermute | solution.py:85
  34.2 9.8 %collective-permute-start.6 = (bf16[16,64,128]{2,1,0:T(8,128)(2,1)S(1)}, bf16[16,64,128]{2,1,0:T(8,128)(2,1)S(1)}, u32[]{:S(2)}, u32[]{:S(2)}) collective-permute-start(bf16[16,64,128]{2,1,0:T(8,128)(2,1)S(1)} %bitcast.34), channel_id=1, source_target_pairs={{0,64},{1,65},{2,66},{3,67},{4,68},{5,69},{6,70},{7,71},{8,72},{9,... | collective-permute-start | bytes 786440 | tf_op jit(solution)/shard_map/ppermute | solution.py:85
  44.0 1.5 %collective-permute-start.9 = (bf16[16,64,128]{2,1,0:T(8,128)(2,1)S(1)}, bf16[16,64,128]{2,1,0:T(8,128)(2,1)S(1)}, u32[]{:S(2)}, u32[]{:S(2)}) collective-permute-start(bf16[16,64,128]{2,1,0:T(8,128)(2,1)S(1)} %get-tuple-element.53.refs_0_), channel_id=1, source_target_pairs={{0,8},{1,9},{2,10},{3,11},{4,12},{5,13},{6,14},{7,15},{8,0},{9,1},... | collective-permute-start | bytes 786440 | tf_op jit(solution)/shard_map/ppermute | solution.py:85
  44.0 1.9 %collective-permute-start.10 = (bf16[16,64,128]{2,1,0:T(8,128)(2,1)S(1)}, bf16[16,64,128]{2,1,0:T(8,128)(2,1)S(1)}, u32[]{:S(2)}, u32[]{:S(2)}) collective-permute-start(bf16[16,64,128]{2,1,0:T(8,128)(2,1)S(1)} %get-tuple-element.54.refs_1_), channel_id=1, source_target_pairs={{0,8},{1,9},{2,10},{3,11},{4,12},{5,13},{6,14},{7,15},{8,0},{9,1},... | collective-permute-start | bytes 786440 | tf_op jit(solution)/shard_map/ppermute | solution.py:85
  44.5 1.8 %collective-permute-start.11 = (bf16[16,64,128]{2,1,0:T(8,128)(2,1)S(1)}, bf16[16,64,128]{2,1,0:T(8,128)(2,1)S(1)}, u32[]{:S(2)}, u32[]{:S(2)}) collective-permute-start(bf16[16,64,128]{2,1,0:T(8,128)(2,1)S(1)} %get-tuple-element.55.refs_2_), channel_id=1, source_target_pairs={{0,8},{1,9},{2,10},{3,11},{4,12},{5,13},{6,14},{7,15},{8,0},{9,1},... | collective-permute-start | bytes 786440 | tf_op jit(solution)/shard_map/ppermute | solution.py:85
  44.5 2.1 %collective-permute-start.12 = (bf16[16,64,128]{2,1,0:T(8,128)(2,1)S(1)}, bf16[16,64,128]{2,1,0:T(8,128)(2,1)S(1)}, u32[]{:S(2)}, u32[]{:S(2)}) collective-permute-start(bf16[16,64,128]{2,1,0:T(8,128)(2,1)S(1)} %get-tuple-element.56.refs_3_), channel_id=1, source_target_pairs={{0,8},{1,9},{2,10},{3,11},{4,12},{5,13},{6,14},{7,15},{8,0},{9,1},... | collective-permute-start | bytes 786440 | tf_op jit(solution)/shard_map/ppermute | solution.py:85
  70.0 5.1 %collective-permute-start.13 = (bf16[64,80,128]{2,1,0:T(8,128)(2,1)}, bf16[64,80,128]{2,1,0:T(8,128)(2,1)}, u32[]{:S(2)}, u32[]{:S(2)}) collective-permute-start(bf16[64,80,128]{2,1,0:T(8,128)(2,1)} %get-tuple-element.71), channel_id=1, source_target_pairs={{0,8},{1,9},{2,10},{3,11},{4,12},{5,13},{6,14},{7,15},{8,0},{9,1},... | collective-permute-start | bytes 3932168 | tf_op jit(solution)/shard_map/ppermute | solution.py:85
  70.1 45.0 %all-to-all-start.1 = ((bf16[8,2,4,64,128]{4,3,2,1,0:T(8,128)(2,1)}), bf16[8,2,4,64,128]{4,3,2,1,0:T(8,128)(2,1)S(1)}, u32[]{:S(2)}, u32[]{:S(2)}) async-start(bf16[8,2,4,64,128]{4,3,2,1,0:T(8,128)(2,1)} %get-tuple-element.67), calls=%async_computation.1 | async-start | bytes 2097152 | tf_op jit(solution)/shard_map/all_to_all | solution.py:384
  76.7 37.2 %copy-start.3 = (bf16[2048,128]{1,0:T(8,128)(2,1)S(1)}, bf16[2048,128]{1,0:T(8,128)(2,1)}, u32[]{:S(2)}) copy-start(bf16[2048,128]{1,0:T(8,128)(2,1)} %copy-done.2) | copy-start | bytes 1572868
  76.7 37.2 %copy-start.5 = (bf16[2048,128]{1,0:T(8,128)(2,1)S(1)}, bf16[2048,128]{1,0:T(8,128)(2,1)}, u32[]{:S(2)}) copy-start(bf16[2048,128]{1,0:T(8,128)(2,1)} %copy-done.4) | copy-start | bytes 1572868
  76.8 12.2 %collective-permute-start.16 = (bf16[16,80,128]{2,1,0:T(8,128)(2,1)S(1)}, bf16[16,80,128]{2,1,0:T(8,128)(2,1)S(1)}, u32[]{:S(2)}, u32[]{:S(2)}) collective-permute-start(bf16[16,80,128]{2,1,0:T(8,128)(2,1)S(1)} %get-tuple-element.87), channel_id=1, source_target_pairs={{0,32},{1,33},{2,34},{3,35},{4,36},{5,37},{6,38},{7,39},{8,40},{9,... | collective-permute-start | bytes 983048 | tf_op jit(solution)/shard_map/ppermute | solution.py:85
  79.1 16.1 %collective-permute-start.15 = (bf16[16,80,128]{2,1,0:T(8,128)(2,1)S(1)}, bf16[16,80,128]{2,1,0:T(8,128)(2,1)S(1)}, u32[]{:S(2)}, u32[]{:S(2)}) collective-permute-start(bf16[16,80,128]{2,1,0:T(8,128)(2,1)S(1)} %get-tuple-element.88), channel_id=1, source_target_pairs={{0,48},{1,49},{2,50},{3,51},{4,52},{5,53},{6,54},{7,55},{8,56},{9,... | collective-permute-start | bytes 983048 | tf_op jit(solution)/shard_map/ppermute | solution.py:85
  80.0 15.2 %collective-permute-start.14 = (bf16[16,80,128]{2,1,0:T(8,128)(2,1)S(1)}, bf16[16,80,128]{2,1,0:T(8,128)(2,1)S(1)}, u32[]{:S(2)}, u32[]{:S(2)}) collective-permute-start(bf16[16,80,128]{2,1,0:T(8,128)(2,1)S(1)} %get-tuple-element.89), channel_id=1, source_target_pairs={{0,16},{1,17},{2,18},{3,19},{4,20},{5,21},{6,22},{7,23},{8,24},{9,... | collective-permute-start | bytes 983048 | tf_op jit(solution)/shard_map/ppermute | solution.py:85
  95.4 25.1 %copy-start.1 = (bf16[32,64,128]{2,1,0:T(8,128)(2,1)S(1)}, bf16[32,64,128]{2,1,0:T(8,128)(2,1)}, u32[]{:S(2)}) copy-start(bf16[32,64,128]{2,1,0:T(8,128)(2,1)} %param.10) | copy-start | bytes 1572868
  95.4 6.0 %collective-permute-start.19 = (bf16[4,80,128]{2,1,0:T(8,128)(2,1)S(1)}, bf16[4,80,128]{2,1,0:T(8,128)(2,1)S(1)}, u32[]{:S(2)}, u32[]{:S(2)}) collective-permute-start(bf16[4,80,128]{2,1,0:T(8,128)(2,1)S(1)} %get-tuple-element.91), channel_id=1, source_target_pairs={{0,4},{1,5},{2,6},{3,7},{4,0},{5,1},{6,2},{7,3},{8,12},{9,13},{10,... | collective-permute-start | bytes 245768 | tf_op jit(solution)/shard_map/ppermute | solution.py:85
  98.7 4.7 %collective-permute-start.18 = (bf16[4,80,128]{2,1,0:T(8,128)(2,1)S(1)}, bf16[4,80,128]{2,1,0:T(8,128)(2,1)S(1)}, u32[]{:S(2)}, u32[]{:S(2)}) collective-permute-start(bf16[4,80,128]{2,1,0:T(8,128)(2,1)S(1)} %get-tuple-element.92), channel_id=1, source_target_pairs={{0,6},{1,7},{2,0},{3,1},{4,2},{5,3},{6,4},{7,5},{8,14},{9,15},{10,... | collective-permute-start | bytes 245768 | tf_op jit(solution)/shard_map/ppermute | solution.py:85
  99.9 5.7 %collective-permute-start.17 = (bf16[4,80,128]{2,1,0:T(8,128)(2,1)S(1)}, bf16[4,80,128]{2,1,0:T(8,128)(2,1)S(1)}, u32[]{:S(2)}, u32[]{:S(2)}) collective-permute-start(bf16[4,80,128]{2,1,0:T(8,128)(2,1)S(1)} %get-tuple-element.93), channel_id=1, source_target_pairs={{0,2},{1,3},{2,4},{3,5},{4,6},{5,7},{6,0},{7,1},{8,10},{9,11},{10,... | collective-permute-start | bytes 245768 | tf_op jit(solution)/shard_map/ppermute | solution.py:85
  105.6 5.4 %collective-permute-start.22 = (bf16[80,128]{1,0:T(8,128)(2,1)S(1)}, bf16[80,128]{1,0:T(8,128)(2,1)S(1)}, u32[]{:S(2)}, u32[]{:S(2)}) collective-permute-start(bf16[80,128]{1,0:T(8,128)(2,1)S(1)} %get-tuple-element.94), channel_id=1, source_target_pairs={{0,1},{1,0},{2,3},{3,2},{4,5},{5,4},{6,7},{7,6},{8,9},{9,8},{10,11... | collective-permute-start | bytes 61448 | tf_op jit(solution)/shard_map/ppermute | solution.py:85
  108.6 3.8 %collective-permute-start.21 = (bf16[80,128]{1,0:T(8,128)(2,1)S(1)}, bf16[80,128]{1,0:T(8,128)(2,1)S(1)}, u32[]{:S(2)}, u32[]{:S(2)}) collective-permute-start(bf16[80,128]{1,0:T(8,128)(2,1)S(1)} %get-tuple-element.95), channel_id=1, source_target_pairs={{0,65},{1,64},{2,67},{3,66},{4,69},{5,68},{6,71},{7,70},{8,73},{9,... | collective-permute-start | bytes 61448 | tf_op jit(solution)/shard_map/ppermute | solution.py:85
  108.9 5.0 %collective-permute-start.20 = (bf16[80,128]{1,0:T(8,128)(2,1)S(1)}, bf16[80,128]{1,0:T(8,128)(2,1)S(1)}, u32[]{:S(2)}, u32[]{:S(2)}) collective-permute-start(bf16[80,128]{1,0:T(8,128)(2,1)S(1)} %get-tuple-element.96), channel_id=1, source_target_pairs={{0,64},{1,65},{2,66},{3,67},{4,68},{5,69},{6,70},{7,71},{8,72},{9,... | collective-permute-start | bytes 61448 | tf_op jit(solution)/shard_map/ppermute | solution.py:85
  115.1 18.8 %all-to-all-start.2 = ((bf16[128,16,128]{2,1,0:T(8,128)(2,1)}), bf16[128,16,128]{2,1,0:T(8,128)(2,1)S(1)}, u32[]{:S(2)}, u32[]{:S(2)}) async-start(bf16[128,16,128]{2,1,0:T(8,128)(2,1)} %get-tuple-element.77), calls=%async_computation.2 | async-start | bytes 1048576 | tf_op jit(solution)/shard_map/all_to_all | solution.py:384
  (9 other events, 101.2 us)

commit v9 on v8

--- a/solution.py
+++ b/solution.py
@@ -123,14 +123,12 @@
     return [held[0]] + [send(held[at], x=HOPS[at]) for at in (1, 2, 3)]
 
 
-def tile_bias_kernel(pair_ref, gain_ref, w_ref, msg_ref, n_ref, u_ref, wb_ref, rows_ref, w_scr):
+def tile_bias_kernel(pair_ref, gain_ref, w_ref, msg_ref, wb_ref, rows_ref, w_scr):
     w_scr[...] = jnp.zeros(w_scr.shape, F32)
     w_scr[0:4, :] = w_ref[...].astype(F32)
     w_scr[8:12, :] = w_ref[...].astype(F32)
     wb_ref[...] = w_scr[...].astype(BF16)
     unit, inverse, normed = normalize(pair_ref[...].astype(F32), gain_ref[...])
-    n_ref[...] = normed
-    u_ref[...] = unit.astype(BF16)
     bias = dot(w_scr[...].astype(BF16), normed, NT)
     for half in range(8):
         first = bias[0:8, half * 128 : half * 128 + 128]
@@ -142,6 +140,12 @@
             rows_ref[base : base + 1, :] = even[head : head + 1]
             rows_ref[base + 1 : base + 2, :] = odd[head : head + 1]
     msg_ref[...] = rows_ref[...].astype(BF16)
+
+
+def tile_units_kernel(pair_ref, gain_ref, sums_ref, n_ref, u_ref):
+    unit, inverse, normed = normalize(pair_ref[...].astype(F32), gain_ref[...])
+    n_ref[...] = normed
+    u_ref[...] = unit.astype(BF16)
 
 
 def pack_kernel(pair_ref, cot_ref, out_ref):
@@ -383,9 +387,9 @@
     def swap(value, axes):
         return lax.all_to_all(value, axes, split_axis=0, concat_axis=0, tiled=True)
 
-    bias_msg, normed_tile, unit_tile, wb_two = pl.pallas_call(
+    bias_msg, wb_two = pl.pallas_call(
         tile_bias_kernel,
-        out_shape=[sds((64, 128), BF16), sds((2048, 128), BF16), sds((2048, 128), BF16), sds((16, 128), BF16)],
+        out_shape=[sds((64, 128), BF16), sds((16, 128), BF16)],
         scratch_shapes=[pltpu.VMEM((64, 128), F32), pltpu.VMEM((16, 128), F32)],
         compiler_params=grant(16),
         name="tile_bias",
@@ -458,6 +462,14 @@
     )(place, attended, dq, dk, dv, gate, grad_gated, normed, unit, both_rows, wcat, w_out, mine, other)
     ug_tile = swap(ug_rows, "col")
     sums = scatter_sums(mine, other)
+    normed_tile, unit_tile = pl.pallas_call(
+        tile_units_kernel,
+        in_specs=[whole((2048, 128)), whole((1, 128)), pl.BlockSpec(memory_space=pl.ANY)],
+        out_shape=[sds((2048, 128), BF16), sds((2048, 128), BF16)],
+        compiler_params=grant(12),
+        cost_estimate=estimate(2),
+        name="tile_units",
+    )(pair_tile, gain, off)
     both, final_msg = pl.pallas_call(
         tile_sums_kernel,
         out_shape=[sds((16, 2048), BF16), sds((128, 16, 128), BF16)],

time: 135 us -> 131 us (0.970)
  transfers between devices with their start and end apart: 26 -> 26, of which waited for: 19 -> 19; matrix products, arithmetic and copies ran while one was open for 1% -> 0% of each run, Pallas kernels for 5% -> 6%
where the time goes in v9:
time: 131 us
  starting transfers between devices  49.1 us (37%)
  waiting for transfers between devices  46.1 us (35%)
  Pallas kernels  33.4 us (25%)
  other arithmetic  1.52 us (1%)
    ppermute x23, waiting for transfers between devices, send(): return lax.ppermute(value, ('row', 'col'), shift_pairs(**shift))  35.1 us
    ppermute x23, starting transfers between devices, send(): return lax.ppermute(value, ('row', 'col'), shift_pairs(**shift))  31.8 us
    pallas_call x1, Pallas kernels, body(): pl.pallas_call(functools.partial(attend_kernel, scale), grid=(2,), in_spe...  18.3 us
    all_to_all x3, starting transfers between devices, swap(): return lax.all_to_all(value, axes, split_axis=0, concat_axis=0, tiled=True)  17.3 us
    all_to_all x3, waiting for transfers between devices, swap(): return lax.all_to_all(value, axes, split_axis=0, concat_axis=0, tiled=True)  11 us
    pallas_call x1, Pallas kernels, body(): pl.pallas_call(post_kernel, grid=(2,), in_specs=[smem, two, two, two_t, t...  3.86 us
    pallas_call x1, Pallas kernels, body(): pl.pallas_call(functools.partial(project_kernel, scale), grid=(4,), in_sp...  2.87 us
  transfers between devices with their start and end apart: 26, of which 19 were waited for; matrix products, arithmetic and copies ran while one was open for 0% of the time, Pallas kernels for 6%

profile of v9, /device:TPU:0, one launch (start us, length us, event | category | flops | bytes accessed | tf_op | source)
XLA Modules:
  0.0 131.1 jit_solution(2035833362696110263)
XLA Ops:
  0.6 2.3 %pack.1 = bf16[8,2,4,64,128]{4,3,2,1,0:T(8,128)(2,1)} custom-call(bf16[8,4,64,128]{3,2,1,0:T(8,128)(2,1)} %bitcast.37, bf16[8,4,64,128]{3,2,1,0:T(8,128)(2,1)} %bitcast.54), custom_call_target="tpu_custom_call" | custom-call | flops 2000000000 | bytes 7200000 | tf_op jit(solution)/shard_map/pack/pallas_call | solution.py:401
  3.0 7.2 %all-to-all-start = ((bf16[8,2,4,64,128]{4,3,2,1,0:T(8,128)(2,1)}), bf16[8,2,4,64,128]{4,3,2,1,0:T(8,128)(2,1)S(1)}, u32[]{:S(2)}, u32[]{:S(2)}) async-start(bf16[8,2,4,64,128]{4,3,2,1,0:T(8,128)(2,1)} %pack.1), calls=%async_computation | async-start | bytes 2097152 | tf_op jit(solution)/shard_map/all_to_all | solution.py:388
  11.0 4.0 %collective-permute-start.2 = (bf16[64,128]{1,0:T(8,128)(2,1)S(1)}, bf16[64,128]{1,0:T(8,128)(2,1)S(1)}, u32[]{:S(2)}, u32[]{:S(2)}) collective-permute-start(bf16[64,128]{1,0:T(8,128)(2,1)S(1)} %get-tuple-element.52), channel_id=1, source_target_pairs={{0,32},{1,33},{2,34},{3,35},{4,36},{5,37},{6,38},{7,39},{8,40},{9,... | collective-permute-start | bytes 49160 | tf_op jit(solution)/shard_map/ppermute | solution.py:85
  15.7 1.3 %collective-permute-start = (bf16[64,128]{1,0:T(8,128)(2,1)S(1)}, bf16[64,128]{1,0:T(8,128)(2,1)S(1)}, u32[]{:S(2)}, u32[]{:S(2)}) collective-permute-start(bf16[64,128]{1,0:T(8,128)(2,1)S(1)} %get-tuple-element.52), channel_id=1, source_target_pairs={{0,16},{1,17},{2,18},{3,19},{4,20},{5,21},{6,22},{7,23},{8,24},{9,... | collective-permute-start | bytes 49160 | tf_op jit(solution)/shard_map/ppermute | solution.py:85
  17.1 1.5 %collective-permute-done.1 = bf16[64,128]{1,0:T(8,128)(2,1)S(1)} collective-permute-done((bf16[64,128]{1,0:T(8,128)(2,1)S(1)}, bf16[64,128]{1,0:T(8,128)(2,1)S(1)}, u32[]{:S(2)}, u32[]{:S(2)}) %collective-permute-start.1) | collective-permute-done | bytes 16416 | tf_op jit(solution)/shard_map/ppermute | solution.py:85
  18.7 1.9 %collective-permute-done = bf16[64,128]{1,0:T(8,128)(2,1)S(1)} collective-permute-done((bf16[64,128]{1,0:T(8,128)(2,1)S(1)}, bf16[64,128]{1,0:T(8,128)(2,1)S(1)}, u32[]{:S(2)}, u32[]{:S(2)}) %collective-permute-start) | collective-permute-done | bytes 16416 | tf_op jit(solution)/shard_map/ppermute | solution.py:85
  20.6 3.3 %collective-permute-start.4 = (bf16[4,64,128]{2,1,0:T(8,128)(2,1)S(1)}, bf16[4,64,128]{2,1,0:T(8,128)(2,1)S(1)}, u32[]{:S(2)}, u32[]{:S(2)}) collective-permute-start(bf16[4,64,128]{2,1,0:T(8,128)(2,1)S(1)} %get-tuple-element.99), channel_id=1, source_target_pairs={{0,6},{1,7},{2,0},{3,1},{4,2},{5,3},{6,4},{7,5},{8,14},{9,15},{10,... | collective-permute-start | bytes 196616 | tf_op jit(solution)/shard_map/ppermute | solution.py:85
  23.9 2.3 %collective-permute-start.5 = (bf16[4,64,128]{2,1,0:T(8,128)(2,1)S(1)}, bf16[4,64,128]{2,1,0:T(8,128)(2,1)S(1)}, u32[]{:S(2)}, u32[]{:S(2)}) collective-permute-start(bf16[4,64,128]{2,1,0:T(8,128)(2,1)S(1)} %get-tuple-element.99), channel_id=1, source_target_pairs={{0,4},{1,5},{2,6},{3,7},{4,0},{5,1},{6,2},{7,3},{8,12},{9,13},{10,... | collective-permute-start | bytes 196616 | tf_op jit(solution)/shard_map/ppermute | solution.py:85
  26.3 3.8 %collective-permute-done.3 = bf16[4,64,128]{2,1,0:T(8,128)(2,1)S(1)} collective-permute-done((bf16[4,64,128]{2,1,0:T(8,128)(2,1)S(1)}, bf16[4,64,128]{2,1,0:T(8,128)(2,1)S(1)}, u32[]{:S(2)}, u32[]{:S(2)}) %collective-permute-start.3) | collective-permute-done | bytes 65568 | tf_op jit(solution)/shard_map/ppermute | solution.py:85
  30.1 3.0 %collective-permute-start.8 = (bf16[16,64,128]{2,1,0:T(8,128)(2,1)S(1)}, bf16[16,64,128]{2,1,0:T(8,128)(2,1)S(1)}, u32[]{:S(2)}, u32[]{:S(2)}) collective-permute-start(bf16[16,64,128]{2,1,0:T(8,128)(2,1)S(1)} %bitcast.32), channel_id=1, source_target_pairs={{0,1},{1,0},{2,3},{3,2},{4,5},{5,4},{6,7},{7,6},{8,9},{9,8},{10,11... | collective-permute-start | bytes 786440 | tf_op jit(solution)/shard_map/ppermute | solution.py:85
  33.5 1.7 %collective-permute-start.6 = (bf16[16,64,128]{2,1,0:T(8,128)(2,1)S(1)}, bf16[16,64,128]{2,1,0:T(8,128)(2,1)S(1)}, u32[]{:S(2)}, u32[]{:S(2)}) collective-permute-start(bf16[16,64,128]{2,1,0:T(8,128)(2,1)S(1)} %bitcast.34), channel_id=1, source_target_pairs={{0,64},{1,65},{2,66},{3,67},{4,68},{5,69},{6,70},{7,71},{8,72},{9,... | collective-permute-start | bytes 786440 | tf_op jit(solution)/shard_map/ppermute | solution.py:85
  35.2 2.9 %project.1 = (bf16[4,512,128]{2,1,0:T(8,128)(2,1)S(1)}, bf16[4,512,128]{2,1,0:T(8,128)(2,1)S(1)}, bf16[4,512,128]{2,1,0:T(8,128)(2,1)S(1)}, bf16[4,512,128]{2,1,...) custom-call(s32[4]{0:T(128)S(1)} %pad_add_fusion.place_ref, ...), custom_call_target="tpu_custom_call" | custom-call | flops 5000000000 | bytes 18000000 | tf_op jit(solution)/shard_map/project/pallas_call | solution.py:414
  38.1 2.8 %collective-permute-done.8.refs_3_ = bf16[16,64,128]{2,1,0:T(8,128)(2,1)S(1)} collective-permute-done((bf16[16,64,128]{2,1,0:T(8,128)(2,1)S(1)}, bf16[16,64,128]{2,1,0:T(8,128)(2,1)S(1)}, u32[]{:S(2)}, u32[]{:S(2)}) %collective-permute-start.8) | collective-permute-done | bytes 262176 | tf_op jit(solution)/shard_map/ppermute | solution.py:85
  40.9 1.5 %collective-permute-done.7.refs_2_ = bf16[16,64,128]{2,1,0:T(8,128)(2,1)S(1)} collective-permute-done((bf16[16,64,128]{2,1,0:T(8,128)(2,1)S(1)}, bf16[16,64,128]{2,1,0:T(8,128)(2,1)S(1)}, u32[]{:S(2)}, u32[]{:S(2)}) %collective-permute-start.7) | collective-permute-done | bytes 262176 | tf_op jit(solution)/shard_map/ppermute | solution.py:85
  42.4 1.3 collective-permute-done.6.refs_1_
  46.3 18.3 %attend.1 = (bf16[4,512,128]{2,1,0:T(8,128)(2,1)S(1)}, bf16[4,512,128]{2,1,0:T(8,128)(2,1)S(1)}, bf16[4,128,512]{2,1,0:T(8,128)(2,1)S(1)}, bf16[4,128,512]{2,1,0...) custom-call(s32[4]{0:T(128)S(1)} %pad_add_fusion.place_ref, ...), custom_call_target="tpu_custom_call" | custom-call | tf_op jit(solution)/shard_map/attend/pallas_call | solution.py:431
  64.7 3.9 %post.1 = (bf16[8,2,4,64,128]{4,3,2,1,0:T(8,128)(2,1)}, bf16[64,80,128]{2,1,0:T(8,128)(2,1)S(1)}, bf16[64,80,128]{2,1,0:T(8,128)(2,1)S(1)}, f32[2,128]{1,0:T(2,128)S(1)}) custom-call(s32[4]{0:T(128)S(1)} %pad_add_fusion.place_ref, bf16[4,512,128]{2,1,0:T(8,128)(2,1)S(1)} %get-tuple-element.57.att_ref, ...), custom_call_target="tpu_custom_call", output_to_operand_aliasing={{1}: (12, {}), {2}: (13, {})} | custom-call | tf_op jit(solution)/shard_map/post/pallas_call | solution.py:449
  68.7 2.9 %collective-permute-done.13 = bf16[64,80,128]{2,1,0:T(8,128)(2,1)S(1)} collective-permute-done((bf16[64,80,128]{2,1,0:T(8,128)(2,1)S(1)}, bf16[64,80,128]{2,1,0:T(8,128)(2,1)S(1)}, u32[]{:S(2)}, u32[]{:S(2)}) %collective-permute-start.13) | collective-permute-done | bytes 1310752 | tf_op jit(solution)/shard_map/ppermute | solution.py:85
  72.7 2.4 %collective-permute-start.16 = (bf16[16,80,128]{2,1,0:T(8,128)(2,1)}, bf16[16,80,128]{2,1,0:T(8,128)(2,1)S(1)}, u32[]{:S(2)}, u32[]{:S(2)}) collective-permute-start(bf16[16,80,128]{2,1,0:T(8,128)(2,1)} %get-tuple-element.87), channel_id=1, source_target_pairs={{0,32},{1,33},{2,34},{3,35},{4,36},{5,37},{6,38},{7,39},{8,40},{9,... | collective-permute-start | bytes 983048 | tf_op jit(solution)/shard_map/ppermute | solution.py:85
  75.2 1.6 %collective-permute-start.15 = (bf16[16,80,128]{2,1,0:T(8,128)(2,1)}, bf16[16,80,128]{2,1,0:T(8,128)(2,1)S(1)}, u32[]{:S(2)}, u32[]{:S(2)}) collective-permute-start(bf16[16,80,128]{2,1,0:T(8,128)(2,1)} %get-tuple-element.88), channel_id=1, source_target_pairs={{0,48},{1,49},{2,50},{3,51},{4,52},{5,53},{6,54},{7,55},{8,56},{9,... | collective-permute-start | bytes 983048 | tf_op jit(solution)/shard_map/ppermute | solution.py:85
  77.2 5.5 %all-to-all-start.1 = ((bf16[8,2,4,64,128]{4,3,2,1,0:T(8,128)(2,1)}), bf16[8,2,4,64,128]{4,3,2,1,0:T(8,128)(2,1)S(1)}, u32[]{:S(2)}, u32[]{:S(2)}) async-start(bf16[8,2,4,64,128]{4,3,2,1,0:T(8,128)(2,1)} %get-tuple-element.67), calls=%async_computation.1 | async-start | bytes 2097152 | tf_op jit(solution)/shard_map/all_to_all | solution.py:388
  82.7 2.3 %collective-permute-done.16 = bf16[16,80,128]{2,1,0:T(8,128)(2,1)S(1)} collective-permute-done((bf16[16,80,128]{2,1,0:T(8,128)(2,1)}, bf16[16,80,128]{2,1,0:T(8,128)(2,1)S(1)}, u32[]{:S(2)}, u32[]{:S(2)}) %collective-permute-start.16) | collective-permute-done | bytes 327712 | tf_op jit(solution)/shard_map/ppermute | solution.py:85
  85.1 6.1 %collective-permute-done.15 = bf16[16,80,128]{2,1,0:T(8,128)(2,1)S(1)} collective-permute-done((bf16[16,80,128]{2,1,0:T(8,128)(2,1)}, bf16[16,80,128]{2,1,0:T(8,128)(2,1)S(1)}, u32[]{:S(2)}, u32[]{:S(2)}) %collective-permute-start.15) | collective-permute-done | bytes 327712 | tf_op jit(solution)/shard_map/ppermute | solution.py:85
  92.6 3.5 %collective-permute-start.18 = (bf16[4,80,128]{2,1,0:T(8,128)(2,1)S(1)}, bf16[4,80,128]{2,1,0:T(8,128)(2,1)S(1)}, u32[]{:S(2)}, u32[]{:S(2)}) collective-permute-start(bf16[4,80,128]{2,1,0:T(8,128)(2,1)S(1)} %get-tuple-element.92), channel_id=1, source_target_pairs={{0,6},{1,7},{2,0},{3,1},{4,2},{5,3},{6,4},{7,5},{8,14},{9,15},{10,... | collective-permute-start | bytes 245768 | tf_op jit(solution)/shard_map/ppermute | solution.py:85
  96.0 4.2 %collective-permute-done.19 = bf16[4,80,128]{2,1,0:T(8,128)(2,1)S(1)} collective-permute-done((bf16[4,80,128]{2,1,0:T(8,128)(2,1)S(1)}, bf16[4,80,128]{2,1,0:T(8,128)(2,1)S(1)}, u32[]{:S(2)}, u32[]{:S(2)}) %collective-permute-start.19) | collective-permute-done | bytes 81952 | tf_op jit(solution)/shard_map/ppermute | solution.py:85
  100.3 1.5 %collective-permute-done.17 = bf16[4,80,128]{2,1,0:T(8,128)(2,1)S(1)} collective-permute-done((bf16[4,80,128]{2,1,0:T(8,128)(2,1)S(1)}, bf16[4,80,128]{2,1,0:T(8,128)(2,1)S(1)}, u32[]{:S(2)}, u32[]{:S(2)}) %collective-permute-start.17) | collective-permute-done | bytes 81952 | tf_op jit(solution)/shard_map/ppermute | solution.py:85
  101.8 2.9 %collective-permute-start.22 = (bf16[80,128]{1,0:T(8,128)(2,1)S(1)}, bf16[80,128]{1,0:T(8,128)(2,1)S(1)}, u32[]{:S(2)}, u32[]{:S(2)}) collective-permute-start(bf16[80,128]{1,0:T(8,128)(2,1)S(1)} %get-tuple-element.94), channel_id=1, source_target_pairs={{0,1},{1,0},{2,3},{3,2},{4,5},{5,4},{6,7},{7,6},{8,9},{9,8},{10,11... | collective-permute-start | bytes 61448 | tf_op jit(solution)/shard_map/ppermute | solution.py:85
  108.5 2.4 %collective-permute-done.20.two_ref = bf16[80,128]{1,0:T(8,128)(2,1)S(1)} collective-permute-done((bf16[80,128]{1,0:T(8,128)(2,1)S(1)}, bf16[80,128]{1,0:T(8,128)(2,1)S(1)}, u32[]{:S(2)}, u32[]{:S(2)}) %collective-permute-start.20) | collective-permute-done | bytes 20512 | tf_op jit(solution)/shard_map/ppermute | solution.py:85
  110.9 1.2 tile_sums.1
  112.2 4.6 %all-to-all-start.2 = ((bf16[128,16,128]{2,1,0:T(8,128)(2,1)}), bf16[128,16,128]{2,1,0:T(8,128)(2,1)S(1)}, u32[]{:S(2)}, u32[]{:S(2)}) async-start(bf16[128,16,128]{2,1,0:T(8,128)(2,1)} %get-tuple-element.77), calls=%async_computation.2 | async-start | bytes 1048576 | tf_op jit(solution)/shard_map/all_to_all | solution.py:388
  116.8 2.4 %tile_final.1 = (bf16[2048,128]{1,0:T(8,128)(2,1)}, bf16[2048,128]{1,0:T(8,128)(2,1)}) custom-call(bf16[2048,128]{1,0:T(8,128)(2,1)S(1)} %bitcast.40, bf16[8,2,256,128]{3,2,1,0:T(8,128)(2,1)S(1)} %bitcast.36, bf16[16,2048]{1,0:T(8,128)(2,1)S(1)} %get-tuple-element.74.both_ref, f32[1,128]{1,0:T(1,128)S(1)} %bitcast.46, ...), custom_call_target="tpu_custom_call" | custom-call | flops 5000000000 | bytes 18000000 | tf_op jit(solution)/shard_map/tile_final/pallas_call | solution.py:481
  119.1 11.0 %all-to-all-done.2.msg_ref = bf16[128,16,128]{2,1,0:T(8,128)(2,1)S(1)} async-done(((bf16[128,16,128]{2,1,0:T(8,128)(2,1)}), bf16[128,16,128]{2,1,0:T(8,128)(2,1)S(1)}, u32[]{:S(2)}, u32[]{:S(2)}) %all-to-all-start.2) | async-done | bytes 524320 | tf_op jit(solution)/shard_map/all_to_all | solution.py:388
  (58 shorter events, 12.6 us)
Async XLA Ops:
  2.9 14.1 %copy-start.5 = (bf16[128,128]{1,0:T(8,128)(2,1)S(1)}, bf16[128,128]{1,0:T(8,128)(2,1)}, u32[]{:S(2)}) copy-start(bf16[128,128]{1,0:T(8,128)(2,1)} %param.13) | copy-start | bytes 98308
  2.9 14.1 %copy-start.6 = (bf16[128,128]{1,0:T(8,128)(2,1)S(1)}, bf16[128,128]{1,0:T(8,128)(2,1)}, u32[]{:S(2)}) copy-start(bf16[128,128]{1,0:T(8,128)(2,1)} %param.14) | copy-start | bytes 98308
  2.9 14.1 %copy-start.7 = (bf16[128,128]{1,0:T(8,128)(2,1)S(1)}, bf16[128,128]{1,0:T(8,128)(2,1)}, u32[]{:S(2)}) copy-start(bf16[128,128]{1,0:T(8,128)(2,1)} %param.15) | copy-start | bytes 98308
  2.9 14.1 %copy-start.8 = (bf16[128,128]{1,0:T(8,128)(2,1)S(1)}, bf16[128,128]{1,0:T(8,128)(2,1)}, u32[]{:S(2)}) copy-start(bf16[128,128]{1,0:T(8,128)(2,1)} %param.16) | copy-start | bytes 98308
  3.0 32.3 %all-to-all-start = ((bf16[8,2,4,64,128]{4,3,2,1,0:T(8,128)(2,1)}), bf16[8,2,4,64,128]{4,3,2,1,0:T(8,128)(2,1)S(1)}, u32[]{:S(2)}, u32[]{:S(2)}) async-start(bf16[8,2,4,64,128]{4,3,2,1,0:T(8,128)(2,1)} %pack.1), calls=%async_computation | async-start | bytes 2097152 | tf_op jit(solution)/shard_map/all_to_all | solution.py:388
  10.1 25.1 %copy-start.1 = (bf16[128,128]{1,0:T(8,128)(2,1)S(1)}, bf16[128,128]{1,0:T(8,128)(2,1)}, u32[]{:S(2)}) copy-start(bf16[128,128]{1,0:T(8,128)(2,1)} %wout_ref.3) | copy-start | bytes 98308
  10.1 25.1 %copy-start.4 = (f32[128]{0:T(128)S(1)}, f32[128]{0:T(128)}, u32[]{:S(2)}) copy-start(f32[128]{0:T(128)} %param.17) | copy-start | bytes 1540
  11.0 6.1 %collective-permute-start.2 = (bf16[64,128]{1,0:T(8,128)(2,1)S(1)}, bf16[64,128]{1,0:T(8,128)(2,1)S(1)}, u32[]{:S(2)}, u32[]{:S(2)}) collective-permute-start(bf16[64,128]{1,0:T(8,128)(2,1)S(1)} %get-tuple-element.52), channel_id=1, source_target_pairs={{0,32},{1,33},{2,34},{3,35},{4,36},{5,37},{6,38},{7,39},{8,40},{9,... | collective-permute-start | bytes 49160 | tf_op jit(solution)/shard_map/ppermute | solution.py:85
  14.9 3.7 %collective-permute-start.1 = (bf16[64,128]{1,0:T(8,128)(2,1)S(1)}, bf16[64,128]{1,0:T(8,128)(2,1)S(1)}, u32[]{:S(2)}, u32[]{:S(2)}) collective-permute-start(bf16[64,128]{1,0:T(8,128)(2,1)S(1)} %get-tuple-element.52), channel_id=1, source_target_pairs={{0,48},{1,49},{2,50},{3,51},{4,52},{5,53},{6,54},{7,55},{8,56},{9,... | collective-permute-start | bytes 49160 | tf_op jit(solution)/shard_map/ppermute | solution.py:85
  15.7 4.9 %collective-permute-start = (bf16[64,128]{1,0:T(8,128)(2,1)S(1)}, bf16[64,128]{1,0:T(8,128)(2,1)S(1)}, u32[]{:S(2)}, u32[]{:S(2)}) collective-permute-start(bf16[64,128]{1,0:T(8,128)(2,1)S(1)} %get-tuple-element.52), channel_id=1, source_target_pairs={{0,16},{1,17},{2,18},{3,19},{4,20},{5,21},{6,22},{7,23},{8,24},{9,... | collective-permute-start | bytes 49160 | tf_op jit(solution)/shard_map/ppermute | solution.py:85
  20.6 5.7 %collective-permute-start.4 = (bf16[4,64,128]{2,1,0:T(8,128)(2,1)S(1)}, bf16[4,64,128]{2,1,0:T(8,128)(2,1)S(1)}, u32[]{:S(2)}, u32[]{:S(2)}) collective-permute-start(bf16[4,64,128]{2,1,0:T(8,128)(2,1)S(1)} %get-tuple-element.99), channel_id=1, source_target_pairs={{0,6},{1,7},{2,0},{3,1},{4,2},{5,3},{6,4},{7,5},{8,14},{9,15},{10,... | collective-permute-start | bytes 196616 | tf_op jit(solution)/shard_map/ppermute | solution.py:85
  23.9 6.2 %collective-permute-start.3 = (bf16[4,64,128]{2,1,0:T(8,128)(2,1)S(1)}, bf16[4,64,128]{2,1,0:T(8,128)(2,1)S(1)}, u32[]{:S(2)}, u32[]{:S(2)}) collective-permute-start(bf16[4,64,128]{2,1,0:T(8,128)(2,1)S(1)} %get-tuple-element.99), channel_id=1, source_target_pairs={{0,2},{1,3},{2,4},{3,5},{4,6},{5,7},{6,0},{7,1},{8,10},{9,11},{10,... | collective-permute-start | bytes 196616 | tf_op jit(solution)/shard_map/ppermute | solution.py:85
  23.9 6.2 %collective-permute-start.5 = (bf16[4,64,128]{2,1,0:T(8,128)(2,1)S(1)}, bf16[4,64,128]{2,1,0:T(8,128)(2,1)S(1)}, u32[]{:S(2)}, u32[]{:S(2)}) collective-permute-start(bf16[4,64,128]{2,1,0:T(8,128)(2,1)S(1)} %get-tuple-element.99), channel_id=1, source_target_pairs={{0,4},{1,5},{2,6},{3,7},{4,0},{5,1},{6,2},{7,3},{8,12},{9,13},{10,... | collective-permute-start | bytes 196616 | tf_op jit(solution)/shard_map/ppermute | solution.py:85
  30.1 10.7 %collective-permute-start.8 = (bf16[16,64,128]{2,1,0:T(8,128)(2,1)S(1)}, bf16[16,64,128]{2,1,0:T(8,128)(2,1)S(1)}, u32[]{:S(2)}, u32[]{:S(2)}) collective-permute-start(bf16[16,64,128]{2,1,0:T(8,128)(2,1)S(1)} %bitcast.32), channel_id=1, source_target_pairs={{0,1},{1,0},{2,3},{3,2},{4,5},{5,4},{6,7},{7,6},{8,9},{9,8},{10,11... | collective-permute-start | bytes 786440 | tf_op jit(solution)/shard_map/ppermute | solution.py:85
  33.2 9.2 %collective-permute-start.7 = (bf16[16,64,128]{2,1,0:T(8,128)(2,1)S(1)}, bf16[16,64,128]{2,1,0:T(8,128)(2,1)S(1)}, u32[]{:S(2)}, u32[]{:S(2)}) collective-permute-start(bf16[16,64,128]{2,1,0:T(8,128)(2,1)S(1)} %bitcast.33), channel_id=1, source_target_pairs={{0,65},{1,64},{2,67},{3,66},{4,69},{5,68},{6,71},{7,70},{8,73},{9,... | collective-permute-start | bytes 786440 | tf_op jit(solution)/shard_map/ppermute | solution.py:85
  33.5 10.2 %collective-permute-start.6 = (bf16[16,64,128]{2,1,0:T(8,128)(2,1)S(1)}, bf16[16,64,128]{2,1,0:T(8,128)(2,1)S(1)}, u32[]{:S(2)}, u32[]{:S(2)}) collective-permute-start(bf16[16,64,128]{2,1,0:T(8,128)(2,1)S(1)} %bitcast.34), channel_id=1, source_target_pairs={{0,64},{1,65},{2,66},{3,67},{4,68},{5,69},{6,70},{7,71},{8,72},{9,... | collective-permute-start | bytes 786440 | tf_op jit(solution)/shard_map/ppermute | solution.py:85
  43.7 1.5 %collective-permute-start.9 = (bf16[16,64,128]{2,1,0:T(8,128)(2,1)S(1)}, bf16[16,64,128]{2,1,0:T(8,128)(2,1)S(1)}, u32[]{:S(2)}, u32[]{:S(2)}) collective-permute-start(bf16[16,64,128]{2,1,0:T(8,128)(2,1)S(1)} %get-tuple-element.53.refs_0_), channel_id=1, source_target_pairs={{0,8},{1,9},{2,10},{3,11},{4,12},{5,13},{6,14},{7,15},{8,0},{9,1},... | collective-permute-start | bytes 786440 | tf_op jit(solution)/shard_map/ppermute | solution.py:85
  43.7 1.9 %collective-permute-start.10 = (bf16[16,64,128]{2,1,0:T(8,128)(2,1)S(1)}, bf16[16,64,128]{2,1,0:T(8,128)(2,1)S(1)}, u32[]{:S(2)}, u32[]{:S(2)}) collective-permute-start(bf16[16,64,128]{2,1,0:T(8,128)(2,1)S(1)} %get-tuple-element.54.refs_1_), channel_id=1, source_target_pairs={{0,8},{1,9},{2,10},{3,11},{4,12},{5,13},{6,14},{7,15},{8,0},{9,1},... | collective-permute-start | bytes 786440 | tf_op jit(solution)/shard_map/ppermute | solution.py:85
  44.2 1.8 %collective-permute-start.11 = (bf16[16,64,128]{2,1,0:T(8,128)(2,1)S(1)}, bf16[16,64,128]{2,1,0:T(8,128)(2,1)S(1)}, u32[]{:S(2)}, u32[]{:S(2)}) collective-permute-start(bf16[16,64,128]{2,1,0:T(8,128)(2,1)S(1)} %get-tuple-element.55.refs_2_), channel_id=1, source_target_pairs={{0,8},{1,9},{2,10},{3,11},{4,12},{5,13},{6,14},{7,15},{8,0},{9,1},... | collective-permute-start | bytes 786440 | tf_op jit(solution)/shard_map/ppermute | solution.py:85
  44.2 2.1 %collective-permute-start.12 = (bf16[16,64,128]{2,1,0:T(8,128)(2,1)S(1)}, bf16[16,64,128]{2,1,0:T(8,128)(2,1)S(1)}, u32[]{:S(2)}, u32[]{:S(2)}) collective-permute-start(bf16[16,64,128]{2,1,0:T(8,128)(2,1)S(1)} %get-tuple-element.56.refs_3_), channel_id=1, source_target_pairs={{0,8},{1,9},{2,10},{3,11},{4,12},{5,13},{6,14},{7,15},{8,0},{9,1},... | collective-permute-start | bytes 786440 | tf_op jit(solution)/shard_map/ppermute | solution.py:85
  68.5 3.0 %collective-permute-start.13 = (bf16[64,80,128]{2,1,0:T(8,128)(2,1)S(1)}, bf16[64,80,128]{2,1,0:T(8,128)(2,1)S(1)}, u32[]{:S(2)}, u32[]{:S(2)}) collective-permute-start(bf16[64,80,128]{2,1,0:T(8,128)(2,1)S(1)} %get-tuple-element.72), channel_id=1, source_target_pairs={{0,8},{1,9},{2,10},{3,11},{4,12},{5,13},{6,14},{7,15},{8,0},{9,1},... | collective-permute-start | bytes 3932168 | tf_op jit(solution)/shard_map/ppermute | solution.py:85
  72.7 12.3 %collective-permute-start.16 = (bf16[16,80,128]{2,1,0:T(8,128)(2,1)}, bf16[16,80,128]{2,1,0:T(8,128)(2,1)S(1)}, u32[]{:S(2)}, u32[]{:S(2)}) collective-permute-start(bf16[16,80,128]{2,1,0:T(8,128)(2,1)} %get-tuple-element.87), channel_id=1, source_target_pairs={{0,32},{1,33},{2,34},{3,35},{4,36},{5,37},{6,38},{7,39},{8,40},{9,... | collective-permute-start | bytes 983048 | tf_op jit(solution)/shard_map/ppermute | solution.py:85
  75.2 16.0 %collective-permute-start.15 = (bf16[16,80,128]{2,1,0:T(8,128)(2,1)}, bf16[16,80,128]{2,1,0:T(8,128)(2,1)S(1)}, u32[]{:S(2)}, u32[]{:S(2)}) collective-permute-start(bf16[16,80,128]{2,1,0:T(8,128)(2,1)} %get-tuple-element.88), channel_id=1, source_target_pairs={{0,48},{1,49},{2,50},{3,51},{4,52},{5,53},{6,54},{7,55},{8,56},{9,... | collective-permute-start | bytes 983048 | tf_op jit(solution)/shard_map/ppermute | solution.py:85
  76.8 14.5 %collective-permute-start.14 = (bf16[16,80,128]{2,1,0:T(8,128)(2,1)S(1)}, bf16[16,80,128]{2,1,0:T(8,128)(2,1)S(1)}, u32[]{:S(2)}, u32[]{:S(2)}) collective-permute-start(bf16[16,80,128]{2,1,0:T(8,128)(2,1)S(1)} %get-tuple-element.89), channel_id=1, source_target_pairs={{0,16},{1,17},{2,18},{3,19},{4,20},{5,21},{6,22},{7,23},{8,24},{9,... | collective-permute-start | bytes 983048 | tf_op jit(solution)/shard_map/ppermute | solution.py:85
  77.2 35.0 %all-to-all-start.1 = ((bf16[8,2,4,64,128]{4,3,2,1,0:T(8,128)(2,1)}), bf16[8,2,4,64,128]{4,3,2,1,0:T(8,128)(2,1)S(1)}, u32[]{:S(2)}, u32[]{:S(2)}) async-start(bf16[8,2,4,64,128]{4,3,2,1,0:T(8,128)(2,1)} %get-tuple-element.67), calls=%async_computation.1 | async-start | bytes 2097152 | tf_op jit(solution)/shard_map/all_to_all | solution.py:388
  91.4 8.8 %collective-permute-start.19 = (bf16[4,80,128]{2,1,0:T(8,128)(2,1)S(1)}, bf16[4,80,128]{2,1,0:T(8,128)(2,1)S(1)}, u32[]{:S(2)}, u32[]{:S(2)}) collective-permute-start(bf16[4,80,128]{2,1,0:T(8,128)(2,1)S(1)} %get-tuple-element.91), channel_id=1, source_target_pairs={{0,4},{1,5},{2,6},{3,7},{4,0},{5,1},{6,2},{7,3},{8,12},{9,13},{10,... | collective-permute-start | bytes 245768 | tf_op jit(solution)/shard_map/ppermute | solution.py:85
  92.6 7.7 %collective-permute-start.18 = (bf16[4,80,128]{2,1,0:T(8,128)(2,1)S(1)}, bf16[4,80,128]{2,1,0:T(8,128)(2,1)S(1)}, u32[]{:S(2)}, u32[]{:S(2)}) collective-permute-start(bf16[4,80,128]{2,1,0:T(8,128)(2,1)S(1)} %get-tuple-element.92), channel_id=1, source_target_pairs={{0,6},{1,7},{2,0},{3,1},{4,2},{5,3},{6,4},{7,5},{8,14},{9,15},{10,... | collective-permute-start | bytes 245768 | tf_op jit(solution)/shard_map/ppermute | solution.py:85
  96.0 5.7 %collective-permute-start.17 = (bf16[4,80,128]{2,1,0:T(8,128)(2,1)S(1)}, bf16[4,80,128]{2,1,0:T(8,128)(2,1)S(1)}, u32[]{:S(2)}, u32[]{:S(2)}) collective-permute-start(bf16[4,80,128]{2,1,0:T(8,128)(2,1)S(1)} %get-tuple-element.93), channel_id=1, source_target_pairs={{0,2},{1,3},{2,4},{3,5},{4,6},{5,7},{6,0},{7,1},{8,10},{9,11},{10,... | collective-permute-start | bytes 245768 | tf_op jit(solution)/shard_map/ppermute | solution.py:85
  101.8 5.6 %collective-permute-start.22 = (bf16[80,128]{1,0:T(8,128)(2,1)S(1)}, bf16[80,128]{1,0:T(8,128)(2,1)S(1)}, u32[]{:S(2)}, u32[]{:S(2)}) collective-permute-start(bf16[80,128]{1,0:T(8,128)(2,1)S(1)} %get-tuple-element.94), channel_id=1, source_target_pairs={{0,1},{1,0},{2,3},{3,2},{4,5},{5,4},{6,7},{7,6},{8,9},{9,8},{10,11... | collective-permute-start | bytes 61448 | tf_op jit(solution)/shard_map/ppermute | solution.py:85
  104.7 3.8 %collective-permute-start.21 = (bf16[80,128]{1,0:T(8,128)(2,1)S(1)}, bf16[80,128]{1,0:T(8,128)(2,1)S(1)}, u32[]{:S(2)}, u32[]{:S(2)}) collective-permute-start(bf16[80,128]{1,0:T(8,128)(2,1)S(1)} %get-tuple-element.95), channel_id=1, source_target_pairs={{0,65},{1,64},{2,67},{3,66},{4,69},{5,68},{6,71},{7,70},{8,73},{9,... | collective-permute-start | bytes 61448 | tf_op jit(solution)/shard_map/ppermute | solution.py:85
  105.9 5.0 %collective-permute-start.20 = (bf16[80,128]{1,0:T(8,128)(2,1)S(1)}, bf16[80,128]{1,0:T(8,128)(2,1)S(1)}, u32[]{:S(2)}, u32[]{:S(2)}) collective-permute-start(bf16[80,128]{1,0:T(8,128)(2,1)S(1)} %get-tuple-element.96), channel_id=1, source_target_pairs={{0,64},{1,65},{2,66},{3,67},{4,68},{5,69},{6,70},{7,71},{8,72},{9,... | collective-permute-start | bytes 61448 | tf_op jit(solution)/shard_map/ppermute | solution.py:85
  112.2 18.0 %all-to-all-start.2 = ((bf16[128,16,128]{2,1,0:T(8,128)(2,1)}), bf16[128,16,128]{2,1,0:T(8,128)(2,1)S(1)}, u32[]{:S(2)}, u32[]{:S(2)}) async-start(bf16[128,16,128]{2,1,0:T(8,128)(2,1)} %get-tuple-element.77), calls=%async_computation.2 | async-start | bytes 1048576 | tf_op jit(solution)/shard_map/all_to_all | solution.py:388
  (3 other events, 21.7 us)
